TPU v7x, 32 devices: a whole 2x2x4 slice. The times are simulated.
32 devices in a mesh: ctx: 8 (over z, y), fsdp: 4 (over x, core).
Axes of the slice: x: 2, y: 2, z: 4, core: 2. Of those that a mesh axis runs over, the one named last changes fastest.
Arguments:
- sig_raw: bfloat16 [1024, 8192], P('ctx', 'fsdp'), may hold values from -6 to 6
- map_raw: bfloat16 [1024, 2048], P('ctx'), may hold values from -1.796875 to 1.796875
- step_size_logits: float32 [1024, 128], P('ctx', 'fsdp'), may hold values from -5.4 to 21.5
- d_out: bfloat16 [1024, 8192], P('ctx', 'fsdp'), may hold values from -6 to 6
- sig_taps: float32 [4, 8192], P(None, 'fsdp'), may hold values from -3 to 3
- map_taps: float32 [4, 2048], P(None, 'fsdp'), may hold values from -3 to 3
- sig_bias: float32 [8192], P('fsdp'), may hold values from -3 to 3
- map_bias: float32 [2048], P('fsdp'), may hold values from -0.6 to 0.6
- a_log: float32 [128], P('fsdp'), as said below
- dt_bias: float32 [128], P('fsdp'), may hold values from -5 to -4.2
- skip_gain: float32 [128], P('fsdp'), may hold values from 0.1 to 3
Outputs:
- d_sig: float32 [1024, 8192], P('ctx', 'fsdp')
- d_map: float32 [1024, 2048], P('ctx', 'fsdp')
- d_dt: float32 [1024, 128], P('ctx', 'fsdp')
- d_sig_taps: float32 [4, 8192], P(None, 'fsdp')
- d_map_taps: float32 [4, 2048], P(None, 'fsdp')
- d_sig_bias: float32 [8192], P('fsdp')
- d_map_bias: float32 [2048], P('fsdp')
- d_a_log: float32 [128], P('fsdp')
- scaled_timestep_shift_grad: float32 [128], P('fsdp')
- d_skip: float32 [128], P('fsdp')
Inputs may be any that keep to these rules, and one draw needn't show every extreme that they name: Each head's rate exp(a_log) lies either between 2 and 4 or between 30 / 1024 and 200 / 1024.
All inputs are finite; a program needn't handle non-finite values.
Results may differ from a plain program's by a relative error of at most 0.0066.
Values may be sent and summed in bfloat16 or wider, within the bound.
No kernel may reach another device: no remote copies, remote signals or barrier semaphores. Data moves between devices by JAX's collectives and lax.ppermute only.
A program may use at most 128 MiB of HBM per device.

v0:
```python
import math

import jax
import jax.numpy as jnp
from jax import lax
from jax.sharding import PartitionSpec as P

HEADS = 128
HDIM = 64
STATE = 128
GROUPS = 8


def prefix(part, axis, combine, identity, reverse):
    count = lax.axis_size(axis)
    place = lax.axis_index(axis)
    ahead = count - 1 - place if reverse else place
    gathered = jax.tree.map(lambda a: lax.all_gather(a, axis), part)
    state = jax.tree.map(lambda a, e: jnp.zeros_like(a) + jnp.asarray(e, a.dtype), part, identity)

    def one(lap, state):
        source = count - 1 - lap if reverse else lap
        return combine(
            state, jax.tree.map(lambda a: lax.dynamic_index_in_dim(a, source, 0, False), gathered)
        )

    return lax.fori_loop(0, ahead, one, state)


def broadcast(x, axis, root):
    mine = lax.axis_index(axis) == root
    return lax.psum(jnp.where(mine, x, jnp.zeros_like(x)), axis)


def extended(block, sides, width):
    for axis, dim in sides:
        count = lax.axis_size(axis)
        forward = [(i, i + 1) for i in range(count - 1)]
        backward = [(target, source) for source, target in forward]
        low = lax.ppermute(
            lax.slice_in_dim(block, block.shape[dim] - width, None, axis=dim), axis, forward
        )
        high = lax.ppermute(lax.slice_in_dim(block, 0, width, axis=dim), axis, backward)
        block = jnp.concatenate([low, block, high], axis=dim)
    return block


def ein(form, left, right):
    return jnp.einsum(form, left, right, preferred_element_type=jnp.float32)


def silu_slope(value):
    sig = jax.nn.sigmoid(value)
    return sig * (1.0 + value * (1.0 - sig))


def block_parts(activated, dt_rows, a_log, dt_bias, groups):
    length = activated.shape[0]
    heads = dt_rows.shape[1]
    inner = heads * HDIM
    shared = groups * STATE
    ratio = heads // groups
    signal = activated[:, :inner].reshape(length, heads, HDIM)
    input_map = activated[:, inner : inner + shared].reshape(length, groups, STATE)
    output_map = activated[:, inner + shared :].reshape(length, groups, STATE)
    input_heads = jnp.repeat(input_map, ratio, axis=1)
    output_heads = jnp.repeat(output_map, ratio, axis=1)
    step = jax.nn.softplus(dt_rows + dt_bias)
    rate = -jnp.exp(a_log)
    row_ids = lax.broadcasted_iota(jnp.int32, (length, length), 0)
    col_ids = lax.broadcasted_iota(jnp.int32, (length, length), 1)
    lower = (row_ids >= col_ids).astype(jnp.float32)
    decay_sum = jnp.dot(lower, step * rate, precision=lax.Precision.HIGHEST)
    to_end = jnp.exp(decay_sum[-1][None, :] - decay_sum)
    scaled = (signal.astype(jnp.float32) * step[:, :, None]).astype(jnp.bfloat16)
    weighted = (scaled.astype(jnp.float32) * to_end[:, :, None]).astype(jnp.bfloat16)
    local = ein("qhp,qhn->hpn", weighted, input_heads)
    return (
        signal,
        input_map,
        output_map,
        input_heads,
        output_heads,
        step,
        rate,
        lower,
        decay_sum,
        scaled,
        to_end,
        weighted,
        local,
    )


def entry_grad(parts, d_rows):
    decay_sum = parts[8]
    output_heads = parts[4]
    scaled_grad = (d_rows.astype(jnp.float32) * jnp.exp(decay_sum)[:, :, None]).astype(jnp.bfloat16)
    return (scaled_grad, ein("thp,thn->hpn", scaled_grad, output_heads))


def block_grads(parts, d_rows, scaled_grad, h_in, carried, skip_gain, dt_rows, dt_bias):
    (
        signal,
        input_map,
        output_map,
        input_heads,
        output_heads,
        step,
        rate,
        lower,
        decay_sum,
        scaled,
        to_end,
        weighted,
        local,
    ) = parts
    length = d_rows.shape[0]
    heads = d_rows.shape[1]
    groups = input_map.shape[1]
    width_state = input_map.shape[2]
    ratio = heads // groups
    grad_f = d_rows.astype(jnp.float32)
    signal_f = signal.astype(jnp.float32)
    grad_skip = jnp.sum(grad_f * signal_f, axis=(0, 2))
    h_low = h_in.astype(jnp.bfloat16)
    carried_low = carried.astype(jnp.bfloat16)
    offset = jnp.exp(decay_sum)[:, :, None] * ein("thn,hpn->thp", output_heads, h_low)
    grad_sum = jnp.sum(grad_f * offset, axis=2)
    out_heads_grad = ein("thp,hpn->thn", scaled_grad, h_low)
    grad_weighted = ein("shn,hpn->shp", input_heads, carried_low)
    in_heads_grad = ein("shp,hpn->shn", weighted, carried_low)
    back = jnp.sum(grad_weighted * scaled.astype(jnp.float32), axis=2) * to_end
    end_term = jnp.exp(decay_sum[-1]) * jnp.sum(h_in * carried, axis=(1, 2))
    last_row = (lax.broadcasted_iota(jnp.int32, (length, 1), 0) == length - 1).astype(jnp.float32)
    grad_sum = grad_sum - back + last_row * (jnp.sum(back, axis=0) + end_term)[None, :]
    spread = decay_sum.T[:, :, None] - decay_sum.T[:, None, :]
    decay = jnp.where(lower[None] > 0, jnp.exp(jnp.minimum(spread, 0.0)), 0.0)
    score = ein("tgn,sgn->gts", output_map, input_map)
    mix = jnp.repeat(score, ratio, axis=0) * decay
    grad_mix = ein("thp,shp->hts", d_rows, scaled)
    grad_scaled = grad_weighted * to_end[:, :, None] + ein(
        "hts,thp->shp", mix.astype(jnp.bfloat16), d_rows
    )
    product = grad_mix * mix
    grad_sum = grad_sum + (jnp.sum(product, axis=2) - jnp.sum(product, axis=1)).T
    grad_score = jnp.sum((grad_mix * decay).reshape(groups, ratio, length, length), axis=1).astype(
        jnp.bfloat16
    )
    grad_outmap = ein("gts,sgn->tgn", grad_score, input_map) + jnp.sum(
        out_heads_grad.reshape(length, groups, ratio, width_state), axis=2
    )
    grad_in = ein("gts,tgn->sgn", grad_score, output_map) + jnp.sum(
        in_heads_grad.reshape(length, groups, ratio, width_state), axis=2
    )
    grad_log = jnp.dot(lower.T, grad_sum, precision=lax.Precision.HIGHEST)
    descent_increment = grad_log * rate + jnp.sum(grad_scaled * signal_f, axis=2)
    grad_signal = skip_gain[None, :, None] * grad_f + grad_scaled * step[:, :, None]
    grad_dt = descent_increment * jax.nn.sigmoid(dt_rows + dt_bias)
    decay_log_gradient = jnp.sum(grad_log * step, axis=0) * rate
    grad_act = jnp.concatenate(
        [
            grad_signal.reshape(length, heads * HDIM),
            grad_in.reshape(length, groups * width_state),
            grad_outmap.reshape(length, groups * width_state),
        ],
        axis=1,
    )
    return (grad_act, grad_dt, decay_log_gradient, jnp.sum(grad_dt, axis=0), grad_skip)


def link(earlier, later):
    return (earlier[0] + later[0], jnp.exp(later[0])[:, None, None] * earlier[1] + later[1])


def link_blocks(lower_pair, upper_pair):
    zero_rate = jnp.zeros_like(lower_pair[0])
    zero_state = jnp.zeros_like(lower_pair[1])
    below = prefix(lower_pair, "ctx", link, (zero_rate, zero_state), False)
    beyond = prefix(upper_pair, "ctx", link, (zero_rate, zero_state), True)
    total = jax.tree.map(
        lambda part: broadcast(part, "ctx", lax.axis_size("ctx") - 1), link(below, lower_pair)
    )
    return jnp.stack([below[1], link(total, beyond)[1]])


def conv_back(grad_pre, wide_grad, kernel_taps, padded, at_end, length):
    rim = kernel_taps.shape[0] - 1
    after = jnp.stack(
        [jnp.where(at_end, grad_pre[1, :rim], wide_grad[3 * rim : 4 * rim]), wide_grad[0:rim]]
    )
    padded_next = jnp.concatenate([grad_pre, after], axis=1)
    grad_raw = jnp.zeros(grad_pre.shape, jnp.float32)
    for tap in range(rim + 1):
        grad_raw = (
            grad_raw
            + kernel_taps[tap][None, None, :] * padded_next[:, rim - tap : rim - tap + length]
        )
    tap_grads = jnp.stack(
        [jnp.sum(grad_pre * padded[:, tap : tap + length], axis=(0, 1)) for tap in range(rim + 1)]
    )
    return (grad_raw, tap_grads, jnp.sum(grad_pre, axis=(0, 1)))


def first_rows(grad_pre, rim):
    return jnp.concatenate([grad_pre[0, :rim], grad_pre[1, :rim]], axis=0)


def shards(
    sig_raw,
    map_raw,
    step_size_logits,
    d_out,
    sig_taps,
    map_taps,
    sig_bias,
    map_bias,
    a_log,
    dt_bias,
    skip_gain,
):
    all_map_taps, all_map_bias = (
        lax.all_gather(map_taps, "fsdp", axis=1, tiled=True),
        lax.all_gather(map_bias, "fsdp", axis=0, tiled=True),
    )
    kernel_taps = jnp.concatenate([sig_taps, all_map_taps], axis=1)
    kernel_bias = jnp.concatenate([sig_bias, all_map_bias], axis=0)
    kernel = kernel_taps.shape[0]
    rim = kernel - 1
    length = sig_raw.shape[0] // 2
    sig_width = sig_raw.shape[1]
    map_width = map_raw.shape[1]
    width = sig_width + map_width
    heads_here = step_size_logits.shape[1]
    ratio = HEADS // GROUPS
    group_count = max(1, heads_here // ratio)
    first_group = lax.axis_index("fsdp") * heads_here // ratio
    fsdp_count = lax.axis_size("fsdp")
    owned = map_width // fsdp_count
    map_start = lax.axis_index("fsdp") * owned
    raw_rows = jnp.concatenate([sig_raw, map_raw], axis=1).reshape(2, length, width)
    tails = jnp.concatenate([raw_rows[1, length - rim :], raw_rows[0, length - rim :]], axis=0)
    wide = extended(tails, (("ctx", 0),), rim)
    at_end = lax.axis_index("ctx") == lax.axis_size("ctx") - 1
    before = jnp.stack(
        [wide[0:rim], jnp.where(at_end, raw_rows[0, length - rim :], wide[3 * rim : 4 * rim])]
    )
    padded = jnp.concatenate([before, raw_rows], axis=1).astype(jnp.float32)
    preact = kernel_bias[None, None, :] + jnp.zeros((2, length, width), jnp.float32)
    for tap in range(kernel):
        preact = preact + kernel_taps[tap][None, None, :] * padded[:, tap : tap + length]
    activated = jax.nn.silu(preact).astype(jnp.bfloat16)
    maps_all = activated[:, :, sig_width:].reshape(2, length, 2, GROUPS, STATE)
    maps_mine = lax.dynamic_slice_in_dim(maps_all, first_group, group_count, 3)
    local_act = jnp.concatenate(
        [activated[:, :, :sig_width], maps_mine.reshape(2, length, 2 * group_count * STATE)], axis=2
    )
    dt_rows = step_size_logits.reshape(2, length, heads_here)
    grad_rows = d_out.reshape(2, length, heads_here, HDIM)

    def parts_of(act_block, dt_block):
        return block_parts(act_block, dt_block, a_log, dt_bias, group_count)

    parts = jax.vmap(parts_of)(local_act, dt_rows)
    scaled_grad, state_grad = jax.vmap(entry_grad)(parts, grad_rows)
    ends = parts[8][:, -1]
    h_ins = link_blocks((ends[0], parts[12][0]), (ends[1], parts[12][1]))
    carried_pair = link_blocks((ends[1], state_grad[1]), (ends[0], state_grad[0]))
    carried = jnp.stack([carried_pair[1], carried_pair[0]])
    grad_act, grad_dt, decay_log_gradient, grad_dtb, grad_skip = jax.vmap(
        block_grads, in_axes=(0, 0, 0, 0, 0, None, 0, None)
    )(parts, grad_rows, scaled_grad, h_ins, carried, skip_gain, dt_rows, dt_bias)
    slope = silu_slope(preact)
    grad_pre_sig = grad_act[:, :, :sig_width] * slope[:, :, :sig_width]
    grad_mine = grad_act[:, :, sig_width:].reshape(2, length, 2, group_count, STATE)
    zero_index = jnp.zeros((), jnp.int32)
    placed = lax.dynamic_update_slice(
        jnp.zeros((2, length, 2, GROUPS, STATE), jnp.float32),
        grad_mine,
        (zero_index, zero_index, zero_index, first_group, zero_index),
    )
    map_term = placed.reshape(2, length, map_width)
    map_owned = lax.psum_scatter(map_term, "fsdp", scatter_dimension=2, tiled=True)
    map_slope = lax.dynamic_slice_in_dim(slope[:, :, sig_width:], map_start, owned, 2)
    grad_pre = jnp.concatenate([grad_pre_sig, map_owned * map_slope], axis=2)
    own_taps = jnp.concatenate([sig_taps, map_taps], axis=1)
    own_padded = jnp.concatenate(
        [
            padded[:, :, :sig_width],
            lax.dynamic_slice_in_dim(padded[:, :, sig_width:], map_start, owned, 2),
        ],
        axis=2,
    )
    wide_grad = extended(first_rows(grad_pre, rim), (("ctx", 0),), rim)
    grad_raw, tap_grads, bias_grads = conv_back(
        grad_pre, wide_grad, own_taps, own_padded, at_end, length
    )
    map_raw_grad = grad_raw[:, :, sig_width:]
    map_tap_grad = tap_grads[:, sig_width:]
    map_bias_grad = bias_grads[sig_width:]
    sig_raw_grad = grad_raw[:, :, :sig_width]
    sig_tap_grad = tap_grads[:, :sig_width]
    sig_bias_grad = bias_grads[:sig_width]
    reduced = lax.psum(
        (
            sig_tap_grad,
            map_tap_grad,
            sig_bias_grad,
            map_bias_grad,
            jnp.sum(decay_log_gradient, axis=0),
            jnp.sum(grad_dtb, axis=0),
            jnp.sum(grad_skip, axis=0),
        ),
        "ctx",
    )
    scale = 1.0 / math.sqrt(float(lax.axis_size("ctx") * 2 * length))
    final = jax.tree.map(lambda grad_part: grad_part * scale, reduced)
    return (
        sig_raw_grad.reshape(2 * length, sig_width),
        map_raw_grad.reshape(2 * length, owned),
        grad_dt.reshape(2 * length, heads_here),
        final[0],
        final[1],
        final[2],
        final[3],
        final[4],
        final[5],
        final[6],
    )


def solution(mesh):
    return jax.shard_map(
        shards,
        mesh=mesh,
        in_specs=(
            P("ctx", "fsdp"),
            P("ctx", None),
            P("ctx", "fsdp"),
            P("ctx", "fsdp"),
            P(None, "fsdp"),
            P(None, "fsdp"),
            P("fsdp"),
            P("fsdp"),
            P("fsdp"),
            P("fsdp"),
            P("fsdp"),
        ),
        out_specs=(
            P("ctx", "fsdp"),
            P("ctx", "fsdp"),
            P("ctx", "fsdp"),
            P(None, "fsdp"),
            P(None, "fsdp"),
            P("fsdp"),
            P("fsdp"),
            P("fsdp"),
            P("fsdp"),
            P("fsdp"),
        ),
        check_vma=False,
    )
```

profile of v0, /device:TPU:0, one launch (start us, length us, event | category | flops | bytes accessed | tf_op | source)
XLA Modules:
  0.0 767.0 jit_solution(15115148341930916914)
XLA Ops:
  7.3 1.3 pad_maximum_fusion.4
  10.7 6.1 collective-permute-start
  18.7 5.2 all_gather.28
  24.6 5.4 all-gather.2
  33.4 1.5 maximum_convert_fusion
  35.0 3.6 add_multiply_fusion
  41.1 1.6 reshape.178
  46.0 1.4 fusion.79
  48.2 1.9 copy.165
  50.2 1.9 multiply_convert_fusion
  53.9 1.4 copy-done.10
  55.3 1.5 fusion.80
  60.1 18.7 %all-gather.1 = f32[8,1,32]{2,1,0:T(1,128)S(1)} all-gather(f32[1,1,32]{2,1,0:T(1,128)S(1)} %get-tuple-element.362), channel_id=3, replica_groups=mesh['ctx'=8,'fsdp'=4] {'ctx'}, dimensions={0}, use_global_device_ids=true | all-gather | bytes 1152 | tf_op jit(solution)/shard_map/all_gather | solution.py:18
  78.9 16.7 %all-gather = f32[8,1,32]{2,1,0:T(1,128)} all-gather(f32[1,1,32]{2,1,0:T(1,128)S(1)} %get-tuple-element.363), channel_id=2, replica_groups=mesh['ctx'=8,'fsdp'=4] {'ctx'}, dimensions={0}, use_global_device_ids=true | all-gather | bytes 1152 | tf_op jit(solution)/shard_map/all_gather | solution.py:18
  97.4 1.7 slice_reduce_fusion.4
  100.3 3.2 fusion.47
  103.5 1.5 copy.176
  105.7 1.5 fusion.32
  107.2 2.5 reduce_sum.190
  111.6 62.6 %all-gather.10.cloned.1.call-done = f32[8,32,64,128]{3,2,1,0:T(8,128)} async-done(((f32[1,32,64,128]{3,2,1,0:T(8,128)}), f32[8,32,64,128]{3,2,1,0:T(8,128)}) %all-gather.10.cloned.1.call-update) | async-done | bytes 8388624 | tf_op jit(solution)/shard_map/all_gather | solution.py:18
  174.4 1.6 copy-done.12
  175.9 1.8 fusion.34
  177.7 121.7 %all-gather.12.cloned.1.call-done = f32[8,32,64,128]{3,2,1,0:T(8,128)} async-done(((f32[1,32,64,128]{3,2,1,0:T(8,128)}), f32[8,32,64,128]{3,2,1,0:T(8,128)}) %all-gather.12.cloned.1.call-update) | async-done | bytes 8388624 | tf_op jit(solution)/shard_map/all_gather | solution.py:18
  300.2 2.4 fusion.33
  302.6 122.0 %all-gather.8.cloned.1.call-done = f32[8,32,64,128]{3,2,1,0:T(8,128)} async-done(((f32[1,32,64,128]{3,2,1,0:T(8,128)}), f32[8,32,64,128]{3,2,1,0:T(8,128)}) %all-gather.8.cloned.1.call-update) | async-done | bytes 8388624 | tf_op jit(solution)/shard_map/all_gather | solution.py:18
  424.8 15.5 %while.52 = (s32[]{:T(128)}, f32[32]{0:T(128)S(1)}, f32[32,64,128]{2,1,0:T(8,128)S(1)}, s32[]{:T(128)}, f32[8,32]{1,0:T(8,128)}, /*index=5*/f32[8,32,64,128]{3,2...) while((s32[]{:T(128)}, f32[32]{0:T(128)S(1)}, f32[32,64,128]{2,1,0:T(8,128)S(1)}, s32[]{:T(128)}, ...), condition=%wide.region_1.2_spmd, body=%wide.region_0.1_spmd.sunk | while | flops 524326 | bytes 3146523 | solution.py:27
  425.5 1.4 bitcast_add_fusion.14
  427.7 1.4 bitcast_add_fusion.14
  429.9 1.4 bitcast_add_fusion.14
  432.1 1.6 bitcast_add_fusion.14
  434.4 1.6 bitcast_add_fusion.14
  436.7 1.4 bitcast_add_fusion.14
  438.9 1.4 bitcast_add_fusion.14
  440.9 109.1 %all-gather.14.cloned.1.call-done = f32[8,32,64,128]{3,2,1,0:T(8,128)} async-done(((f32[1,32,64,128]{3,2,1,0:T(8,128)}), f32[8,32,64,128]{3,2,1,0:T(8,128)}) %all-gather.14.cloned.1.call-update) | async-done | bytes 8388624 | tf_op jit(solution)/shard_map/all_gather | solution.py:18
  551.0 23.7 %while.55 = (s32[]{:T(128)}, f32[32]{0:T(128)S(1)}, f32[32,64,128]{2,1,0:T(8,128)}, s32[]{:T(128)}, f32[8,32]{1,0:T(8,128)}, /*index=5*/f32[8,32,64,128]{3,2,1,0...) while((s32[]{:T(128)}, f32[32]{0:T(128)S(1)}, f32[32,64,128]{2,1,0:T(8,128)}, s32[]{:T(128)}, ...), condition=%wide.region_10.11_spmd, body=%wide.region_9.10_spmd.sunk | while | flops 524326 | bytes 3146523 | solution.py:27
  551.7 2.7 bitcast_add_fusion.17
  555.1 2.7 bitcast_add_fusion.17
  558.5 2.7 bitcast_add_fusion.17
  561.8 2.7 bitcast_add_fusion.17
  565.2 2.7 bitcast_add_fusion.17
  568.6 2.7 bitcast_add_fusion.17
  572.0 2.7 bitcast_add_fusion.17
  575.3 78.6 %all-reduce.4.cloned.1.call-done = (f32[32,64,128]{2,1,0:T(8,128)}, f32[32,64,128]{2,1,0:T(8,128)}) async-done(((f32[32,64,128]{2,1,0:T(8,128)}, f32[32,64,128]{2,1,0:T(8,128)}), (f32[32,64,128]{2,1,0:T(8,128)}, f32[32,64,128]{2,1,0:T(8,128)})) %all-reduce.4.cloned.1.call-update) | async-done | bytes 2097168 | tf_op jit(solution)/shard_map/psum | solution.py:32
  653.9 1.5 add_bitcast_fusion.1
  655.4 1.9 fusion.45
  657.3 2.5 reduce_sum.191
  659.8 1.9 fusion.28
  661.6 1.4 add_bitcast_fusion
  663.1 1.9 fusion.39
  665.0 1.8 reduce_sum.192
  668.9 7.3 dynamic_update_slice.3
  676.3 2.4 reshape.188
  678.7 3.0 fusion.1
  681.9 3.0 multiply_reduce_fusion
  684.9 3.3 copy.164
  688.2 1.5 copy.174
  689.7 3.2 fusion.4
  692.8 1.5 copy.175
  694.3 1.7 multiply_reduce_fusion.1
  697.3 6.2 reduce-scatter.2.cloned.1.call-done
  706.3 4.1 collective-permute-done.2
  710.4 4.3 collective-permute-start.3
  716.5 1.5 fusion.18
  720.0 36.2 %all-reduce = (f32[4,2048]{1,0:T(4,128)S(1)}, f32[4,512]{1,0:T(4,128)S(1)}, f32[2048]{0:T(1024)S(1)}, f32[512]{0:T(512)S(1)}, f32[32]{0:T(128)S(1)}, /*index=5*/f32[32]{0:T(128)S(1)}, f32[32]{0:T(128)S(1)}) all-reduce(f32[4,2048]{1,0:T(4,128)S(1)} %slice.240, ...), channel_id=1, replica_groups=mesh['ctx'=8,'fsdp'=4] {'ctx'}, use_global_device_ids=true, to_apply=%region_25.26 | all-reduce | flops 12896 | bytes 103168 | tf_op jit(solution)/shard_map/psum | solution.py:304
  (251 shorter events, 52.1 us)
Async XLA Ops:
  7.2 9.6 %copy-start.68 = (f32[32]{0:T(128)S(1)}, f32[32]{0:T(128)}, u32[]{:S(2)}) copy-start(f32[32]{0:T(128)} %param.27) | copy-start | bytes 388
  7.2 9.6 %copy-start.55 = (f32[128,32]{0,1:T(8,128)S(1)}, f32[128,32]{0,1:T(8,128)}, u32[]{:S(2)}) copy-start(f32[128,32]{0,1:T(8,128)} %param.21) | copy-start | bytes 49156
  7.2 9.7 %copy-start.64 = (f32[32]{0:T(128)S(1)}, f32[32]{0:T(128)}, u32[]{:S(2)}) copy-start(f32[32]{0:T(128)} %param.28) | copy-start | bytes 388
  7.2 10.9 %copy-start.49 = (f32[4,2048]{1,0:T(4,128)S(1)}, f32[4,2048]{1,0:T(4,128)}, u32[]{:S(2)}) copy-start(f32[4,2048]{1,0:T(4,128)} %param.23) | copy-start | bytes 98308
  7.2 11.5 %copy-start.50 = (f32[4,512]{1,0:T(4,128)S(1)}, f32[4,512]{1,0:T(4,128)}, u32[]{:S(2)}) copy-start(f32[4,512]{1,0:T(4,128)} %param.24) | copy-start | bytes 24580
  7.2 17.4 %copy-start.62 = (f32[512]{0:T(512)S(1)}, f32[512]{0:T(512)}, u32[]{:S(2)}) copy-start(f32[512]{0:T(512)} %param.26) | copy-start | bytes 6148
  7.2 22.8 %copy-start.57 = (f32[2048]{0:T(1024)S(1)}, f32[2048]{0:T(1024)}, u32[]{:S(2)}) copy-start(f32[2048]{0:T(1024)} %param.25) | copy-start | bytes 24580
  7.3 22.9 %copy-start.23 = (bf16[128,2048]{1,0:T(8,128)(2,1)S(1)}, bf16[128,2048]{1,0:T(8,128)(2,1)}, u32[]{:S(2)}) copy-start(bf16[128,2048]{1,0:T(8,128)(2,1)} %param.22) | copy-start | bytes 1572868
  7.3 166.9 %all-gather.10.cloned.1.call-start = ((), (), s32[]{:S(2)}) async-start(), calls=%async_computation.2 | async-start | bytes 9437184 | tf_op jit(solution)/shard_map/all_gather | solution.py:18
  8.6 23.9 %copy-start.20 = (bf16[128,4096]{1,0:T(8,128)(2,1)}, bf16[128,4096]{1,0:T(8,128)(2,1)S(1)}, u32[]{:S(2)}) copy-start(bf16[128,4096]{1,0:T(8,128)(2,1)S(1)} %pad_maximum_fusion.4) | copy-start | bytes 3145732
  9.4 23.1 %collective-permute-start.1 = (bf16[3,4096]{1,0:T(4,128)(2,1)}, bf16[3,4096]{1,0:T(4,128)(2,1)}, u32[]{:S(2)}, u32[]{:S(2)}) collective-permute-start(bf16[3,4096]{1,0:T(4,128)(2,1)} %get-tuple-element.357), channel_id=1, source_target_pairs={{4,0},{8,4},{12,8},{16,12},{20,16},{24,20},{28,24},{5,1},{9,5},{13... | collective-permute-start | bytes 73736 | tf_op jit(solution)/shard_map/ppermute | solution.py:43
  10.7 22.7 %collective-permute-start = (bf16[3,4096]{1,0:T(4,128)(2,1)}, bf16[3,4096]{1,0:T(4,128)(2,1)}, u32[]{:S(2)}, u32[]{:S(2)}) collective-permute-start(bf16[3,4096]{1,0:T(4,128)(2,1)} %get-tuple-element.356), channel_id=1, source_target_pairs={{0,4},{4,8},{8,12},{12,16},{16,20},{20,24},{24,28},{1,5},{5,9},{9,... | collective-permute-start | bytes 73736 | tf_op jit(solution)/shard_map/ppermute | solution.py:40
  16.9 13.2 %copy-start.43 = (f32[2,64,32]{1,0,2:T(2,128)}, f32[2,64,32]{1,0,2:T(2,128)S(1)}, u32[]{:S(2)}) copy-start(f32[2,64,32]{1,0,2:T(2,128)S(1)} %reshape.175) | copy-start | bytes 49156
  17.9 12.3 %copy-start.38 = (f32[64,2,32]{2,1,0:T(2,128)}, f32[64,2,32]{2,1,0:T(2,128)S(1)}, u32[]{:S(2)}) copy-start(f32[64,2,32]{2,1,0:T(2,128)S(1)} %copy.151) | copy-start | bytes 49156
  30.2 14.4 %copy-start.35 = (f32[2,64,32]{1,2,0:T(8,128)}, f32[2,64,32]{1,2,0:T(8,128)S(1)}, u32[]{:S(2)}) copy-start(f32[2,64,32]{1,2,0:T(8,128)S(1)} %copy.153) | copy-start | bytes 49156
  32.5 12.1 %copy-start.6 = (bf16[2,64,32,64]{1,3,2,0:T(8,128)(2,1)}, bf16[2,64,32,64]{1,3,2,0:T(8,128)(2,1)S(1)}, u32[]{:S(2)}) copy-start(bf16[2,64,32,64]{1,3,2,0:T(8,128)(2,1)S(1)} %copy.149) | copy-start | bytes 1572868
  46.0 2.1 copy-start.11
  46.0 2.2 copy-start.14
  48.1 251.3 %all-gather.12.cloned.1.call-start = ((), (), s32[]{:S(2)}) async-start(), calls=%async_computation.3 | async-start | bytes 9437184 | tf_op jit(solution)/shard_map/all_gather | solution.py:18
  48.2 4.2 copy-start.29
  50.1 2.0 copy-start.39
  52.1 48.2 %copy-start.4 = (bf16[2,64,32,64]{1,3,2,0:T(8,128)(2,1)}, bf16[2,64,32,64]{1,3,2,0:T(8,128)(2,1)S(1)}, u32[]{:S(2)}) copy-start(bf16[2,64,32,64]{1,3,2,0:T(8,128)(2,1)S(1)} %multiply_convert_fusion) | copy-start | bytes 1572868
  56.8 39.4 %copy-start.51 = (f32[4,512]{1,0:T(4,128)S(1)}, f32[4,512]{1,0:T(4,128)}, u32[]{:S(2)}) copy-start(f32[4,512]{1,0:T(4,128)} %param.24) | copy-start | bytes 24580
  56.8 367.9 %all-gather.8.cloned.1.call-start = ((), (), s32[]{:S(2)}) async-start(), calls=%async_computation.1 | async-start | bytes 9437184 | tf_op jit(solution)/shard_map/all_gather | solution.py:18
  57.5 492.4 %all-gather.14.cloned.1.call-start = ((), (), s32[]{:S(2)}) async-start(), calls=%async_computation.4 | async-start | bytes 9437184 | tf_op jit(solution)/shard_map/all_gather | solution.py:18
  58.1 595.8 %all-reduce.4.cloned.1.call-start = ((), (), s32[]{:S(2)}) async-start(), calls=%async_computation.6 | async-start | bytes 4194304 | tf_op jit(solution)/shard_map/psum | solution.py:32
  58.9 41.5 %copy-start.7 = (bf16[2,64,32,64]{1,3,2,0:T(8,128)(2,1)S(1)}, bf16[2,64,32,64]{1,3,2,0:T(8,128)(2,1)}, u32[]{:S(2)}) copy-start(bf16[2,64,32,64]{1,3,2,0:T(8,128)(2,1)} %copy-done.6) | copy-start | bytes 1572868
  58.9 41.5 %copy-start.53 = (pred[64,64]{0,1:T(8,128)(4,1)S(1)}, pred[64,64]{0,1:T(8,128)(4,1)}, u32[]{:S(2)}) copy-start(pred[64,64]{0,1:T(8,128)(4,1)} %copy.161) | copy-start | bytes 12292
  100.3 3.2 copy-start.17
  174.3 125.2 %copy-start.56 = (f32[8,32]{1,0:T(8,128)}, f32[8,32]{1,0:T(8,128)S(1)}, u32[]{:S(2)}) copy-start(f32[8,32]{1,0:T(8,128)S(1)} %get-tuple-element.667) | copy-start | bytes 3076
  302.6 400.9 %reduce-scatter.2.cloned.1.call-start = ((), (), s32[]{:S(2)}) async-start(), calls=%async_computation.5 | async-start | bytes 1310720 | tf_op jit(solution)/shard_map/reduce_scatter | solution.py:283
  655.3 2.0 copy-start.2
  657.3 4.3 copy-start
  657.3 4.3 copy-start.67
  659.8 3.3 copy-start.8
  659.8 3.3 copy-start.36
  665.0 2.0 copy-start.32
  668.9 9.7 %copy-start.3 = (f32[1,32,64,128]{3,2,1,0:T(8,128)S(1)}, f32[1,32,64,128]{3,2,1,0:T(8,128)}, u32[]{:S(2)}) copy-start(f32[1,32,64,128]{3,2,1,0:T(8,128)} %copy-done.2) | copy-start | bytes 3145732
  678.7 3.1 copy-start.1
  678.7 3.1 copy-start.9
  678.7 3.2 copy-start.18
  678.7 3.1 copy-start.31
  678.7 3.1 copy-start.33
  678.7 3.1 copy-start.54
  678.7 3.1 copy-start.63
  684.9 4.8 copy-start.37
  694.3 2.5 copy-start.40
  694.3 2.5 copy-start.41
  694.3 2.5 copy-start.42
  694.3 2.5 copy-start.66
  694.3 2.7 copy-start.16
  694.3 2.7 copy-start.21
  697.2 8.6 %copy-start.34 = (f32[2,64,32]{1,2,0:T(8,128)S(1)}, f32[2,64,32]{1,2,0:T(8,128)}, u32[]{:S(2)}) copy-start(f32[2,64,32]{1,2,0:T(8,128)} %get-tuple-element.337) | copy-start | bytes 49156
  697.2 8.6 %copy-start.44 = (f32[2,64,32]{1,0,2:T(2,128)S(1)}, f32[2,64,32]{1,0,2:T(2,128)}, u32[]{:S(2)}) copy-start(f32[2,64,32]{1,0,2:T(2,128)} %copy-done.43) | copy-start | bytes 49156
  697.2 8.6 %copy-start.48 = (f32[2,64,32]{1,2,0:T(8,128)S(1)}, f32[2,64,32]{1,2,0:T(8,128)}, u32[]{:S(2)}) copy-start(f32[2,64,32]{1,2,0:T(8,128)} %get-tuple-element.345) | copy-start | bytes 49156
  697.2 8.6 %copy-start.52 = (f32[64,64]{1,0:T(8,128)S(1)}, f32[64,64]{1,0:T(8,128)}, u32[]{:S(2)}) copy-start(f32[64,64]{1,0:T(8,128)} %fusion.64) | copy-start | bytes 49156
  697.3 8.6 %copy-start.60 = (f32[32]{0:T(128)S(1)}, f32[32]{0:T(128)}, u32[]{:S(2)}) copy-start(f32[32]{0:T(128)} %copy-done.59) | copy-start | bytes 388
  697.3 8.6 %copy-start.65 = (f32[32]{0:T(128)S(1)}, f32[32]{0:T(128)}, u32[]{:S(2)}) copy-start(f32[32]{0:T(128)} %param.28) | copy-start | bytes 388
  704.5 5.9 collective-permute-start.2
  706.3 10.2 %copy-start.19 = (f32[2,67,2048]{2,1,0:T(8,128)S(1)}, f32[2,67,2048]{2,1,0:T(8,128)}, u32[]{:S(2)}) copy-start(f32[2,67,2048]{2,1,0:T(8,128)} %get-tuple-element.343) | copy-start | bytes 3293188
  706.3 10.2 %copy-start.45 = (f32[2560]{0:T(1024)S(1)}, f32[2560]{0:T(1024)}, u32[]{:S(2)}) copy-start(f32[2560]{0:T(1024)} %get-tuple-element.274) | copy-start | bytes 30724
  706.3 10.2 %copy-start.46 = (f32[2560]{0:T(1024)S(1)}, f32[2560]{0:T(1024)}, u32[]{:S(2)}) copy-start(f32[2560]{0:T(1024)} %get-tuple-element.275) | copy-start | bytes 30724
  706.3 10.2 %copy-start.47 = (f32[2560]{0:T(1024)S(1)}, f32[2560]{0:T(1024)}, u32[]{:S(2)}) copy-start(f32[2560]{0:T(1024)} %get-tuple-element.276) | copy-start | bytes 30724
  710.4 5.9 collective-permute-start.3
  (15 other events, 20.4 us)
Sparse Core Ops, SparseCore 0:
  48.2 125.9 all-gather.9
  176.3 123.0 all-gather.11
  301.5 123.1 all-gather.7
  426.7 123.2 all-gather.13
  553.5 100.3 all-reduce.3
  678.8 24.6 reduce-scatter.1
where the time goes:
time: 769 us; the launch traced here: 767 us
  waiting for transfers between devices  506 us (66%)
  blocking collectives  82.2 us (11%)
  other arithmetic  77.3 us (10%)
  local copies, waits for them, and re-layouts  51.7 us (7%)
  matrix products  20.6 us (3%)
  between operations  15.2 us (2%)
  starting transfers between devices  13.2 us (2%)
    all_gather x4, waiting for transfers between devices, prefix(): gathered = jax.tree.map(lambda a: lax.all_gather(a, axis), part)  415 us
    psum x1, waiting for transfers between devices, broadcast(): return lax.psum(jnp.where(mine, x, jnp.zeros_like(x)), axis)  78.6 us
    psum x1, blocking collectives, shards(): lax.psum((sig_tap_grad, map_tap_grad, sig_bias_grad, map_bias_grad, jnp.s...  36.2 us
    all_gather x2, blocking collectives, prefix(): gathered = jax.tree.map(lambda a: lax.all_gather(a, axis), part)  35.5 us
    add x14, other arithmetic, link(): jnp.exp(later[0])[:, None, None] * earlier[1] + later[1]  29.2 us
    dot_general x11, matrix products, ein(): return jnp.einsum(form, left, right, preferred_element_type=jnp.float32)  20.1 us
  transfers between devices with their start and end apart: 10, of which 8 were waited for; matrix products, arithmetic and copies ran while one was open for 12% of the time, Pallas kernels for 0%

commit v1 on v0

--- a/solution.py
+++ b/solution.py
@@ -1,8 +1,11 @@
+import functools
 import math
 
 import jax
 import jax.numpy as jnp
 from jax import lax
+from jax.experimental import pallas as pl
+from jax.experimental.pallas import tpu as pltpu
 from jax.sharding import PartitionSpec as P
 
 HEADS = 128
@@ -206,7 +209,7 @@
     return jnp.concatenate([grad_pre[0, :rim], grad_pre[1, :rim]], axis=0)
 
 
-def shards(
+def shards_chain(
     sig_raw,
     map_raw,
     step_size_logits,
@@ -327,6 +330,544 @@
         final[5],
         final[6],
     )
+
+
+TILE = 128
+NT = (((1,), (1,)), ((), ()))
+TN = (((0,), (0,)), ((), ()))
+NN = (((1,), (0,)), ((), ()))
+BF = jnp.bfloat16
+F32 = jnp.float32
+
+
+def mm(a, b, dims=NN):
+    return lax.dot_general(a, b, dims, preferred_element_type=F32)
+
+
+def mm_f32(a, b, dims=NN):
+    return lax.dot_general(a, b, dims, precision=lax.Precision.HIGHEST, preferred_element_type=F32)
+
+
+def split3(x):
+    hi = x.astype(BF)
+    rest = x - hi.astype(F32)
+    mid = rest.astype(BF)
+    return hi, mid, (rest - mid.astype(F32)).astype(BF)
+
+
+def ids(shape, dim):
+    return lax.broadcasted_iota(jnp.int32, shape, dim)
+
+
+def pack_kernel(ctx, rows, sig_ref, map_ref, dt_ref, dy_ref, out_ref, dt_rows):
+    heads = dt_ref.shape[1]
+    mine = heads // ctx
+    fsdp_place = lax.axis_index("fsdp")
+    half = map_ref.shape[1] // 2
+    padded = jnp.concatenate([dt_ref[...], jnp.zeros((rows, TILE - heads), F32)], axis=1)
+    dt_rows[0:TILE, :] = jnp.transpose(padded)
+    low = ids((8, TILE), 0) < mine
+    for c in range(ctx):
+        for j in range(2):
+            cols = slice(c * 2 * TILE + j * TILE, c * 2 * TILE + (j + 1) * TILE)
+            out_ref[c, j * TILE : (j + 1) * TILE, :] = sig_ref[:, cols]
+            out_ref[c, (2 + j) * TILE : (3 + j) * TILE, :] = dy_ref[:, cols]
+            first = (2 * fsdp_place + c // 4) * TILE + j * half
+            out_ref[c, (4 + j) * TILE : (5 + j) * TILE, :] = map_ref[
+                :, pl.ds(pl.multiple_of(first, TILE), TILE)
+            ]
+        hi, mid, lo = split3(dt_rows[c * mine : c * mine + 8, :])
+        both = jnp.where(low, hi.astype(F32), pltpu.roll(mid.astype(F32), mine, 0))
+        out_ref[c, 6 * TILE : 6 * TILE + 16, :] = jnp.concatenate(
+            [both, lo.astype(F32)], axis=0
+        ).astype(BF)
+
+
+def core_kernel(
+    scale,
+    x_ref,
+    taps_ref,
+    bias_ref,
+    mtaps_ref,
+    alog_ref,
+    dtb_ref,
+    skip_ref,
+    out_ref,
+    xp,
+    dp,
+    act,
+    slope,
+    gp,
+    scaled_s,
+    weighted_s,
+    sgrad_s,
+    step_e,
+    toend_e,
+    exp_e,
+    h_s,
+    sg_s,
+    carry,
+    step_r,
+    ds_r,
+    sig_r,
+    ddt_r,
+    tap_acc,
+    skip_acc,
+    alog_acc,
+    ddt_acc,
+    after,
+):
+    ctx_place = lax.axis_index("ctx")
+    fsdp_place = lax.axis_index("fsdp")
+    chunks = 8
+    heads = 4
+    half_lane = ids((TILE, TILE), 1) < TILE // 2
+    lane_row = ids((1, TILE), 1)
+    row8 = ids((8, TILE), 0)
+    lane8 = ids((8, TILE), 1)
+    used8 = row8 < heads
+
+    def blocks_of(chunk):
+        found = []
+        for e in range(2):
+            b = 2 * chunk + e
+            found.append((b, 0) if b < 8 else (15 - b, TILE // 2))
+        return found
+
+    xp[0:8, :] = jnp.zeros((8, 4 * TILE), F32)
+    after[...] = jnp.zeros_like(after)
+    rate8 = jnp.zeros((8, TILE), F32)
+    bias8 = jnp.zeros((8, TILE), F32)
+    skip_row = []
+    for h in range(heads):
+        at = ctx_place * heads + h
+        rate8 = jnp.where(row8 == h, alog_ref[at], rate8)
+        bias8 = jnp.where(row8 == h, dtb_ref[at], bias8)
+    rate8 = -jnp.exp(rate8)
+    for j in range(2):
+        at = ctx_place * heads + 2 * j
+        skip_row.append(jnp.where(lane_row < TILE // 2, skip_ref[at], skip_ref[at + 1]))
+    dts = []
+    for s in range(8):
+        packed = x_ref[s, 6 * TILE : 6 * TILE + 16, :].astype(F32)
+        top = packed[0:8]
+        value = top + pltpu.roll(top, 4, 0) + packed[8:16]
+        dts.append(jnp.where(used8, value, 0.0))
+    for i in range(chunks):
+        (s0, o0), (s1, o1) = blocks_of(i)
+        for e, (s, o) in enumerate(((s0, o0), (s1, o1))):
+            r = i * TILE + e * 64
+            for j in range(2):
+                xp[8 + r : 8 + r + 64, j * TILE : (j + 1) * TILE] = x_ref[
+                    s, j * TILE + o : j * TILE + o + 64, :
+                ].astype(F32)
+                xp[8 + r : 8 + r + 64, (2 + j) * TILE : (3 + j) * TILE] = x_ref[
+                    s, (4 + j) * TILE + o : (4 + j) * TILE + o + 64, :
+                ].astype(F32)
+                dp[r : r + 64, j * TILE : (j + 1) * TILE] = x_ref[
+                    s, (2 + j) * TILE + o : (2 + j) * TILE + o + 64, :
+                ]
+        a = dts[s0] if o0 == 0 else pltpu.roll(dts[s0], 64, 1)
+        b = dts[s1] if o1 != 0 else pltpu.roll(dts[s1], 64, 1)
+        logits = jnp.where(lane8 < 64, a, b) + bias8
+        small = jnp.exp(-jnp.abs(logits))
+        step = jnp.maximum(logits, 0.0) + jnp.log1p(small)
+        step_r[8 * i : 8 * i + 8, :] = jnp.where(used8, step, 0.0)
+        sig_r[8 * i : 8 * i + 8, :] = jnp.where(logits >= 0, 1.0, small) / (1.0 + small)
+        ds_r[8 * i : 8 * i + 8, :] = jnp.where(used8, step * rate8, 0.0)
+    row_q = ids((TILE, TILE), 0)
+    col_q = ids((TILE, TILE), 1)
+    upto = (row_q <= col_q).astype(F32)
+    ds_r[...] = mm_f32(ds_r[...], upto)
+    tail_sums = jnp.concatenate(
+        [(row_q >= col_q).astype(F32), (row_q < col_q).astype(F32)], axis=0
+    )
+    seen = row_q <= col_q
+
+    def weights(j):
+        if j < 2:
+            at = pl.ds(pl.multiple_of(ctx_place * 2 * TILE + j * TILE, TILE), TILE)
+            return [taps_ref[k : k + 1, at] for k in range(4)], bias_ref[0:1, at]
+        group = 2 * fsdp_place + ctx_place // 4
+        owner = 2 * (j - 2) + fsdp_place // 2
+        at = pl.ds(pl.multiple_of((group % 4) * TILE, TILE), TILE)
+        return [mtaps_ref[owner, k : k + 1, at] for k in range(4)], mtaps_ref[owner, 4:5, at]
+
+    def shifted(block, k):
+        return block[8:] if k == 3 else pltpu.roll(block, 3 - k, 0)[8:]
+
+    def columns(i):
+        both = jnp.concatenate(
+            [
+                step_r[pl.ds(pl.multiple_of(8 * i, 8), 8), :],
+                ds_r[pl.ds(pl.multiple_of(8 * i, 8), 8), :],
+            ],
+            axis=0,
+        )
+        full = jnp.concatenate([both, jnp.zeros((TILE - 16, TILE), F32)], axis=0)
+        return jnp.transpose(full)
+
+    carry[...] = jnp.zeros_like(carry)
+
+    def forward(i, _):
+        r0 = pl.multiple_of(i * TILE, TILE)
+        rows = pl.ds(r0, TILE)
+        for j in range(4):
+            lanes = slice(j * TILE, (j + 1) * TILE)
+            block = xp[pl.ds(r0, TILE + 8), lanes]
+            taps, bias = weights(j)
+            pre = bias + taps[0] * shifted(block, 0)
+            for k in range(1, 4):
+                pre = pre + taps[k] * shifted(block, k)
+            sig = 1.0 / (1.0 + jnp.exp(-pre))
+            act[rows, lanes] = (pre * sig).astype(BF)
+            slope[rows, lanes] = sig * (1.0 + pre * (1.0 - sig))
+        cols = columns(i)
+        end = []
+        for j in range(2):
+            lanes = slice(j * TILE, (j + 1) * TILE)
+            step = jnp.where(half_lane, cols[:, 2 * j : 2 * j + 1], cols[:, 2 * j + 1 : 2 * j + 2])
+            ds = jnp.where(half_lane, cols[:, 8 + 2 * j : 9 + 2 * j], cols[:, 9 + 2 * j : 10 + 2 * j])
+            last = ds[TILE - 1 : TILE, :]
+            grow = jnp.exp(ds)
+            toend = jnp.exp(last - ds)
+            step_e[rows, lanes] = step
+            toend_e[rows, lanes] = toend
+            exp_e[rows, lanes] = grow
+            end.append(jnp.exp(last))
+            scaled = (act[rows, lanes].astype(F32) * step).astype(BF)
+            scaled_s[rows, lanes] = scaled
+            weighted_s[rows, lanes] = (scaled.astype(F32) * toend).astype(BF)
+            sgrad_s[rows, lanes] = (dp[rows, lanes].astype(F32) * grow).astype(BF)
+        in_map = act[rows, 2 * TILE : 3 * TILE]
+        out_map = act[rows, 3 * TILE : 4 * TILE]
+        local = mm(in_map, weighted_s[rows, :], TN)
+        sg_s[i] = mm(out_map, sgrad_s[rows, :], TN)
+        h_s[i] = carry[...]
+        carry[...] = carry[...] * jnp.concatenate(end, axis=1) + local
+        return 0
+
+    lax.fori_loop(0, chunks, forward, 0)
+
+    carry[...] = jnp.zeros_like(carry)
+    tap_acc[...] = jnp.zeros_like(tap_acc)
+    skip_acc[...] = jnp.zeros_like(skip_acc)
+    alog_acc[...] = jnp.zeros_like(alog_acc)
+    ddt_acc[...] = jnp.zeros_like(ddt_acc)
+
+    def head_sums(x, j):
+        pick = (row8 == 2 * j + lane8 // 64).astype(BF)
+        hi = x.astype(BF)
+        lo = (x - hi.astype(F32)).astype(BF)
+        return mm(pick, hi, NT) + mm(pick, lo, NT)
+
+    def eights(x):
+        return jnp.sum(x.reshape(x.shape[0] // 8, 8, x.shape[1]), axis=0)
+
+    def backward(n, _):
+        i = chunks - 1 - n
+        r0 = pl.multiple_of(i * TILE, TILE)
+        rows = pl.ds(r0, TILE)
+        at8 = pl.ds(pl.multiple_of(8 * i, 8), 8)
+        in_map = act[rows, 2 * TILE : 3 * TILE]
+        out_map = act[rows, 3 * TILE : 4 * TILE]
+        h_in = h_s[i]
+        carried = carry[...]
+        h_low = h_in.astype(BF)
+        c_low = carried.astype(BF)
+        off = mm(out_map, h_low)
+        gw = mm(in_map, c_low)
+        out_grad = mm(sgrad_s[rows, :], h_low, NT)
+        in_grad = mm(weighted_s[rows, :], c_low, NT)
+        score = mm(in_map, out_map, NT)
+        end = exp_e[pl.ds(r0 + TILE - 8, 8), :][7:8, :]
+        ends = jnp.sum(h_in * carried, axis=0, keepdims=True) * end
+        carry[...] = sg_s[i] + carried * end
+        cols = columns(i)
+        ds8 = ds_r[at8, :]
+        grad_score = jnp.zeros((TILE, TILE), F32)
+        gsum = jnp.zeros((8, TILE), F32)
+        back = jnp.zeros((8, TILE), F32)
+        stepsum = jnp.zeros((8, TILE), F32)
+        end_sum = jnp.zeros((8, TILE), F32)
+        rcol = jnp.zeros((TILE, TILE), F32)
+        for j in range(2):
+            lanes = slice(j * TILE, (j + 1) * TILE)
+            sc = scaled_s[rows, lanes]
+            dy = dp[rows, lanes]
+            diag = jnp.zeros((TILE, TILE), F32)
+            for e in range(2):
+                h = 2 * j + e
+                part = half_lane if e == 0 else jnp.logical_not(half_lane)
+                gm = mm(jnp.where(part, sc, jnp.zeros_like(sc)), dy, NT)
+                spread = ds8[h : h + 1, :] - cols[:, 8 + h : 9 + h]
+                decay = jnp.exp(jnp.where(seen, spread, -1e30))
+                gd = gm * decay
+                grad_score = grad_score + gd
+                both = gd * score
+                rcol = jnp.where(col_q == h, jnp.sum(both, axis=1, keepdims=True), rcol)
+                gsum = gsum + jnp.where(row8 == h, jnp.sum(both, axis=0, keepdims=True), 0.0)
+                mix = (score * decay).astype(BF)
+                diag = diag + mm(mix, jnp.where(part, dy, jnp.zeros_like(dy)))
+            dyf = dy.astype(F32)
+            scf = sc.astype(F32)
+            sigf = act[rows, lanes].astype(F32)
+            gwe = gw[:, lanes] * toend_e[rows, lanes]
+            grad_scaled = gwe + diag
+            gsum = gsum + head_sums(dyf * exp_e[rows, lanes] * off[:, lanes], j)
+            back = back + head_sums(gwe * scf, j)
+            stepsum = stepsum + head_sums(grad_scaled * sigf, j)
+            end_sum = end_sum + head_sums(jnp.broadcast_to(ends[:, lanes], (TILE, TILE)), j)
+            skip_acc[:, lanes] += eights(dyf * sigf)
+            grad_sig = skip_row[j] * dyf + grad_scaled * step_e[rows, lanes]
+            gp[rows, lanes] = grad_sig * slope[rows, lanes]
+        gs = grad_score.astype(BF)
+        gp[rows, 2 * TILE : 3 * TILE] = (in_grad + mm(gs, out_map)) * slope[rows, 2 * TILE : 3 * TILE]
+        gp[rows, 3 * TILE : 4 * TILE] = (out_grad + mm(gs, in_map, TN)) * slope[
+            rows, 3 * TILE : 4 * TILE
+        ]
+        gsum = gsum - jnp.transpose(rcol)[0:8, :]
+        grad_log = mm_f32(jnp.concatenate([gsum, back], axis=1), tail_sums) + end_sum
+        step8 = step_r[at8, :]
+        ddt = jnp.where(used8, (grad_log * rate8 + stepsum) * sig_r[at8, :], 0.0)
+        ddt_r[at8, :] = ddt
+        ddt_acc[...] += ddt
+        alog_acc[...] += grad_log * step8
+        for j in range(4):
+            lanes = slice(j * TILE, (j + 1) * TILE)
+            grads = jnp.concatenate([gp[rows, lanes], after[:, lanes]], axis=0)
+            block = xp[pl.ds(r0, TILE + 8), lanes]
+            taps, bias = weights(j)
+            here = grads[0:TILE]
+            after[:, lanes] = here[0:8]
+            raw = taps[3] * here
+            for k in range(3):
+                raw = raw + taps[k] * pltpu.roll(grads, 5 + k, 0)[8:]
+            for k in range(4):
+                tap_acc[k, :, lanes] += eights(here * shifted(block, k))
+            tap_acc[4, :, lanes] += eights(here)
+            out = raw.astype(BF)
+            for e in range(2):
+                b = 2 * i + e
+                s = jnp.where(b < 8, b, 15 - b)
+                o = jnp.where(b < 8, 0, 64)
+                out_ref[s, pl.ds(pl.multiple_of(j * TILE + o, 64), 64), :] = out[
+                    e * 64 : (e + 1) * 64
+                ]
+        return 0
+
+    lax.fori_loop(0, chunks, backward, 0)
+
+    rows = []
+    for j in range(4):
+        lanes = slice(j * TILE, (j + 1) * TILE)
+        for k in range(5):
+            rows.append(jnp.sum(tap_acc[k, :, lanes], axis=0, keepdims=True))
+    alog = jnp.sum(alog_acc[...] * rate8, axis=1, keepdims=True)
+    ddtb = jnp.sum(ddt_acc[...], axis=1, keepdims=True)
+    skips = jnp.zeros((8, TILE), F32)
+    for j in range(2):
+        total = jnp.sum(skip_acc[:, j * TILE : (j + 1) * TILE], axis=0, keepdims=True)
+        for e in range(2):
+            part = jnp.sum(jnp.where(lane_row // 64 == e, total, 0.0), axis=1, keepdims=True)
+            skips = jnp.where(row8 == 2 * j + e, part, skips)
+    trio = jnp.where(lane8 == 0, alog, jnp.where(lane8 == 1, ddtb, skips))
+    trio = jnp.where(lane8 < 3, trio, 0.0)
+    params = jnp.concatenate(rows + [jnp.zeros((4, TILE), F32), trio], axis=0) * scale
+    p_hi, p_lo, _ = split3(params)
+    param_rows = jnp.concatenate([p_hi, p_lo], axis=0)
+    for s in range(8):
+        low = ddt_r[8 * (s // 2) : 8 * (s // 2) + 8, :]
+        up_chunk = (15 - s) // 2
+        high = ddt_r[8 * up_chunk : 8 * up_chunk + 8, :]
+        if s % 2 == 1:
+            low = pltpu.roll(low, 64, 1)
+        if (15 - s) % 2 == 0:
+            high = pltpu.roll(high, 64, 1)
+        here = jnp.where(lane8 < 64, low, high)
+        hi, mid, lo = split3(here)
+        both = hi.astype(F32) + pltpu.roll(mid.astype(F32), 4, 0)
+        out_ref[s, 4 * TILE : 4 * TILE + 16, :] = jnp.concatenate(
+            [both, lo.astype(F32)], axis=0
+        ).astype(BF)
+        out_ref[s, 4 * TILE + 16 : 4 * TILE + 80, :] = param_rows
+
+
+def unpack_kernel(y_ref, dsig_ref, ddt_ref, taps_ref, bias_ref, trio_ref, one_ref, two_ref):
+    fsdp_place = lax.axis_index("fsdp")
+    even = lax.rem(fsdp_place, 2) == 0
+    row8 = ids((8, TILE), 0)
+    dt_rows = []
+    trios = []
+    for c in range(8):
+        for j in range(2):
+            lanes = slice((2 * c + j) * TILE, (2 * c + j + 1) * TILE)
+            dsig_ref[:, lanes] = y_ref[c, j * TILE : (j + 1) * TILE, :].astype(F32)
+        packed = y_ref[c, 4 * TILE : 4 * TILE + 16, :].astype(F32)
+        top = packed[0:8]
+        value = jnp.where(row8 < 4, top + pltpu.roll(top, 4, 0) + packed[8:16], 0.0)
+        if c % 2 == 0:
+            dt_rows.append(value)
+        else:
+            dt_rows[-1] = dt_rows[-1] + pltpu.roll(value, 4, 0)
+        params = y_ref[c, 4 * TILE + 16 : 4 * TILE + 48, :].astype(F32) + y_ref[
+            c, 4 * TILE + 48 : 4 * TILE + 80, :
+        ].astype(F32)
+        for j in range(2):
+            lanes = slice((2 * c + j) * TILE, (2 * c + j + 1) * TILE)
+            taps_ref[0:4, lanes] = params[5 * j : 5 * j + 4]
+            bias_ref[0:1, lanes] = params[5 * j + 4 : 5 * j + 5]
+        trio = params[24:32]
+        if c % 2 == 0:
+            trios.append(jnp.where(row8 < 4, trio, 0.0))
+        else:
+            trios[-1] = trios[-1] + jnp.where(row8 >= 4, pltpu.roll(trio, 4, 0), 0.0)
+    full = jnp.concatenate(dt_rows + [jnp.zeros((TILE - 32, TILE), F32)], axis=0)
+    ddt_ref[...] = jnp.transpose(full)[:, 0:32]
+    full = jnp.concatenate(trios + [jnp.zeros((TILE - 32, TILE), F32)], axis=0)
+    trio_ref[...] = jnp.transpose(full)[0:8, :]
+    for g in range(2):
+        lanes = slice(g * TILE, (g + 1) * TILE)
+        sums = []
+        for j in range(2):
+            main = jnp.zeros((TILE, TILE), F32)
+            param = jnp.zeros((32, TILE), F32)
+            for c in range(4 * g, 4 * g + 4):
+                main = main + y_ref[c, (2 + j) * TILE : (3 + j) * TILE, :].astype(F32)
+                param = (
+                    param
+                    + y_ref[c, 4 * TILE + 16 : 4 * TILE + 48, :].astype(F32)
+                    + y_ref[c, 4 * TILE + 48 : 4 * TILE + 80, :].astype(F32)
+                )
+            five = jnp.zeros((8, TILE), F32)
+            for k in range(5):
+                five = jnp.where(row8 == k, param[10 + 5 * j + k : 11 + 5 * j + k], five)
+            sums.append((main, five))
+        one_ref[0:TILE, lanes] = jnp.where(even, sums[0][0], sums[1][0])
+        one_ref[TILE : TILE + 8, lanes] = jnp.where(even, sums[0][1], sums[1][1])
+        two_ref[0:TILE, lanes] = jnp.where(even, sums[1][0], sums[0][0])
+        two_ref[TILE : TILE + 8, lanes] = jnp.where(even, sums[1][1], sums[0][1])
+
+
+ROUTE_ONE = [(0, 0), (2, 1), (1, 2), (3, 3)]
+ROUTE_TWO = [(0, 2), (2, 3), (1, 0), (3, 1)]
+
+
+def shards_whole(
+    sig_raw,
+    map_raw,
+    step_size_logits,
+    d_out,
+    sig_taps,
+    map_taps,
+    sig_bias,
+    map_bias,
+    a_log,
+    dt_bias,
+    skip_gain,
+):
+    ctx = lax.axis_size("ctx")
+    fsdp = lax.axis_size("fsdp")
+    rows, sig_width = sig_raw.shape
+    owned = map_taps.shape[1]
+    params = pltpu.CompilerParams(vmem_limit_bytes=48 * 1024 * 1024)
+    vmem = pl.BlockSpec(memory_space=pltpu.VMEM)
+    smem = pl.BlockSpec(memory_space=pltpu.SMEM)
+    map_params = lax.all_gather(
+        jnp.concatenate([map_taps, map_bias[None, :]], axis=0), "fsdp", axis=0
+    )
+    packed = pl.pallas_call(
+        functools.partial(pack_kernel, ctx, rows),
+        out_shape=jax.ShapeDtypeStruct((ctx, 6 * TILE + 16, TILE), BF),
+        in_specs=[vmem] * 4,
+        out_specs=vmem,
+        scratch_shapes=[pltpu.VMEM((TILE + 8, TILE), F32)],
+        compiler_params=params,
+    )(sig_raw, map_raw, step_size_logits, d_out)
+    got = lax.all_to_all(packed, "ctx", 0, 0, tiled=True)
+    scale = 1.0 / math.sqrt(float(ctx * rows))
+    total = ctx * rows
+    wide = pltpu.VMEM((total, 2 * TILE), F32)
+    narrow = pltpu.VMEM((total, 2 * TILE), BF)
+    row64 = pltpu.VMEM((64, TILE), F32)
+    done = pl.pallas_call(
+        functools.partial(core_kernel, scale),
+        out_shape=jax.ShapeDtypeStruct((ctx, 4 * TILE + 80, TILE), BF),
+        in_specs=[vmem] * 4 + [smem] * 3,
+        out_specs=vmem,
+        scratch_shapes=[
+            pltpu.VMEM((total + 8, 4 * TILE), F32),
+            narrow,
+            pltpu.VMEM((total, 4 * TILE), BF),
+            pltpu.VMEM((total, 4 * TILE), F32),
+            pltpu.VMEM((total + 8, 4 * TILE), F32),
+            narrow,
+            narrow,
+            narrow,
+            wide,
+            wide,
+            wide,
+            pltpu.VMEM((8, TILE, 2 * TILE), F32),
+            pltpu.VMEM((8, TILE, 2 * TILE), F32),
+            pltpu.VMEM((TILE, 2 * TILE), F32),
+            row64,
+            row64,
+            row64,
+            row64,
+            pltpu.VMEM((5, 8, 4 * TILE), F32),
+            pltpu.VMEM((8, 2 * TILE), F32),
+            pltpu.VMEM((8, TILE), F32),
+            pltpu.VMEM((8, TILE), F32),
+            pltpu.VMEM((8, 4 * TILE), F32),
+        ],
+        compiler_params=params,
+    )(got, sig_taps, sig_bias[None, :], map_params, a_log, dt_bias, skip_gain)
+    back = lax.all_to_all(done, "ctx", 0, 0, tiled=True)
+    d_sig, d_dt, taps, bias, trio, one, two = pl.pallas_call(
+        unpack_kernel,
+        out_shape=(
+            jax.ShapeDtypeStruct((rows, sig_width), F32),
+            jax.ShapeDtypeStruct((rows, 32), F32),
+            jax.ShapeDtypeStruct((4, sig_width), F32),
+            jax.ShapeDtypeStruct((1, sig_width), F32),
+            jax.ShapeDtypeStruct((8, TILE), F32),
+            jax.ShapeDtypeStruct((TILE + 8, 2 * TILE), F32),
+            jax.ShapeDtypeStruct((TILE + 8, 2 * TILE), F32),
+        ),
+        in_specs=[vmem],
+        out_specs=(vmem,) * 7,
+        compiler_params=params,
+    )(back)
+    one = lax.ppermute(one, "fsdp", ROUTE_ONE)
+    two = lax.ppermute(two, "fsdp", ROUTE_TWO)
+    swap = lax.axis_index("fsdp") >= fsdp // 2
+    d_map = jnp.concatenate([jnp.where(swap, two, one), jnp.where(swap, one, two)], axis=1)
+    return (
+        d_sig,
+        d_map[:rows],
+        d_dt,
+        taps,
+        d_map[rows : rows + 4],
+        bias[0],
+        d_map[rows + 4],
+        trio[0, :32],
+        trio[1, :32],
+        trio[2, :32],
+    )
+
+
+def shards(*args):
+    sig_raw, map_raw, step_size_logits = args[:3]
+    ctx = lax.axis_size("ctx")
+    fsdp = lax.axis_size("fsdp")
+    fits = (
+        ctx == 8
+        and fsdp == 4
+        and sig_raw.shape == (TILE, 2048)
+        and map_raw.shape == (TILE, 2 * GROUPS * STATE)
+        and step_size_logits.shape[1] == 32
+    )
+    return shards_whole(*args) if fits else shards_chain(*args)
 
 
 def solution(mesh):

time: 769 us -> 111 us (0.14)
  the two profiles are of different devices: /device:TPU:0 before, /device:TPU:1 now
where the time goes in v1:
time: 111 us; the launch traced here: 110 us
  waiting for transfers between devices  61.6 us (55%)
  Pallas kernels  19 us (17%)
  starting transfers between devices  15.8 us (14%)
  blocking collectives  6.03 us (5%)
  local copies, waits for them, and re-layouts  5.17 us (5%)
  other arithmetic  1.95 us (2%)
    all_to_all x1, waiting for transfers between devices, shards_whole(): got = lax.all_to_all(packed, 'ctx', 0, 0, tiled=True)  30.8 us
    all_to_all x1, waiting for transfers between devices, shards_whole(): back = lax.all_to_all(done, 'ctx', 0, 0, tiled=True)  28.6 us
    pallas_call x1, Pallas kernels, shards_whole(): pl.pallas_call(functools.partial(core_kernel, scale), out_shape=jax.Shape...  16.4 us
    all_to_all x1, starting transfers between devices, shards_whole(): got = lax.all_to_all(packed, 'ctx', 0, 0, tiled=True)  6.53 us
    all_gather x1, blocking collectives, shards_whole(): lax.all_gather(jnp.concatenate([map_taps, map_bias[None, :]], axis=0), 'f...  6.03 us
    all_to_all x1, starting transfers between devices, shards_whole(): back = lax.all_to_all(done, 'ctx', 0, 0, tiled=True)  4.69 us
    unnamed x22, local copies, waits for them, and re-layouts  4.65 us
    ppermute x1, starting transfers between devices, shards_whole(): one = lax.ppermute(one, 'fsdp', ROUTE_ONE)  3 us
  transfers between devices with their start and end apart: 4, of which 3 were waited for; matrix products, arithmetic and copies ran while one was open for 1% of the time, Pallas kernels for 0%

profile of v1, /device:TPU:1, one launch (start us, length us, event | category | flops | bytes accessed | tf_op | source)
XLA Modules:
  0.0 110.3 jit_solution(6252095559795123130)
XLA Ops:
  0.6 0.8 copy.23.dt_ref
  1.5 0.0 copy-start
  1.5 1.0 copy-done
  2.5 0.0 copy-start.1
  2.5 1.0 copy-done.1
  3.5 0.0 copy-start.2
  3.5 1.0 copy-done.2
  4.6 1.4 %shard_map.186 = bf16[8,784,128]{2,1,0:T(8,128)(2,1)} custom-call(bf16[128,2048]{1,0:T(8,128)(2,1)S(1)} %copy-done, bf16[128,2048]{1,0:T(8,128)(2,1)S(1)} %copy-done.1, f32[128,32]{1,0:T(8,128)S(1)} %copy.23.dt_ref, bf16[128,2048]{1,0:T(8,128)(2,1)S(1)} %copy-done.2), custom_call_target="tpu_custom_call" | custom-call | tf_op jit(solution)/shard_map/pallas_call | solution.py:779
  6.0 0.0 copy-start.8
  6.0 0.0 copy-start.9
  6.0 0.0 copy-start.3
  6.0 0.0 copy-start.4
  6.0 0.0 copy-start.5
  6.1 0.0 copy-start.6
  6.1 0.0 copy-start.7
  6.1 6.5 %all-to-all-start = ((bf16[8,784,128]{2,1,0:T(8,128)(2,1)}), bf16[8,784,128]{2,1,0:T(8,128)(2,1)S(1)}, u32[]{:S(2)}, u32[]{:S(2)}) async-start(bf16[8,784,128]{2,1,0:T(8,128)(2,1)} %shard_map.186), calls=%async_computation | async-start | bytes 3211264 | tf_op jit(solution)/shard_map/all_to_all | solution.py:787
  12.6 0.0 copy-done.8
  12.6 0.0 copy-done.9
  12.6 6.0 %all-gather.1.mtaps_ref = f32[4,5,512]{2,1,0:T(8,128)S(1)} all-gather(f32[1,5,512]{2,1,0:T(8,128)S(1)} %maximum_bitcast_fusion), channel_id=2, replica_groups=mesh['ctx'=8,'fsdp'=4] {'fsdp'}, dimensions={0}, use_global_device_ids=true | all-gather | bytes 51200 | tf_op jit(solution)/shard_map/all_gather | solution.py:776
  18.7 30.8 %all-to-all-done.x_ref = bf16[8,784,128]{2,1,0:T(8,128)(2,1)S(1)} async-done(((bf16[8,784,128]{2,1,0:T(8,128)(2,1)}), bf16[8,784,128]{2,1,0:T(8,128)(2,1)S(1)}, u32[]{:S(2)}, u32[]{:S(2)}) %all-to-all-start) | async-done | bytes 1605664 | tf_op jit(solution)/shard_map/all_to_all | solution.py:787
  49.4 0.0 copy-done.3
  49.4 0.0 copy-done.4
  49.5 0.0 copy-done.5
  49.5 0.0 copy-done.6
  49.5 0.0 copy-done.7
  49.5 16.4 %shard_map.187 = bf16[8,592,128]{2,1,0:T(8,128)(2,1)} custom-call(bf16[8,784,128]{2,1,0:T(8,128)(2,1)S(1)} %all-to-all-done.x_ref, f32[4,2048]{1,0:T(4,128)S(1)} %copy-done.3, f32[1,2048]{1,0:T(1,128)S(1)} %bitcast.12, f32[4,5,512]{2,1,0:T(8,128)S(1)} %all-gather.1.mtaps_ref, f32[32]{0:T(128)S(1)} %copy-done.5, f32[32]{0:T(128)S(1)} %copy-done.6, ...), custom_call_target="tpu_custom_call" | custom-call | tf_op jit(solution)/shard_map/pallas_call | solution.py:793
  65.9 4.7 %all-to-all-start.1 = ((bf16[8,592,128]{2,1,0:T(8,128)(2,1)}), bf16[8,592,128]{2,1,0:T(8,128)(2,1)S(1)}, u32[]{:S(2)}, u32[]{:S(2)}) async-start(bf16[8,592,128]{2,1,0:T(8,128)(2,1)} %shard_map.187), calls=%async_computation.1 | async-start | bytes 2424832 | tf_op jit(solution)/shard_map/all_to_all | solution.py:825
  70.6 28.6 %all-to-all-done.1.y_ref = bf16[8,592,128]{2,1,0:T(8,128)(2,1)S(1)} async-done(((bf16[8,592,128]{2,1,0:T(8,128)(2,1)}), bf16[8,592,128]{2,1,0:T(8,128)(2,1)S(1)}, u32[]{:S(2)}, u32[]{:S(2)}) %all-to-all-start.1) | async-done | bytes 1212448 | tf_op jit(solution)/shard_map/all_to_all | solution.py:825
  99.2 1.1 %shard_map.188 = (f32[128,2048]{1,0:T(8,128)}, f32[128,32]{1,0:T(8,128)S(1)}, f32[4,2048]{1,0:T(4,128)}, f32[1,2048]{1,0:T(1,128)}, f32[8,128]{1,0:T(8,128)S(1)}...) custom-call(bf16[8,592,128]{2,1,0:T(8,128)(2,1)S(1)} %all-to-all-done.1.y_ref), custom_call_target="tpu_custom_call" | custom-call | tf_op jit(solution)/shard_map/pallas_call | solution.py:826
  100.4 1.6 %collective-permute-start = (f32[136,256]{1,0:T(8,128)S(1)}, f32[136,256]{1,0:T(8,128)S(1)}, u32[]{:S(2)}, u32[]{:S(2)}) collective-permute-start(f32[136,256]{1,0:T(8,128)S(1)} %get-tuple-element.18), channel_id=1, source_target_pairs={{0,2},{2,3},{1,0},{3,1},{4,6},{6,7},{5,4},{7,5},{8,10},{10,11},{9,... | collective-permute-start | bytes 417800 | tf_op jit(solution)/shard_map/ppermute | solution.py:842
  102.0 3.0 %collective-permute-start.1 = (f32[136,256]{1,0:T(8,128)S(1)}, f32[136,256]{1,0:T(8,128)S(1)}, u32[]{:S(2)}, u32[]{:S(2)}) collective-permute-start(f32[136,256]{1,0:T(8,128)S(1)} %get-tuple-element.19), channel_id=1, source_target_pairs={{0,0},{2,1},{1,2},{3,3},{4,4},{6,5},{5,6},{7,7},{8,8},{10,9},{9,10... | collective-permute-start | bytes 417800 | tf_op jit(solution)/shard_map/ppermute | solution.py:841
  105.0 0.7 copy.24
  105.7 0.5 slice_bitcast_fusion
  106.2 0.0 collective-permute-done
  106.2 2.1 %collective-permute-done.1 = f32[136,256]{1,0:T(8,128)S(1)} collective-permute-done((f32[136,256]{1,0:T(8,128)S(1)}, f32[136,256]{1,0:T(8,128)S(1)}, u32[]{:S(2)}, u32[]{:S(2)}) %collective-permute-start.1) | collective-permute-done | bytes 139296 | tf_op jit(solution)/shard_map/ppermute | solution.py:841
  108.4 0.6 pad_maximum_fusion
  108.9 0.6 fusion.1
  109.5 0.7 fusion
  (2 shorter events, 0.0 us)
Async XLA Ops:
  1.5 1.0 copy-start
  2.5 1.0 copy-start.1
  3.5 1.0 copy-start.2
  6.0 6.6 %copy-start.8 = (f32[4,512]{1,0:T(4,128)S(1)}, f32[4,512]{1,0:T(4,128)}, u32[]{:S(2)}) copy-start(f32[4,512]{1,0:T(4,128)} %param.16) | copy-start | bytes 24580
  6.0 6.6 %copy-start.9 = (f32[512]{0:T(512)S(1)}, f32[512]{0:T(512)}, u32[]{:S(2)}) copy-start(f32[512]{0:T(512)} %param.18) | copy-start | bytes 6148
  6.0 43.4 %copy-start.3 = (f32[4,2048]{1,0:T(4,128)S(1)}, f32[4,2048]{1,0:T(4,128)}, u32[]{:S(2)}) copy-start(f32[4,2048]{1,0:T(4,128)} %taps_ref.1) | copy-start | bytes 98308
  6.0 43.4 %copy-start.4 = (f32[2048]{0:T(1024)S(1)}, f32[2048]{0:T(1024)}, u32[]{:S(2)}) copy-start(f32[2048]{0:T(1024)} %param.17) | copy-start | bytes 24580
  6.0 43.4 %copy-start.5 = (f32[32]{0:T(128)S(1)}, f32[32]{0:T(128)}, u32[]{:S(2)}) copy-start(f32[32]{0:T(128)} %alog_ref.1) | copy-start | bytes 388
  6.1 43.4 %copy-start.6 = (f32[32]{0:T(128)S(1)}, f32[32]{0:T(128)}, u32[]{:S(2)}) copy-start(f32[32]{0:T(128)} %dtb_ref.1) | copy-start | bytes 388
  6.1 43.4 %copy-start.7 = (f32[32]{0:T(128)S(1)}, f32[32]{0:T(128)}, u32[]{:S(2)}) copy-start(f32[32]{0:T(128)} %skip_ref.1) | copy-start | bytes 388
  6.1 43.4 %all-to-all-start = ((bf16[8,784,128]{2,1,0:T(8,128)(2,1)}), bf16[8,784,128]{2,1,0:T(8,128)(2,1)S(1)}, u32[]{:S(2)}, u32[]{:S(2)}) async-start(bf16[8,784,128]{2,1,0:T(8,128)(2,1)} %shard_map.186), calls=%async_computation | async-start | bytes 3211264 | tf_op jit(solution)/shard_map/all_to_all | solution.py:787
  65.9 33.3 %all-to-all-start.1 = ((bf16[8,592,128]{2,1,0:T(8,128)(2,1)}), bf16[8,592,128]{2,1,0:T(8,128)(2,1)S(1)}, u32[]{:S(2)}, u32[]{:S(2)}) async-start(bf16[8,592,128]{2,1,0:T(8,128)(2,1)} %shard_map.187), calls=%async_computation.1 | async-start | bytes 2424832 | tf_op jit(solution)/shard_map/all_to_all | solution.py:825
  100.4 5.8 %collective-permute-start = (f32[136,256]{1,0:T(8,128)S(1)}, f32[136,256]{1,0:T(8,128)S(1)}, u32[]{:S(2)}, u32[]{:S(2)}) collective-permute-start(f32[136,256]{1,0:T(8,128)S(1)} %get-tuple-element.18), channel_id=1, source_target_pairs={{0,2},{2,3},{1,0},{3,1},{4,6},{6,7},{5,4},{7,5},{8,10},{10,11},{9,... | collective-permute-start | bytes 417800 | tf_op jit(solution)/shard_map/ppermute | solution.py:842
  102.0 6.4 %collective-permute-start.1 = (f32[136,256]{1,0:T(8,128)S(1)}, f32[136,256]{1,0:T(8,128)S(1)}, u32[]{:S(2)}, u32[]{:S(2)}) collective-permute-start(f32[136,256]{1,0:T(8,128)S(1)} %get-tuple-element.19), channel_id=1, source_target_pairs={{0,0},{2,1},{1,2},{3,3},{4,4},{6,5},{5,6},{7,7},{8,8},{10,9},{9,10... | collective-permute-start | bytes 417800 | tf_op jit(solution)/shard_map/ppermute | solution.py:841

commit v2 on v0

--- a/solution.py
+++ b/solution.py
@@ -1,8 +1,11 @@
+import functools
 import math
 
 import jax
 import jax.numpy as jnp
 from jax import lax
+from jax.experimental import pallas as pl
+from jax.experimental.pallas import tpu as pltpu
 from jax.sharding import PartitionSpec as P
 
 HEADS = 128
@@ -206,7 +209,7 @@
     return jnp.concatenate([grad_pre[0, :rim], grad_pre[1, :rim]], axis=0)
 
 
-def shards(
+def shards_chain(
     sig_raw,
     map_raw,
     step_size_logits,
@@ -327,6 +330,743 @@
         final[5],
         final[6],
     )
+
+
+TILE = 128
+HALF = 64
+NT = (((1,), (1,)), ((), ()))
+TN = (((0,), (0,)), ((), ()))
+NN = (((1,), (0,)), ((), ()))
+BF = jnp.bfloat16
+F32 = jnp.float32
+
+
+def mm(a, b, dims=NN):
+    return lax.dot_general(a, b, dims, preferred_element_type=F32)
+
+
+def mm_f32(a, b, dims=NN):
+    return lax.dot_general(a, b, dims, precision=lax.Precision.HIGHEST, preferred_element_type=F32)
+
+
+def split3(x):
+    hi = x.astype(BF)
+    rest = x - hi.astype(F32)
+    mid = rest.astype(BF)
+    return hi, mid, (rest - mid.astype(F32)).astype(BF)
+
+
+def ids(shape, dim):
+    return lax.broadcasted_iota(jnp.int32, shape, dim)
+
+
+def lanes_of(j):
+    return slice(j * TILE, (j + 1) * TILE)
+
+
+def place():
+    ctx_place = lax.axis_index("ctx")
+    quad = lax.div(ctx_place, 4)
+    return quad, lax.rem(ctx_place, 4), lax.axis_index("fsdp")
+
+
+def at_tile(start, width=TILE):
+    return pl.ds(pl.multiple_of(start, TILE), width)
+
+
+def pack_kernel(sig_ref, map_ref, dt_ref, dy_ref, *rest):
+    x_refs, halo_refs, (dt_rows, sems) = rest[:4], rest[4:8], rest[8:]
+    quad, r, f = place()
+    copies = []
+
+    def send(source, target):
+        copy = pltpu.make_async_copy(source, target, sems.at[len(copies)])
+        copy.start()
+        copies.append(copy)
+
+    half = map_ref.shape[1] // 2
+    for k in (1, 2, 3, 0):
+        dest = lax.bitwise_xor(r, k)
+        x = x_refs[k]
+        cols = at_tile(dest * 4 * TILE, 4 * TILE)
+        send(sig_ref.at[:, cols], x.at[0:TILE, :])
+        send(dy_ref.at[:, cols], x.at[TILE : 2 * TILE, :])
+        group = (2 * f + lax.div(dest, 2)) * TILE
+        for j in range(2):
+            for e in range(2):
+                send(
+                    map_ref.at[e * HALF : (e + 1) * HALF, at_tile(group + j * half)],
+                    x.at[2 * TILE : 2 * TILE + HALF, lanes_of(2 * j + e)],
+                )
+    for m in range(4):
+        dest = jnp.where(quad == 0, m, 3 - m)
+        rows = pl.ds(pl.multiple_of(jnp.where(quad == 0, HALF - 16, TILE - 16), 16), 16)
+        send(sig_ref.at[rows, at_tile(dest * 4 * TILE, 4 * TILE)], halo_refs[m].at[:, 0 : 4 * TILE])
+        group = (2 * f + lax.div(dest, 2)) * TILE
+        for j in range(2):
+            send(map_ref.at[rows, at_tile(group + j * half)], halo_refs[m].at[:, lanes_of(4 + j)])
+    for k in range(4):
+        dest = lax.bitwise_xor(r, k)
+        hi, mid, lo = split3(dt_ref[pl.ds(pl.multiple_of(8 * dest, 8), 8), :])
+        zero = jnp.zeros((8, TILE), F32)
+        dt_rows[k, :, 0:TILE] = jnp.concatenate([hi.astype(F32), mid.astype(F32)], axis=0).astype(BF)
+        dt_rows[k, :, TILE : 2 * TILE] = jnp.concatenate([lo.astype(F32), zero], axis=0).astype(BF)
+        dt_rows[k, :, 2 * TILE : 4 * TILE] = jnp.zeros((16, 2 * TILE), BF)
+        send(dt_rows.at[k], x_refs[k].at[2 * TILE + HALF : 2 * TILE + HALF + 16, :])
+    for copy in copies:
+        copy.wait()
+
+
+def tap_rows(j, taps_ref, bias_ref, mtaps_ref):
+    quad, r, f = place()
+    if j < 4:
+        at = at_tile((4 * r + j) * TILE)
+        return [taps_ref[k : k + 1, at] for k in range(4)], bias_ref[0:1, at]
+    group = 2 * f + lax.div(r, 2)
+    owner = 2 * (j - 4) + lax.div(f, 2)
+    at = at_tile(lax.rem(group, 4) * TILE)
+    return [mtaps_ref[owner, k : k + 1, at] for k in range(4)], mtaps_ref[owner, 4:5, at]
+
+
+def shifted(block, k):
+    return block[8:] if k == 3 else pltpu.roll(block, 3 - k, 0)[8:]
+
+
+def columns(*rows8):
+    total = 8 * len(rows8)
+    full = jnp.concatenate(list(rows8) + [jnp.zeros((TILE - total, TILE), F32)], axis=0)
+    return jnp.transpose(full)
+
+
+def head_row(ref, r):
+    row8 = ids((8, TILE), 0)
+    out = jnp.zeros((8, TILE), F32)
+    for h in range(8):
+        out = jnp.where(row8 == h, ref[8 * r + h], out)
+    return out
+
+
+def first_kernel(
+    x0,
+    x1,
+    x2,
+    x3,
+    b0,
+    b1,
+    b2,
+    b3,
+    taps_ref,
+    bias_ref,
+    mtaps_ref,
+    alog_ref,
+    dtb_ref,
+    mid_ref,
+    xp,
+    dp,
+    act,
+    slope,
+    scaled_s,
+    weighted_s,
+    sgrad_s,
+    step_e,
+    toend_e,
+    exp_e,
+    s_s,
+    t_s,
+    step_r,
+    ds_r,
+    sig_r,
+    dt_src,
+):
+    quad, r, f = place()
+    high = quad == 1
+    half_lane = ids((TILE, TILE), 1) < HALF
+    lane8 = ids((8, TILE), 1)
+    for k, x in enumerate((x0, x1, x2, x3)):
+        s = lax.bitwise_xor(r, k)
+        low_at = pl.multiple_of(HALF * s, HALF)
+        up_at = pl.multiple_of(HALF * (3 - s), HALF)
+        for e, at in ((0, low_at), (1, up_at)):
+            here = slice(e * HALF, (e + 1) * HALF)
+            rows = pl.ds(pl.multiple_of(8 + at, 8), HALF)
+            xp[e, rows, 0 : 4 * TILE] = x[here, :].astype(F32)
+            for j in range(2):
+                xp[e, rows, lanes_of(4 + j)] = x[
+                    2 * TILE : 2 * TILE + HALF, lanes_of(2 * j + e)
+                ].astype(F32)
+            dp[pl.ds(pl.multiple_of(2 * TILE * e + at, HALF), HALF), :] = x[
+                TILE + e * HALF : TILE + (e + 1) * HALF, :
+            ]
+        packed = x[2 * TILE + HALF : 2 * TILE + HALF + 16, 0 : 2 * TILE].astype(F32)
+        dt_src[s] = packed[0:8, 0:TILE] + packed[8:16, 0:TILE] + packed[0:8, TILE : 2 * TILE]
+    edge = jnp.zeros((8, 6 * TILE), F32)
+    for b in (b0, b1, b2, b3):
+        edge = edge + b[...].astype(F32)[8:16]
+    xp[0, 0:8, :] = jnp.where(high, edge, 0.0)
+    xp[1, 0:8, :] = jnp.where(high, xp[0, 2 * TILE : 2 * TILE + 8, :], edge)
+
+    rate8 = -jnp.exp(head_row(alog_ref, r))
+    bias8 = head_row(dtb_ref, r)
+    for i in range(4):
+        if i < 2:
+            a, b = dt_src[2 * i], pltpu.roll(dt_src[2 * i + 1], HALF, 1)
+        else:
+            a, b = pltpu.roll(dt_src[7 - 2 * i], HALF, 1), dt_src[6 - 2 * i]
+        logits = jnp.where(lane8 < HALF, a, b) + bias8
+        small = jnp.exp(-jnp.abs(logits))
+        step = jnp.maximum(logits, 0.0) + jnp.log1p(small)
+        at8 = slice(8 * i, 8 * i + 8)
+        step_r[at8, :] = step
+        sig_r[at8, :] = jnp.where(logits >= 0, 1.0, small) / (1.0 + small)
+        ds_r[at8, :] = step * rate8
+    upto = (ids((TILE, TILE), 0) <= ids((TILE, TILE), 1)).astype(F32)
+    ds_r[...] = mm_f32(ds_r[...], upto)
+
+    ends = []
+    for i in range(4):
+        rows = slice(i * TILE, (i + 1) * TILE)
+        base = (i % 2) * TILE
+        for j in range(6):
+            lanes = lanes_of(j)
+            block = xp[i // 2, base : base + TILE + 8, lanes]
+            taps, bias = tap_rows(j, taps_ref, bias_ref, mtaps_ref)
+            pre = bias + taps[0] * shifted(block, 0)
+            for k in range(1, 4):
+                pre = pre + taps[k] * shifted(block, k)
+            sig = 1.0 / (1.0 + jnp.exp(-pre))
+            act[rows, lanes] = (pre * sig).astype(BF)
+            slope[rows, lanes] = sig * (1.0 + pre * (1.0 - sig))
+        cols = columns(step_r[8 * i : 8 * i + 8, :], ds_r[8 * i : 8 * i + 8, :])
+        end = []
+        for j in range(4):
+            lanes = lanes_of(j)
+            step = jnp.where(half_lane, cols[:, 2 * j : 2 * j + 1], cols[:, 2 * j + 1 : 2 * j + 2])
+            ds = jnp.where(
+                half_lane, cols[:, 8 + 2 * j : 9 + 2 * j], cols[:, 9 + 2 * j : 10 + 2 * j]
+            )
+            last = ds[TILE - 1 : TILE, :]
+            grow = jnp.exp(ds)
+            toend = jnp.exp(last - ds)
+            step_e[rows, lanes] = step
+            toend_e[rows, lanes] = toend
+            exp_e[rows, lanes] = grow
+            end.append(jnp.exp(last))
+            scaled = (act[rows, lanes].astype(F32) * step).astype(BF)
+            scaled_s[rows, lanes] = scaled
+            weighted_s[rows, lanes] = (scaled.astype(F32) * toend).astype(BF)
+            sgrad_s[rows, lanes] = (dp[rows, lanes].astype(F32) * grow).astype(BF)
+        ends.append(jnp.concatenate(end, axis=1))
+        s_s[i] = mm(act[rows, lanes_of(4)], weighted_s[rows, :], TN)
+        t_s[i] = mm(act[rows, lanes_of(5)], sgrad_s[rows, :], TN)
+    f_a = ends[1] * s_s[0] + s_s[1]
+    f_b = ends[3] * s_s[2] + s_s[3]
+    g_a = t_s[0] + ends[0] * t_s[1]
+    g_b = t_s[2] + ends[2] * t_s[3]
+    d_a = ends[0] * ends[1]
+    d_b = ends[2] * ends[3]
+    mid_ref[0:TILE, :] = jnp.where(high, d_b * f_a + f_b, f_a).astype(BF)
+    mid_ref[TILE : 2 * TILE, :] = jnp.where(high, g_a + d_a * g_b, g_b).astype(BF)
+    hi, mid, lo = split3(jnp.broadcast_to(d_a * d_b, (16, 4 * TILE)))
+    row16 = ids((16, 4 * TILE), 0)
+    parts = jnp.where(
+        row16 == 0,
+        hi.astype(F32),
+        jnp.where(row16 == 1, mid.astype(F32), jnp.where(row16 == 2, lo.astype(F32), 0.0)),
+    )
+    mid_ref[2 * TILE : 2 * TILE + 16, :] = parts.astype(BF)
+
+
+def second_kernel(dp, act, scaled_s, ds_r, diag_ref, gmap_ref, gsum_ref):
+    half_lane = ids((TILE, TILE), 1) < HALF
+    row8 = ids((8, TILE), 0)
+    col_q = ids((TILE, TILE), 1)
+    seen = ids((TILE, TILE), 0) <= col_q
+    for i in range(4):
+        rows = slice(i * TILE, (i + 1) * TILE)
+        in_map = act[rows, lanes_of(4)]
+        out_map = act[rows, lanes_of(5)]
+        score = mm(in_map, out_map, NT)
+        ds8 = ds_r[8 * i : 8 * i + 8, :]
+        cols = columns(ds8)
+        grad_score = jnp.zeros((TILE, TILE), F32)
+        gsum = jnp.zeros((8, TILE), F32)
+        rcol = jnp.zeros((TILE, TILE), F32)
+        for j in range(4):
+            sc = scaled_s[rows, lanes_of(j)]
+            dy = dp[rows, lanes_of(j)]
+            diag = jnp.zeros((TILE, TILE), F32)
+            for e in range(2):
+                h = 2 * j + e
+                part = half_lane if e == 0 else jnp.logical_not(half_lane)
+                gm = mm(jnp.where(part, sc, jnp.zeros_like(sc)), dy, NT)
+                spread = ds8[h : h + 1, :] - cols[:, h : h + 1]
+                decay = jnp.exp(jnp.where(seen, spread, -1e30))
+                gd = gm * decay
+                grad_score = grad_score + gd
+                both = gd * score
+                rcol = jnp.where(col_q == h, jnp.sum(both, axis=1, keepdims=True), rcol)
+                gsum = gsum + jnp.where(row8 == h, jnp.sum(both, axis=0, keepdims=True), 0.0)
+                mix = (score * decay).astype(BF)
+                diag = diag + mm(mix, jnp.where(part, dy, jnp.zeros_like(dy)))
+            diag_ref[rows, lanes_of(j)] = diag
+        gs = grad_score.astype(BF)
+        gmap_ref[rows, lanes_of(0)] = mm(gs, out_map)
+        gmap_ref[rows, lanes_of(1)] = mm(gs, in_map, TN)
+        gsum_ref[8 * i : 8 * i + 8, :] = gsum - jnp.transpose(rcol)[0:8, :]
+
+
+def eights(x):
+    return jnp.sum(x.reshape(x.shape[0] // 8, 8, x.shape[1]), axis=0)
+
+
+def third_kernel(
+    scale,
+    mid_ref,
+    xp,
+    dp,
+    act,
+    slope,
+    scaled_s,
+    weighted_s,
+    sgrad_s,
+    step_e,
+    toend_e,
+    exp_e,
+    s_s,
+    t_s,
+    step_r,
+    ds_r,
+    sig_r,
+    diag_ref,
+    gmap_ref,
+    gsum_ref,
+    taps_ref,
+    bias_ref,
+    mtaps_ref,
+    alog_ref,
+    skip_ref,
+    y0,
+    y1,
+    y2,
+    y3,
+    cross_ref,
+    h_s,
+    c_s,
+    gp,
+    dx,
+    blk,
+):
+    quad, r, f = place()
+    high = quad == 1
+    lane_row = ids((1, TILE), 1)
+    row8 = ids((8, TILE), 0)
+    lane8 = ids((8, TILE), 1)
+    rate8 = -jnp.exp(head_row(alog_ref, r))
+    ends = [exp_e[(i + 1) * TILE - 8 : (i + 1) * TILE, :][7:8, :] for i in range(4)]
+    f_in = mid_ref[0:TILE, :].astype(F32)
+    g_in = mid_ref[TILE : 2 * TILE, :].astype(F32)
+    across = jnp.sum(mid_ref[2 * TILE : 2 * TILE + 16, :].astype(F32), axis=0, keepdims=True)
+    f_a = ends[1] * s_s[0] + s_s[1]
+    h_s[0] = jnp.where(high, f_in, 0.0)
+    h_s[1] = ends[0] * h_s[0] + s_s[0]
+    h_s[2] = jnp.where(high, ends[1] * h_s[1] + s_s[1], across * f_a + f_in)
+    h_s[3] = ends[2] * h_s[2] + s_s[2]
+    g_b = t_s[2] + ends[2] * t_s[3]
+    c_s[3] = jnp.where(high, g_in, 0.0)
+    c_s[2] = t_s[3] + ends[3] * c_s[3]
+    c_s[1] = jnp.where(high, t_s[2] + ends[2] * c_s[2], g_in + across * g_b)
+    c_s[0] = t_s[1] + ends[1] * c_s[1]
+
+    row_q = ids((TILE, TILE), 0)
+    col_q = ids((TILE, TILE), 1)
+    tail_sums = jnp.concatenate(
+        [(row_q >= col_q).astype(F32), (row_q < col_q).astype(F32)], axis=0
+    )
+    skip_row = []
+    for j in range(4):
+        at = 8 * r + 2 * j
+        skip_row.append(jnp.where(lane_row < HALF, skip_ref[at], skip_ref[at + 1]))
+
+    def head_sums(x, j):
+        pick = (row8 == 2 * j + lane8 // HALF).astype(BF)
+        hi = x.astype(BF)
+        lo = (x - hi.astype(F32)).astype(BF)
+        return mm(pick, hi, NT) + mm(pick, lo, NT)
+
+    taps_of = [tap_rows(j, taps_ref, bias_ref, mtaps_ref)[0] for j in range(6)]
+    after = [jnp.zeros((8, TILE), F32) for _ in range(6)]
+    tap_acc = [[jnp.zeros((8, TILE), F32) for _ in range(5)] for _ in range(6)]
+    skip_acc = [jnp.zeros((8, TILE), F32) for _ in range(4)]
+    alog_acc = jnp.zeros((8, TILE), F32)
+    ddt_acc = jnp.zeros((8, TILE), F32)
+    first_low = None
+    for i in (3, 2, 1, 0):
+        rows = slice(i * TILE, (i + 1) * TILE)
+        at8 = slice(8 * i, 8 * i + 8)
+        in_map = act[rows, lanes_of(4)]
+        out_map = act[rows, lanes_of(5)]
+        h_low = h_s[i].astype(BF)
+        c_low = c_s[i].astype(BF)
+        off = mm(out_map, h_low)
+        gw = mm(in_map, c_low)
+        out_grad = mm(sgrad_s[rows, :], h_low, NT)
+        in_grad = mm(weighted_s[rows, :], c_low, NT)
+        end_row = jnp.sum(h_s[i] * c_s[i], axis=0, keepdims=True) * ends[i]
+        gsum = gsum_ref[at8, :]
+        back = jnp.zeros((8, TILE), F32)
+        stepsum = jnp.zeros((8, TILE), F32)
+        end_sum = jnp.zeros((8, TILE), F32)
+        for j in range(4):
+            lanes = lanes_of(j)
+            dyf = dp[rows, lanes].astype(F32)
+            scf = scaled_s[rows, lanes].astype(F32)
+            sigf = act[rows, lanes].astype(F32)
+            gwe = gw[:, lanes] * toend_e[rows, lanes]
+            grad_scaled = gwe + diag_ref[rows, lanes]
+            gsum = gsum + head_sums(dyf * exp_e[rows, lanes] * off[:, lanes], j)
+            back = back + head_sums(gwe * scf, j)
+            stepsum = stepsum + head_sums(grad_scaled * sigf, j)
+            end_sum = end_sum + jnp.where(row8 == 2 * j + lane8 // HALF, end_row[:, lanes], 0.0)
+            skip_acc[j] = skip_acc[j] + eights(dyf * sigf)
+            grad_sig = skip_row[j] * dyf + grad_scaled * step_e[rows, lanes]
+            gp[:, lanes] = grad_sig * slope[rows, lanes]
+        gp[:, lanes_of(4)] = (in_grad + gmap_ref[rows, lanes_of(0)]) * slope[rows, lanes_of(4)]
+        gp[:, lanes_of(5)] = (out_grad + gmap_ref[rows, lanes_of(1)]) * slope[rows, lanes_of(5)]
+        grad_log = mm_f32(jnp.concatenate([gsum, back], axis=1), tail_sums) + jnp.sum(
+            end_sum, axis=1, keepdims=True
+        )
+        ddt = (grad_log * rate8 + stepsum) * sig_r[at8, :]
+        blk[2 * i] = ddt
+        blk[2 * i + 1] = pltpu.roll(ddt, HALF, 1)
+        ddt_acc = ddt_acc + ddt
+        alog_acc = alog_acc + grad_log * step_r[at8, :]
+        base = (i % 2) * TILE
+        starts = []
+        for j in range(6):
+            lanes = lanes_of(j)
+            here = gp[:, lanes]
+            grads = jnp.concatenate([here, after[j]], axis=0)
+            block = xp[i // 2, base : base + TILE + 8, lanes]
+            taps = taps_of[j]
+            raw = taps[3] * here
+            for k in range(3):
+                raw = raw + taps[k] * pltpu.roll(grads, 5 + k, 0)[8:]
+            for k in range(4):
+                tap_acc[j][k] = tap_acc[j][k] + eights(here * shifted(block, k))
+            tap_acc[j][4] = tap_acc[j][4] + eights(here)
+            dx[rows, lanes] = raw.astype(BF)
+            starts.append(here[0:8])
+            after[j] = jnp.where(high, starts[j], 0.0) if i == 2 else starts[j]
+        if i == 2:
+            first_low = starts
+        if i == 0:
+            first_high = starts
+
+    for j in range(6):
+        first = jnp.where(high, first_high[j], first_low[j])
+        grads = jnp.concatenate([jnp.zeros((8, TILE), F32), first], axis=0)
+        spill = jnp.zeros((8, TILE), F32)
+        for k in range(3):
+            spill = spill + taps_of[j][k] * pltpu.roll(grads, 5 + k, 0)[8:]
+        starts[j] = spill
+    zero8 = jnp.zeros((8, TILE), F32)
+    cross_ref[0:16, :] = jnp.concatenate(
+        [
+            jnp.concatenate(starts[0:4], axis=1),
+            jnp.concatenate([starts[4], starts[5], zero8, zero8], axis=1),
+        ],
+        axis=0,
+    ).astype(BF)
+    rows = []
+    for j in range(6):
+        for k in range(5):
+            rows.append(jnp.sum(tap_acc[j][k], axis=0, keepdims=True))
+    trio = jnp.zeros((TILE, TILE), F32)
+    alog = jnp.sum(alog_acc * rate8, axis=1, keepdims=True)
+    ddtb = jnp.sum(ddt_acc, axis=1, keepdims=True)
+    skips = jnp.zeros((8, TILE), F32)
+    for j in range(4):
+        total = jnp.sum(skip_acc[j], axis=0, keepdims=True)
+        skips = skips + jnp.where(row8 == 2 * j + lane8 // HALF, total, 0.0)
+    skips = jnp.sum(skips, axis=1, keepdims=True)
+    three = jnp.where(lane8 == 0, alog, jnp.where(lane8 == 1, ddtb, skips))
+    flat = columns(jnp.where(lane8 < 3, three, 0.0))
+    trio = flat[0:1] + pltpu.roll(flat[0:8], 32, 1)[1:2] + pltpu.roll(flat[0:8], 64, 1)[2:3]
+    trio = pltpu.roll(jnp.broadcast_to(trio, (8, TILE)), 8 * r, 1)[0:1]
+    params = jnp.concatenate(rows + [trio, jnp.zeros((1, TILE), F32)], axis=0) * scale
+    p_hi, p_lo, _ = split3(params)
+    param_rows = jnp.concatenate([p_hi[0:16], p_hi[16:32], p_lo[0:16], p_lo[16:32]], axis=1)
+    cross_ref[16:32, :] = param_rows
+    for k, y in enumerate((y0, y1, y2, y3)):
+        s = lax.bitwise_xor(r, k)
+        low_rows = pl.ds(pl.multiple_of(HALF * s, HALF), HALF)
+        up_rows = pl.ds(pl.multiple_of(2 * TILE + HALF * (3 - s), HALF), HALF)
+        y[0:HALF, :] = dx[low_rows, 0 : 4 * TILE]
+        y[HALF:TILE, :] = dx[up_rows, 0 : 4 * TILE]
+        for j in range(2):
+            y[TILE : TILE + HALF, lanes_of(2 * j)] = dx[low_rows, lanes_of(4 + j)]
+            y[TILE : TILE + HALF, lanes_of(2 * j + 1)] = dx[up_rows, lanes_of(4 + j)]
+        here = jnp.where(lane8 < HALF, blk[s], pltpu.roll(blk[7 - s], HALF, 1))
+        hi, mid, lo = split3(here)
+        top = jnp.concatenate([hi.astype(F32), mid.astype(F32)], axis=0)
+        low = jnp.concatenate([lo.astype(F32), zero8], axis=0)
+        y[TILE + HALF : TILE + HALF + 16, :] = jnp.concatenate(
+            [top, low, jnp.zeros((16, 2 * TILE), F32)], axis=1
+        ).astype(BF)
+        y[TILE + HALF + 16 : TILE + HALF + 32, :] = param_rows
+
+
+def whole_params(ref, start):
+    value = ref[start : start + 16, :].astype(F32)
+    return jnp.concatenate(
+        [
+            value[:, lanes_of(0)] + value[:, lanes_of(2)],
+            value[:, lanes_of(1)] + value[:, lanes_of(3)],
+        ],
+        axis=0,
+    )
+
+
+PARAMS_AT = TILE + HALF + 16
+
+
+def maps_kernel(y0, y1, y2, y3, z0, z1, z2, z3, one_ref, two_ref):
+    quad, r, f = place()
+    ys, zs = (y0, y1, y2, y3), (z0, z1, z2, z3)
+    even = lax.rem(f, 2) == 0
+    own = lax.div(r, 2)
+    row8 = ids((8, TILE), 0)
+    third = jnp.logical_and(quad == 0, r == 3)
+    fourth = jnp.logical_and(quad == 1, r == 0)
+    for pair in range(2):
+        group = own if pair == 0 else 1 - own
+        lanes = at_tile(group * TILE)
+        sums = []
+        for j in range(2):
+            halves = []
+            for e in range(2):
+                total = jnp.zeros((HALF, TILE), F32)
+                spill = jnp.zeros((8, TILE), F32)
+                for k in (2 * pair, 2 * pair + 1):
+                    total = total + ys[k][TILE : TILE + HALF, lanes_of(2 * j + e)].astype(F32)
+                    spill = spill + zs[k][0:16, lanes_of(j)].astype(F32)[8:16]
+                here = third if e == 0 else fourth
+                spill = jnp.where(here, spill, 0.0)
+                halves += [total[0 : HALF - 8], total[HALF - 8 : HALF] + spill]
+            five = jnp.zeros((8, TILE), F32)
+            for k in (2 * pair, 2 * pair + 1):
+                for ref, start in ((ys[k], PARAMS_AT), (zs[k], 16)):
+                    param = whole_params(ref, start)
+                    for t in range(5):
+                        five = five + jnp.where(row8 == t, param[20 + 5 * j + t : 21 + 5 * j + t], 0.0)
+            sums.append(jnp.concatenate(halves + [five], axis=0))
+        one_ref[:, lanes] = jnp.where(even, sums[0], sums[1])
+        two_ref[:, lanes] = jnp.where(even, sums[1], sums[0])
+
+
+def rows_kernel(y0, y1, y2, y3, z0, z1, z2, z3, dsig_ref, ddt_ref, taps_ref, bias_ref, trio_ref):
+    quad, r, f = place()
+    third = jnp.logical_and(quad == 0, r == 3)
+    fourth = jnp.logical_and(quad == 1, r == 0)
+    trio = jnp.zeros((1, TILE), F32)
+    for k, (y, z) in enumerate(((y0, z0), (y1, z1), (y2, z2), (y3, z3))):
+        s = lax.bitwise_xor(r, k)
+        cols = at_tile(s * 4 * TILE, 4 * TILE)
+        dsig_ref[:, cols] = y[0:TILE, :].astype(F32)
+        spill = z[0:16, :].astype(F32)[0:8]
+        dsig_ref[HALF - 8 : HALF, cols] += jnp.where(third, spill, 0.0)
+        dsig_ref[TILE - 8 : TILE, cols] += jnp.where(fourth, spill, 0.0)
+        packed = y[TILE + HALF : TILE + HALF + 16, 0 : 2 * TILE].astype(F32)
+        ddt_ref[pl.ds(pl.multiple_of(8 * s, 8), 8), :] = (
+            packed[0:8, 0:TILE] + packed[8:16, 0:TILE] + packed[0:8, TILE : 2 * TILE]
+        )
+        params = whole_params(y, PARAMS_AT) + whole_params(z, 16)
+        for j in range(4):
+            lanes = at_tile((4 * s + j) * TILE)
+            taps_ref[0:4, lanes] = params[5 * j : 5 * j + 4]
+            bias_ref[0:1, lanes] = params[5 * j + 4 : 5 * j + 5]
+        trio = trio + params[30:31]
+    trio_ref[...] = jnp.broadcast_to(trio, (8, TILE))
+
+
+ROUTE_ONE = [(0, 0), (2, 1), (1, 2), (3, 3)]
+ROUTE_TWO = [(0, 2), (2, 3), (1, 0), (3, 1)]
+
+
+def shards_quad(
+    sig_raw,
+    map_raw,
+    step_size_logits,
+    d_out,
+    sig_taps,
+    map_taps,
+    sig_bias,
+    map_bias,
+    a_log,
+    dt_bias,
+    skip_gain,
+):
+    ctx = lax.axis_size("ctx")
+    fsdp = lax.axis_size("fsdp")
+    rows, sig_width = sig_raw.shape
+    vmem = pl.BlockSpec(memory_space=pltpu.VMEM)
+    smem = pl.BlockSpec(memory_space=pltpu.SMEM)
+    any_space = pl.BlockSpec(memory_space=pl.ANY)
+
+    def call(kernel, out_shape, in_specs, out_specs, scratch, mib, cost):
+        return pl.pallas_call(
+            kernel,
+            out_shape=out_shape,
+            in_specs=in_specs,
+            out_specs=out_specs,
+            scratch_shapes=scratch,
+            compiler_params=pltpu.CompilerParams(vmem_limit_bytes=mib * 1024 * 1024),
+            cost_estimate=pl.CostEstimate(flops=cost, bytes_accessed=cost // 100, transcendentals=0),
+        )
+
+    def shape(*dims, kind=F32):
+        return jax.ShapeDtypeStruct(dims, kind)
+
+    inside = [[(c, c ^ k) for c in range(ctx)] for k in range(4)]
+    over = [[(c, c ^ 4 ^ k) for c in range(ctx)] for k in range(4)]
+    x_rows = 2 * TILE + HALF + 16
+    packed = call(
+        pack_kernel,
+        (shape(x_rows, 4 * TILE, kind=BF),) * 4 + (shape(16, 6 * TILE, kind=BF),) * 4,
+        [any_space, any_space, vmem, any_space],
+        (any_space,) * 8,
+        [pltpu.VMEM((4, 16, 4 * TILE), BF), pltpu.SemaphoreType.DMA((40,))],
+        16,
+        10**6,
+    )(sig_raw, map_raw, step_size_logits.T, d_out)
+    xs = [packed[0]] + [lax.ppermute(packed[k], "ctx", inside[k]) for k in (1, 2, 3)]
+    halos = [lax.ppermute(packed[4 + m], "ctx", [(3, 4 + m), (4, 3 - m)]) for m in range(4)]
+    map_params = lax.all_gather(
+        jnp.concatenate([map_taps, map_bias[None, :]], axis=0), "fsdp", axis=0
+    )
+    total = 4 * TILE
+    mid, *kept = call(
+        first_kernel,
+        (
+            shape(2 * TILE + 16, 4 * TILE, kind=BF),
+            shape(2, 2 * TILE + 8, 6 * TILE),
+            shape(total, 4 * TILE, kind=BF),
+            shape(total, 6 * TILE, kind=BF),
+            shape(total, 6 * TILE),
+            shape(total, 4 * TILE, kind=BF),
+            shape(total, 4 * TILE, kind=BF),
+            shape(total, 4 * TILE, kind=BF),
+            shape(total, 4 * TILE),
+            shape(total, 4 * TILE),
+            shape(total, 4 * TILE),
+            shape(4, TILE, 4 * TILE),
+            shape(4, TILE, 4 * TILE),
+            shape(32, TILE),
+            shape(32, TILE),
+            shape(32, TILE),
+        ),
+        [vmem] * 11 + [smem] * 2,
+        (vmem,) * 16,
+        [pltpu.VMEM((4, 8, TILE), F32)],
+        24,
+        10**9,
+    )(*xs, *halos, sig_taps, sig_bias[None, :], map_params, a_log, dt_bias)
+    xp, dp, act, slope, scaled, weighted, sgrad, step_e, toend_e, exp_e, s_s, t_s = kept[:12]
+    step_r, ds_r, sig_r = kept[12:]
+    mid = lax.ppermute(mid, "ctx", over[0])
+    diag, gmap, gsum = call(
+        second_kernel,
+        (shape(total, 4 * TILE), shape(total, 2 * TILE), shape(32, TILE)),
+        [vmem] * 4,
+        (vmem,) * 3,
+        [],
+        16,
+        10**9,
+    )(dp, act, scaled, ds_r)
+    scale = 1.0 / math.sqrt(float(ctx * rows))
+    y_rows = TILE + HALF + 32
+    *ys, cross = call(
+        functools.partial(third_kernel, scale),
+        (shape(y_rows, 4 * TILE, kind=BF),) * 4 + (shape(32, 4 * TILE, kind=BF),),
+        [vmem] * 22 + [smem] * 2,
+        (vmem,) * 5,
+        [
+            pltpu.VMEM((4, TILE, 4 * TILE), F32),
+            pltpu.VMEM((4, TILE, 4 * TILE), F32),
+            pltpu.VMEM((TILE, 6 * TILE), F32),
+            pltpu.VMEM((total, 6 * TILE), BF),
+            pltpu.VMEM((8, 8, TILE), F32),
+        ],
+        32,
+        10**9,
+    )(
+        mid,
+        *kept,
+        diag,
+        gmap,
+        gsum,
+        sig_taps,
+        sig_bias[None, :],
+        map_params,
+        a_log,
+        skip_gain,
+    )
+    ys = [ys[0]] + [lax.ppermute(ys[k], "ctx", inside[k]) for k in (1, 2, 3)]
+    zs = [lax.ppermute(cross, "ctx", over[k]) for k in range(4)]
+    one, two = call(
+        maps_kernel,
+        (shape(TILE + 8, 2 * TILE), shape(TILE + 8, 2 * TILE)),
+        [vmem] * 8,
+        (vmem,) * 2,
+        [],
+        16,
+        10**6,
+    )(*ys, *zs)
+    one = lax.ppermute(one, "fsdp", ROUTE_ONE)
+    two = lax.ppermute(two, "fsdp", ROUTE_TWO)
+    d_sig, d_dt, taps, bias, trio = call(
+        rows_kernel,
+        (
+            shape(rows, sig_width),
+            shape(32, TILE),
+            shape(4, sig_width),
+            shape(1, sig_width),
+            shape(8, TILE),
+        ),
+        [vmem] * 8,
+        (vmem,) * 5,
+        [],
+        16,
+        10**8,
+    )(*ys, *zs)
+    swap = lax.axis_index("fsdp") >= fsdp // 2
+    d_map = jnp.concatenate([jnp.where(swap, two, one), jnp.where(swap, one, two)], axis=1)
+    return (
+        d_sig,
+        d_map[:rows],
+        d_dt.T,
+        taps,
+        d_map[rows : rows + 4],
+        bias[0],
+        d_map[rows + 4],
+        trio[0, 0:32],
+        trio[0, 32:64],
+        trio[0, 64:96],
+    )
+
+
+def shards(*args):
+    sig_raw, map_raw, step_size_logits = args[:3]
+    ctx = lax.axis_size("ctx")
+    fsdp = lax.axis_size("fsdp")
+    fits = (
+        ctx == 8
+        and fsdp == 4
+        and sig_raw.shape == (TILE, 2048)
+        and map_raw.shape == (TILE, 2 * GROUPS * STATE)
+        and step_size_logits.shape[1] == 32
+    )
+    return shards_quad(*args) if fits else shards_chain(*args)
 
 
 def solution(mesh):

time: 769 us -> 79.2 us (0.10)
  the two profiles are of different devices: /device:TPU:0 before, /device:TPU:1 now
where the time goes in v2:
time: 79.2 us; the launch traced here: 78.8 us
  waiting for transfers between devices  24.8 us (31%)
  starting transfers between devices  24.4 us (31%)
  Pallas kernels  15.4 us (19%)
  blocking collectives  6.29 us (8%)
  local copies, waits for them, and re-layouts  4.46 us (6%)
  other arithmetic  2.67 us (3%)
  between operations  0.81 us (1%)
    ppermute x4, waiting for transfers between devices, shards_quad(): zs = [lax.ppermute(cross, 'ctx', over[k]) for k in range(4)]  9.83 us
    ppermute x1, waiting for transfers between devices, shards_quad(): mid = lax.ppermute(mid, 'ctx', over[0])  8.81 us
    all_gather x1, blocking collectives, shards_quad(): lax.all_gather(jnp.concatenate([map_taps, map_bias[None, :]], axis=0), 'f...  6.29 us
    pallas_call x1, Pallas kernels, shards_quad(): call(functools.partial(third_kernel, scale), (shape(y_rows, 4 * TILE, kin...  5.39 us
    ppermute x1, starting transfers between devices, shards_quad(): mid = lax.ppermute(mid, 'ctx', over[0])  4.47 us
    ppermute x4, starting transfers between devices, shards_quad(): zs = [lax.ppermute(cross, 'ctx', over[k]) for k in range(4)]  4.04 us
    pallas_call x1, Pallas kernels, shards_quad(): call(second_kernel, (shape(total, 4 * TILE), shape(total, 2 * TILE), shap...  4.03 us
    pallas_call x1, Pallas kernels, shards_quad(): call(first_kernel, (shape(2 * TILE + 16, 4 * TILE, kind=BF), shape(2, 2 *...  3.96 us
  transfers between devices with their start and end apart: 17, of which 8 were waited for; matrix products, arithmetic and copies ran while one was open for 2% of the time, Pallas kernels for 6%

profile of v2, /device:TPU:1, one launch (start us, length us, event | category | flops | bytes accessed | tf_op | source)
XLA Modules:
  0.0 78.8 jit_solution(502285579581872527)
XLA Ops:
  0.6 0.0 copy-start.6
  0.7 0.0 copy-start.8
  0.7 0.0 copy-start
  0.7 1.0 %copy-done = bf16[128,2048]{1,0:T(8,128)(2,1)S(1)} copy-done((bf16[128,2048]{1,0:T(8,128)(2,1)S(1)}, bf16[128,2048]{1,0:T(8,128)(2,1)}, u32[]{:S(2)}) %copy-start) | copy-done | bytes 524312
  1.7 0.0 copy-start.1
  1.7 1.0 %copy-done.1 = bf16[128,2048]{1,0:T(8,128)(2,1)S(1)} copy-done((bf16[128,2048]{1,0:T(8,128)(2,1)S(1)}, bf16[128,2048]{1,0:T(8,128)(2,1)}, u32[]{:S(2)}) %copy-start.1) | copy-done | bytes 524312
  2.8 0.0 copy-start.2
  2.8 1.0 %copy-done.2 = bf16[128,2048]{1,0:T(8,128)(2,1)S(1)} copy-done((bf16[128,2048]{1,0:T(8,128)(2,1)S(1)}, bf16[128,2048]{1,0:T(8,128)(2,1)}, u32[]{:S(2)}) %copy-start.2) | copy-done | bytes 524312
  3.8 0.0 copy-start.4
  3.8 0.7 copy-done.4
  4.5 0.0 copy-start.3
  4.5 0.0 copy-start.5
  4.5 0.9 %shard_map.186 = (bf16[336,512]{1,0:T(8,128)(2,1)S(1)}, bf16[336,512]{1,0:T(8,128)(2,1)S(1)}, bf16[336,512]{1,0:T(8,128)(2,1)S(1)}, bf16[336,512]{1,0:T(8,128)(2...) custom-call(bf16[128,2048]{1,0:T(8,128)(2,1)S(1)} %copy-done, ...), custom_call_target="tpu_custom_call" | custom-call | flops 1000000 | bytes 10000 | tf_op jit(solution)/shard_map/pallas_call | solution.py:933
  5.4 2.1 %collective-permute-start = (bf16[336,512]{1,0:T(8,128)(2,1)S(1)}, bf16[336,512]{1,0:T(8,128)(2,1)S(1)}, u32[]{:S(2)}, u32[]{:S(2)}) collective-permute-start(bf16[336,512]{1,0:T(8,128)(2,1)S(1)} %get-tuple-element.50), channel_id=1, source_target_pairs={{0,4},{4,0},{8,12},{12,8},{16,20},{20,16},{24,28},{28,24},{1,5},{5... | collective-permute-start | bytes 1032200 | tf_op jit(solution)/shard_map/ppermute | solution.py:942
  7.6 1.3 %collective-permute-start.1 = (bf16[336,512]{1,0:T(8,128)(2,1)S(1)}, bf16[336,512]{1,0:T(8,128)(2,1)S(1)}, u32[]{:S(2)}, u32[]{:S(2)}) collective-permute-start(bf16[336,512]{1,0:T(8,128)(2,1)S(1)} %get-tuple-element.51), channel_id=1, source_target_pairs={{0,8},{4,12},{8,0},{12,4},{16,24},{20,28},{24,16},{28,20},{1,9},{5... | collective-permute-start | bytes 1032200 | tf_op jit(solution)/shard_map/ppermute | solution.py:942
  8.9 0.0 collective-permute-start.2
  8.9 0.7 collective-permute-start.3
  9.5 0.7 collective-permute-start.4
  10.2 0.0 collective-permute-done.3.b0
  10.2 0.7 collective-permute-start.5
  10.9 0.0 collective-permute-done.4.b1
  10.9 1.3 %collective-permute-start.6 = (bf16[16,768]{1,0:T(8,128)(2,1)S(1)}, bf16[16,768]{1,0:T(8,128)(2,1)S(1)}, u32[]{:S(2)}, u32[]{:S(2)}) collective-permute-start(bf16[16,768]{1,0:T(8,128)(2,1)S(1)} %get-tuple-element.56), channel_id=1, source_target_pairs={{12,28},{16,0},{13,29},{17,1},{14,30},{18,2},{15,31},{19,3}} | collective-permute-start | bytes 73736 | tf_op jit(solution)/shard_map/ppermute | solution.py:943
  12.2 0.7 maximum_bitcast_fusion
  12.9 6.3 %all-gather.1.mtaps_ref = f32[4,5,512]{2,1,0:T(8,128)S(1)} all-gather(f32[1,5,512]{2,1,0:T(8,128)S(1)} %maximum_bitcast_fusion), channel_id=2, replica_groups=mesh['ctx'=8,'fsdp'=4] {'fsdp'}, dimensions={0}, use_global_device_ids=true | all-gather | bytes 51200 | tf_op jit(solution)/shard_map/all_gather | solution.py:944
  19.2 0.0 collective-permute-done.5.b2
  19.2 1.7 %collective-permute-done.6.b3 = bf16[16,768]{1,0:T(8,128)(2,1)S(1)} collective-permute-done((bf16[16,768]{1,0:T(8,128)(2,1)S(1)}, bf16[16,768]{1,0:T(8,128)(2,1)S(1)}, u32[]{:S(2)}, u32[]{:S(2)}) %collective-permute-start.6) | collective-permute-done | bytes 24608 | tf_op jit(solution)/shard_map/ppermute | solution.py:943
  20.9 0.0 collective-permute-done.x1
  20.9 0.0 collective-permute-done.1.x2
  20.9 2.7 %collective-permute-done.2.x3 = bf16[336,512]{1,0:T(8,128)(2,1)S(1)} collective-permute-done((bf16[336,512]{1,0:T(8,128)(2,1)S(1)}, bf16[336,512]{1,0:T(8,128)(2,1)S(1)}, u32[]{:S(2)}, u32[]{:S(2)}) %collective-permute-start.2) | collective-permute-done | bytes 344096 | tf_op jit(solution)/shard_map/ppermute | solution.py:942
  23.7 0.0 copy-done.6
  23.7 0.0 copy-done.8
  23.7 0.0 copy-done.3
  23.7 0.0 copy-done.5
  23.7 4.0 %shard_map.187 = (bf16[272,512]{1,0:T(8,128)(2,1)S(1)}, f32[2,264,768]{2,1,0:T(8,128)S(1)}, bf16[512,512]{1,0:T(8,128)(2,1)S(1)}, bf16[512,768]{1,0:T(8,128)(2,1...) custom-call(bf16[336,512]{1,0:T(8,128)(2,1)S(1)} %get-tuple-element., ...), custom_call_target="tpu_custom_call" | custom-call | flops 1000000000 | bytes 10000000 | tf_op jit(solution)/shard_map/pallas_call | solution.py:948
  27.7 4.5 %collective-permute-start.7 = (bf16[272,512]{1,0:T(8,128)(2,1)S(1)}, bf16[272,512]{1,0:T(8,128)(2,1)S(1)}, u32[]{:S(2)}, u32[]{:S(2)}) collective-permute-start(bf16[272,512]{1,0:T(8,128)(2,1)S(1)} %get-tuple-element.57), channel_id=1, source_target_pairs={{0,16},{4,20},{8,24},{12,28},{16,0},{20,4},{24,8},{28,12},{1,17},{... | collective-permute-start | bytes 835592 | tf_op jit(solution)/shard_map/ppermute | solution.py:976
  32.1 0.0 copy-start.7
  32.1 4.0 %shard_map.188 = (f32[512,512]{1,0:T(8,128)S(1)}, f32[512,256]{1,0:T(8,128)S(1)}, f32[32,128]{1,0:T(8,128)S(1)}) custom-call(bf16[512,512]{1,0:T(8,128)(2,1)S(1)} %get-tuple-element.59.dp, bf16[512,768]{1,0:T(8,128)(2,1)S(1)} %get-tuple-element.60.act, bf16[512,512]{1,0:T(8,128)(2,1)S(1)} %get-tuple-element.62.scaled_s, f32[32,128]{1,0:T(8,128)S(1)} %get-tuple-element.71.ds_r), custom_call_target="tpu_custom_call" | custom-call | flops 1000000000 | bytes 10000000 | tf_op jit(solution)/shard_map/pallas_call | solution.py:977
  36.2 8.8 %collective-permute-done.7.mid_ref = bf16[272,512]{1,0:T(8,128)(2,1)S(1)} collective-permute-done((bf16[272,512]{1,0:T(8,128)(2,1)S(1)}, bf16[272,512]{1,0:T(8,128)(2,1)S(1)}, u32[]{:S(2)}, u32[]{:S(2)}) %collective-permute-start.7) | collective-permute-done | bytes 278560 | tf_op jit(solution)/shard_map/ppermute | solution.py:976
  45.0 0.0 copy-done.7
  45.0 5.4 %shard_map.189 = (bf16[224,512]{1,0:T(8,128)(2,1)S(1)}, bf16[224,512]{1,0:T(8,128)(2,1)S(1)}, bf16[224,512]{1,0:T(8,128)(2,1)S(1)}, bf16[224,512]{1,0:T(8,128)(2,1)S(1)}, bf16[32,512]{1,0:T(8,128)(2,1)S(1)}) custom-call(bf16[272,512]{1,0:T(8,128)(2,1)S(1)} %collective-permute-done.7.mid_ref, f32[2,264,768]{2,1,0:T(8,128)S(1)} %get-tuple-element.58.xp, ...), custom_call_target="tpu_custom_call" | custom-call | flops 1000000000 | bytes 10000000 | tf_op jit(solution)/shard_map/pallas_call | solution.py:988
  50.4 0.1 collective-permute-start.10
  50.4 0.1 collective-permute-start.8
  50.5 2.6 %collective-permute-start.9 = (bf16[224,512]{1,0:T(8,128)(2,1)S(1)}, bf16[224,512]{1,0:T(8,128)(2,1)S(1)}, u32[]{:S(2)}, u32[]{:S(2)}) collective-permute-start(bf16[224,512]{1,0:T(8,128)(2,1)S(1)} %get-tuple-element.78), channel_id=1, source_target_pairs={{0,8},{4,12},{8,0},{12,4},{16,24},{20,28},{24,16},{28,20},{1,9},{5... | collective-permute-start | bytes 688136 | tf_op jit(solution)/shard_map/ppermute | solution.py:1014
  53.1 0.1 collective-permute-start.11
  53.2 2.0 %collective-permute-start.12 = (bf16[32,512]{1,0:T(8,128)(2,1)S(1)}, bf16[32,512]{1,0:T(8,128)(2,1)S(1)}, u32[]{:S(2)}, u32[]{:S(2)}) collective-permute-start(bf16[32,512]{1,0:T(8,128)(2,1)S(1)} %get-tuple-element.80), channel_id=1, source_target_pairs={{0,20},{4,16},{8,28},{12,24},{16,4},{20,0},{24,12},{28,8},{1,21},{... | collective-permute-start | bytes 98312 | tf_op jit(solution)/shard_map/ppermute | solution.py:1015
  55.2 5.5 %collective-permute-done.11.z0 = bf16[32,512]{1,0:T(8,128)(2,1)S(1)} collective-permute-done((bf16[32,512]{1,0:T(8,128)(2,1)S(1)}, bf16[32,512]{1,0:T(8,128)(2,1)S(1)}, u32[]{:S(2)}, u32[]{:S(2)}) %collective-permute-start.11) | collective-permute-done | bytes 32800 | tf_op jit(solution)/shard_map/ppermute | solution.py:1015
  60.6 0.2 collective-permute-start.13
  60.8 0.5 collective-permute-done.12.z1
  61.3 1.7 %collective-permute-start.14 = (bf16[32,512]{1,0:T(8,128)(2,1)S(1)}, bf16[32,512]{1,0:T(8,128)(2,1)S(1)}, u32[]{:S(2)}, u32[]{:S(2)}) collective-permute-start(bf16[32,512]{1,0:T(8,128)(2,1)S(1)} %get-tuple-element.80), channel_id=1, source_target_pairs={{0,28},{4,24},{8,20},{12,16},{16,12},{20,8},{24,4},{28,0},{1,29},{... | collective-permute-start | bytes 98312 | tf_op jit(solution)/shard_map/ppermute | solution.py:1015
  63.1 2.1 %collective-permute-done.13.z2 = bf16[32,512]{1,0:T(8,128)(2,1)S(1)} collective-permute-done((bf16[32,512]{1,0:T(8,128)(2,1)S(1)}, bf16[32,512]{1,0:T(8,128)(2,1)S(1)}, u32[]{:S(2)}, u32[]{:S(2)}) %collective-permute-start.13) | collective-permute-done | bytes 32800 | tf_op jit(solution)/shard_map/ppermute | solution.py:1015
  65.2 1.8 %collective-permute-done.14.z3 = bf16[32,512]{1,0:T(8,128)(2,1)S(1)} collective-permute-done((bf16[32,512]{1,0:T(8,128)(2,1)S(1)}, bf16[32,512]{1,0:T(8,128)(2,1)S(1)}, u32[]{:S(2)}, u32[]{:S(2)}) %collective-permute-start.14) | collective-permute-done | bytes 32800 | tf_op jit(solution)/shard_map/ppermute | solution.py:1015
  66.9 0.0 collective-permute-done.10.y3
  66.9 0.0 collective-permute-done.8.y1
  67.0 0.0 collective-permute-done.9.y2
  67.0 0.1 shard_map.191
  67.1 3.5 %collective-permute-start.15 = (f32[136,256]{1,0:T(8,128)S(1)}, f32[136,256]{1,0:T(8,128)S(1)}, u32[]{:S(2)}, u32[]{:S(2)}) collective-permute-start(f32[136,256]{1,0:T(8,128)S(1)} %get-tuple-element.82), channel_id=1, source_target_pairs={{0,2},{2,3},{1,0},{3,1},{4,6},{6,7},{5,4},{7,5},{8,10},{10,11},{9,... | collective-permute-start | bytes 417800 | tf_op jit(solution)/shard_map/ppermute | solution.py:1026
  70.5 3.0 %collective-permute-start.16 = (f32[136,256]{1,0:T(8,128)S(1)}, f32[136,256]{1,0:T(8,128)S(1)}, u32[]{:S(2)}, u32[]{:S(2)}) collective-permute-start(f32[136,256]{1,0:T(8,128)S(1)} %get-tuple-element.83), channel_id=1, source_target_pairs={{0,0},{2,1},{1,2},{3,3},{4,4},{6,5},{5,6},{7,7},{8,8},{10,9},{9,10... | collective-permute-start | bytes 417800 | tf_op jit(solution)/shard_map/ppermute | solution.py:1025
  73.5 1.1 %shard_map.190 = (f32[128,2048]{1,0:T(8,128)}, f32[32,128]{1,0:T(8,128)}, f32[4,2048]{1,0:T(4,128)}, f32[1,2048]{1,0:T(1,128)}, f32[8,128]{1,0:T(8,128)S(1)}) custom-call(bf16[224,512]{1,0:T(8,128)(2,1)S(1)} %get-tuple-element.76.y0, bf16[224,512]{1,0:T(8,128)(2,1)S(1)} %collective-permute-done.8.y1, bf16[224,512]{1,0:T(8,128)(2,1)S(1)} %collective-permute-done.9.y2, ...), custom_call_target="tpu_custom_call" | custom-call | flops 100000000 | bytes 1000000 | tf_op jit(solution)/shard_map/pallas_call | solution.py:1027
  74.6 0.6 slice_bitcast_fusion
  75.2 0.0 collective-permute-done.15
  75.2 1.7 %collective-permute-done.16 = f32[136,256]{1,0:T(8,128)S(1)} collective-permute-done((f32[136,256]{1,0:T(8,128)S(1)}, f32[136,256]{1,0:T(8,128)S(1)}, u32[]{:S(2)}, u32[]{:S(2)}) %collective-permute-start.16) | collective-permute-done | bytes 139296 | tf_op jit(solution)/shard_map/ppermute | solution.py:1025
  76.9 0.6 pad_maximum_fusion
  77.5 0.6 fusion.1
  78.1 0.7 fusion
  (1 shorter events, 0.0 us)
Async XLA Ops:
  0.6 23.0 %copy-start.6 = (f32[32]{0:T(128)S(1)}, f32[32]{0:T(128)}, u32[]{:S(2)}) copy-start(f32[32]{0:T(128)} %alog_ref.3) | copy-start | bytes 388
  0.7 23.0 %copy-start.8 = (f32[32]{0:T(128)S(1)}, f32[32]{0:T(128)}, u32[]{:S(2)}) copy-start(f32[32]{0:T(128)} %dtb_ref.1) | copy-start | bytes 388
  0.7 1.1 %copy-start = (bf16[128,2048]{1,0:T(8,128)(2,1)S(1)}, bf16[128,2048]{1,0:T(8,128)(2,1)}, u32[]{:S(2)}) copy-start(bf16[128,2048]{1,0:T(8,128)(2,1)} %sig_ref.1) | copy-start | bytes 1572868
  1.7 1.0 %copy-start.1 = (bf16[128,2048]{1,0:T(8,128)(2,1)S(1)}, bf16[128,2048]{1,0:T(8,128)(2,1)}, u32[]{:S(2)}) copy-start(bf16[128,2048]{1,0:T(8,128)(2,1)} %map_ref.1) | copy-start | bytes 1572868
  2.8 1.0 %copy-start.2 = (bf16[128,2048]{1,0:T(8,128)(2,1)S(1)}, bf16[128,2048]{1,0:T(8,128)(2,1)}, u32[]{:S(2)}) copy-start(bf16[128,2048]{1,0:T(8,128)(2,1)} %dy_ref.1) | copy-start | bytes 1572868
  3.8 0.7 copy-start.4
  4.5 19.1 %copy-start.3 = (f32[4,2048]{1,0:T(4,128)S(1)}, f32[4,2048]{1,0:T(4,128)}, u32[]{:S(2)}) copy-start(f32[4,2048]{1,0:T(4,128)} %taps_ref.3) | copy-start | bytes 98308
  4.5 19.2 %copy-start.5 = (f32[2048]{0:T(1024)S(1)}, f32[2048]{0:T(1024)}, u32[]{:S(2)}) copy-start(f32[2048]{0:T(1024)} %param.17) | copy-start | bytes 24580
  5.4 15.5 %collective-permute-start = (bf16[336,512]{1,0:T(8,128)(2,1)S(1)}, bf16[336,512]{1,0:T(8,128)(2,1)S(1)}, u32[]{:S(2)}, u32[]{:S(2)}) collective-permute-start(bf16[336,512]{1,0:T(8,128)(2,1)S(1)} %get-tuple-element.50), channel_id=1, source_target_pairs={{0,4},{4,0},{8,12},{12,8},{16,20},{20,16},{24,28},{28,24},{1,5},{5... | collective-permute-start | bytes 1032200 | tf_op jit(solution)/shard_map/ppermute | solution.py:942
  7.6 13.4 %collective-permute-start.1 = (bf16[336,512]{1,0:T(8,128)(2,1)S(1)}, bf16[336,512]{1,0:T(8,128)(2,1)S(1)}, u32[]{:S(2)}, u32[]{:S(2)}) collective-permute-start(bf16[336,512]{1,0:T(8,128)(2,1)S(1)} %get-tuple-element.51), channel_id=1, source_target_pairs={{0,8},{4,12},{8,0},{12,4},{16,24},{20,28},{24,16},{28,20},{1,9},{5... | collective-permute-start | bytes 1032200 | tf_op jit(solution)/shard_map/ppermute | solution.py:942
  8.9 14.8 %collective-permute-start.2 = (bf16[336,512]{1,0:T(8,128)(2,1)S(1)}, bf16[336,512]{1,0:T(8,128)(2,1)S(1)}, u32[]{:S(2)}, u32[]{:S(2)}) collective-permute-start(bf16[336,512]{1,0:T(8,128)(2,1)S(1)} %get-tuple-element.52), channel_id=1, source_target_pairs={{0,12},{4,8},{8,4},{12,0},{16,28},{20,24},{24,20},{28,16},{1,13},{... | collective-permute-start | bytes 1032200 | tf_op jit(solution)/shard_map/ppermute | solution.py:942
  8.9 1.3 %collective-permute-start.3 = (bf16[16,768]{1,0:T(8,128)(2,1)S(1)}, bf16[16,768]{1,0:T(8,128)(2,1)S(1)}, u32[]{:S(2)}, u32[]{:S(2)}) collective-permute-start(bf16[16,768]{1,0:T(8,128)(2,1)S(1)} %get-tuple-element.53), channel_id=1, source_target_pairs={{12,16},{16,12},{13,17},{17,13},{14,18},{18,14},{15,19},{19,15}} | collective-permute-start | bytes 73736 | tf_op jit(solution)/shard_map/ppermute | solution.py:943
  9.5 1.4 %collective-permute-start.4 = (bf16[16,768]{1,0:T(8,128)(2,1)S(1)}, bf16[16,768]{1,0:T(8,128)(2,1)S(1)}, u32[]{:S(2)}, u32[]{:S(2)}) collective-permute-start(bf16[16,768]{1,0:T(8,128)(2,1)S(1)} %get-tuple-element.54), channel_id=1, source_target_pairs={{12,20},{16,8},{13,21},{17,9},{14,22},{18,10},{15,23},{19,11}} | collective-permute-start | bytes 73736 | tf_op jit(solution)/shard_map/ppermute | solution.py:943
  10.2 9.0 %collective-permute-start.5 = (bf16[16,768]{1,0:T(8,128)(2,1)S(1)}, bf16[16,768]{1,0:T(8,128)(2,1)S(1)}, u32[]{:S(2)}, u32[]{:S(2)}) collective-permute-start(bf16[16,768]{1,0:T(8,128)(2,1)S(1)} %get-tuple-element.55), channel_id=1, source_target_pairs={{12,24},{16,4},{13,25},{17,5},{14,26},{18,6},{15,27},{19,7}} | collective-permute-start | bytes 73736 | tf_op jit(solution)/shard_map/ppermute | solution.py:943
  10.9 10.0 %collective-permute-start.6 = (bf16[16,768]{1,0:T(8,128)(2,1)S(1)}, bf16[16,768]{1,0:T(8,128)(2,1)S(1)}, u32[]{:S(2)}, u32[]{:S(2)}) collective-permute-start(bf16[16,768]{1,0:T(8,128)(2,1)S(1)} %get-tuple-element.56), channel_id=1, source_target_pairs={{12,28},{16,0},{13,29},{17,1},{14,30},{18,2},{15,31},{19,3}} | collective-permute-start | bytes 73736 | tf_op jit(solution)/shard_map/ppermute | solution.py:943
  27.7 17.3 %collective-permute-start.7 = (bf16[272,512]{1,0:T(8,128)(2,1)S(1)}, bf16[272,512]{1,0:T(8,128)(2,1)S(1)}, u32[]{:S(2)}, u32[]{:S(2)}) collective-permute-start(bf16[272,512]{1,0:T(8,128)(2,1)S(1)} %get-tuple-element.57), channel_id=1, source_target_pairs={{0,16},{4,20},{8,24},{12,28},{16,0},{20,4},{24,8},{28,12},{1,17},{... | collective-permute-start | bytes 835592 | tf_op jit(solution)/shard_map/ppermute | solution.py:976
  32.1 12.8 %copy-start.7 = (f32[32]{0:T(128)S(1)}, f32[32]{0:T(128)}, u32[]{:S(2)}) copy-start(f32[32]{0:T(128)} %skip_ref.1) | copy-start | bytes 388
  50.4 16.6 %collective-permute-start.10 = (bf16[224,512]{1,0:T(8,128)(2,1)S(1)}, bf16[224,512]{1,0:T(8,128)(2,1)S(1)}, u32[]{:S(2)}, u32[]{:S(2)}) collective-permute-start(bf16[224,512]{1,0:T(8,128)(2,1)S(1)} %get-tuple-element.79), channel_id=1, source_target_pairs={{0,12},{4,8},{8,4},{12,0},{16,28},{20,24},{24,20},{28,16},{1,13},{... | collective-permute-start | bytes 688136 | tf_op jit(solution)/shard_map/ppermute | solution.py:1014
  50.4 16.5 %collective-permute-start.8 = (bf16[224,512]{1,0:T(8,128)(2,1)S(1)}, bf16[224,512]{1,0:T(8,128)(2,1)S(1)}, u32[]{:S(2)}, u32[]{:S(2)}) collective-permute-start(bf16[224,512]{1,0:T(8,128)(2,1)S(1)} %get-tuple-element.77), channel_id=1, source_target_pairs={{0,4},{4,0},{8,12},{12,8},{16,20},{20,16},{24,28},{28,24},{1,5},{5... | collective-permute-start | bytes 688136 | tf_op jit(solution)/shard_map/ppermute | solution.py:1014
  50.5 16.4 %collective-permute-start.9 = (bf16[224,512]{1,0:T(8,128)(2,1)S(1)}, bf16[224,512]{1,0:T(8,128)(2,1)S(1)}, u32[]{:S(2)}, u32[]{:S(2)}) collective-permute-start(bf16[224,512]{1,0:T(8,128)(2,1)S(1)} %get-tuple-element.78), channel_id=1, source_target_pairs={{0,8},{4,12},{8,0},{12,4},{16,24},{20,28},{24,16},{28,20},{1,9},{5... | collective-permute-start | bytes 688136 | tf_op jit(solution)/shard_map/ppermute | solution.py:1014
  53.1 7.5 %collective-permute-start.11 = (bf16[32,512]{1,0:T(8,128)(2,1)S(1)}, bf16[32,512]{1,0:T(8,128)(2,1)S(1)}, u32[]{:S(2)}, u32[]{:S(2)}) collective-permute-start(bf16[32,512]{1,0:T(8,128)(2,1)S(1)} %get-tuple-element.80), channel_id=1, source_target_pairs={{0,16},{4,20},{8,24},{12,28},{16,0},{20,4},{24,8},{28,12},{1,17},{... | collective-permute-start | bytes 98312 | tf_op jit(solution)/shard_map/ppermute | solution.py:1015
  53.2 8.2 %collective-permute-start.12 = (bf16[32,512]{1,0:T(8,128)(2,1)S(1)}, bf16[32,512]{1,0:T(8,128)(2,1)S(1)}, u32[]{:S(2)}, u32[]{:S(2)}) collective-permute-start(bf16[32,512]{1,0:T(8,128)(2,1)S(1)} %get-tuple-element.80), channel_id=1, source_target_pairs={{0,20},{4,16},{8,28},{12,24},{16,4},{20,0},{24,12},{28,8},{1,21},{... | collective-permute-start | bytes 98312 | tf_op jit(solution)/shard_map/ppermute | solution.py:1015
  60.6 4.6 %collective-permute-start.13 = (bf16[32,512]{1,0:T(8,128)(2,1)S(1)}, bf16[32,512]{1,0:T(8,128)(2,1)S(1)}, u32[]{:S(2)}, u32[]{:S(2)}) collective-permute-start(bf16[32,512]{1,0:T(8,128)(2,1)S(1)} %get-tuple-element.80), channel_id=1, source_target_pairs={{0,24},{4,28},{8,16},{12,20},{16,8},{20,12},{24,0},{28,4},{1,25},{... | collective-permute-start | bytes 98312 | tf_op jit(solution)/shard_map/ppermute | solution.py:1015
  61.3 5.6 %collective-permute-start.14 = (bf16[32,512]{1,0:T(8,128)(2,1)S(1)}, bf16[32,512]{1,0:T(8,128)(2,1)S(1)}, u32[]{:S(2)}, u32[]{:S(2)}) collective-permute-start(bf16[32,512]{1,0:T(8,128)(2,1)S(1)} %get-tuple-element.80), channel_id=1, source_target_pairs={{0,28},{4,24},{8,20},{12,16},{16,12},{20,8},{24,4},{28,0},{1,29},{... | collective-permute-start | bytes 98312 | tf_op jit(solution)/shard_map/ppermute | solution.py:1015
  67.1 8.1 %collective-permute-start.15 = (f32[136,256]{1,0:T(8,128)S(1)}, f32[136,256]{1,0:T(8,128)S(1)}, u32[]{:S(2)}, u32[]{:S(2)}) collective-permute-start(f32[136,256]{1,0:T(8,128)S(1)} %get-tuple-element.82), channel_id=1, source_target_pairs={{0,2},{2,3},{1,0},{3,1},{4,6},{6,7},{5,4},{7,5},{8,10},{10,11},{9,... | collective-permute-start | bytes 417800 | tf_op jit(solution)/shard_map/ppermute | solution.py:1026
  70.5 6.4 %collective-permute-start.16 = (f32[136,256]{1,0:T(8,128)S(1)}, f32[136,256]{1,0:T(8,128)S(1)}, u32[]{:S(2)}, u32[]{:S(2)}) collective-permute-start(f32[136,256]{1,0:T(8,128)S(1)} %get-tuple-element.83), channel_id=1, source_target_pairs={{0,0},{2,1},{1,2},{3,3},{4,4},{6,5},{5,6},{7,7},{8,8},{10,9},{9,10... | collective-permute-start | bytes 417800 | tf_op jit(solution)/shard_map/ppermute | solution.py:1025

commit v3 on v2

--- a/solution.py
+++ b/solution.py
@@ -374,10 +374,12 @@
     return pl.ds(pl.multiple_of(start, TILE), width)
 
 
-def pack_kernel(sig_ref, map_ref, dt_ref, dy_ref, *rest):
-    x_refs, halo_refs, (dt_rows, sems) = rest[:4], rest[4:8], rest[8:]
+def pack_kernel(sig_ref, map_ref, dt_ref, dy_ref, mtaps_ref, mbias_ref, *rest):
+    x_refs, halo_refs, tap_ref, (dt_in, sems) = rest[:4], rest[4:8], rest[8], rest[9:]
     quad, r, f = place()
     copies = []
+    dt_copy = pltpu.make_async_copy(dt_ref, dt_in, sems.at[36])
+    dt_copy.start()
 
     def send(source, target):
         copy = pltpu.make_async_copy(source, target, sems.at[len(copies)])
@@ -405,14 +407,19 @@
         group = (2 * f + lax.div(dest, 2)) * TILE
         for j in range(2):
             send(map_ref.at[rows, at_tile(group + j * half)], halo_refs[m].at[:, lanes_of(4 + j)])
+    tap_ref[0:4, :] = mtaps_ref[...]
+    tap_ref[4:5, :] = mbias_ref[...]
+    tap_ref[5:8, :] = jnp.zeros_like(tap_ref[5:8, :])
+    dt_copy.wait()
+    zero = jnp.zeros((8, TILE), F32)
     for k in range(4):
         dest = lax.bitwise_xor(r, k)
-        hi, mid, lo = split3(dt_ref[pl.ds(pl.multiple_of(8 * dest, 8), 8), :])
-        zero = jnp.zeros((8, TILE), F32)
-        dt_rows[k, :, 0:TILE] = jnp.concatenate([hi.astype(F32), mid.astype(F32)], axis=0).astype(BF)
-        dt_rows[k, :, TILE : 2 * TILE] = jnp.concatenate([lo.astype(F32), zero], axis=0).astype(BF)
-        dt_rows[k, :, 2 * TILE : 4 * TILE] = jnp.zeros((16, 2 * TILE), BF)
-        send(dt_rows.at[k], x_refs[k].at[2 * TILE + HALF : 2 * TILE + HALF + 16, :])
+        hi, mid, lo = split3(dt_in[pl.ds(pl.multiple_of(8 * dest, 8), 8), :])
+        top = jnp.concatenate([hi.astype(F32), mid.astype(F32)], axis=0)
+        low = jnp.concatenate([lo.astype(F32), zero], axis=0)
+        x_refs[k][2 * TILE + HALF : 2 * TILE + HALF + 16, :] = jnp.concatenate(
+            [top, low, jnp.zeros((16, 2 * TILE), F32)], axis=1
+        ).astype(BF)
     for copy in copies:
         copy.wait()
 
@@ -619,50 +626,58 @@
     return jnp.sum(x.reshape(x.shape[0] // 8, 8, x.shape[1]), axis=0)
 
 
-def third_kernel(
-    scale,
+def end_rows_of(exp_e):
+    return [exp_e[(i + 1) * TILE - 8 : (i + 1) * TILE, :][7:8, :] for i in range(4)]
+
+
+def taps_back(here, after, taps):
+    grads = jnp.concatenate([here, after], axis=0)
+    raw = taps[3] * here
+    for k in range(3):
+        raw = raw + taps[k] * pltpu.roll(grads, 5 + k, 0)[8:]
+    return raw
+
+
+def spill_of(first, taps):
+    grads = jnp.concatenate([jnp.zeros((8, TILE), F32), first], axis=0)
+    spill = jnp.zeros((8, TILE), F32)
+    for k in range(3):
+        spill = spill + taps[k] * pltpu.roll(grads, 5 + k, 0)[8:]
+    return spill
+
+
+def tap_sums(here, block, sums):
+    for k in range(4):
+        sums[k] = sums[k] + eights(here * shifted(block, k))
+    sums[4] = sums[4] + eights(here)
+
+
+def maps_kernel(
     mid_ref,
-    xp,
-    dp,
+    s_s,
+    t_s,
+    exp_e,
     act,
     slope,
-    scaled_s,
     weighted_s,
     sgrad_s,
-    step_e,
-    toend_e,
-    exp_e,
-    s_s,
-    t_s,
-    step_r,
-    ds_r,
-    sig_r,
-    diag_ref,
     gmap_ref,
-    gsum_ref,
+    xp,
     taps_ref,
     bias_ref,
     mtaps_ref,
-    alog_ref,
-    skip_ref,
-    y0,
-    y1,
-    y2,
-    y3,
-    cross_ref,
+    one_ref,
+    two_ref,
+    hlow_ref,
+    clow_ref,
+    endrow_ref,
     h_s,
     c_s,
-    gp,
-    dx,
-    blk,
 ):
     quad, r, f = place()
     high = quad == 1
-    lane_row = ids((1, TILE), 1)
-    row8 = ids((8, TILE), 0)
-    lane8 = ids((8, TILE), 1)
-    rate8 = -jnp.exp(head_row(alog_ref, r))
-    ends = [exp_e[(i + 1) * TILE - 8 : (i + 1) * TILE, :][7:8, :] for i in range(4)]
+    even = lax.rem(f, 2) == 0
+    ends = end_rows_of(exp_e)
     f_in = mid_ref[0:TILE, :].astype(F32)
     g_in = mid_ref[TILE : 2 * TILE, :].astype(F32)
     across = jnp.sum(mid_ref[2 * TILE : 2 * TILE + 16, :].astype(F32), axis=0, keepdims=True)
@@ -676,7 +691,82 @@
     c_s[2] = t_s[3] + ends[3] * c_s[3]
     c_s[1] = jnp.where(high, t_s[2] + ends[2] * c_s[2], g_in + across * g_b)
     c_s[0] = t_s[1] + ends[1] * c_s[1]
-
+    taps_of = [tap_rows(4 + j, taps_ref, bias_ref, mtaps_ref)[0] for j in range(2)]
+    after = [jnp.zeros((8, TILE), F32) for _ in range(2)]
+    sums = [[jnp.zeros((8, TILE), F32) for _ in range(5)] for _ in range(2)]
+    first = [None, None]
+    end_rows = [None] * 4
+    for i in (3, 2, 1, 0):
+        rows = slice(i * TILE, (i + 1) * TILE)
+        hlow_ref[i] = h_s[i].astype(BF)
+        clow_ref[i] = c_s[i].astype(BF)
+        end_rows[i] = jnp.sum(h_s[i] * c_s[i], axis=0, keepdims=True) * ends[i]
+        grads = (
+            mm(weighted_s[rows, :], clow_ref[i], NT) + gmap_ref[rows, lanes_of(0)],
+            mm(sgrad_s[rows, :], hlow_ref[i], NT) + gmap_ref[rows, lanes_of(1)],
+        )
+        base = (i % 2) * TILE
+        raws = []
+        for j in range(2):
+            here = grads[j] * slope[rows, lanes_of(4 + j)]
+            raws.append(taps_back(here, after[j], taps_of[j]))
+            tap_sums(here, xp[i // 2, base : base + TILE + 8, lanes_of(4 + j)], sums[j])
+            start = here[0:8]
+            after[j] = jnp.where(high, start, 0.0) if i == 2 else start
+            if i == 2:
+                first[j] = start
+            if i == 0:
+                first[j] = jnp.where(high, start, first[j])
+        one_ref[rows, :] = jnp.where(even, raws[0], raws[1]).astype(BF)
+        two_ref[rows, :] = jnp.where(even, raws[1], raws[0]).astype(BF)
+    endrow_ref[...] = jnp.concatenate(end_rows + [jnp.zeros((4, 4 * TILE), F32)], axis=0)
+    row8 = ids((8, TILE), 0)
+    tails = []
+    for j in range(2):
+        five = jnp.zeros((8, TILE), F32)
+        for t in range(5):
+            five = jnp.where(row8 == t, jnp.sum(sums[j][t], axis=0, keepdims=True), five)
+        hi, lo, _ = split3(five)
+        zero8 = jnp.zeros((8, TILE), F32)
+        tails.append(
+            jnp.concatenate(
+                [spill_of(first[j], taps_of[j]), zero8, hi.astype(F32), lo.astype(F32)], axis=0
+            )
+        )
+    one_ref[4 * TILE : 4 * TILE + 32, :] = jnp.where(even, tails[0], tails[1]).astype(BF)
+    two_ref[4 * TILE : 4 * TILE + 32, :] = jnp.where(even, tails[1], tails[0]).astype(BF)
+
+
+def third_kernel(
+    hlow_ref,
+    clow_ref,
+    endrow_ref,
+    xp,
+    dp,
+    act,
+    slope,
+    scaled_s,
+    step_e,
+    toend_e,
+    exp_e,
+    step_r,
+    sig_r,
+    diag_ref,
+    gsum_ref,
+    taps_ref,
+    alog_ref,
+    skip_ref,
+    gp,
+    blk,
+    spill_ref,
+    params_ref,
+):
+    quad, r, f = place()
+    high = quad == 1
+    lane_row = ids((1, TILE), 1)
+    row8 = ids((8, TILE), 0)
+    lane8 = ids((8, TILE), 1)
+    rate8 = -jnp.exp(head_row(alog_ref, r))
     row_q = ids((TILE, TILE), 0)
     col_q = ids((TILE, TILE), 1)
     tail_sums = jnp.concatenate(
@@ -693,25 +783,17 @@
         lo = (x - hi.astype(F32)).astype(BF)
         return mm(pick, hi, NT) + mm(pick, lo, NT)
 
-    taps_of = [tap_rows(j, taps_ref, bias_ref, mtaps_ref)[0] for j in range(6)]
-    after = [jnp.zeros((8, TILE), F32) for _ in range(6)]
-    tap_acc = [[jnp.zeros((8, TILE), F32) for _ in range(5)] for _ in range(6)]
+    sums = [[jnp.zeros((8, TILE), F32) for _ in range(5)] for _ in range(4)]
     skip_acc = [jnp.zeros((8, TILE), F32) for _ in range(4)]
     alog_acc = jnp.zeros((8, TILE), F32)
     ddt_acc = jnp.zeros((8, TILE), F32)
-    first_low = None
-    for i in (3, 2, 1, 0):
+    for i in range(4):
         rows = slice(i * TILE, (i + 1) * TILE)
         at8 = slice(8 * i, 8 * i + 8)
-        in_map = act[rows, lanes_of(4)]
-        out_map = act[rows, lanes_of(5)]
-        h_low = h_s[i].astype(BF)
-        c_low = c_s[i].astype(BF)
-        off = mm(out_map, h_low)
-        gw = mm(in_map, c_low)
-        out_grad = mm(sgrad_s[rows, :], h_low, NT)
-        in_grad = mm(weighted_s[rows, :], c_low, NT)
-        end_row = jnp.sum(h_s[i] * c_s[i], axis=0, keepdims=True) * ends[i]
+        base = (i % 2) * TILE
+        off = mm(act[rows, lanes_of(5)], hlow_ref[i])
+        gw = mm(act[rows, lanes_of(4)], clow_ref[i])
+        end_row = endrow_ref[i : i + 1, :]
         gsum = gsum_ref[at8, :]
         back = jnp.zeros((8, TILE), F32)
         stepsum = jnp.zeros((8, TILE), F32)
@@ -729,9 +811,9 @@
             end_sum = end_sum + jnp.where(row8 == 2 * j + lane8 // HALF, end_row[:, lanes], 0.0)
             skip_acc[j] = skip_acc[j] + eights(dyf * sigf)
             grad_sig = skip_row[j] * dyf + grad_scaled * step_e[rows, lanes]
-            gp[:, lanes] = grad_sig * slope[rows, lanes]
-        gp[:, lanes_of(4)] = (in_grad + gmap_ref[rows, lanes_of(0)]) * slope[rows, lanes_of(4)]
-        gp[:, lanes_of(5)] = (out_grad + gmap_ref[rows, lanes_of(1)]) * slope[rows, lanes_of(5)]
+            here = grad_sig * slope[rows, lanes]
+            gp[rows, lanes] = here
+            tap_sums(here, xp[i // 2, base : base + TILE + 8, lanes], sums[j])
         grad_log = mm_f32(jnp.concatenate([gsum, back], axis=1), tail_sums) + jnp.sum(
             end_sum, axis=1, keepdims=True
         )
@@ -740,48 +822,13 @@
         blk[2 * i + 1] = pltpu.roll(ddt, HALF, 1)
         ddt_acc = ddt_acc + ddt
         alog_acc = alog_acc + grad_log * step_r[at8, :]
-        base = (i % 2) * TILE
-        starts = []
-        for j in range(6):
-            lanes = lanes_of(j)
-            here = gp[:, lanes]
-            grads = jnp.concatenate([here, after[j]], axis=0)
-            block = xp[i // 2, base : base + TILE + 8, lanes]
-            taps = taps_of[j]
-            raw = taps[3] * here
-            for k in range(3):
-                raw = raw + taps[k] * pltpu.roll(grads, 5 + k, 0)[8:]
-            for k in range(4):
-                tap_acc[j][k] = tap_acc[j][k] + eights(here * shifted(block, k))
-            tap_acc[j][4] = tap_acc[j][4] + eights(here)
-            dx[rows, lanes] = raw.astype(BF)
-            starts.append(here[0:8])
-            after[j] = jnp.where(high, starts[j], 0.0) if i == 2 else starts[j]
-        if i == 2:
-            first_low = starts
-        if i == 0:
-            first_high = starts
-
-    for j in range(6):
-        first = jnp.where(high, first_high[j], first_low[j])
-        grads = jnp.concatenate([jnp.zeros((8, TILE), F32), first], axis=0)
-        spill = jnp.zeros((8, TILE), F32)
-        for k in range(3):
-            spill = spill + taps_of[j][k] * pltpu.roll(grads, 5 + k, 0)[8:]
-        starts[j] = spill
-    zero8 = jnp.zeros((8, TILE), F32)
-    cross_ref[0:16, :] = jnp.concatenate(
-        [
-            jnp.concatenate(starts[0:4], axis=1),
-            jnp.concatenate([starts[4], starts[5], zero8, zero8], axis=1),
-        ],
-        axis=0,
-    ).astype(BF)
     rows = []
-    for j in range(6):
-        for k in range(5):
-            rows.append(jnp.sum(tap_acc[j][k], axis=0, keepdims=True))
-    trio = jnp.zeros((TILE, TILE), F32)
+    for j in range(4):
+        taps = [taps_ref[k : k + 1, at_tile((4 * r + j) * TILE)] for k in range(4)]
+        first = jnp.where(high, gp[0:8, lanes_of(j)], gp[2 * TILE : 2 * TILE + 8, lanes_of(j)])
+        spill_ref[:, lanes_of(j)] = spill_of(first, taps)
+        for t in range(5):
+            rows.append(jnp.sum(sums[j][t], axis=0, keepdims=True))
     alog = jnp.sum(alog_acc * rate8, axis=1, keepdims=True)
     ddtb = jnp.sum(ddt_acc, axis=1, keepdims=True)
     skips = jnp.zeros((8, TILE), F32)
@@ -793,31 +840,16 @@
     flat = columns(jnp.where(lane8 < 3, three, 0.0))
     trio = flat[0:1] + pltpu.roll(flat[0:8], 32, 1)[1:2] + pltpu.roll(flat[0:8], 64, 1)[2:3]
     trio = pltpu.roll(jnp.broadcast_to(trio, (8, TILE)), 8 * r, 1)[0:1]
-    params = jnp.concatenate(rows + [trio, jnp.zeros((1, TILE), F32)], axis=0) * scale
-    p_hi, p_lo, _ = split3(params)
-    param_rows = jnp.concatenate([p_hi[0:16], p_hi[16:32], p_lo[0:16], p_lo[16:32]], axis=1)
-    cross_ref[16:32, :] = param_rows
-    for k, y in enumerate((y0, y1, y2, y3)):
-        s = lax.bitwise_xor(r, k)
-        low_rows = pl.ds(pl.multiple_of(HALF * s, HALF), HALF)
-        up_rows = pl.ds(pl.multiple_of(2 * TILE + HALF * (3 - s), HALF), HALF)
-        y[0:HALF, :] = dx[low_rows, 0 : 4 * TILE]
-        y[HALF:TILE, :] = dx[up_rows, 0 : 4 * TILE]
-        for j in range(2):
-            y[TILE : TILE + HALF, lanes_of(2 * j)] = dx[low_rows, lanes_of(4 + j)]
-            y[TILE : TILE + HALF, lanes_of(2 * j + 1)] = dx[up_rows, lanes_of(4 + j)]
-        here = jnp.where(lane8 < HALF, blk[s], pltpu.roll(blk[7 - s], HALF, 1))
-        hi, mid, lo = split3(here)
-        top = jnp.concatenate([hi.astype(F32), mid.astype(F32)], axis=0)
-        low = jnp.concatenate([lo.astype(F32), zero8], axis=0)
-        y[TILE + HALF : TILE + HALF + 16, :] = jnp.concatenate(
-            [top, low, jnp.zeros((16, 2 * TILE), F32)], axis=1
-        ).astype(BF)
-        y[TILE + HALF + 16 : TILE + HALF + 32, :] = param_rows
-
-
-def whole_params(ref, start):
-    value = ref[start : start + 16, :].astype(F32)
+    params_ref[...] = jnp.concatenate(rows + [trio, jnp.zeros((3, TILE), F32)], axis=0)
+
+
+def split_params(params):
+    hi, lo, _ = split3(params)
+    return jnp.concatenate([hi[0:16], hi[16:32], lo[0:16], lo[16:32]], axis=1)
+
+
+def whole_params(value):
+    value = value.astype(F32)
     return jnp.concatenate(
         [
             value[:, lanes_of(0)] + value[:, lanes_of(2)],
@@ -827,66 +859,121 @@
     )
 
 
-PARAMS_AT = TILE + HALF + 16
-
-
-def maps_kernel(y0, y1, y2, y3, z0, z1, z2, z3, one_ref, two_ref):
+def cross_kernel(scale, params_ref, spill_ref, one_ref, two_ref, cross_ref):
+    tails = [ref[4 * TILE : 4 * TILE + 32, :].astype(F32) for ref in (one_ref, two_ref)]
+    fives = [tail[16:24] + tail[24:32] for tail in tails]
+    params = jnp.concatenate(
+        [
+            params_ref[0:20],
+            fives[0][0:5],
+            fives[1][0:5],
+            params_ref[20:21],
+            jnp.zeros((1, TILE), F32),
+        ],
+        axis=0,
+    )
+    maps = jnp.concatenate([tails[0][0:8], tails[1][0:8], jnp.zeros((8, 2 * TILE), F32)], axis=1)
+    cross_ref[0:16, :] = jnp.concatenate([spill_ref[...], maps], axis=0).astype(BF)
+    cross_ref[16:32, :] = split_params(params * scale)
+
+
+def send_kernel(gp, taps_ref, y0, y1, y2, y3, dx):
     quad, r, f = place()
-    ys, zs = (y0, y1, y2, y3), (z0, z1, z2, z3)
-    even = lax.rem(f, 2) == 0
-    own = lax.div(r, 2)
-    row8 = ids((8, TILE), 0)
+    high = quad == 1
+    for j in range(4):
+        lanes = lanes_of(j)
+        taps = [taps_ref[k : k + 1, at_tile((4 * r + j) * TILE)] for k in range(4)]
+        for i in range(4):
+            rows = slice(i * TILE, (i + 1) * TILE)
+            if i == 3:
+                after = jnp.zeros((8, TILE), F32)
+            else:
+                after = gp[(i + 1) * TILE : (i + 1) * TILE + 8, lanes]
+            if i == 1:
+                after = jnp.where(high, after, 0.0)
+            dx[rows, lanes] = taps_back(gp[rows, lanes], after, taps).astype(BF)
+    for k, y in enumerate((y0, y1, y2, y3)):
+        s = lax.bitwise_xor(r, k)
+        for e, at in ((0, HALF * s), (1, 2 * TILE + HALF * (3 - s))):
+            y[e * HALF : (e + 1) * HALF, :] = dx[pl.ds(pl.multiple_of(at, HALF), HALF), :]
+
+
+def merge_kernel(own_ref, other_ref, one_ref, two_ref, blk, w0, w1, w2, w3):
+    quad, r, f = place()
+    lane8 = ids((8, TILE), 1)
+    param_rows = split_params(
+        whole_params(own_ref[16:32, :]) + whole_params(other_ref[16:32, :])
+    )
+    for k, w in enumerate((w0, w1, w2, w3)):
+        s = lax.bitwise_xor(r, k)
+        for e, at in ((0, HALF * s), (1, 2 * TILE + HALF * (3 - s))):
+            rows = pl.ds(pl.multiple_of(at, HALF), HALF)
+            w[0:HALF, lanes_of(e)] = one_ref[rows, :]
+            w[0:HALF, lanes_of(2 + e)] = two_ref[rows, :]
+        here = jnp.where(lane8 < HALF, blk[s], pltpu.roll(blk[7 - s], HALF, 1))
+        hi, mid, lo = split3(here)
+        top = jnp.concatenate([hi.astype(F32), mid.astype(F32)], axis=0)
+        low = jnp.concatenate([lo.astype(F32), jnp.zeros((8, TILE), F32)], axis=0)
+        w[HALF : HALF + 16, :] = jnp.concatenate(
+            [top, low, jnp.zeros((16, 2 * TILE), F32)], axis=1
+        ).astype(BF)
+        w[HALF + 16 : HALF + 32, :] = other_ref[0:16, :]
+        w[HALF + 32 : HALF + 48, :] = param_rows
+
+
+def last_kernel(
+    y0, y1, y2, y3, w0, w1, w2, w3, dsig_ref, dmap_ref, ddt_ref, taps_ref, mtaps_ref, bias_ref, mbias_ref, *trio_refs
+):
+    quad, r, f = place()
+    ys = (y0, y1, y2, y3)
+    ws = (w0, w1, w2, w3)
     third = jnp.logical_and(quad == 0, r == 3)
     fourth = jnp.logical_and(quad == 1, r == 0)
-    for pair in range(2):
-        group = own if pair == 0 else 1 - own
-        lanes = at_tile(group * TILE)
-        sums = []
-        for j in range(2):
-            halves = []
-            for e in range(2):
-                total = jnp.zeros((HALF, TILE), F32)
-                spill = jnp.zeros((8, TILE), F32)
-                for k in (2 * pair, 2 * pair + 1):
-                    total = total + ys[k][TILE : TILE + HALF, lanes_of(2 * j + e)].astype(F32)
-                    spill = spill + zs[k][0:16, lanes_of(j)].astype(F32)[8:16]
-                here = third if e == 0 else fourth
-                spill = jnp.where(here, spill, 0.0)
-                halves += [total[0 : HALF - 8], total[HALF - 8 : HALF] + spill]
-            five = jnp.zeros((8, TILE), F32)
-            for k in (2 * pair, 2 * pair + 1):
-                for ref, start in ((ys[k], PARAMS_AT), (zs[k], 16)):
-                    param = whole_params(ref, start)
-                    for t in range(5):
-                        five = five + jnp.where(row8 == t, param[20 + 5 * j + t : 21 + 5 * j + t], 0.0)
-            sums.append(jnp.concatenate(halves + [five], axis=0))
-        one_ref[:, lanes] = jnp.where(even, sums[0], sums[1])
-        two_ref[:, lanes] = jnp.where(even, sums[1], sums[0])
-
-
-def rows_kernel(y0, y1, y2, y3, z0, z1, z2, z3, dsig_ref, ddt_ref, taps_ref, bias_ref, trio_ref):
-    quad, r, f = place()
-    third = jnp.logical_and(quad == 0, r == 3)
-    fourth = jnp.logical_and(quad == 1, r == 0)
+    params = []
     trio = jnp.zeros((1, TILE), F32)
-    for k, (y, z) in enumerate(((y0, z0), (y1, z1), (y2, z2), (y3, z3))):
+    for k, y in enumerate(ys):
         s = lax.bitwise_xor(r, k)
         cols = at_tile(s * 4 * TILE, 4 * TILE)
         dsig_ref[:, cols] = y[0:TILE, :].astype(F32)
-        spill = z[0:16, :].astype(F32)[0:8]
+        spill = ws[k][HALF + 16 : HALF + 32, :].astype(F32)[0:8]
         dsig_ref[HALF - 8 : HALF, cols] += jnp.where(third, spill, 0.0)
         dsig_ref[TILE - 8 : TILE, cols] += jnp.where(fourth, spill, 0.0)
-        packed = y[TILE + HALF : TILE + HALF + 16, 0 : 2 * TILE].astype(F32)
+        packed = ws[k][HALF : HALF + 16, 0 : 2 * TILE].astype(F32)
         ddt_ref[pl.ds(pl.multiple_of(8 * s, 8), 8), :] = (
             packed[0:8, 0:TILE] + packed[8:16, 0:TILE] + packed[0:8, TILE : 2 * TILE]
         )
-        params = whole_params(y, PARAMS_AT) + whole_params(z, 16)
+        param = whole_params(ws[k][HALF + 32 : HALF + 48, :])
+        params.append(param)
         for j in range(4):
             lanes = at_tile((4 * s + j) * TILE)
-            taps_ref[0:4, lanes] = params[5 * j : 5 * j + 4]
-            bias_ref[0:1, lanes] = params[5 * j + 4 : 5 * j + 5]
-        trio = trio + params[30:31]
-    trio_ref[...] = jnp.broadcast_to(trio, (8, TILE))
+            taps_ref[0:4, lanes] = param[5 * j : 5 * j + 4]
+            bias_ref[0:1, lanes] = param[5 * j + 4 : 5 * j + 5]
+        trio = trio + param[30:31]
+    trio = jnp.broadcast_to(trio, (8, TILE))
+    for t, ref in enumerate(trio_refs):
+        moved = trio if t == 0 else pltpu.roll(trio, TILE - 32 * t, 1)
+        ref[...] = moved[0:1, 0:32]
+    own = lax.div(r, 2)
+    swap = f >= 2
+    for pair in range(2):
+        group = own if pair == 0 else 1 - own
+        a, b = 2 * pair, 2 * pair + 1
+        for j in range(2):
+            where = jnp.where(swap, 1 - j, j)
+            lanes = at_tile((2 * where + group) * TILE)
+            for e in range(2):
+                dmap_ref[e * HALF : (e + 1) * HALF, lanes] = ws[a][
+                    0:HALF, lanes_of(2 * j + e)
+                ].astype(F32) + ws[b][0:HALF, lanes_of(2 * j + e)].astype(F32)
+            spill = (
+                ws[a][HALF + 16 : HALF + 32, lanes_of(j)].astype(F32)[8:16]
+                + ws[b][HALF + 16 : HALF + 32, lanes_of(j)].astype(F32)[8:16]
+            )
+            dmap_ref[HALF - 8 : HALF, lanes] += jnp.where(third, spill, 0.0)
+            dmap_ref[TILE - 8 : TILE, lanes] += jnp.where(fourth, spill, 0.0)
+            five = params[a][20 + 5 * j : 25 + 5 * j] + params[b][20 + 5 * j : 25 + 5 * j]
+            mtaps_ref[0:4, lanes] = five[0:4]
+            mbias_ref[0:1, lanes] = five[4:5]
 
 
 ROUTE_ONE = [(0, 0), (2, 1), (1, 2), (3, 3)]
@@ -907,11 +994,10 @@
     skip_gain,
 ):
     ctx = lax.axis_size("ctx")
-    fsdp = lax.axis_size("fsdp")
     rows, sig_width = sig_raw.shape
     vmem = pl.BlockSpec(memory_space=pltpu.VMEM)
     smem = pl.BlockSpec(memory_space=pltpu.SMEM)
-    any_space = pl.BlockSpec(memory_space=pl.ANY)
+    hbm = pl.BlockSpec(memory_space=pltpu.HBM)
 
     def call(kernel, out_shape, in_specs, out_specs, scratch, mib, cost):
         return pl.pallas_call(
@@ -928,39 +1014,42 @@
         return jax.ShapeDtypeStruct(dims, kind)
 
     inside = [[(c, c ^ k) for c in range(ctx)] for k in range(4)]
-    over = [[(c, c ^ 4 ^ k) for c in range(ctx)] for k in range(4)]
-    x_rows = 2 * TILE + HALF + 16
+    over = [(c, c ^ 4) for c in range(ctx)]
+    total = 4 * TILE
+    wide, narrow = 6 * TILE, 4 * TILE
+    owned = map_taps.shape[1]
+    sig_bias_row = sig_bias[None, :]
     packed = call(
         pack_kernel,
-        (shape(x_rows, 4 * TILE, kind=BF),) * 4 + (shape(16, 6 * TILE, kind=BF),) * 4,
-        [any_space, any_space, vmem, any_space],
-        (any_space,) * 8,
-        [pltpu.VMEM((4, 16, 4 * TILE), BF), pltpu.SemaphoreType.DMA((40,))],
-        16,
+        (shape(2 * TILE + HALF + 16, narrow, kind=BF),) * 4
+        + (shape(16, wide, kind=BF),) * 4
+        + (shape(8, owned),),
+        [hbm, hbm, hbm, hbm, vmem, vmem],
+        (vmem,) * 9,
+        [pltpu.VMEM((32, TILE), F32), pltpu.SemaphoreType.DMA((37,))],
+        60,
         10**6,
-    )(sig_raw, map_raw, step_size_logits.T, d_out)
+    )(sig_raw, map_raw, step_size_logits.T, d_out, map_taps, map_bias[None, :])
     xs = [packed[0]] + [lax.ppermute(packed[k], "ctx", inside[k]) for k in (1, 2, 3)]
     halos = [lax.ppermute(packed[4 + m], "ctx", [(3, 4 + m), (4, 3 - m)]) for m in range(4)]
-    map_params = lax.all_gather(
-        jnp.concatenate([map_taps, map_bias[None, :]], axis=0), "fsdp", axis=0
-    )
-    total = 4 * TILE
+    map_params = lax.all_gather(packed[8], "fsdp", axis=0)
+    own_taps = (sig_taps, sig_bias_row, map_params)
     mid, *kept = call(
         first_kernel,
         (
-            shape(2 * TILE + 16, 4 * TILE, kind=BF),
-            shape(2, 2 * TILE + 8, 6 * TILE),
-            shape(total, 4 * TILE, kind=BF),
-            shape(total, 6 * TILE, kind=BF),
-            shape(total, 6 * TILE),
-            shape(total, 4 * TILE, kind=BF),
-            shape(total, 4 * TILE, kind=BF),
-            shape(total, 4 * TILE, kind=BF),
-            shape(total, 4 * TILE),
-            shape(total, 4 * TILE),
-            shape(total, 4 * TILE),
-            shape(4, TILE, 4 * TILE),
-            shape(4, TILE, 4 * TILE),
+            shape(2 * TILE + 16, narrow, kind=BF),
+            shape(2, 2 * TILE + 8, wide),
+            shape(total, narrow, kind=BF),
+            shape(total, wide, kind=BF),
+            shape(total, wide),
+            shape(total, narrow, kind=BF),
+            shape(total, narrow, kind=BF),
+            shape(total, narrow, kind=BF),
+            shape(total, narrow),
+            shape(total, narrow),
+            shape(total, narrow),
+            shape(4, TILE, narrow),
+            shape(4, TILE, narrow),
             shape(32, TILE),
             shape(32, TILE),
             shape(32, TILE),
@@ -969,89 +1058,123 @@
         (vmem,) * 16,
         [pltpu.VMEM((4, 8, TILE), F32)],
         24,
-        10**9,
-    )(*xs, *halos, sig_taps, sig_bias[None, :], map_params, a_log, dt_bias)
+        4 * 10**9,
+    )(*xs, *halos, *own_taps, a_log, dt_bias)
     xp, dp, act, slope, scaled, weighted, sgrad, step_e, toend_e, exp_e, s_s, t_s = kept[:12]
     step_r, ds_r, sig_r = kept[12:]
-    mid = lax.ppermute(mid, "ctx", over[0])
+    mid = lax.ppermute(mid, "ctx", over)
     diag, gmap, gsum = call(
         second_kernel,
-        (shape(total, 4 * TILE), shape(total, 2 * TILE), shape(32, TILE)),
+        (shape(total, narrow), shape(total, 2 * TILE), shape(32, TILE)),
         [vmem] * 4,
         (vmem,) * 3,
         [],
         16,
-        10**9,
+        4 * 10**9,
     )(dp, act, scaled, ds_r)
-    scale = 1.0 / math.sqrt(float(ctx * rows))
-    y_rows = TILE + HALF + 32
-    *ys, cross = call(
-        functools.partial(third_kernel, scale),
-        (shape(y_rows, 4 * TILE, kind=BF),) * 4 + (shape(32, 4 * TILE, kind=BF),),
-        [vmem] * 22 + [smem] * 2,
+    one, two, hlow, clow, endrow = call(
+        maps_kernel,
+        (
+            shape(total + 32, TILE, kind=BF),
+            shape(total + 32, TILE, kind=BF),
+            shape(4, TILE, narrow, kind=BF),
+            shape(4, TILE, narrow, kind=BF),
+            shape(8, narrow),
+        ),
+        [vmem] * 13,
         (vmem,) * 5,
-        [
-            pltpu.VMEM((4, TILE, 4 * TILE), F32),
-            pltpu.VMEM((4, TILE, 4 * TILE), F32),
-            pltpu.VMEM((TILE, 6 * TILE), F32),
-            pltpu.VMEM((total, 6 * TILE), BF),
-            pltpu.VMEM((8, 8, TILE), F32),
-        ],
-        32,
-        10**9,
+        [pltpu.VMEM((4, TILE, narrow), F32), pltpu.VMEM((4, TILE, narrow), F32)],
+        24,
+        2 * 10**9,
+    )(mid, s_s, t_s, exp_e, act, slope, weighted, sgrad, gmap, xp, *own_taps)
+    one = lax.ppermute(one, "fsdp", ROUTE_ONE)
+    two = lax.ppermute(two, "fsdp", ROUTE_TWO)
+    gp, blk, spill, params = call(
+        third_kernel,
+        (shape(total, narrow), shape(8, 8, TILE), shape(8, narrow), shape(24, TILE)),
+        [vmem] * 16 + [smem] * 2,
+        (vmem,) * 4,
+        [],
+        24,
+        3 * 10**9,
     )(
-        mid,
-        *kept,
+        hlow,
+        clow,
+        endrow,
+        xp,
+        dp,
+        act,
+        slope,
+        scaled,
+        step_e,
+        toend_e,
+        exp_e,
+        step_r,
+        sig_r,
         diag,
-        gmap,
         gsum,
         sig_taps,
-        sig_bias[None, :],
-        map_params,
         a_log,
         skip_gain,
     )
-    ys = [ys[0]] + [lax.ppermute(ys[k], "ctx", inside[k]) for k in (1, 2, 3)]
-    zs = [lax.ppermute(cross, "ctx", over[k]) for k in range(4)]
-    one, two = call(
-        maps_kernel,
-        (shape(TILE + 8, 2 * TILE), shape(TILE + 8, 2 * TILE)),
-        [vmem] * 8,
-        (vmem,) * 2,
+    scale = 1.0 / math.sqrt(float(ctx * rows))
+    cross = call(
+        functools.partial(cross_kernel, scale),
+        shape(32, narrow, kind=BF),
+        [vmem] * 4,
+        vmem,
         [],
         16,
         10**6,
-    )(*ys, *zs)
-    one = lax.ppermute(one, "fsdp", ROUTE_ONE)
-    two = lax.ppermute(two, "fsdp", ROUTE_TWO)
-    d_sig, d_dt, taps, bias, trio = call(
-        rows_kernel,
+    )(params, spill, one, two)
+    other = lax.ppermute(cross, "ctx", over)
+    ys = call(
+        send_kernel,
+        (shape(TILE, narrow, kind=BF),) * 4,
+        [vmem] * 2,
+        (vmem,) * 4,
+        [pltpu.VMEM((total, narrow), BF)],
+        16,
+        10**9,
+    )(gp, sig_taps)
+    ys = [ys[0]] + [lax.ppermute(ys[k], "ctx", inside[k]) for k in (1, 2, 3)]
+    ws = call(
+        merge_kernel,
+        (shape(HALF + 48, narrow, kind=BF),) * 4,
+        [vmem] * 5,
+        (vmem,) * 4,
+        [],
+        16,
+        10**6,
+    )(cross, other, one, two, blk)
+    ws = [ws[0]] + [lax.ppermute(ws[k], "ctx", inside[k]) for k in (1, 2, 3)]
+    d_sig, d_map, d_dt, taps, map_taps_grad, bias, map_bias_grad, *trio = call(
+        last_kernel,
         (
             shape(rows, sig_width),
+            shape(rows, owned),
             shape(32, TILE),
             shape(4, sig_width),
+            shape(4, owned),
             shape(1, sig_width),
-            shape(8, TILE),
-        ),
+            shape(1, owned),
+        )
+        + (shape(1, 32),) * 3,
         [vmem] * 8,
-        (vmem,) * 5,
+        (vmem,) * 10,
         [],
         16,
-        10**8,
-    )(*ys, *zs)
-    swap = lax.axis_index("fsdp") >= fsdp // 2
-    d_map = jnp.concatenate([jnp.where(swap, two, one), jnp.where(swap, one, two)], axis=1)
+        10**6,
+    )(*ys, *ws)
     return (
         d_sig,
-        d_map[:rows],
+        d_map,
         d_dt.T,
         taps,
-        d_map[rows : rows + 4],
+        map_taps_grad,
         bias[0],
-        d_map[rows + 4],
-        trio[0, 0:32],
-        trio[0, 32:64],
-        trio[0, 64:96],
+        map_bias_grad[0],
+        *(t[0] for t in trio),
     )
 
 

time: 79.2 us -> 73.1 us (0.923)
  the two profiles are of different devices: /device:TPU:1 before, /device:TPU:0 now
where the time goes in v3:
time: 73.1 us; the launch traced here: 72.7 us
  waiting for transfers between devices  23.3 us (32%)
  starting transfers between devices  23 us (31%)
  Pallas kernels  19.1 us (26%)
  blocking collectives  5.46 us (7%)
  local copies, waits for them, and re-layouts  0.99 us (1%)
  between operations  0.82 us (1%)
    ppermute x1, waiting for transfers between devices, shards_quad(): mid = lax.ppermute(mid, 'ctx', over)  9.1 us
    ppermute x4, waiting for transfers between devices, shards_quad(): lax.ppermute(packed[4 + m], 'ctx', [(3, 4 + m), (4, 3 - m)])  5.94 us
    all_gather x1, blocking collectives, shards_quad(): map_params = lax.all_gather(packed[8], 'fsdp', axis=0)  5.46 us
    ppermute x3, starting transfers between devices, shards_quad(): ys = [ys[0]] + [lax.ppermute(ys[k], 'ctx', inside[k]) for k in (1, 2, 3)]  5.02 us
    pallas_call x1, Pallas kernels, shards_quad(): call(third_kernel, (shape(total, narrow), shape(8, 8, TILE), shape(8, nar...  4.72 us
    ppermute x3, starting transfers between devices, shards_quad(): lax.ppermute(packed[k], 'ctx', inside[k])  4.61 us
    ppermute x3, waiting for transfers between devices, shards_quad(): ws = [ws[0]] + [lax.ppermute(ws[k], 'ctx', inside[k]) for k in (1, 2, 3)]  4.06 us
    pallas_call x1, Pallas kernels, shards_quad(): call(second_kernel, (shape(total, narrow), shape(total, 2 * TILE), shape(...  4.03 us
  transfers between devices with their start and end apart: 17, of which 8 were waited for; matrix products, arithmetic and copies ran while one was open for 0% of the time, Pallas kernels for 13%

profile of v3, /device:TPU:0, one launch (start us, length us, event | category | flops | bytes accessed | tf_op | source)
XLA Modules:
  0.0 72.7 jit_solution(14113922633454592578)
XLA Ops:
  0.6 0.0 copy-start
  0.7 0.0 copy-start.4
  0.7 0.0 copy-start.3
  0.7 0.0 copy-start.1
  0.7 3.6 %shard_map.186 = (bf16[336,512]{1,0:T(8,128)(2,1)}, bf16[336,512]{1,0:T(8,128)(2,1)}, bf16[336,512]{1,0:T(8,128)(2,1)}, bf16[336,512]{1,0:T(8,128)(2,1)}, bf16[1...) custom-call(bf16[128,2048]{1,0:T(8,128)(2,1)} %sig_ref.1, ...), custom_call_target="tpu_custom_call" | custom-call | flops 1000000 | bytes 10000 | tf_op jit(solution)/shard_map/pallas_call | solution.py:1022
  4.3 3.0 %collective-permute-start = (bf16[336,512]{1,0:T(8,128)(2,1)}, bf16[336,512]{1,0:T(8,128)(2,1)S(1)}, u32[]{:S(2)}, u32[]{:S(2)}) collective-permute-start(bf16[336,512]{1,0:T(8,128)(2,1)} %get-tuple-element.66), channel_id=1, source_target_pairs={{0,4},{4,0},{8,12},{12,8},{16,20},{20,16},{24,28},{28,24},{1,5},{5... | collective-permute-start | bytes 1032200 | tf_op jit(solution)/shard_map/ppermute | solution.py:1033
  7.3 1.6 %collective-permute-start.1 = (bf16[336,512]{1,0:T(8,128)(2,1)}, bf16[336,512]{1,0:T(8,128)(2,1)S(1)}, u32[]{:S(2)}, u32[]{:S(2)}) collective-permute-start(bf16[336,512]{1,0:T(8,128)(2,1)} %get-tuple-element.67), channel_id=1, source_target_pairs={{0,8},{4,12},{8,0},{12,4},{16,24},{20,28},{24,16},{28,20},{1,9},{5... | collective-permute-start | bytes 1032200 | tf_op jit(solution)/shard_map/ppermute | solution.py:1033
  8.9 0.0 collective-permute-start.2
  8.9 0.7 collective-permute-start.3
  9.5 0.7 collective-permute-start.4
  10.2 0.0 collective-permute-done.3.b0
  10.2 0.7 collective-permute-start.5
  10.9 0.0 collective-permute-done.4.b1
  10.9 1.3 %collective-permute-start.6 = (bf16[16,768]{1,0:T(8,128)(2,1)}, bf16[16,768]{1,0:T(8,128)(2,1)S(1)}, u32[]{:S(2)}, u32[]{:S(2)}) collective-permute-start(bf16[16,768]{1,0:T(8,128)(2,1)} %get-tuple-element.72), channel_id=1, source_target_pairs={{12,28},{16,0},{13,29},{17,1},{14,30},{18,2},{15,31},{19,3}} | collective-permute-start | bytes 73736 | tf_op jit(solution)/shard_map/ppermute | solution.py:1034
  12.2 5.5 %all-gather = f32[32,512]{1,0:T(8,128)S(1)} all-gather(f32[8,512]{1,0:T(8,128)} %get-tuple-element.73), channel_id=2, replica_groups=mesh['ctx'=8,'fsdp'=4] {'fsdp'}, dimensions={0}, use_global_device_ids=true | all-gather | bytes 81920 | tf_op jit(solution)/shard_map/all_gather | solution.py:1035
  17.7 0.0 collective-permute-done.5.b2
  17.7 5.9 %collective-permute-done.6.b3 = bf16[16,768]{1,0:T(8,128)(2,1)S(1)} collective-permute-done((bf16[16,768]{1,0:T(8,128)(2,1)}, bf16[16,768]{1,0:T(8,128)(2,1)S(1)}, u32[]{:S(2)}, u32[]{:S(2)}) %collective-permute-start.6) | collective-permute-done | bytes 24608 | tf_op jit(solution)/shard_map/ppermute | solution.py:1034
  23.6 0.0 collective-permute-done.x1
  23.6 0.0 collective-permute-done.1.x2
  23.6 0.6 collective-permute-done.2.x3
  24.2 0.0 copy-done
  24.2 0.0 copy-done.4
  24.2 0.0 copy-done.3
  24.2 0.0 copy-done.1
  24.2 0.0 copy-start.2
  24.2 1.0 %copy-done.2 = bf16[336,512]{1,0:T(8,128)(2,1)S(1)} copy-done((bf16[336,512]{1,0:T(8,128)(2,1)S(1)}, bf16[336,512]{1,0:T(8,128)(2,1)}, u32[]{:S(2)}) %copy-start.2) | copy-done | bytes 344088
  25.2 3.9 %shard_map.187 = (bf16[272,512]{1,0:T(8,128)(2,1)S(1)}, f32[2,264,768]{2,1,0:T(8,128)S(1)}, bf16[512,512]{1,0:T(8,128)(2,1)S(1)}, bf16[512,768]{1,0:T(8,128)(2,1...) custom-call(bf16[336,512]{1,0:T(8,128)(2,1)S(1)} %copy-done.2, ...), custom_call_target="tpu_custom_call" | custom-call | flops 4000000000 | bytes 40000000 | tf_op jit(solution)/shard_map/pallas_call | solution.py:1037
  29.1 2.9 %collective-permute-start.7 = (bf16[272,512]{1,0:T(8,128)(2,1)S(1)}, bf16[272,512]{1,0:T(8,128)(2,1)S(1)}, u32[]{:S(2)}, u32[]{:S(2)}) collective-permute-start(bf16[272,512]{1,0:T(8,128)(2,1)S(1)} %get-tuple-element.74), channel_id=1, source_target_pairs={{0,16},{4,20},{8,24},{12,28},{16,0},{20,4},{24,8},{28,12},{1,17},{... | collective-permute-start | bytes 835592 | tf_op jit(solution)/shard_map/ppermute | solution.py:1065
  32.0 4.0 %shard_map.188 = (f32[512,512]{1,0:T(8,128)S(1)}, f32[512,256]{1,0:T(8,128)S(1)}, f32[32,128]{1,0:T(8,128)S(1)}) custom-call(bf16[512,512]{1,0:T(8,128)(2,1)S(1)} %get-tuple-element.82.dp, bf16[512,768]{1,0:T(8,128)(2,1)S(1)} %get-tuple-element.78.act, bf16[512,512]{1,0:T(8,128)(2,1)S(1)} %get-tuple-element.83.scaled_s, f32[32,128]{1,0:T(8,128)S(1)} %get-tuple-element.84.ds_r), custom_call_target="tpu_custom_call" | custom-call | flops 4000000000 | bytes 40000000 | tf_op jit(solution)/shard_map/pallas_call | solution.py:1066
  36.1 9.1 %collective-permute-done.7.mid_ref = bf16[272,512]{1,0:T(8,128)(2,1)S(1)} collective-permute-done((bf16[272,512]{1,0:T(8,128)(2,1)S(1)}, bf16[272,512]{1,0:T(8,128)(2,1)S(1)}, u32[]{:S(2)}, u32[]{:S(2)}) %collective-permute-start.7) | collective-permute-done | bytes 278560 | tf_op jit(solution)/shard_map/ppermute | solution.py:1065
  45.2 0.0 copy-start.5
  45.2 1.1 %shard_map.189 = (bf16[544,128]{1,0:T(8,128)(2,1)S(1)}, bf16[544,128]{1,0:T(8,128)(2,1)S(1)}, bf16[4,128,512]{2,1,0:T(8,128)(2,1)S(1)}, bf16[4,128,512]{2,1,0:T(8,128)(2,1)S(1)}, f32[8,512]{1,0:T(8,128)S(1)}) custom-call(bf16[272,512]{1,0:T(8,128)(2,1)S(1)} %collective-permute-done.7.mid_ref, f32[4,128,512]{2,1,0:T(8,128)S(1)} %get-tuple-element.75.s_s, ...), custom_call_target="tpu_custom_call" | custom-call | flops 2000000000 | bytes 20000000 | tf_op jit(solution)/shard_map/pallas_call | solution.py:1075
  46.3 0.8 %collective-permute-start.11 = (bf16[544,128]{1,0:T(8,128)(2,1)S(1)}, bf16[544,128]{1,0:T(8,128)(2,1)S(1)}, u32[]{:S(2)}, u32[]{:S(2)}) collective-permute-start(bf16[544,128]{1,0:T(8,128)(2,1)S(1)} %get-tuple-element.103), channel_id=1, source_target_pairs={{0,0},{2,1},{1,2},{3,3},{4,4},{6,5},{5,6},{7,7},{8,8},{10,9},{9,10... | collective-permute-start | bytes 417800 | tf_op jit(solution)/shard_map/ppermute | solution.py:1090
  47.1 2.8 %collective-permute-start.12 = (bf16[544,128]{1,0:T(8,128)(2,1)S(1)}, bf16[544,128]{1,0:T(8,128)(2,1)S(1)}, u32[]{:S(2)}, u32[]{:S(2)}) collective-permute-start(bf16[544,128]{1,0:T(8,128)(2,1)S(1)} %get-tuple-element.104), channel_id=1, source_target_pairs={{0,2},{2,3},{1,0},{3,1},{4,6},{6,7},{5,4},{7,5},{8,10},{10,11},{9,... | collective-permute-start | bytes 417800 | tf_op jit(solution)/shard_map/ppermute | solution.py:1091
  49.9 0.0 copy-done.5
  49.9 4.7 %shard_map.190 = (f32[512,512]{1,0:T(8,128)S(1)}, f32[8,8,128]{2,1,0:T(8,128)S(1)}, f32[8,512]{1,0:T(8,128)S(1)}, f32[24,128]{1,0:T(8,128)S(1)}) custom-call(bf16[4,128,512]{2,1,0:T(8,128)(2,1)S(1)} %get-tuple-element.87.hlow_ref, bf16[4,128,512]{2,1,0:T(8,128)(2,1)S(1)} %get-tuple-element.88.clow_ref, f32[8,512]{1,0:T(8,128)S(1)} %get-tuple-element.89.endrow_ref, ...), custom_call_target="tpu_custom_call" | custom-call | flops 3000000000 | bytes 30000000 | tf_op jit(solution)/shard_map/pallas_call | solution.py:1092
  54.6 0.5 shard_map.191
  55.2 0.9 %collective-permute-start.8 = (bf16[128,512]{1,0:T(8,128)(2,1)S(1)}, bf16[128,512]{1,0:T(8,128)(2,1)S(1)}, u32[]{:S(2)}, u32[]{:S(2)}) collective-permute-start(bf16[128,512]{1,0:T(8,128)(2,1)S(1)} %get-tuple-element.98), channel_id=1, source_target_pairs={{0,4},{4,0},{8,12},{12,8},{16,20},{20,16},{24,28},{28,24},{1,5},{5... | collective-permute-start | bytes 393224 | tf_op jit(solution)/shard_map/ppermute | solution.py:1140
  56.1 0.0 collective-permute-done.11.one_ref
  56.1 0.0 collective-permute-done.12.two_ref
  56.1 0.1 collective-permute-start.13
  56.2 3.1 %collective-permute-start.9 = (bf16[128,512]{1,0:T(8,128)(2,1)S(1)}, bf16[128,512]{1,0:T(8,128)(2,1)S(1)}, u32[]{:S(2)}, u32[]{:S(2)}) collective-permute-start(bf16[128,512]{1,0:T(8,128)(2,1)S(1)} %get-tuple-element.99), channel_id=1, source_target_pairs={{0,8},{4,12},{8,0},{12,4},{16,24},{20,28},{24,16},{28,20},{1,9},{5... | collective-permute-start | bytes 393224 | tf_op jit(solution)/shard_map/ppermute | solution.py:1140
  59.3 1.0 %collective-permute-start.10 = (bf16[128,512]{1,0:T(8,128)(2,1)S(1)}, bf16[128,512]{1,0:T(8,128)(2,1)S(1)}, u32[]{:S(2)}, u32[]{:S(2)}) collective-permute-start(bf16[128,512]{1,0:T(8,128)(2,1)S(1)} %get-tuple-element.100), channel_id=1, source_target_pairs={{0,12},{4,8},{8,4},{12,0},{16,28},{20,24},{24,20},{28,16},{1,13},{... | collective-permute-start | bytes 393224 | tf_op jit(solution)/shard_map/ppermute | solution.py:1140
  60.3 0.8 %collective-permute-done.13.other_ref = bf16[32,512]{1,0:T(8,128)(2,1)S(1)} collective-permute-done((bf16[32,512]{1,0:T(8,128)(2,1)S(1)}, bf16[32,512]{1,0:T(8,128)(2,1)S(1)}, u32[]{:S(2)}, u32[]{:S(2)}) %collective-permute-start.13) | collective-permute-done | bytes 32800 | tf_op jit(solution)/shard_map/ppermute | solution.py:1130
  61.1 0.1 shard_map.193
  61.2 1.5 %collective-permute-start.14 = (bf16[112,512]{1,0:T(8,128)(2,1)S(1)}, bf16[112,512]{1,0:T(8,128)(2,1)S(1)}, u32[]{:S(2)}, u32[]{:S(2)}) collective-permute-start(bf16[112,512]{1,0:T(8,128)(2,1)S(1)} %get-tuple-element.107), channel_id=1, source_target_pairs={{0,4},{4,0},{8,12},{12,8},{16,20},{20,16},{24,28},{28,24},{1,5},{5... | collective-permute-start | bytes 344072 | tf_op jit(solution)/shard_map/ppermute | solution.py:1150
  62.7 0.5 collective-permute-start.15
  63.2 0.0 collective-permute-done.8.y1
  63.2 1.6 %collective-permute-start.16 = (bf16[112,512]{1,0:T(8,128)(2,1)S(1)}, bf16[112,512]{1,0:T(8,128)(2,1)S(1)}, u32[]{:S(2)}, u32[]{:S(2)}) collective-permute-start(bf16[112,512]{1,0:T(8,128)(2,1)S(1)} %get-tuple-element.109), channel_id=1, source_target_pairs={{0,12},{4,8},{8,4},{12,0},{16,28},{20,24},{24,20},{28,16},{1,13},{... | collective-permute-start | bytes 344072 | tf_op jit(solution)/shard_map/ppermute | solution.py:1150
  64.8 0.0 collective-permute-done.9.y2
  64.8 2.8 %collective-permute-done.10.y3 = bf16[128,512]{1,0:T(8,128)(2,1)S(1)} collective-permute-done((bf16[128,512]{1,0:T(8,128)(2,1)S(1)}, bf16[128,512]{1,0:T(8,128)(2,1)S(1)}, u32[]{:S(2)}, u32[]{:S(2)}) %collective-permute-start.10) | collective-permute-done | bytes 131104 | tf_op jit(solution)/shard_map/ppermute | solution.py:1140
  67.5 0.4 collective-permute-done.14.w1
  68.0 1.3 %collective-permute-done.15.w2 = bf16[112,512]{1,0:T(8,128)(2,1)S(1)} collective-permute-done((bf16[112,512]{1,0:T(8,128)(2,1)S(1)}, bf16[112,512]{1,0:T(8,128)(2,1)S(1)}, u32[]{:S(2)}, u32[]{:S(2)}) %collective-permute-start.15) | collective-permute-done | bytes 114720 | tf_op jit(solution)/shard_map/ppermute | solution.py:1150
  69.3 2.4 %collective-permute-done.16.w3 = bf16[112,512]{1,0:T(8,128)(2,1)S(1)} collective-permute-done((bf16[112,512]{1,0:T(8,128)(2,1)S(1)}, bf16[112,512]{1,0:T(8,128)(2,1)S(1)}, u32[]{:S(2)}, u32[]{:S(2)}) %collective-permute-start.16) | collective-permute-done | bytes 114720 | tf_op jit(solution)/shard_map/ppermute | solution.py:1150
  71.6 1.1 %shard_map.194 = (f32[128,2048]{1,0:T(8,128)}, f32[128,512]{1,0:T(8,128)}, f32[32,128]{1,0:T(8,128)}, f32[4,2048]{1,0:T(4,128)}, f32[4,512]{1,0:T(4,128)}, /*ind...) custom-call(bf16[128,512]{1,0:T(8,128)(2,1)S(1)} %get-tuple-element.97.y0, ...), custom_call_target="tpu_custom_call" | custom-call | flops 1000000 | bytes 10000 | tf_op jit(solution)/shard_map/pallas_call | solution.py:1151
  (1 shorter events, 0.0 us)
Async XLA Ops:
  0.6 23.6 %copy-start = (f32[4,2048]{1,0:T(4,128)S(1)}, f32[4,2048]{1,0:T(4,128)}, u32[]{:S(2)}) copy-start(f32[4,2048]{1,0:T(4,128)} %taps_ref.7) | copy-start | bytes 98308
  0.7 23.6 %copy-start.4 = (f32[32]{0:T(128)S(1)}, f32[32]{0:T(128)}, u32[]{:S(2)}) copy-start(f32[32]{0:T(128)} %alog_ref.3) | copy-start | bytes 388
  0.7 23.5 %copy-start.3 = (f32[32]{0:T(128)S(1)}, f32[32]{0:T(128)}, u32[]{:S(2)}) copy-start(f32[32]{0:T(128)} %dtb_ref.1) | copy-start | bytes 388
  0.7 23.5 %copy-start.1 = (f32[2048]{0:T(1024)S(1)}, f32[2048]{0:T(1024)}, u32[]{:S(2)}) copy-start(f32[2048]{0:T(1024)} %param.17) | copy-start | bytes 24580
  4.3 19.3 %collective-permute-start = (bf16[336,512]{1,0:T(8,128)(2,1)}, bf16[336,512]{1,0:T(8,128)(2,1)S(1)}, u32[]{:S(2)}, u32[]{:S(2)}) collective-permute-start(bf16[336,512]{1,0:T(8,128)(2,1)} %get-tuple-element.66), channel_id=1, source_target_pairs={{0,4},{4,0},{8,12},{12,8},{16,20},{20,16},{24,28},{28,24},{1,5},{5... | collective-permute-start | bytes 1032200 | tf_op jit(solution)/shard_map/ppermute | solution.py:1033
  7.3 16.3 %collective-permute-start.1 = (bf16[336,512]{1,0:T(8,128)(2,1)}, bf16[336,512]{1,0:T(8,128)(2,1)S(1)}, u32[]{:S(2)}, u32[]{:S(2)}) collective-permute-start(bf16[336,512]{1,0:T(8,128)(2,1)} %get-tuple-element.67), channel_id=1, source_target_pairs={{0,8},{4,12},{8,0},{12,4},{16,24},{20,28},{24,16},{28,20},{1,9},{5... | collective-permute-start | bytes 1032200 | tf_op jit(solution)/shard_map/ppermute | solution.py:1033
  8.9 15.3 %collective-permute-start.2 = (bf16[336,512]{1,0:T(8,128)(2,1)}, bf16[336,512]{1,0:T(8,128)(2,1)S(1)}, u32[]{:S(2)}, u32[]{:S(2)}) collective-permute-start(bf16[336,512]{1,0:T(8,128)(2,1)} %get-tuple-element.68), channel_id=1, source_target_pairs={{0,12},{4,8},{8,4},{12,0},{16,28},{20,24},{24,20},{28,16},{1,13},{... | collective-permute-start | bytes 1032200 | tf_op jit(solution)/shard_map/ppermute | solution.py:1033
  8.9 1.3 %collective-permute-start.3 = (bf16[16,768]{1,0:T(8,128)(2,1)}, bf16[16,768]{1,0:T(8,128)(2,1)S(1)}, u32[]{:S(2)}, u32[]{:S(2)}) collective-permute-start(bf16[16,768]{1,0:T(8,128)(2,1)} %get-tuple-element.69), channel_id=1, source_target_pairs={{12,16},{16,12},{13,17},{17,13},{14,18},{18,14},{15,19},{19,15}} | collective-permute-start | bytes 73736 | tf_op jit(solution)/shard_map/ppermute | solution.py:1034
  9.5 1.4 %collective-permute-start.4 = (bf16[16,768]{1,0:T(8,128)(2,1)}, bf16[16,768]{1,0:T(8,128)(2,1)S(1)}, u32[]{:S(2)}, u32[]{:S(2)}) collective-permute-start(bf16[16,768]{1,0:T(8,128)(2,1)} %get-tuple-element.70), channel_id=1, source_target_pairs={{12,20},{16,8},{13,21},{17,9},{14,22},{18,10},{15,23},{19,11}} | collective-permute-start | bytes 73736 | tf_op jit(solution)/shard_map/ppermute | solution.py:1034
  10.2 7.4 %collective-permute-start.5 = (bf16[16,768]{1,0:T(8,128)(2,1)}, bf16[16,768]{1,0:T(8,128)(2,1)S(1)}, u32[]{:S(2)}, u32[]{:S(2)}) collective-permute-start(bf16[16,768]{1,0:T(8,128)(2,1)} %get-tuple-element.71), channel_id=1, source_target_pairs={{12,24},{16,4},{13,25},{17,5},{14,26},{18,6},{15,27},{19,7}} | collective-permute-start | bytes 73736 | tf_op jit(solution)/shard_map/ppermute | solution.py:1034
  10.9 12.7 %collective-permute-start.6 = (bf16[16,768]{1,0:T(8,128)(2,1)}, bf16[16,768]{1,0:T(8,128)(2,1)S(1)}, u32[]{:S(2)}, u32[]{:S(2)}) collective-permute-start(bf16[16,768]{1,0:T(8,128)(2,1)} %get-tuple-element.72), channel_id=1, source_target_pairs={{12,28},{16,0},{13,29},{17,1},{14,30},{18,2},{15,31},{19,3}} | collective-permute-start | bytes 73736 | tf_op jit(solution)/shard_map/ppermute | solution.py:1034
  24.2 1.0 %copy-start.2 = (bf16[336,512]{1,0:T(8,128)(2,1)S(1)}, bf16[336,512]{1,0:T(8,128)(2,1)}, u32[]{:S(2)}) copy-start(bf16[336,512]{1,0:T(8,128)(2,1)} %get-tuple-element.65.x0) | copy-start | bytes 1032196
  29.1 16.0 %collective-permute-start.7 = (bf16[272,512]{1,0:T(8,128)(2,1)S(1)}, bf16[272,512]{1,0:T(8,128)(2,1)S(1)}, u32[]{:S(2)}, u32[]{:S(2)}) collective-permute-start(bf16[272,512]{1,0:T(8,128)(2,1)S(1)} %get-tuple-element.74), channel_id=1, source_target_pairs={{0,16},{4,20},{8,24},{12,28},{16,0},{20,4},{24,8},{28,12},{1,17},{... | collective-permute-start | bytes 835592 | tf_op jit(solution)/shard_map/ppermute | solution.py:1065
  45.2 4.7 %copy-start.5 = (f32[32]{0:T(128)S(1)}, f32[32]{0:T(128)}, u32[]{:S(2)}) copy-start(f32[32]{0:T(128)} %skip_ref.1) | copy-start | bytes 388
  46.3 9.8 %collective-permute-start.11 = (bf16[544,128]{1,0:T(8,128)(2,1)S(1)}, bf16[544,128]{1,0:T(8,128)(2,1)S(1)}, u32[]{:S(2)}, u32[]{:S(2)}) collective-permute-start(bf16[544,128]{1,0:T(8,128)(2,1)S(1)} %get-tuple-element.103), channel_id=1, source_target_pairs={{0,0},{2,1},{1,2},{3,3},{4,4},{6,5},{5,6},{7,7},{8,8},{10,9},{9,10... | collective-permute-start | bytes 417800 | tf_op jit(solution)/shard_map/ppermute | solution.py:1090
  47.1 8.9 %collective-permute-start.12 = (bf16[544,128]{1,0:T(8,128)(2,1)S(1)}, bf16[544,128]{1,0:T(8,128)(2,1)S(1)}, u32[]{:S(2)}, u32[]{:S(2)}) collective-permute-start(bf16[544,128]{1,0:T(8,128)(2,1)S(1)} %get-tuple-element.104), channel_id=1, source_target_pairs={{0,2},{2,3},{1,0},{3,1},{4,6},{6,7},{5,4},{7,5},{8,10},{10,11},{9,... | collective-permute-start | bytes 417800 | tf_op jit(solution)/shard_map/ppermute | solution.py:1091
  55.2 8.0 %collective-permute-start.8 = (bf16[128,512]{1,0:T(8,128)(2,1)S(1)}, bf16[128,512]{1,0:T(8,128)(2,1)S(1)}, u32[]{:S(2)}, u32[]{:S(2)}) collective-permute-start(bf16[128,512]{1,0:T(8,128)(2,1)S(1)} %get-tuple-element.98), channel_id=1, source_target_pairs={{0,4},{4,0},{8,12},{12,8},{16,20},{20,16},{24,28},{28,24},{1,5},{5... | collective-permute-start | bytes 393224 | tf_op jit(solution)/shard_map/ppermute | solution.py:1140
  56.1 5.0 %collective-permute-start.13 = (bf16[32,512]{1,0:T(8,128)(2,1)S(1)}, bf16[32,512]{1,0:T(8,128)(2,1)S(1)}, u32[]{:S(2)}, u32[]{:S(2)}) collective-permute-start(bf16[32,512]{1,0:T(8,128)(2,1)S(1)} %shard_map.192.own_ref), channel_id=1, source_target_pairs={{0,16},{4,20},{8,24},{12,28},{16,0},{20,4},{24,8},{28,12},{1,17},{... | collective-permute-start | bytes 98312 | tf_op jit(solution)/shard_map/ppermute | solution.py:1130
  56.2 8.6 %collective-permute-start.9 = (bf16[128,512]{1,0:T(8,128)(2,1)S(1)}, bf16[128,512]{1,0:T(8,128)(2,1)S(1)}, u32[]{:S(2)}, u32[]{:S(2)}) collective-permute-start(bf16[128,512]{1,0:T(8,128)(2,1)S(1)} %get-tuple-element.99), channel_id=1, source_target_pairs={{0,8},{4,12},{8,0},{12,4},{16,24},{20,28},{24,16},{28,20},{1,9},{5... | collective-permute-start | bytes 393224 | tf_op jit(solution)/shard_map/ppermute | solution.py:1140
  59.3 8.2 %collective-permute-start.10 = (bf16[128,512]{1,0:T(8,128)(2,1)S(1)}, bf16[128,512]{1,0:T(8,128)(2,1)S(1)}, u32[]{:S(2)}, u32[]{:S(2)}) collective-permute-start(bf16[128,512]{1,0:T(8,128)(2,1)S(1)} %get-tuple-element.100), channel_id=1, source_target_pairs={{0,12},{4,8},{8,4},{12,0},{16,28},{20,24},{24,20},{28,16},{1,13},{... | collective-permute-start | bytes 393224 | tf_op jit(solution)/shard_map/ppermute | solution.py:1140
  61.2 6.8 %collective-permute-start.14 = (bf16[112,512]{1,0:T(8,128)(2,1)S(1)}, bf16[112,512]{1,0:T(8,128)(2,1)S(1)}, u32[]{:S(2)}, u32[]{:S(2)}) collective-permute-start(bf16[112,512]{1,0:T(8,128)(2,1)S(1)} %get-tuple-element.107), channel_id=1, source_target_pairs={{0,4},{4,0},{8,12},{12,8},{16,20},{20,16},{24,28},{28,24},{1,5},{5... | collective-permute-start | bytes 344072 | tf_op jit(solution)/shard_map/ppermute | solution.py:1150
  62.7 6.6 %collective-permute-start.15 = (bf16[112,512]{1,0:T(8,128)(2,1)S(1)}, bf16[112,512]{1,0:T(8,128)(2,1)S(1)}, u32[]{:S(2)}, u32[]{:S(2)}) collective-permute-start(bf16[112,512]{1,0:T(8,128)(2,1)S(1)} %get-tuple-element.108), channel_id=1, source_target_pairs={{0,8},{4,12},{8,0},{12,4},{16,24},{20,28},{24,16},{28,20},{1,9},{5... | collective-permute-start | bytes 344072 | tf_op jit(solution)/shard_map/ppermute | solution.py:1150
  63.2 8.4 %collective-permute-start.16 = (bf16[112,512]{1,0:T(8,128)(2,1)S(1)}, bf16[112,512]{1,0:T(8,128)(2,1)S(1)}, u32[]{:S(2)}, u32[]{:S(2)}) collective-permute-start(bf16[112,512]{1,0:T(8,128)(2,1)S(1)} %get-tuple-element.109), channel_id=1, source_target_pairs={{0,12},{4,8},{8,4},{12,0},{16,28},{20,24},{24,20},{28,16},{1,13},{... | collective-permute-start | bytes 344072 | tf_op jit(solution)/shard_map/ppermute | solution.py:1150

commit v4 on v3

--- a/solution.py
+++ b/solution.py
@@ -374,11 +374,11 @@
     return pl.ds(pl.multiple_of(start, TILE), width)
 
 
-def pack_kernel(sig_ref, map_ref, dt_ref, dy_ref, mtaps_ref, mbias_ref, *rest):
-    x_refs, halo_refs, tap_ref, (dt_in, sems) = rest[:4], rest[4:8], rest[8], rest[9:]
+def pack_kernel(map_ref, dt_ref, dy_ref, mtaps_ref, mbias_ref, *rest):
+    u_refs, tap_ref, (dt_in, sems) = rest[:4], rest[4], rest[5:]
     quad, r, f = place()
     copies = []
-    dt_copy = pltpu.make_async_copy(dt_ref, dt_in, sems.at[36])
+    dt_copy = pltpu.make_async_copy(dt_ref, dt_in, sems.at[20])
     dt_copy.start()
 
     def send(source, target):
@@ -389,24 +389,15 @@
     half = map_ref.shape[1] // 2
     for k in (1, 2, 3, 0):
         dest = lax.bitwise_xor(r, k)
-        x = x_refs[k]
         cols = at_tile(dest * 4 * TILE, 4 * TILE)
-        send(sig_ref.at[:, cols], x.at[0:TILE, :])
-        send(dy_ref.at[:, cols], x.at[TILE : 2 * TILE, :])
+        send(dy_ref.at[:, cols], u_refs[k].at[0:TILE, :])
         group = (2 * f + lax.div(dest, 2)) * TILE
         for j in range(2):
             for e in range(2):
                 send(
                     map_ref.at[e * HALF : (e + 1) * HALF, at_tile(group + j * half)],
-                    x.at[2 * TILE : 2 * TILE + HALF, lanes_of(2 * j + e)],
+                    u_refs[k].at[TILE : TILE + HALF, lanes_of(2 * j + e)],
                 )
-    for m in range(4):
-        dest = jnp.where(quad == 0, m, 3 - m)
-        rows = pl.ds(pl.multiple_of(jnp.where(quad == 0, HALF - 16, TILE - 16), 16), 16)
-        send(sig_ref.at[rows, at_tile(dest * 4 * TILE, 4 * TILE)], halo_refs[m].at[:, 0 : 4 * TILE])
-        group = (2 * f + lax.div(dest, 2)) * TILE
-        for j in range(2):
-            send(map_ref.at[rows, at_tile(group + j * half)], halo_refs[m].at[:, lanes_of(4 + j)])
     tap_ref[0:4, :] = mtaps_ref[...]
     tap_ref[4:5, :] = mbias_ref[...]
     tap_ref[5:8, :] = jnp.zeros_like(tap_ref[5:8, :])
@@ -417,25 +408,44 @@
         hi, mid, lo = split3(dt_in[pl.ds(pl.multiple_of(8 * dest, 8), 8), :])
         top = jnp.concatenate([hi.astype(F32), mid.astype(F32)], axis=0)
         low = jnp.concatenate([lo.astype(F32), zero], axis=0)
-        x_refs[k][2 * TILE + HALF : 2 * TILE + HALF + 16, :] = jnp.concatenate(
+        u_refs[k][TILE + HALF : TILE + HALF + 16, :] = jnp.concatenate(
             [top, low, jnp.zeros((16, 2 * TILE), F32)], axis=1
         ).astype(BF)
     for copy in copies:
         copy.wait()
 
 
-def tap_rows(j, taps_ref, bias_ref, mtaps_ref):
-    quad, r, f = place()
-    if j < 4:
-        at = at_tile((4 * r + j) * TILE)
-        return [taps_ref[k : k + 1, at] for k in range(4)], bias_ref[0:1, at]
-    group = 2 * f + lax.div(r, 2)
-    owner = 2 * (j - 4) + lax.div(f, 2)
-    at = at_tile(lax.rem(group, 4) * TILE)
-    return [mtaps_ref[owner, k : k + 1, at] for k in range(4)], mtaps_ref[owner, 4:5, at]
-
-
-def shifted(block, k):
+def pack_sig_kernel(sig_ref, *rest):
+    v_refs, sems = rest[:4], rest[4]
+    r = place()[1]
+    copies = []
+    for k in (1, 2, 3, 0):
+        dest = lax.bitwise_xor(r, k)
+        copy = pltpu.make_async_copy(
+            sig_ref.at[:, at_tile(dest * 4 * TILE, 4 * TILE)], v_refs[k], sems.at[k]
+        )
+        copy.start()
+        copies.append(copy)
+    for copy in copies:
+        copy.wait()
+
+
+def sig_tap_rows(j, taps_ref, bias_ref):
+    at = at_tile((4 * place()[1] + j) * TILE)
+    return [taps_ref[k : k + 1, at] for k in range(4)], bias_ref[0:1, at]
+
+
+def map_tap_rows(j, mine_ref):
+    return [mine_ref[8 * j + k : 8 * j + k + 1, :] for k in range(4)], mine_ref[
+        8 * j + 4 : 8 * j + 5, :
+    ]
+
+
+def sigmoid(v):
+    return 0.5 * jnp.tanh(0.5 * v) + 0.5
+
+
+def rolled(block, k):
     return block[8:] if k == 3 else pltpu.roll(block, 3 - k, 0)[8:]
 
 
@@ -453,64 +463,76 @@
     return out
 
 
-def first_kernel(
-    x0,
-    x1,
-    x2,
-    x3,
-    b0,
-    b1,
-    b2,
-    b3,
-    taps_ref,
-    bias_ref,
-    mtaps_ref,
+def conv(block, taps, bias):
+    pre = bias + taps[0] * rolled(block, 0)
+    for k in range(1, 4):
+        pre = pre + taps[k] * rolled(block, k)
+    return pre
+
+
+def boundary_chunk(i, high):
+    return high if i == 0 else jnp.logical_not(high)
+
+
+def patched(ref, lanes, patch, patch_lanes, i, high):
+    rows = slice(i * TILE, (i + 1) * TILE)
+    if i % 2 == 1:
+        return ref[rows, lanes]
+    first = jnp.where(
+        boundary_chunk(i, high), patch[:, patch_lanes], ref[i * TILE : i * TILE + 16, lanes]
+    )
+    return jnp.concatenate([first, ref[i * TILE + 16 : (i + 1) * TILE, lanes]], axis=0)
+
+
+def grads_kernel(
+    u0,
+    u1,
+    u2,
+    u3,
+    one_taps,
+    two_taps,
     alog_ref,
     dtb_ref,
     mid_ref,
-    xp,
     dp,
-    act,
-    slope,
-    scaled_s,
-    weighted_s,
+    xm,
+    actm,
+    prem,
     sgrad_s,
     step_e,
     toend_e,
     exp_e,
-    s_s,
     t_s,
     step_r,
     ds_r,
     sig_r,
+    mine_ref,
     dt_src,
 ):
     quad, r, f = place()
     high = quad == 1
     half_lane = ids((TILE, TILE), 1) < HALF
     lane8 = ids((8, TILE), 1)
-    for k, x in enumerate((x0, x1, x2, x3)):
+    group = 2 * f + lax.div(r, 2)
+    at = at_tile(lax.rem(group, 4) * TILE)
+    for j in range(2):
+        mine_ref[8 * j : 8 * j + 8, :] = jnp.where(
+            lax.rem(f, 2) == j, one_taps[:, at], two_taps[:, at]
+        )
+    for k, u in enumerate((u0, u1, u2, u3)):
         s = lax.bitwise_xor(r, k)
-        low_at = pl.multiple_of(HALF * s, HALF)
-        up_at = pl.multiple_of(HALF * (3 - s), HALF)
-        for e, at in ((0, low_at), (1, up_at)):
-            here = slice(e * HALF, (e + 1) * HALF)
-            rows = pl.ds(pl.multiple_of(8 + at, 8), HALF)
-            xp[e, rows, 0 : 4 * TILE] = x[here, :].astype(F32)
+        for e, start in ((0, HALF * s), (1, HALF * (3 - s))):
             for j in range(2):
-                xp[e, rows, lanes_of(4 + j)] = x[
-                    2 * TILE : 2 * TILE + HALF, lanes_of(2 * j + e)
+                xm[e, pl.ds(pl.multiple_of(8 + start, 8), HALF), lanes_of(j)] = u[
+                    TILE : TILE + HALF, lanes_of(2 * j + e)
                 ].astype(F32)
-            dp[pl.ds(pl.multiple_of(2 * TILE * e + at, HALF), HALF), :] = x[
-                TILE + e * HALF : TILE + (e + 1) * HALF, :
+            dp[pl.ds(pl.multiple_of(2 * TILE * e + start, HALF), HALF), :] = u[
+                e * HALF : (e + 1) * HALF, :
             ]
-        packed = x[2 * TILE + HALF : 2 * TILE + HALF + 16, 0 : 2 * TILE].astype(F32)
+        packed = u[TILE + HALF : TILE + HALF + 16, 0 : 2 * TILE].astype(F32)
         dt_src[s] = packed[0:8, 0:TILE] + packed[8:16, 0:TILE] + packed[0:8, TILE : 2 * TILE]
-    edge = jnp.zeros((8, 6 * TILE), F32)
-    for b in (b0, b1, b2, b3):
-        edge = edge + b[...].astype(F32)[8:16]
-    xp[0, 0:8, :] = jnp.where(high, edge, 0.0)
-    xp[1, 0:8, :] = jnp.where(high, xp[0, 2 * TILE : 2 * TILE + 8, :], edge)
+    xm[0, 0:8, :] = jnp.zeros((8, 2 * TILE), F32)
+    xm[1, 0:8, :] = jnp.where(high, xm[0, 2 * TILE : 2 * TILE + 8, :], 0.0)
 
     rate8 = -jnp.exp(head_row(alog_ref, r))
     bias8 = head_row(dtb_ref, r)
@@ -533,18 +555,14 @@
     for i in range(4):
         rows = slice(i * TILE, (i + 1) * TILE)
         base = (i % 2) * TILE
-        for j in range(6):
+        for j in range(2):
             lanes = lanes_of(j)
-            block = xp[i // 2, base : base + TILE + 8, lanes]
-            taps, bias = tap_rows(j, taps_ref, bias_ref, mtaps_ref)
-            pre = bias + taps[0] * shifted(block, 0)
-            for k in range(1, 4):
-                pre = pre + taps[k] * shifted(block, k)
-            sig = 1.0 / (1.0 + jnp.exp(-pre))
-            act[rows, lanes] = (pre * sig).astype(BF)
-            slope[rows, lanes] = sig * (1.0 + pre * (1.0 - sig))
+            taps, bias = map_tap_rows(j, mine_ref)
+            pre = conv(xm[i // 2, base : base + TILE + 8, lanes], taps, bias)
+            actm[rows, lanes] = (pre * sigmoid(pre)).astype(BF)
+            prem[rows, lanes] = pre
         cols = columns(step_r[8 * i : 8 * i + 8, :], ds_r[8 * i : 8 * i + 8, :])
-        end = []
+        end, masked = [], []
         for j in range(4):
             lanes = lanes_of(j)
             step = jnp.where(half_lane, cols[:, 2 * j : 2 * j + 1], cols[:, 2 * j + 1 : 2 * j + 2])
@@ -553,53 +571,204 @@
             )
             last = ds[TILE - 1 : TILE, :]
             grow = jnp.exp(ds)
-            toend = jnp.exp(last - ds)
             step_e[rows, lanes] = step
-            toend_e[rows, lanes] = toend
+            toend_e[rows, lanes] = jnp.exp(last - ds)
             exp_e[rows, lanes] = grow
             end.append(jnp.exp(last))
-            scaled = (act[rows, lanes].astype(F32) * step).astype(BF)
+            grown = (dp[rows, lanes].astype(F32) * grow).astype(BF)
+            sgrad_s[rows, lanes] = grown
+            if i % 2 == 0:
+                unknown = jnp.logical_and(boundary_chunk(i, high), ids((16, TILE), 0) < 3)
+                first = jnp.where(unknown, 0.0, grown[0:16].astype(F32)).astype(BF)
+                grown = jnp.concatenate([first, grown[16:]], axis=0)
+            masked.append(grown)
+        ends.append(jnp.concatenate(end, axis=1))
+        t_s[i] = mm(actm[rows, lanes_of(1)], jnp.concatenate(masked, axis=1), TN)
+    g_a = t_s[0] + ends[0] * t_s[1]
+    g_b = t_s[2] + ends[2] * t_s[3]
+    mid_ref[...] = jnp.where(high, g_a + ends[0] * ends[1] * g_b, g_b).astype(BF)
+
+
+def edge_kernel(v0, v1, v2, v3, xm, out_ref):
+    quad, r, f = place()
+    high = quad == 1
+    wanted = lax.bitwise_xor(r, jnp.where(high, 0, 3))
+    found = jnp.zeros((16, 4 * TILE), F32)
+    for k, v in enumerate((v0, v1, v2, v3)):
+        rows = jnp.where(high, v[TILE - 16 : TILE, :], v[HALF - 16 : HALF, :]).astype(F32)
+        found = found + jnp.where(wanted == k, rows, 0.0)
+    out_ref[:, 0 : 4 * TILE] = found.astype(BF)
+    last = slice(8 + 2 * TILE - 16, 8 + 2 * TILE)
+    out_ref[:, 4 * TILE : 6 * TILE] = jnp.where(high, xm[1, last, :], xm[0, last, :]).astype(BF)
+
+
+def first_kernel(
+    v0, v1, v2, v3, step_e, toend_e, taps_ref, bias_ref, xs, acts, pres, scaled_s, weighted_s
+):
+    quad, r, f = place()
+    high = quad == 1
+    for k, v in enumerate((v0, v1, v2, v3)):
+        s = lax.bitwise_xor(r, k)
+        for e, start in ((0, HALF * s), (1, HALF * (3 - s))):
+            xs[e, pl.ds(pl.multiple_of(8 + start, 8), HALF), :] = v[
+                e * HALF : (e + 1) * HALF, :
+            ].astype(F32)
+    xs[0, 0:8, :] = jnp.zeros((8, 4 * TILE), F32)
+    xs[1, 0:8, :] = jnp.where(high, xs[0, 2 * TILE : 2 * TILE + 8, :], 0.0)
+    for i in range(4):
+        rows = slice(i * TILE, (i + 1) * TILE)
+        base = (i % 2) * TILE
+        for j in range(4):
+            lanes = lanes_of(j)
+            taps, bias = sig_tap_rows(j, taps_ref, bias_ref)
+            pre = conv(xs[i // 2, base : base + TILE + 8, lanes], taps, bias)
+            value = (pre * sigmoid(pre)).astype(BF)
+            acts[rows, lanes] = value
+            pres[rows, lanes] = pre
+            scaled = (value.astype(F32) * step_e[rows, lanes]).astype(BF)
             scaled_s[rows, lanes] = scaled
-            weighted_s[rows, lanes] = (scaled.astype(F32) * toend).astype(BF)
-            sgrad_s[rows, lanes] = (dp[rows, lanes].astype(F32) * grow).astype(BF)
-        ends.append(jnp.concatenate(end, axis=1))
-        s_s[i] = mm(act[rows, lanes_of(4)], weighted_s[rows, :], TN)
-        t_s[i] = mm(act[rows, lanes_of(5)], sgrad_s[rows, :], TN)
+            weighted_s[rows, lanes] = (scaled.astype(F32) * toend_e[rows, lanes]).astype(BF)
+
+
+def states_kernel(
+    halo_ref,
+    xs,
+    xm,
+    actm,
+    weighted_s,
+    sgrad_s,
+    step_e,
+    toend_e,
+    exp_e,
+    taps_ref,
+    bias_ref,
+    mine_ref,
+    mid_ref,
+    s_s,
+    delta_ref,
+    edge_ref,
+    act_p,
+    pre_p,
+    scaled_p,
+    weighted_p,
+):
+    quad, r, f = place()
+    high = quad == 1
+    edge = halo_ref[...].astype(F32)[8:16]
+    edge_ref[...] = edge
+    segment = jnp.where(high, 0, 1)
+    rows16 = pl.ds(pl.multiple_of(2 * TILE * segment, 16), 16)
+    for j in range(6):
+        lanes = lanes_of(j)
+        if j < 4:
+            taps, bias = sig_tap_rows(j, taps_ref, bias_ref)
+            first = xs[segment, 8:24, lanes]
+        else:
+            taps, bias = map_tap_rows(j - 4, mine_ref)
+            first = xm[segment, 8:24, lanes_of(j - 4)]
+        pre = conv(jnp.concatenate([edge[:, lanes], first], axis=0), taps, bias)
+        value = (pre * sigmoid(pre)).astype(BF)
+        act_p[:, lanes] = value
+        pre_p[:, lanes] = pre
+        if j < 4:
+            scaled = (value.astype(F32) * step_e[rows16, lanes]).astype(BF)
+            scaled_p[:, lanes] = scaled
+            weighted_p[:, lanes] = (scaled.astype(F32) * toend_e[rows16, lanes]).astype(BF)
+    every = slice(0, 4 * TILE)
+    for i in range(4):
+        s_s[i] = mm(
+            patched(actm, lanes_of(0), act_p, lanes_of(4), i, high),
+            patched(weighted_s, every, weighted_p, every, i, high),
+            TN,
+        )
+    ends = end_rows_of(exp_e)
     f_a = ends[1] * s_s[0] + s_s[1]
     f_b = ends[3] * s_s[2] + s_s[3]
-    g_a = t_s[0] + ends[0] * t_s[1]
-    g_b = t_s[2] + ends[2] * t_s[3]
-    d_a = ends[0] * ends[1]
     d_b = ends[2] * ends[3]
     mid_ref[0:TILE, :] = jnp.where(high, d_b * f_a + f_b, f_a).astype(BF)
-    mid_ref[TILE : 2 * TILE, :] = jnp.where(high, g_a + d_a * g_b, g_b).astype(BF)
-    hi, mid, lo = split3(jnp.broadcast_to(d_a * d_b, (16, 4 * TILE)))
-    row16 = ids((16, 4 * TILE), 0)
-    parts = jnp.where(
-        row16 == 0,
-        hi.astype(F32),
-        jnp.where(row16 == 1, mid.astype(F32), jnp.where(row16 == 2, lo.astype(F32), 0.0)),
-    )
-    mid_ref[2 * TILE : 2 * TILE + 16, :] = parts.astype(BF)
-
-
-def second_kernel(dp, act, scaled_s, ds_r, diag_ref, gmap_ref, gsum_ref):
+    grown = sgrad_s[rows16, :].astype(F32)
+    out_rows = act_p[:, lanes_of(5)].astype(F32)
+    known = jnp.where(ids((16, TILE), 0) < 3, out_rows, 0.0).astype(BF)
+    delta_ref[...] = mm(known, grown.astype(BF), TN)
+    hi, mid, lo = [part.astype(F32) for part in split3(ends[0] * ends[1] * d_b)]
+    pieces = [hi, mid, lo, grown[0:1], grown[1:2], grown[2:3]]
+    for k in range(3):
+        pieces.append(
+            jnp.concatenate([out_rows[k : k + 1], jnp.zeros((1, 3 * TILE), F32)], axis=1)
+        )
+    pieces.append(jnp.zeros((7, 4 * TILE), F32))
+    mid_ref[TILE : TILE + 16, :] = jnp.concatenate(pieces, axis=0).astype(BF)
+
+
+def slope_of(pre):
+    sig = sigmoid(pre)
+    return sig * (1.0 + pre * (1.0 - sig))
+
+
+def head_sums(*quantities):
+    found = []
+    head = ids((8, 4 * TILE), 1) // HALF
+    pick = (ids((8, 4 * TILE), 0) == head).astype(BF)
+    for tiles in quantities:
+        x = jnp.concatenate(tiles, axis=1)
+        hi = x.astype(BF)
+        lo = (x - hi.astype(F32)).astype(BF)
+        found.append(mm(pick, hi, NT) + mm(pick, lo, NT))
+    return found
+
+
+def skip_rows(skip_ref, r):
+    lane_row = ids((1, TILE), 1)
+    found = []
+    for j in range(4):
+        at = 8 * r + 2 * j
+        found.append(jnp.where(lane_row < HALF, skip_ref[at], skip_ref[at + 1]))
+    return found
+
+
+def second_kernel(
+    dp,
+    acts,
+    actm,
+    pres,
+    prem,
+    scaled_s,
+    step_e,
+    toend_e,
+    ds_r,
+    act_p,
+    pre_p,
+    scaled_p,
+    skip_ref,
+    base_ref,
+    coef_ref,
+    mslope_ref,
+    gmap_ref,
+    gsum_ref,
+    stepsum_ref,
+    skip_acc,
+):
+    quad, r, f = place()
+    high = quad == 1
+    skip_row = skip_rows(skip_ref, r)
+    skip_acc[...] = jnp.zeros_like(skip_acc)
     half_lane = ids((TILE, TILE), 1) < HALF
     row8 = ids((8, TILE), 0)
     col_q = ids((TILE, TILE), 1)
     seen = ids((TILE, TILE), 0) <= col_q
     for i in range(4):
         rows = slice(i * TILE, (i + 1) * TILE)
-        in_map = act[rows, lanes_of(4)]
-        out_map = act[rows, lanes_of(5)]
+        in_map = patched(actm, lanes_of(0), act_p, lanes_of(4), i, high)
+        out_map = patched(actm, lanes_of(1), act_p, lanes_of(5), i, high)
         score = mm(in_map, out_map, NT)
         ds8 = ds_r[8 * i : 8 * i + 8, :]
         cols = columns(ds8)
         grad_score = jnp.zeros((TILE, TILE), F32)
         gsum = jnp.zeros((8, TILE), F32)
         rcol = jnp.zeros((TILE, TILE), F32)
+        products = []
         for j in range(4):
-            sc = scaled_s[rows, lanes_of(j)]
+            sc = patched(scaled_s, lanes_of(j), scaled_p, lanes_of(j), i, high)
             dy = dp[rows, lanes_of(j)]
             diag = jnp.zeros((TILE, TILE), F32)
             for e in range(2):
@@ -615,7 +784,20 @@
                 gsum = gsum + jnp.where(row8 == h, jnp.sum(both, axis=0, keepdims=True), 0.0)
                 mix = (score * decay).astype(BF)
                 diag = diag + mm(mix, jnp.where(part, dy, jnp.zeros_like(dy)))
-            diag_ref[rows, lanes_of(j)] = diag
+            lanes = lanes_of(j)
+            sigf = patched(acts, lanes, act_p, lanes, i, high).astype(F32)
+            dyf = dy.astype(F32)
+            step = step_e[rows, lanes]
+            slope = slope_of(patched(pres, lanes, pre_p, lanes, i, high))
+            base_ref[rows, lanes] = (skip_row[j] * dyf + diag * step) * slope
+            coef_ref[rows, lanes] = toend_e[rows, lanes] * step * slope
+            products.append(diag * sigf)
+            skip_acc[:, lanes] += eights(dyf * sigf)
+        stepsum_ref[8 * i : 8 * i + 8, :] = head_sums(products)[0]
+        for j in range(2):
+            mslope_ref[rows, lanes_of(j)] = slope_of(
+                patched(prem, lanes_of(j), pre_p, lanes_of(4 + j), i, high)
+            )
         gs = grad_score.astype(BF)
         gmap_ref[rows, lanes_of(0)] = mm(gs, out_map)
         gmap_ref[rows, lanes_of(1)] = mm(gs, in_map, TN)
@@ -630,12 +812,19 @@
     return [exp_e[(i + 1) * TILE - 8 : (i + 1) * TILE, :][7:8, :] for i in range(4)]
 
 
-def taps_back(here, after, taps):
-    grads = jnp.concatenate([here, after], axis=0)
-    raw = taps[3] * here
+def taps_back(gp, i, lanes, taps):
+    base = (i % 2) * TILE
+    raw = taps[3] * gp[i // 2, base : base + TILE, lanes]
     for k in range(3):
-        raw = raw + taps[k] * pltpu.roll(grads, 5 + k, 0)[8:]
+        start = base + 3 - k
+        raw = raw + taps[k] * gp[i // 2, start : start + TILE, lanes]
     return raw
+
+
+def fill_pads(gp, high):
+    first = gp[1, 0:8, :]
+    gp[0, 2 * TILE : 2 * TILE + 8, :] = jnp.where(high, first, jnp.zeros_like(first))
+    gp[1, 2 * TILE : 2 * TILE + 8, :] = jnp.zeros_like(first)
 
 
 def spill_of(first, taps):
@@ -646,26 +835,36 @@
     return spill
 
 
-def tap_sums(here, block, sums):
+def tap_sums(here, x, edge_ref, i, lanes, edge_lanes, high, sums):
+    base = (i % 2) * TILE
+    if i % 2 == 1:
+        windows = [x[i // 2, base + 5 + k : base + 5 + k + TILE, lanes] for k in range(4)]
+    else:
+        first = x[i // 2, 0:8, lanes] + jnp.where(
+            boundary_chunk(i, high), edge_ref[:, edge_lanes], 0.0
+        )
+        block = jnp.concatenate([first, x[i // 2, 8 : TILE + 8, lanes]], axis=0)
+        windows = [rolled(block, k) for k in range(4)]
     for k in range(4):
-        sums[k] = sums[k] + eights(here * shifted(block, k))
+        sums[k] = sums[k] + eights(here * windows[k])
     sums[4] = sums[4] + eights(here)
 
 
 def maps_kernel(
-    mid_ref,
+    midg_ref,
+    midf_ref,
     s_s,
     t_s,
+    delta_ref,
     exp_e,
-    act,
-    slope,
+    mslope_ref,
     weighted_s,
+    weighted_p,
     sgrad_s,
     gmap_ref,
-    xp,
-    taps_ref,
-    bias_ref,
-    mtaps_ref,
+    xm,
+    edge_ref,
+    mine_ref,
     one_ref,
     two_ref,
     hlow_ref,
@@ -673,52 +872,56 @@
     endrow_ref,
     h_s,
     c_s,
+    gm,
 ):
     quad, r, f = place()
     high = quad == 1
     even = lax.rem(f, 2) == 0
     ends = end_rows_of(exp_e)
-    f_in = mid_ref[0:TILE, :].astype(F32)
-    g_in = mid_ref[TILE : 2 * TILE, :].astype(F32)
-    across = jnp.sum(mid_ref[2 * TILE : 2 * TILE + 16, :].astype(F32), axis=0, keepdims=True)
+    f_in = midf_ref[0:TILE, :].astype(F32)
+    extra = midf_ref[TILE : TILE + 16, :].astype(F32)
+    row16 = ids((16, 4 * TILE), 0)
+    across = jnp.sum(jnp.where(row16 < 3, extra, 0.0), axis=0, keepdims=True)
+    left_out = jnp.logical_and(row16 >= 3, row16 < 6)
+    grown = jnp.where(left_out, extra, 0.0).astype(BF)
+    out_rows = jnp.where(left_out[:, 0:TILE], pltpu.roll(extra[:, 0:TILE], 13, 0), 0.0).astype(BF)
+    g_in = midg_ref[...].astype(F32) + mm(out_rows, grown, TN)
+    t2 = t_s[2] + jnp.where(high, 0.0, delta_ref[...])
     f_a = ends[1] * s_s[0] + s_s[1]
     h_s[0] = jnp.where(high, f_in, 0.0)
     h_s[1] = ends[0] * h_s[0] + s_s[0]
     h_s[2] = jnp.where(high, ends[1] * h_s[1] + s_s[1], across * f_a + f_in)
     h_s[3] = ends[2] * h_s[2] + s_s[2]
-    g_b = t_s[2] + ends[2] * t_s[3]
+    g_b = t2 + ends[2] * t_s[3]
     c_s[3] = jnp.where(high, g_in, 0.0)
     c_s[2] = t_s[3] + ends[3] * c_s[3]
-    c_s[1] = jnp.where(high, t_s[2] + ends[2] * c_s[2], g_in + across * g_b)
+    c_s[1] = jnp.where(high, t2 + ends[2] * c_s[2], g_in + across * g_b)
     c_s[0] = t_s[1] + ends[1] * c_s[1]
-    taps_of = [tap_rows(4 + j, taps_ref, bias_ref, mtaps_ref)[0] for j in range(2)]
-    after = [jnp.zeros((8, TILE), F32) for _ in range(2)]
+    taps_of = [map_tap_rows(j, mine_ref)[0] for j in range(2)]
     sums = [[jnp.zeros((8, TILE), F32) for _ in range(5)] for _ in range(2)]
-    first = [None, None]
-    end_rows = [None] * 4
-    for i in (3, 2, 1, 0):
+    end_rows = []
+    every = slice(0, 4 * TILE)
+    for i in range(4):
         rows = slice(i * TILE, (i + 1) * TILE)
+        base = (i % 2) * TILE
         hlow_ref[i] = h_s[i].astype(BF)
         clow_ref[i] = c_s[i].astype(BF)
-        end_rows[i] = jnp.sum(h_s[i] * c_s[i], axis=0, keepdims=True) * ends[i]
+        end_rows.append(jnp.sum(h_s[i] * c_s[i], axis=0, keepdims=True) * ends[i])
         grads = (
-            mm(weighted_s[rows, :], clow_ref[i], NT) + gmap_ref[rows, lanes_of(0)],
+            mm(patched(weighted_s, every, weighted_p, every, i, high), clow_ref[i], NT) + gmap_ref[rows, lanes_of(0)],
             mm(sgrad_s[rows, :], hlow_ref[i], NT) + gmap_ref[rows, lanes_of(1)],
         )
-        base = (i % 2) * TILE
-        raws = []
         for j in range(2):
-            here = grads[j] * slope[rows, lanes_of(4 + j)]
-            raws.append(taps_back(here, after[j], taps_of[j]))
-            tap_sums(here, xp[i // 2, base : base + TILE + 8, lanes_of(4 + j)], sums[j])
-            start = here[0:8]
-            after[j] = jnp.where(high, start, 0.0) if i == 2 else start
-            if i == 2:
-                first[j] = start
-            if i == 0:
-                first[j] = jnp.where(high, start, first[j])
+            here = grads[j] * mslope_ref[rows, lanes_of(j)]
+            gm[i // 2, base : base + TILE, lanes_of(j)] = here
+            tap_sums(here, xm, edge_ref, i, lanes_of(j), lanes_of(4 + j), high, sums[j])
+    fill_pads(gm, high)
+    for i in range(4):
+        rows = slice(i * TILE, (i + 1) * TILE)
+        raws = [taps_back(gm, i, lanes_of(j), taps_of[j]) for j in range(2)]
         one_ref[rows, :] = jnp.where(even, raws[0], raws[1]).astype(BF)
         two_ref[rows, :] = jnp.where(even, raws[1], raws[0]).astype(BF)
+    first = jnp.where(high, gm[0, 0:8, :], gm[1, 0:8, :])
     endrow_ref[...] = jnp.concatenate(end_rows + [jnp.zeros((4, 4 * TILE), F32)], axis=0)
     row8 = ids((8, TILE), 0)
     tails = []
@@ -730,7 +933,7 @@
         zero8 = jnp.zeros((8, TILE), F32)
         tails.append(
             jnp.concatenate(
-                [spill_of(first[j], taps_of[j]), zero8, hi.astype(F32), lo.astype(F32)], axis=0
+                [spill_of(first[:, lanes_of(j)], taps_of[j]), zero8, hi.astype(F32), lo.astype(F32)], axis=0
             )
         )
     one_ref[4 * TILE : 4 * TILE + 32, :] = jnp.where(even, tails[0], tails[1]).astype(BF)
@@ -741,21 +944,23 @@
     hlow_ref,
     clow_ref,
     endrow_ref,
-    xp,
+    xs,
     dp,
-    act,
-    slope,
-    scaled_s,
-    step_e,
+    acts,
+    actm,
+    edge_ref,
+    act_p,
     toend_e,
     exp_e,
     step_r,
     sig_r,
-    diag_ref,
+    base_ref,
+    coef_ref,
     gsum_ref,
+    stepsum_ref,
+    skip_acc,
     taps_ref,
     alog_ref,
-    skip_ref,
     gp,
     blk,
     spill_ref,
@@ -763,7 +968,6 @@
 ):
     quad, r, f = place()
     high = quad == 1
-    lane_row = ids((1, TILE), 1)
     row8 = ids((8, TILE), 0)
     lane8 = ids((8, TILE), 1)
     rate8 = -jnp.exp(head_row(alog_ref, r))
@@ -772,48 +976,32 @@
     tail_sums = jnp.concatenate(
         [(row_q >= col_q).astype(F32), (row_q < col_q).astype(F32)], axis=0
     )
-    skip_row = []
-    for j in range(4):
-        at = 8 * r + 2 * j
-        skip_row.append(jnp.where(lane_row < HALF, skip_ref[at], skip_ref[at + 1]))
-
-    def head_sums(x, j):
-        pick = (row8 == 2 * j + lane8 // HALF).astype(BF)
-        hi = x.astype(BF)
-        lo = (x - hi.astype(F32)).astype(BF)
-        return mm(pick, hi, NT) + mm(pick, lo, NT)
-
     sums = [[jnp.zeros((8, TILE), F32) for _ in range(5)] for _ in range(4)]
-    skip_acc = [jnp.zeros((8, TILE), F32) for _ in range(4)]
     alog_acc = jnp.zeros((8, TILE), F32)
     ddt_acc = jnp.zeros((8, TILE), F32)
     for i in range(4):
         rows = slice(i * TILE, (i + 1) * TILE)
         at8 = slice(8 * i, 8 * i + 8)
         base = (i % 2) * TILE
-        off = mm(act[rows, lanes_of(5)], hlow_ref[i])
-        gw = mm(act[rows, lanes_of(4)], clow_ref[i])
+        off = mm(patched(actm, lanes_of(1), act_p, lanes_of(5), i, high), hlow_ref[i])
+        gw = mm(patched(actm, lanes_of(0), act_p, lanes_of(4), i, high), clow_ref[i])
         end_row = endrow_ref[i : i + 1, :]
         gsum = gsum_ref[at8, :]
-        back = jnp.zeros((8, TILE), F32)
-        stepsum = jnp.zeros((8, TILE), F32)
         end_sum = jnp.zeros((8, TILE), F32)
+        offs, backs = [], []
         for j in range(4):
             lanes = lanes_of(j)
-            dyf = dp[rows, lanes].astype(F32)
-            scf = scaled_s[rows, lanes].astype(F32)
-            sigf = act[rows, lanes].astype(F32)
-            gwe = gw[:, lanes] * toend_e[rows, lanes]
-            grad_scaled = gwe + diag_ref[rows, lanes]
-            gsum = gsum + head_sums(dyf * exp_e[rows, lanes] * off[:, lanes], j)
-            back = back + head_sums(gwe * scf, j)
-            stepsum = stepsum + head_sums(grad_scaled * sigf, j)
+            sigf = patched(acts, lanes, act_p, lanes, i, high).astype(F32)
+            offs.append(dp[rows, lanes].astype(F32) * exp_e[rows, lanes] * off[:, lanes])
+            backs.append(gw[:, lanes] * toend_e[rows, lanes] * sigf)
             end_sum = end_sum + jnp.where(row8 == 2 * j + lane8 // HALF, end_row[:, lanes], 0.0)
-            skip_acc[j] = skip_acc[j] + eights(dyf * sigf)
-            grad_sig = skip_row[j] * dyf + grad_scaled * step_e[rows, lanes]
-            here = grad_sig * slope[rows, lanes]
-            gp[rows, lanes] = here
-            tap_sums(here, xp[i // 2, base : base + TILE + 8, lanes], sums[j])
+            here = base_ref[rows, lanes] + gw[:, lanes] * coef_ref[rows, lanes]
+            gp[i // 2, base : base + TILE, lanes] = here
+            tap_sums(here, xs, edge_ref, i, lanes, lanes, high, sums[j])
+        offsum, backsum = head_sums(offs, backs)
+        gsum = gsum + offsum
+        stepsum = stepsum_ref[at8, :] + backsum
+        back = backsum * step_r[at8, :]
         grad_log = mm_f32(jnp.concatenate([gsum, back], axis=1), tail_sums) + jnp.sum(
             end_sum, axis=1, keepdims=True
         )
@@ -822,10 +1010,11 @@
         blk[2 * i + 1] = pltpu.roll(ddt, HALF, 1)
         ddt_acc = ddt_acc + ddt
         alog_acc = alog_acc + grad_log * step_r[at8, :]
+    fill_pads(gp, high)
     rows = []
     for j in range(4):
         taps = [taps_ref[k : k + 1, at_tile((4 * r + j) * TILE)] for k in range(4)]
-        first = jnp.where(high, gp[0:8, lanes_of(j)], gp[2 * TILE : 2 * TILE + 8, lanes_of(j)])
+        first = jnp.where(high, gp[0, 0:8, lanes_of(j)], gp[1, 0:8, lanes_of(j)])
         spill_ref[:, lanes_of(j)] = spill_of(first, taps)
         for t in range(5):
             rows.append(jnp.sum(sums[j][t], axis=0, keepdims=True))
@@ -833,7 +1022,7 @@
     ddtb = jnp.sum(ddt_acc, axis=1, keepdims=True)
     skips = jnp.zeros((8, TILE), F32)
     for j in range(4):
-        total = jnp.sum(skip_acc[j], axis=0, keepdims=True)
+        total = jnp.sum(skip_acc[:, lanes_of(j)], axis=0, keepdims=True)
         skips = skips + jnp.where(row8 == 2 * j + lane8 // HALF, total, 0.0)
     skips = jnp.sum(skips, axis=1, keepdims=True)
     three = jnp.where(lane8 == 0, alog, jnp.where(lane8 == 1, ddtb, skips))
@@ -879,19 +1068,11 @@
 
 def send_kernel(gp, taps_ref, y0, y1, y2, y3, dx):
     quad, r, f = place()
-    high = quad == 1
     for j in range(4):
         lanes = lanes_of(j)
         taps = [taps_ref[k : k + 1, at_tile((4 * r + j) * TILE)] for k in range(4)]
         for i in range(4):
-            rows = slice(i * TILE, (i + 1) * TILE)
-            if i == 3:
-                after = jnp.zeros((8, TILE), F32)
-            else:
-                after = gp[(i + 1) * TILE : (i + 1) * TILE + 8, lanes]
-            if i == 1:
-                after = jnp.where(high, after, 0.0)
-            dx[rows, lanes] = taps_back(gp[rows, lanes], after, taps).astype(BF)
+            dx[i * TILE : (i + 1) * TILE, lanes] = taps_back(gp, i, lanes, taps).astype(BF)
     for k, y in enumerate((y0, y1, y2, y3)):
         s = lax.bitwise_xor(r, k)
         for e, at in ((0, HALF * s), (1, 2 * TILE + HALF * (3 - s))):
@@ -904,6 +1085,7 @@
     param_rows = split_params(
         whole_params(own_ref[16:32, :]) + whole_params(other_ref[16:32, :])
     )
+    spill = other_ref[0:16, :].astype(F32)
     for k, w in enumerate((w0, w1, w2, w3)):
         s = lax.bitwise_xor(r, k)
         for e, at in ((0, HALF * s), (1, 2 * TILE + HALF * (3 - s))):
@@ -911,14 +1093,22 @@
             w[0:HALF, lanes_of(e)] = one_ref[rows, :]
             w[0:HALF, lanes_of(2 + e)] = two_ref[rows, :]
         here = jnp.where(lane8 < HALF, blk[s], pltpu.roll(blk[7 - s], HALF, 1))
-        hi, mid, lo = split3(here)
-        top = jnp.concatenate([hi.astype(F32), mid.astype(F32)], axis=0)
-        low = jnp.concatenate([lo.astype(F32), jnp.zeros((8, TILE), F32)], axis=0)
+        hi, mid, _ = split3(here)
         w[HALF : HALF + 16, :] = jnp.concatenate(
-            [top, low, jnp.zeros((16, 2 * TILE), F32)], axis=1
+            [
+                jnp.concatenate([hi.astype(F32), spill[0:8, 0 : 2 * TILE], spill[8:16, 0:TILE]], axis=1),
+                jnp.concatenate(
+                    [
+                        mid.astype(F32),
+                        spill[0:8, 2 * TILE : 4 * TILE],
+                        spill[8:16, TILE : 2 * TILE],
+                    ],
+                    axis=1,
+                ),
+            ],
+            axis=0,
         ).astype(BF)
-        w[HALF + 16 : HALF + 32, :] = other_ref[0:16, :]
-        w[HALF + 32 : HALF + 48, :] = param_rows
+        w[HALF + 16 : HALF + 32, :] = param_rows
 
 
 def last_kernel(
@@ -935,14 +1125,14 @@
         s = lax.bitwise_xor(r, k)
         cols = at_tile(s * 4 * TILE, 4 * TILE)
         dsig_ref[:, cols] = y[0:TILE, :].astype(F32)
-        spill = ws[k][HALF + 16 : HALF + 32, :].astype(F32)[0:8]
+        extra = ws[k][HALF : HALF + 16, :].astype(F32)
+        spill = jnp.concatenate(
+            [extra[0:8, TILE : 3 * TILE], extra[8:16, TILE : 3 * TILE]], axis=1
+        )
         dsig_ref[HALF - 8 : HALF, cols] += jnp.where(third, spill, 0.0)
         dsig_ref[TILE - 8 : TILE, cols] += jnp.where(fourth, spill, 0.0)
-        packed = ws[k][HALF : HALF + 16, 0 : 2 * TILE].astype(F32)
-        ddt_ref[pl.ds(pl.multiple_of(8 * s, 8), 8), :] = (
-            packed[0:8, 0:TILE] + packed[8:16, 0:TILE] + packed[0:8, TILE : 2 * TILE]
-        )
-        param = whole_params(ws[k][HALF + 32 : HALF + 48, :])
+        ddt_ref[pl.ds(pl.multiple_of(8 * s, 8), 8), :] = extra[0:8, 0:TILE] + extra[8:16, 0:TILE]
+        param = whole_params(ws[k][HALF + 16 : HALF + 32, :])
         params.append(param)
         for j in range(4):
             lanes = at_tile((4 * s + j) * TILE)
@@ -965,10 +1155,10 @@
                 dmap_ref[e * HALF : (e + 1) * HALF, lanes] = ws[a][
                     0:HALF, lanes_of(2 * j + e)
                 ].astype(F32) + ws[b][0:HALF, lanes_of(2 * j + e)].astype(F32)
-            spill = (
-                ws[a][HALF + 16 : HALF + 32, lanes_of(j)].astype(F32)[8:16]
-                + ws[b][HALF + 16 : HALF + 32, lanes_of(j)].astype(F32)[8:16]
-            )
+            spill = jnp.zeros((8, TILE), F32)
+            for w in (ws[a], ws[b]):
+                extra = w[HALF : HALF + 16, 3 * TILE : 4 * TILE].astype(F32)
+                spill = spill + extra[8 * j : 8 * j + 8]
             dmap_ref[HALF - 8 : HALF, lanes] += jnp.where(third, spill, 0.0)
             dmap_ref[TILE - 8 : TILE, lanes] += jnp.where(fourth, spill, 0.0)
             five = params[a][20 + 5 * j : 25 + 5 * j] + params[b][20 + 5 * j : 25 + 5 * j]
@@ -978,6 +1168,10 @@
 
 ROUTE_ONE = [(0, 0), (2, 1), (1, 2), (3, 3)]
 ROUTE_TWO = [(0, 2), (2, 3), (1, 0), (3, 1)]
+
+
+def back(route):
+    return [(target, source) for source, target in route]
 
 
 def shards_quad(
@@ -1019,59 +1213,120 @@
     wide, narrow = 6 * TILE, 4 * TILE
     owned = map_taps.shape[1]
     sig_bias_row = sig_bias[None, :]
-    packed = call(
+    *packed, map_params = call(
         pack_kernel,
-        (shape(2 * TILE + HALF + 16, narrow, kind=BF),) * 4
-        + (shape(16, wide, kind=BF),) * 4
-        + (shape(8, owned),),
-        [hbm, hbm, hbm, hbm, vmem, vmem],
-        (vmem,) * 9,
-        [pltpu.VMEM((32, TILE), F32), pltpu.SemaphoreType.DMA((37,))],
+        (shape(TILE + HALF + 16, narrow, kind=BF),) * 4 + (shape(8, owned),),
+        [hbm, hbm, hbm, vmem, vmem],
+        (vmem,) * 5,
+        [pltpu.VMEM((32, TILE), F32), pltpu.SemaphoreType.DMA((21,))],
         60,
         10**6,
-    )(sig_raw, map_raw, step_size_logits.T, d_out, map_taps, map_bias[None, :])
-    xs = [packed[0]] + [lax.ppermute(packed[k], "ctx", inside[k]) for k in (1, 2, 3)]
-    halos = [lax.ppermute(packed[4 + m], "ctx", [(3, 4 + m), (4, 3 - m)]) for m in range(4)]
-    map_params = lax.all_gather(packed[8], "fsdp", axis=0)
-    own_taps = (sig_taps, sig_bias_row, map_params)
-    mid, *kept = call(
-        first_kernel,
+    )(map_raw, step_size_logits.T, d_out, map_taps, map_bias[None, :])
+    us = [packed[0]] + [lax.ppermute(packed[k], "ctx", inside[k]) for k in (1, 2, 3)]
+    map_one = lax.ppermute(map_params, "fsdp", back(ROUTE_ONE))
+    map_two = lax.ppermute(map_params, "fsdp", back(ROUTE_TWO))
+    packed = call(
+        pack_sig_kernel,
+        (shape(TILE, narrow, kind=BF),) * 4,
+        [hbm],
+        (vmem,) * 4,
+        [pltpu.SemaphoreType.DMA((4,))],
+        60,
+        10**6,
+    )(sig_raw)
+    vs = [packed[0]] + [lax.ppermute(packed[k], "ctx", inside[k]) for k in (1, 2, 3)]
+    midg, dp, xm, actm, prem, sgrad, step_e, toend_e, exp_e, t_s, step_r, ds_r, sig_r, mine = call(
+        grads_kernel,
         (
-            shape(2 * TILE + 16, narrow, kind=BF),
-            shape(2, 2 * TILE + 8, wide),
+            shape(TILE, narrow, kind=BF),
             shape(total, narrow, kind=BF),
-            shape(total, wide, kind=BF),
-            shape(total, wide),
-            shape(total, narrow, kind=BF),
-            shape(total, narrow, kind=BF),
+            shape(2, 2 * TILE + 8, 2 * TILE),
+            shape(total, 2 * TILE, kind=BF),
+            shape(total, 2 * TILE),
             shape(total, narrow, kind=BF),
             shape(total, narrow),
             shape(total, narrow),
             shape(total, narrow),
             shape(4, TILE, narrow),
-            shape(4, TILE, narrow),
             shape(32, TILE),
             shape(32, TILE),
             shape(32, TILE),
+            shape(16, TILE),
         ),
-        [vmem] * 11 + [smem] * 2,
-        (vmem,) * 16,
+        [vmem] * 6 + [smem] * 2,
+        (vmem,) * 14,
         [pltpu.VMEM((4, 8, TILE), F32)],
         24,
-        4 * 10**9,
-    )(*xs, *halos, *own_taps, a_log, dt_bias)
-    xp, dp, act, slope, scaled, weighted, sgrad, step_e, toend_e, exp_e, s_s, t_s = kept[:12]
-    step_r, ds_r, sig_r = kept[12:]
-    mid = lax.ppermute(mid, "ctx", over)
-    diag, gmap, gsum = call(
+        2 * 10**9,
+    )(*us, map_one, map_two, a_log, dt_bias)
+    midg = lax.ppermute(midg, "ctx", over)
+    halo = call(edge_kernel, shape(16, wide, kind=BF), [vmem] * 5, vmem, [], 16, 10**6)(*vs, xm)
+    halo = lax.ppermute(halo, "ctx", over)
+    xs, acts, pres, scaled, weighted = call(
+        first_kernel,
+        (
+            shape(2, 2 * TILE + 8, narrow),
+            shape(total, narrow, kind=BF),
+            shape(total, narrow),
+            shape(total, narrow, kind=BF),
+            shape(total, narrow, kind=BF),
+        ),
+        [vmem] * 8,
+        (vmem,) * 5,
+        [],
+        24,
+        2 * 10**9,
+    )(*vs, step_e, toend_e, sig_taps, sig_bias_row)
+    midf, s_s, delta, edge, act_p, pre_p, scaled_p, weighted_p = call(
+        states_kernel,
+        (
+            shape(TILE + 16, narrow, kind=BF),
+            shape(4, TILE, narrow),
+            shape(TILE, narrow),
+            shape(8, wide),
+            shape(16, wide, kind=BF),
+            shape(16, wide),
+            shape(16, narrow, kind=BF),
+            shape(16, narrow, kind=BF),
+        ),
+        [vmem] * 12,
+        (vmem,) * 8,
+        [],
+        24,
+        10**9,
+    )(halo, xs, xm, actm, weighted, sgrad, step_e, toend_e, exp_e, sig_taps, sig_bias_row, mine)
+    midf = lax.ppermute(midf, "ctx", over)
+    base, coef, mslope, gmap, gsum, stepsum, skips = call(
         second_kernel,
-        (shape(total, narrow), shape(total, 2 * TILE), shape(32, TILE)),
-        [vmem] * 4,
-        (vmem,) * 3,
+        (
+            shape(total, narrow),
+            shape(total, narrow),
+            shape(total, 2 * TILE),
+            shape(total, 2 * TILE),
+            shape(32, TILE),
+            shape(32, TILE),
+            shape(8, narrow),
+        ),
+        [vmem] * 12 + [smem],
+        (vmem,) * 7,
         [],
-        16,
-        4 * 10**9,
-    )(dp, act, scaled, ds_r)
+        24,
+        5 * 10**9,
+    )(
+        dp,
+        acts,
+        actm,
+        pres,
+        prem,
+        scaled,
+        step_e,
+        toend_e,
+        ds_r,
+        act_p,
+        pre_p,
+        scaled_p,
+        skip_gain,
+    )
     one, two, hlow, clow, endrow = call(
         maps_kernel,
         (
@@ -1081,18 +1336,42 @@
             shape(4, TILE, narrow, kind=BF),
             shape(8, narrow),
         ),
-        [vmem] * 13,
+        [vmem] * 14,
         (vmem,) * 5,
-        [pltpu.VMEM((4, TILE, narrow), F32), pltpu.VMEM((4, TILE, narrow), F32)],
+        [
+            pltpu.VMEM((4, TILE, narrow), F32),
+            pltpu.VMEM((4, TILE, narrow), F32),
+            pltpu.VMEM((2, 2 * TILE + 8, 2 * TILE), F32),
+        ],
         24,
         2 * 10**9,
-    )(mid, s_s, t_s, exp_e, act, slope, weighted, sgrad, gmap, xp, *own_taps)
+    )(
+        midg,
+        midf,
+        s_s,
+        t_s,
+        delta,
+        exp_e,
+        mslope,
+        weighted,
+        weighted_p,
+        sgrad,
+        gmap,
+        xm,
+        edge,
+        mine,
+    )
     one = lax.ppermute(one, "fsdp", ROUTE_ONE)
     two = lax.ppermute(two, "fsdp", ROUTE_TWO)
     gp, blk, spill, params = call(
         third_kernel,
-        (shape(total, narrow), shape(8, 8, TILE), shape(8, narrow), shape(24, TILE)),
-        [vmem] * 16 + [smem] * 2,
+        (
+            shape(2, 2 * TILE + 8, narrow),
+            shape(8, 8, TILE),
+            shape(8, narrow),
+            shape(24, TILE),
+        ),
+        [vmem] * 19 + [smem],
         (vmem,) * 4,
         [],
         24,
@@ -1101,21 +1380,23 @@
         hlow,
         clow,
         endrow,
-        xp,
+        xs,
         dp,
-        act,
-        slope,
-        scaled,
-        step_e,
+        acts,
+        actm,
+        edge,
+        act_p,
         toend_e,
         exp_e,
         step_r,
         sig_r,
-        diag,
+        base,
+        coef,
         gsum,
+        stepsum,
+        skips,
         sig_taps,
         a_log,
-        skip_gain,
     )
     scale = 1.0 / math.sqrt(float(ctx * rows))
     cross = call(
@@ -1140,7 +1421,7 @@
     ys = [ys[0]] + [lax.ppermute(ys[k], "ctx", inside[k]) for k in (1, 2, 3)]
     ws = call(
         merge_kernel,
-        (shape(HALF + 48, narrow, kind=BF),) * 4,
+        (shape(HALF + 32, narrow, kind=BF),) * 4,
         [vmem] * 5,
         (vmem,) * 4,
         [],

time: 73.1 us -> 66.6 us (0.911)
  waiting for transfers between devices: 23.3 us -> 16.7 us
  blocking collectives: 5.46 us -> 0 us
  starting transfers between devices: 23 us -> 27.2 us
  Pallas kernels: 19.1 us -> 20.6 us
    ppermute x5, waiting for transfers between devices: 15 us -> 6.58 us  [the longest x1 5.26 us: shards_quad(): midf = lax.ppermute(midf, 'ctx', over)]
    all_gather x1 -> x0, blocking collectives: 5.46 us -> none  [shards_quad(): map_params = lax.all_gather(packed[8], 'fsdp', axis=0)]
    ppermute x3 -> x6, starting transfers between devices: 4.61 us -> 8.11 us  [shards_quad(): lax.ppermute(packed[k], 'ctx', inside[k])]
    ppermute x3 -> x6, waiting for transfers between devices: 0.6 us -> 3.75 us  [shards_quad(): lax.ppermute(packed[k], 'ctx', inside[k])]
    ppermute x3, waiting for transfers between devices: 4.06 us -> 2.63 us  [shards_quad(): ws = [ws[0]] + [lax.ppermute(ws[k], 'ctx', inside[k]) for k in (1, 2, 3)]]
    pallas_call x5 -> x9, Pallas kernels: 16.3 us -> 17.6 us  [the longest x1 4.69 us: shards_quad(): call(second_kernel, (shape(total, narrow), shape(total, narrow), shape(to...]
    ppermute x5, starting transfers between devices: 6.14 us -> 7.32 us  [the longest x1 2.96 us: shards_quad(): midf = lax.ppermute(midf, 'ctx', over)]
    ppermute x1, waiting for transfers between devices: 0.83 us -> 1.69 us  [shards_quad(): other = lax.ppermute(cross, 'ctx', over)]
  transfers between devices with their start and end apart: 17 -> 20, of which waited for: 8 -> 10; matrix products, arithmetic and copies ran while one was open for 0% -> 0% of each run, Pallas kernels for 13% -> 23%
where the time goes in v4:
time: 66.6 us; the launch traced here: 66.2 us
  starting transfers between devices  27.2 us (41%)
  Pallas kernels  20.6 us (31%)
  waiting for transfers between devices  16.7 us (25%)
  local copies, waits for them, and re-layouts  0.96 us (1%)
  between operations  0.8 us (1%)
    ppermute x6, starting transfers between devices, shards_quad(): lax.ppermute(packed[k], 'ctx', inside[k])  8.11 us
    ppermute x1, waiting for transfers between devices, shards_quad(): midf = lax.ppermute(midf, 'ctx', over)  5.26 us
    ppermute x3, starting transfers between devices, shards_quad(): ys = [ys[0]] + [lax.ppermute(ys[k], 'ctx', inside[k]) for k in (1, 2, 3)]  5.24 us
    pallas_call x1, Pallas kernels, shards_quad(): call(second_kernel, (shape(total, narrow), shape(total, narrow), shape(to...  4.69 us
    ppermute x6, waiting for transfers between devices, shards_quad(): lax.ppermute(packed[k], 'ctx', inside[k])  3.75 us
    ppermute x3, starting transfers between devices, shards_quad(): ws = [ws[0]] + [lax.ppermute(ws[k], 'ctx', inside[k]) for k in (1, 2, 3)]  3.53 us
    pallas_call x1, Pallas kernels, shards_quad(): call(third_kernel, (shape(2, 2 * TILE + 8, narrow), shape(8, 8, TILE), sh...  3.53 us
    pallas_call x1, Pallas kernels, shards_quad(): call(pack_kernel, (shape(TILE + HALF + 16, narrow, kind=BF),) * 4 + (shap...  3.03 us
  transfers between devices with their start and end apart: 20, of which 10 were waited for; matrix products, arithmetic and copies ran while one was open for 0% of the time, Pallas kernels for 23%

profile of v4, /device:TPU:0, one launch (start us, length us, event | category | flops | bytes accessed | tf_op | source)
XLA Modules:
  0.0 66.2 jit_solution(5230081763026393740)
XLA Ops:
  0.6 0.0 copy-start.6
  0.7 0.0 copy-start.4
  0.7 3.0 %shard_map.186 = (bf16[208,512]{1,0:T(8,128)(2,1)}, bf16[208,512]{1,0:T(8,128)(2,1)}, bf16[208,512]{1,0:T(8,128)(2,1)}, bf16[208,512]{1,0:T(8,128)(2,1)}, f32[8,512]{1,0:T(8,128)}) custom-call(bf16[128,2048]{1,0:T(8,128)(2,1)} %map_ref.1, f32[32,128]{1,0:T(8,128)} %bitcast.11, bf16[128,2048]{1,0:T(8,128)(2,1)} %dy_ref.1, f32[4,512]{1,0:T(4,128)} %mtaps_ref.1, ...), custom_call_target="tpu_custom_call" | custom-call | flops 1000000 | bytes 10000 | tf_op jit(solution)/shard_map/pallas_call | solution.py:1216
  3.7 3.0 %collective-permute-start = (bf16[208,512]{1,0:T(8,128)(2,1)}, bf16[208,512]{1,0:T(8,128)(2,1)S(1)}, u32[]{:S(2)}, u32[]{:S(2)}) collective-permute-start(bf16[208,512]{1,0:T(8,128)(2,1)} %get-tuple-element.81), channel_id=1, source_target_pairs={{0,4},{4,0},{8,12},{12,8},{16,20},{20,16},{24,28},{28,24},{1,5},{5... | collective-permute-start | bytes 638984 | tf_op jit(solution)/shard_map/ppermute | solution.py:1225
  6.7 1.6 %collective-permute-start.1 = (bf16[208,512]{1,0:T(8,128)(2,1)}, bf16[208,512]{1,0:T(8,128)(2,1)S(1)}, u32[]{:S(2)}, u32[]{:S(2)}) collective-permute-start(bf16[208,512]{1,0:T(8,128)(2,1)} %get-tuple-element.82), channel_id=1, source_target_pairs={{0,8},{4,12},{8,0},{12,4},{16,24},{20,28},{24,16},{28,20},{1,9},{5... | collective-permute-start | bytes 638984 | tf_op jit(solution)/shard_map/ppermute | solution.py:1225
  8.3 0.0 collective-permute-start.2
  8.3 0.0 collective-permute-start.4
  8.3 1.4 %collective-permute-start.3 = (f32[8,512]{1,0:T(8,128)}, f32[8,512]{1,0:T(8,128)S(1)}, u32[]{:S(2)}, u32[]{:S(2)}) collective-permute-start(f32[8,512]{1,0:T(8,128)} %get-tuple-element.84), channel_id=1, source_target_pairs={{0,0},{1,2},{2,1},{3,3},{4,4},{5,6},{6,5},{7,7},{8,8},{9,10},{10,9... | collective-permute-start | bytes 49160 | tf_op jit(solution)/shard_map/ppermute | solution.py:1226
  9.7 1.9 %shard_map.188 = (bf16[128,512]{1,0:T(8,128)(2,1)}, bf16[128,512]{1,0:T(8,128)(2,1)}, bf16[128,512]{1,0:T(8,128)(2,1)}, bf16[128,512]{1,0:T(8,128)(2,1)}) custom-call(bf16[128,2048]{1,0:T(8,128)(2,1)} %sig_ref.1), custom_call_target="tpu_custom_call" | custom-call | flops 1000000 | bytes 10000 | tf_op jit(solution)/shard_map/pallas_call | solution.py:1228
  11.6 0.6 collective-permute-done.4.two_taps
  12.3 1.9 %collective-permute-start.6 = (bf16[128,512]{1,0:T(8,128)(2,1)}, bf16[128,512]{1,0:T(8,128)(2,1)S(1)}, u32[]{:S(2)}, u32[]{:S(2)}) collective-permute-start(bf16[128,512]{1,0:T(8,128)(2,1)} %get-tuple-element.87), channel_id=1, source_target_pairs={{0,4},{4,0},{8,12},{12,8},{16,20},{20,16},{24,28},{28,24},{1,5},{5... | collective-permute-start | bytes 393224 | tf_op jit(solution)/shard_map/ppermute | solution.py:1237
  14.2 0.0 collective-permute-done.3.one_taps
  14.2 1.6 %collective-permute-start.7 = (bf16[128,512]{1,0:T(8,128)(2,1)}, bf16[128,512]{1,0:T(8,128)(2,1)S(1)}, u32[]{:S(2)}, u32[]{:S(2)}) collective-permute-start(bf16[128,512]{1,0:T(8,128)(2,1)} %get-tuple-element.88), channel_id=1, source_target_pairs={{0,8},{4,12},{8,0},{12,4},{16,24},{20,28},{24,16},{28,20},{1,9},{5... | collective-permute-start | bytes 393224 | tf_op jit(solution)/shard_map/ppermute | solution.py:1237
  15.8 0.0 collective-permute-done.u1
  15.8 0.0 collective-permute-start.8
  15.8 0.0 collective-permute-done.1.u2
  15.8 2.3 %collective-permute-done.2.u3 = bf16[208,512]{1,0:T(8,128)(2,1)S(1)} collective-permute-done((bf16[208,512]{1,0:T(8,128)(2,1)}, bf16[208,512]{1,0:T(8,128)(2,1)S(1)}, u32[]{:S(2)}, u32[]{:S(2)}) %collective-permute-start.2) | collective-permute-done | bytes 213024 | tf_op jit(solution)/shard_map/ppermute | solution.py:1225
  18.1 0.0 copy-done.6
  18.1 0.0 copy-done.4
  18.1 0.0 copy-start.3
  18.1 0.9 %copy-done.3 = bf16[208,512]{1,0:T(8,128)(2,1)S(1)} copy-done((bf16[208,512]{1,0:T(8,128)(2,1)S(1)}, bf16[208,512]{1,0:T(8,128)(2,1)}, u32[]{:S(2)}) %copy-start.3) | copy-done | bytes 213016
  19.1 0.0 copy-start
  19.1 2.8 %shard_map.187 = (bf16[128,512]{1,0:T(8,128)(2,1)S(1)}, bf16[512,512]{1,0:T(8,128)(2,1)S(1)}, f32[2,264,256]{2,1,0:T(8,128)S(1)}, bf16[512,256]{1,0:T(8,128)(2,1...) custom-call(bf16[208,512]{1,0:T(8,128)(2,1)S(1)} %copy-done.3, ...), custom_call_target="tpu_custom_call" | custom-call | flops 2000000000 | bytes 20000000 | tf_op jit(solution)/shard_map/pallas_call | solution.py:1238
  21.9 0.0 copy-start.1
  21.9 0.0 copy-start.2
  21.9 0.0 collective-permute-done.6.v1
  21.9 0.0 collective-permute-done.7.v2
  21.9 1.4 %collective-permute-done.8.v3 = bf16[128,512]{1,0:T(8,128)(2,1)S(1)} collective-permute-done((bf16[128,512]{1,0:T(8,128)(2,1)}, bf16[128,512]{1,0:T(8,128)(2,1)S(1)}, u32[]{:S(2)}, u32[]{:S(2)}) %collective-permute-start.8) | collective-permute-done | bytes 131104 | tf_op jit(solution)/shard_map/ppermute | solution.py:1237
  23.3 0.0 copy-done
  23.3 2.7 %collective-permute-start.9 = (bf16[16,768]{1,0:T(8,128)(2,1)S(1)}, bf16[16,768]{1,0:T(8,128)(2,1)S(1)}, u32[]{:S(2)}, u32[]{:S(2)}) collective-permute-start(bf16[16,768]{1,0:T(8,128)(2,1)S(1)} %shard_map.189), channel_id=1, source_target_pairs={{0,16},{4,20},{8,24},{12,28},{16,0},{20,4},{24,8},{28,12},{1,17},{... | collective-permute-start | bytes 73736 | tf_op jit(solution)/shard_map/ppermute | solution.py:1264
  26.0 0.3 collective-permute-start.5
  26.3 0.0 copy-done.1
  26.3 0.0 copy-done.2
  26.3 1.1 %shard_map.190 = (f32[2,264,512]{2,1,0:T(8,128)S(1)}, bf16[512,512]{1,0:T(8,128)(2,1)S(1)}, f32[512,512]{1,0:T(8,128)S(1)}, bf16[512,512]{1,0:T(8,128)(2,1)S(1)}, bf16[512,512]{1,0:T(8,128)(2,1)S(1)}) custom-call(bf16[128,512]{1,0:T(8,128)(2,1)S(1)} %copy-done, bf16[128,512]{1,0:T(8,128)(2,1)S(1)} %collective-permute-done.6.v1, ...), custom_call_target="tpu_custom_call" | custom-call | flops 2000000000 | bytes 20000000 | tf_op jit(solution)/shard_map/pallas_call | solution.py:1265
  27.4 0.7 %collective-permute-done.9.halo_ref = bf16[16,768]{1,0:T(8,128)(2,1)S(1)} collective-permute-done((bf16[16,768]{1,0:T(8,128)(2,1)S(1)}, bf16[16,768]{1,0:T(8,128)(2,1)S(1)}, u32[]{:S(2)}, u32[]{:S(2)}) %collective-permute-start.9) | collective-permute-done | bytes 24608 | tf_op jit(solution)/shard_map/ppermute | solution.py:1264
  28.1 0.4 shard_map.191
  28.5 3.0 %collective-permute-start.10 = (bf16[144,512]{1,0:T(8,128)(2,1)S(1)}, bf16[144,512]{1,0:T(8,128)(2,1)S(1)}, u32[]{:S(2)}, u32[]{:S(2)}) collective-permute-start(bf16[144,512]{1,0:T(8,128)(2,1)S(1)} %get-tuple-element.99), channel_id=1, source_target_pairs={{0,16},{4,20},{8,24},{12,28},{16,0},{20,4},{24,8},{28,12},{1,17},{... | collective-permute-start | bytes 442376 | tf_op jit(solution)/shard_map/ppermute | solution.py:1298
  31.5 0.0 copy-done.5
  31.5 4.7 %shard_map.192 = (f32[512,512]{1,0:T(8,128)S(1)}, f32[512,512]{1,0:T(8,128)S(1)}, f32[512,256]{1,0:T(8,128)S(1)}, f32[512,256]{1,0:T(8,128)S(1)}, f32[32,128]{1,...) custom-call(bf16[512,512]{1,0:T(8,128)(2,1)S(1)} %get-tuple-element.103.dp, ...), custom_call_target="tpu_custom_call" | custom-call | flops 5000000000 | bytes 50000000 | tf_op jit(solution)/shard_map/pallas_call | solution.py:1299
  36.2 0.0 collective-permute-done.5.midg_ref
  36.2 5.3 %collective-permute-done.10.midf_ref = bf16[144,512]{1,0:T(8,128)(2,1)S(1)} collective-permute-done((bf16[144,512]{1,0:T(8,128)(2,1)S(1)}, bf16[144,512]{1,0:T(8,128)(2,1)S(1)}, u32[]{:S(2)}, u32[]{:S(2)}) %collective-permute-start.10) | collective-permute-done | bytes 147488 | tf_op jit(solution)/shard_map/ppermute | solution.py:1298
  41.5 1.2 %shard_map.193 = (bf16[544,128]{1,0:T(8,128)(2,1)S(1)}, bf16[544,128]{1,0:T(8,128)(2,1)S(1)}, bf16[4,128,512]{2,1,0:T(8,128)(2,1)S(1)}, bf16[4,128,512]{2,1,0:T(8,128)(2,1)S(1)}, f32[8,512]{1,0:T(8,128)S(1)}) custom-call(bf16[128,512]{1,0:T(8,128)(2,1)S(1)} %collective-permute-done.5.midg_ref, bf16[144,512]{1,0:T(8,128)(2,1)S(1)} %collective-permute-done.10.midf_ref, ...), custom_call_target="tpu_custom_call" | custom-call | flops 2000000000 | bytes 20000000 | tf_op jit(solution)/shard_map/pallas_call | solution.py:1330
  42.7 0.8 %collective-permute-start.14 = (bf16[544,128]{1,0:T(8,128)(2,1)S(1)}, bf16[544,128]{1,0:T(8,128)(2,1)S(1)}, u32[]{:S(2)}, u32[]{:S(2)}) collective-permute-start(bf16[544,128]{1,0:T(8,128)(2,1)S(1)} %get-tuple-element.133), channel_id=1, source_target_pairs={{0,0},{2,1},{1,2},{3,3},{4,4},{6,5},{5,6},{7,7},{8,8},{10,9},{9,10... | collective-permute-start | bytes 417800 | tf_op jit(solution)/shard_map/ppermute | solution.py:1364
  43.5 2.1 %collective-permute-start.15 = (bf16[544,128]{1,0:T(8,128)(2,1)S(1)}, bf16[544,128]{1,0:T(8,128)(2,1)S(1)}, u32[]{:S(2)}, u32[]{:S(2)}) collective-permute-start(bf16[544,128]{1,0:T(8,128)(2,1)S(1)} %get-tuple-element.134), channel_id=1, source_target_pairs={{0,2},{2,3},{1,0},{3,1},{4,6},{6,7},{5,4},{7,5},{8,10},{10,11},{9,... | collective-permute-start | bytes 417800 | tf_op jit(solution)/shard_map/ppermute | solution.py:1365
  45.6 3.5 %shard_map.194 = (f32[2,264,512]{2,1,0:T(8,128)S(1)}, f32[8,8,128]{2,1,0:T(8,128)S(1)}, f32[8,512]{1,0:T(8,128)S(1)}, f32[24,128]{1,0:T(8,128)S(1)}) custom-call(bf16[4,128,512]{2,1,0:T(8,128)(2,1)S(1)} %get-tuple-element.116.hlow_ref, bf16[4,128,512]{2,1,0:T(8,128)(2,1)S(1)} %get-tuple-element.117.clow_ref, f32[8,512]{1,0:T(8,128)S(1)} %get-tuple-element.118.endrow_ref, ...), custom_call_target="tpu_custom_call" | custom-call | flops 3000000000 | bytes 30000000 | tf_op jit(solution)/shard_map/pallas_call | solution.py:1366
  49.2 0.6 shard_map.195
  49.7 1.8 %collective-permute-start.11 = (bf16[128,512]{1,0:T(8,128)(2,1)S(1)}, bf16[128,512]{1,0:T(8,128)(2,1)S(1)}, u32[]{:S(2)}, u32[]{:S(2)}) collective-permute-start(bf16[128,512]{1,0:T(8,128)(2,1)S(1)} %get-tuple-element.128), channel_id=1, source_target_pairs={{0,4},{4,0},{8,12},{12,8},{16,20},{20,16},{24,28},{28,24},{1,5},{5... | collective-permute-start | bytes 393224 | tf_op jit(solution)/shard_map/ppermute | solution.py:1421
  51.5 0.0 collective-permute-done.14.one_ref
  51.5 0.0 collective-permute-done.15.two_ref
  51.5 0.1 collective-permute-start.16
  51.6 3.5 %collective-permute-start.12 = (bf16[128,512]{1,0:T(8,128)(2,1)S(1)}, bf16[128,512]{1,0:T(8,128)(2,1)S(1)}, u32[]{:S(2)}, u32[]{:S(2)}) collective-permute-start(bf16[128,512]{1,0:T(8,128)(2,1)S(1)} %get-tuple-element.129), channel_id=1, source_target_pairs={{0,8},{4,12},{8,0},{12,4},{16,24},{20,28},{24,16},{28,20},{1,9},{5... | collective-permute-start | bytes 393224 | tf_op jit(solution)/shard_map/ppermute | solution.py:1421
  55.1 0.0 collective-permute-start.13
  55.1 1.7 %collective-permute-done.16.other_ref = bf16[32,512]{1,0:T(8,128)(2,1)S(1)} collective-permute-done((bf16[32,512]{1,0:T(8,128)(2,1)S(1)}, bf16[32,512]{1,0:T(8,128)(2,1)S(1)}, u32[]{:S(2)}, u32[]{:S(2)}) %collective-permute-start.16) | collective-permute-done | bytes 32800 | tf_op jit(solution)/shard_map/ppermute | solution.py:1411
  56.8 0.1 shard_map.197
  56.9 0.2 collective-permute-start.17
  57.1 1.7 %collective-permute-start.18 = (bf16[96,512]{1,0:T(8,128)(2,1)S(1)}, bf16[96,512]{1,0:T(8,128)(2,1)S(1)}, u32[]{:S(2)}, u32[]{:S(2)}) collective-permute-start(bf16[96,512]{1,0:T(8,128)(2,1)S(1)} %get-tuple-element.138), channel_id=1, source_target_pairs={{0,8},{4,12},{8,0},{12,4},{16,24},{20,28},{24,16},{28,20},{1,9},{5... | collective-permute-start | bytes 294920 | tf_op jit(solution)/shard_map/ppermute | solution.py:1431
  58.7 0.0 collective-permute-done.11.y1
  58.7 1.7 %collective-permute-start.19 = (bf16[96,512]{1,0:T(8,128)(2,1)S(1)}, bf16[96,512]{1,0:T(8,128)(2,1)S(1)}, u32[]{:S(2)}, u32[]{:S(2)}) collective-permute-start(bf16[96,512]{1,0:T(8,128)(2,1)S(1)} %get-tuple-element.139), channel_id=1, source_target_pairs={{0,12},{4,8},{8,4},{12,0},{16,28},{20,24},{24,20},{28,16},{1,13},{... | collective-permute-start | bytes 294920 | tf_op jit(solution)/shard_map/ppermute | solution.py:1431
  60.4 0.0 collective-permute-done.12.y2
  60.4 2.0 %collective-permute-done.13.y3 = bf16[128,512]{1,0:T(8,128)(2,1)S(1)} collective-permute-done((bf16[128,512]{1,0:T(8,128)(2,1)S(1)}, bf16[128,512]{1,0:T(8,128)(2,1)S(1)}, u32[]{:S(2)}, u32[]{:S(2)}) %collective-permute-start.13) | collective-permute-done | bytes 131104 | tf_op jit(solution)/shard_map/ppermute | solution.py:1421
  62.5 1.1 %collective-permute-done.17.w1 = bf16[96,512]{1,0:T(8,128)(2,1)S(1)} collective-permute-done((bf16[96,512]{1,0:T(8,128)(2,1)S(1)}, bf16[96,512]{1,0:T(8,128)(2,1)S(1)}, u32[]{:S(2)}, u32[]{:S(2)}) %collective-permute-start.17) | collective-permute-done | bytes 98336 | tf_op jit(solution)/shard_map/ppermute | solution.py:1431
  63.6 0.4 collective-permute-done.18.w2
  63.9 1.2 %collective-permute-done.19.w3 = bf16[96,512]{1,0:T(8,128)(2,1)S(1)} collective-permute-done((bf16[96,512]{1,0:T(8,128)(2,1)S(1)}, bf16[96,512]{1,0:T(8,128)(2,1)S(1)}, u32[]{:S(2)}, u32[]{:S(2)}) %collective-permute-start.19) | collective-permute-done | bytes 98336 | tf_op jit(solution)/shard_map/ppermute | solution.py:1431
  65.1 1.1 %shard_map.198 = (f32[128,2048]{1,0:T(8,128)}, f32[128,512]{1,0:T(8,128)}, f32[32,128]{1,0:T(8,128)}, f32[4,2048]{1,0:T(4,128)}, f32[4,512]{1,0:T(4,128)}, /*ind...) custom-call(bf16[128,512]{1,0:T(8,128)(2,1)S(1)} %get-tuple-element.127.y0, ...), custom_call_target="tpu_custom_call" | custom-call | flops 1000000 | bytes 10000 | tf_op jit(solution)/shard_map/pallas_call | solution.py:1432
  (3 shorter events, 0.0 us)
Async XLA Ops:
  0.6 17.5 %copy-start.6 = (f32[32]{0:T(128)S(1)}, f32[32]{0:T(128)}, u32[]{:S(2)}) copy-start(f32[32]{0:T(128)} %alog_ref.3) | copy-start | bytes 388
  0.7 17.5 %copy-start.4 = (f32[32]{0:T(128)S(1)}, f32[32]{0:T(128)}, u32[]{:S(2)}) copy-start(f32[32]{0:T(128)} %dtb_ref.1) | copy-start | bytes 388
  3.7 12.1 %collective-permute-start = (bf16[208,512]{1,0:T(8,128)(2,1)}, bf16[208,512]{1,0:T(8,128)(2,1)S(1)}, u32[]{:S(2)}, u32[]{:S(2)}) collective-permute-start(bf16[208,512]{1,0:T(8,128)(2,1)} %get-tuple-element.81), channel_id=1, source_target_pairs={{0,4},{4,0},{8,12},{12,8},{16,20},{20,16},{24,28},{28,24},{1,5},{5... | collective-permute-start | bytes 638984 | tf_op jit(solution)/shard_map/ppermute | solution.py:1225
  6.7 9.0 %collective-permute-start.1 = (bf16[208,512]{1,0:T(8,128)(2,1)}, bf16[208,512]{1,0:T(8,128)(2,1)S(1)}, u32[]{:S(2)}, u32[]{:S(2)}) collective-permute-start(bf16[208,512]{1,0:T(8,128)(2,1)} %get-tuple-element.82), channel_id=1, source_target_pairs={{0,8},{4,12},{8,0},{12,4},{16,24},{20,28},{24,16},{28,20},{1,9},{5... | collective-permute-start | bytes 638984 | tf_op jit(solution)/shard_map/ppermute | solution.py:1225
  8.3 9.8 %collective-permute-start.2 = (bf16[208,512]{1,0:T(8,128)(2,1)}, bf16[208,512]{1,0:T(8,128)(2,1)S(1)}, u32[]{:S(2)}, u32[]{:S(2)}) collective-permute-start(bf16[208,512]{1,0:T(8,128)(2,1)} %get-tuple-element.83), channel_id=1, source_target_pairs={{0,12},{4,8},{8,4},{12,0},{16,28},{20,24},{24,20},{28,16},{1,13},{... | collective-permute-start | bytes 638984 | tf_op jit(solution)/shard_map/ppermute | solution.py:1225
  8.3 3.9 %collective-permute-start.4 = (f32[8,512]{1,0:T(8,128)}, f32[8,512]{1,0:T(8,128)S(1)}, u32[]{:S(2)}, u32[]{:S(2)}) collective-permute-start(f32[8,512]{1,0:T(8,128)} %get-tuple-element.84), channel_id=1, source_target_pairs={{2,0},{3,2},{0,1},{1,3},{6,4},{7,6},{4,5},{5,7},{10,8},{11,10},{8,... | collective-permute-start | bytes 49160 | tf_op jit(solution)/shard_map/ppermute | solution.py:1227
  8.3 5.9 %collective-permute-start.3 = (f32[8,512]{1,0:T(8,128)}, f32[8,512]{1,0:T(8,128)S(1)}, u32[]{:S(2)}, u32[]{:S(2)}) collective-permute-start(f32[8,512]{1,0:T(8,128)} %get-tuple-element.84), channel_id=1, source_target_pairs={{0,0},{1,2},{2,1},{3,3},{4,4},{5,6},{6,5},{7,7},{8,8},{9,10},{10,9... | collective-permute-start | bytes 49160 | tf_op jit(solution)/shard_map/ppermute | solution.py:1226
  12.3 9.6 %collective-permute-start.6 = (bf16[128,512]{1,0:T(8,128)(2,1)}, bf16[128,512]{1,0:T(8,128)(2,1)S(1)}, u32[]{:S(2)}, u32[]{:S(2)}) collective-permute-start(bf16[128,512]{1,0:T(8,128)(2,1)} %get-tuple-element.87), channel_id=1, source_target_pairs={{0,4},{4,0},{8,12},{12,8},{16,20},{20,16},{24,28},{28,24},{1,5},{5... | collective-permute-start | bytes 393224 | tf_op jit(solution)/shard_map/ppermute | solution.py:1237
  14.2 7.7 %collective-permute-start.7 = (bf16[128,512]{1,0:T(8,128)(2,1)}, bf16[128,512]{1,0:T(8,128)(2,1)S(1)}, u32[]{:S(2)}, u32[]{:S(2)}) collective-permute-start(bf16[128,512]{1,0:T(8,128)(2,1)} %get-tuple-element.88), channel_id=1, source_target_pairs={{0,8},{4,12},{8,0},{12,4},{16,24},{20,28},{24,16},{28,20},{1,9},{5... | collective-permute-start | bytes 393224 | tf_op jit(solution)/shard_map/ppermute | solution.py:1237
  15.8 7.5 %collective-permute-start.8 = (bf16[128,512]{1,0:T(8,128)(2,1)}, bf16[128,512]{1,0:T(8,128)(2,1)S(1)}, u32[]{:S(2)}, u32[]{:S(2)}) collective-permute-start(bf16[128,512]{1,0:T(8,128)(2,1)} %get-tuple-element.89), channel_id=1, source_target_pairs={{0,12},{4,8},{8,4},{12,0},{16,28},{20,24},{24,20},{28,16},{1,13},{... | collective-permute-start | bytes 393224 | tf_op jit(solution)/shard_map/ppermute | solution.py:1237
  18.1 0.9 %copy-start.3 = (bf16[208,512]{1,0:T(8,128)(2,1)S(1)}, bf16[208,512]{1,0:T(8,128)(2,1)}, u32[]{:S(2)}) copy-start(bf16[208,512]{1,0:T(8,128)(2,1)} %get-tuple-element.80.u0) | copy-start | bytes 638980
  19.1 4.2 %copy-start = (bf16[128,512]{1,0:T(8,128)(2,1)S(1)}, bf16[128,512]{1,0:T(8,128)(2,1)}, u32[]{:S(2)}) copy-start(bf16[128,512]{1,0:T(8,128)(2,1)} %get-tuple-element.86.v0) | copy-start | bytes 393220
  21.9 4.5 %copy-start.1 = (f32[4,2048]{1,0:T(4,128)S(1)}, f32[4,2048]{1,0:T(4,128)}, u32[]{:S(2)}) copy-start(f32[4,2048]{1,0:T(4,128)} %taps_ref.7) | copy-start | bytes 98308
  21.9 4.5 %copy-start.2 = (f32[2048]{0:T(1024)S(1)}, f32[2048]{0:T(1024)}, u32[]{:S(2)}) copy-start(f32[2048]{0:T(1024)} %param.17) | copy-start | bytes 24580
  23.3 4.8 %collective-permute-start.9 = (bf16[16,768]{1,0:T(8,128)(2,1)S(1)}, bf16[16,768]{1,0:T(8,128)(2,1)S(1)}, u32[]{:S(2)}, u32[]{:S(2)}) collective-permute-start(bf16[16,768]{1,0:T(8,128)(2,1)S(1)} %shard_map.189), channel_id=1, source_target_pairs={{0,16},{4,20},{8,24},{12,28},{16,0},{20,4},{24,8},{28,12},{1,17},{... | collective-permute-start | bytes 73736 | tf_op jit(solution)/shard_map/ppermute | solution.py:1264
  26.0 10.2 %collective-permute-start.5 = (bf16[128,512]{1,0:T(8,128)(2,1)S(1)}, bf16[128,512]{1,0:T(8,128)(2,1)S(1)}, u32[]{:S(2)}, u32[]{:S(2)}) collective-permute-start(bf16[128,512]{1,0:T(8,128)(2,1)S(1)} %get-tuple-element.85), channel_id=1, source_target_pairs={{0,16},{4,20},{8,24},{12,28},{16,0},{20,4},{24,8},{28,12},{1,17},{... | collective-permute-start | bytes 393224 | tf_op jit(solution)/shard_map/ppermute | solution.py:1262
  28.1 3.4 %copy-start.5 = (f32[32]{0:T(128)S(1)}, f32[32]{0:T(128)}, u32[]{:S(2)}) copy-start(f32[32]{0:T(128)} %skip_ref.1) | copy-start | bytes 388
  28.5 12.9 %collective-permute-start.10 = (bf16[144,512]{1,0:T(8,128)(2,1)S(1)}, bf16[144,512]{1,0:T(8,128)(2,1)S(1)}, u32[]{:S(2)}, u32[]{:S(2)}) collective-permute-start(bf16[144,512]{1,0:T(8,128)(2,1)S(1)} %get-tuple-element.99), channel_id=1, source_target_pairs={{0,16},{4,20},{8,24},{12,28},{16,0},{20,4},{24,8},{28,12},{1,17},{... | collective-permute-start | bytes 442376 | tf_op jit(solution)/shard_map/ppermute | solution.py:1298
  42.7 8.8 %collective-permute-start.14 = (bf16[544,128]{1,0:T(8,128)(2,1)S(1)}, bf16[544,128]{1,0:T(8,128)(2,1)S(1)}, u32[]{:S(2)}, u32[]{:S(2)}) collective-permute-start(bf16[544,128]{1,0:T(8,128)(2,1)S(1)} %get-tuple-element.133), channel_id=1, source_target_pairs={{0,0},{2,1},{1,2},{3,3},{4,4},{6,5},{5,6},{7,7},{8,8},{10,9},{9,10... | collective-permute-start | bytes 417800 | tf_op jit(solution)/shard_map/ppermute | solution.py:1364
  43.5 8.0 %collective-permute-start.15 = (bf16[544,128]{1,0:T(8,128)(2,1)S(1)}, bf16[544,128]{1,0:T(8,128)(2,1)S(1)}, u32[]{:S(2)}, u32[]{:S(2)}) collective-permute-start(bf16[544,128]{1,0:T(8,128)(2,1)S(1)} %get-tuple-element.134), channel_id=1, source_target_pairs={{0,2},{2,3},{1,0},{3,1},{4,6},{6,7},{5,4},{7,5},{8,10},{10,11},{9,... | collective-permute-start | bytes 417800 | tf_op jit(solution)/shard_map/ppermute | solution.py:1365
  49.7 9.0 %collective-permute-start.11 = (bf16[128,512]{1,0:T(8,128)(2,1)S(1)}, bf16[128,512]{1,0:T(8,128)(2,1)S(1)}, u32[]{:S(2)}, u32[]{:S(2)}) collective-permute-start(bf16[128,512]{1,0:T(8,128)(2,1)S(1)} %get-tuple-element.128), channel_id=1, source_target_pairs={{0,4},{4,0},{8,12},{12,8},{16,20},{20,16},{24,28},{28,24},{1,5},{5... | collective-permute-start | bytes 393224 | tf_op jit(solution)/shard_map/ppermute | solution.py:1421
  51.5 5.2 %collective-permute-start.16 = (bf16[32,512]{1,0:T(8,128)(2,1)S(1)}, bf16[32,512]{1,0:T(8,128)(2,1)S(1)}, u32[]{:S(2)}, u32[]{:S(2)}) collective-permute-start(bf16[32,512]{1,0:T(8,128)(2,1)S(1)} %shard_map.196.own_ref), channel_id=1, source_target_pairs={{0,16},{4,20},{8,24},{12,28},{16,0},{20,4},{24,8},{28,12},{1,17},{... | collective-permute-start | bytes 98312 | tf_op jit(solution)/shard_map/ppermute | solution.py:1411
  51.6 8.8 %collective-permute-start.12 = (bf16[128,512]{1,0:T(8,128)(2,1)S(1)}, bf16[128,512]{1,0:T(8,128)(2,1)S(1)}, u32[]{:S(2)}, u32[]{:S(2)}) collective-permute-start(bf16[128,512]{1,0:T(8,128)(2,1)S(1)} %get-tuple-element.129), channel_id=1, source_target_pairs={{0,8},{4,12},{8,0},{12,4},{16,24},{20,28},{24,16},{28,20},{1,9},{5... | collective-permute-start | bytes 393224 | tf_op jit(solution)/shard_map/ppermute | solution.py:1421
  55.1 7.4 %collective-permute-start.13 = (bf16[128,512]{1,0:T(8,128)(2,1)S(1)}, bf16[128,512]{1,0:T(8,128)(2,1)S(1)}, u32[]{:S(2)}, u32[]{:S(2)}) collective-permute-start(bf16[128,512]{1,0:T(8,128)(2,1)S(1)} %get-tuple-element.130), channel_id=1, source_target_pairs={{0,12},{4,8},{8,4},{12,0},{16,28},{20,24},{24,20},{28,16},{1,13},{... | collective-permute-start | bytes 393224 | tf_op jit(solution)/shard_map/ppermute | solution.py:1421
  56.9 6.7 %collective-permute-start.17 = (bf16[96,512]{1,0:T(8,128)(2,1)S(1)}, bf16[96,512]{1,0:T(8,128)(2,1)S(1)}, u32[]{:S(2)}, u32[]{:S(2)}) collective-permute-start(bf16[96,512]{1,0:T(8,128)(2,1)S(1)} %get-tuple-element.137), channel_id=1, source_target_pairs={{0,4},{4,0},{8,12},{12,8},{16,20},{20,16},{24,28},{28,24},{1,5},{5... | collective-permute-start | bytes 294920 | tf_op jit(solution)/shard_map/ppermute | solution.py:1431
  57.1 6.8 %collective-permute-start.18 = (bf16[96,512]{1,0:T(8,128)(2,1)S(1)}, bf16[96,512]{1,0:T(8,128)(2,1)S(1)}, u32[]{:S(2)}, u32[]{:S(2)}) collective-permute-start(bf16[96,512]{1,0:T(8,128)(2,1)S(1)} %get-tuple-element.138), channel_id=1, source_target_pairs={{0,8},{4,12},{8,0},{12,4},{16,24},{20,28},{24,16},{28,20},{1,9},{5... | collective-permute-start | bytes 294920 | tf_op jit(solution)/shard_map/ppermute | solution.py:1431
  58.7 6.3 %collective-permute-start.19 = (bf16[96,512]{1,0:T(8,128)(2,1)S(1)}, bf16[96,512]{1,0:T(8,128)(2,1)S(1)}, u32[]{:S(2)}, u32[]{:S(2)}) collective-permute-start(bf16[96,512]{1,0:T(8,128)(2,1)S(1)} %get-tuple-element.139), channel_id=1, source_target_pairs={{0,12},{4,8},{8,4},{12,0},{16,28},{20,24},{24,20},{28,16},{1,13},{... | collective-permute-start | bytes 294920 | tf_op jit(solution)/shard_map/ppermute | solution.py:1431

commit v5 on v4

--- a/solution.py
+++ b/solution.py
@@ -374,12 +374,15 @@
     return pl.ds(pl.multiple_of(start, TILE), width)
 
 
-def pack_kernel(map_ref, dt_ref, dy_ref, mtaps_ref, mbias_ref, *rest):
-    u_refs, tap_ref, (dt_in, sems) = rest[:4], rest[4], rest[5:]
+def pack_kernel(sig_ref, map_ref, dt_ref, dy_ref, mtaps_ref, mbias_ref, *rest):
+    u_refs, tap_ref, (dt_in, sig_in, sems) = rest[:4], rest[4], rest[5:]
     quad, r, f = place()
     copies = []
     dt_copy = pltpu.make_async_copy(dt_ref, dt_in, sems.at[20])
     dt_copy.start()
+    ends = pl.ds(pl.multiple_of(jnp.where(quad == 0, HALF - 16, TILE - 16), 16), 16)
+    sig_copy = pltpu.make_async_copy(sig_ref.at[ends, :], sig_in, sems.at[21])
+    sig_copy.start()
 
     def send(source, target):
         copy = pltpu.make_async_copy(source, target, sems.at[len(copies)])
@@ -402,15 +405,16 @@
     tap_ref[4:5, :] = mbias_ref[...]
     tap_ref[5:8, :] = jnp.zeros_like(tap_ref[5:8, :])
     dt_copy.wait()
-    zero = jnp.zeros((8, TILE), F32)
+    sig_copy.wait()
     for k in range(4):
         dest = lax.bitwise_xor(r, k)
         hi, mid, lo = split3(dt_in[pl.ds(pl.multiple_of(8 * dest, 8), 8), :])
-        top = jnp.concatenate([hi.astype(F32), mid.astype(F32)], axis=0)
-        low = jnp.concatenate([lo.astype(F32), zero], axis=0)
-        u_refs[k][TILE + HALF : TILE + HALF + 16, :] = jnp.concatenate(
-            [top, low, jnp.zeros((16, 2 * TILE), F32)], axis=1
-        ).astype(BF)
+        edge = sig_in[:, at_tile(dest * 4 * TILE, 4 * TILE)].astype(F32)[8:16]
+        top = jnp.concatenate([hi.astype(F32), lo.astype(F32), edge[:, 0 : 2 * TILE]], axis=1)
+        low = jnp.concatenate(
+            [mid.astype(F32), edge[:, 2 * TILE : 4 * TILE], jnp.zeros((8, TILE), F32)], axis=1
+        )
+        u_refs[k][TILE + HALF : TILE + HALF + 16, :] = jnp.concatenate([top, low], axis=0).astype(BF)
     for copy in copies:
         copy.wait()
 
@@ -430,6 +434,11 @@
         copy.wait()
 
 
+def own_kernel(u_ref, v_ref, u_out, v_out):
+    u_out[...] = u_ref[...]
+    v_out[...] = v_ref[...]
+
+
 def sig_tap_rows(j, taps_ref, bias_ref):
     at = at_tile((4 * place()[1] + j) * TILE)
     return [taps_ref[k : k + 1, at] for k in range(4)], bias_ref[0:1, at]
@@ -486,9 +495,9 @@
 
 def grads_kernel(
     u0,
+    u3,
+    u2,
     u1,
-    u2,
-    u3,
     one_taps,
     two_taps,
     alog_ref,
@@ -507,11 +516,11 @@
     ds_r,
     sig_r,
     mine_ref,
+    halo_ref,
     dt_src,
 ):
     quad, r, f = place()
     high = quad == 1
-    half_lane = ids((TILE, TILE), 1) < HALF
     lane8 = ids((8, TILE), 1)
     group = 2 * f + lax.div(r, 2)
     at = at_tile(lax.rem(group, 4) * TILE)
@@ -519,6 +528,7 @@
         mine_ref[8 * j : 8 * j + 8, :] = jnp.where(
             lax.rem(f, 2) == j, one_taps[:, at], two_taps[:, at]
         )
+    edge = jnp.zeros((8, 4 * TILE), F32)
     for k, u in enumerate((u0, u1, u2, u3)):
         s = lax.bitwise_xor(r, k)
         for e, start in ((0, HALF * s), (1, HALF * (3 - s))):
@@ -529,8 +539,15 @@
             dp[pl.ds(pl.multiple_of(2 * TILE * e + start, HALF), HALF), :] = u[
                 e * HALF : (e + 1) * HALF, :
             ]
-        packed = u[TILE + HALF : TILE + HALF + 16, 0 : 2 * TILE].astype(F32)
+        packed = u[TILE + HALF : TILE + HALF + 16, :].astype(F32)
         dt_src[s] = packed[0:8, 0:TILE] + packed[8:16, 0:TILE] + packed[0:8, TILE : 2 * TILE]
+        last = jnp.concatenate(
+            [packed[0:8, 2 * TILE : 4 * TILE], packed[8:16, TILE : 3 * TILE]], axis=1
+        )
+        edge = edge + jnp.where(s == jnp.where(high, 0, 3), last, 0.0)
+    last = slice(2 * TILE, 2 * TILE + 8)
+    edge = jnp.concatenate([edge, jnp.where(high, xm[1, last, :], xm[0, last, :])], axis=1)
+    halo_ref[...] = jnp.concatenate([jnp.zeros_like(edge), edge], axis=0).astype(BF)
     xm[0, 0:8, :] = jnp.zeros((8, 2 * TILE), F32)
     xm[1, 0:8, :] = jnp.where(high, xm[0, 2 * TILE : 2 * TILE + 8, :], 0.0)
 
@@ -551,6 +568,8 @@
     upto = (ids((TILE, TILE), 0) <= ids((TILE, TILE), 1)).astype(F32)
     ds_r[...] = mm_f32(ds_r[...], upto)
 
+    row48 = jnp.bitwise_and(ids((48, 8 * TILE), 0), 15)
+    expand = (row48 == ids((48, 8 * TILE), 1) // HALF).astype(BF)
     ends = []
     for i in range(4):
         rows = slice(i * TILE, (i + 1) * TILE)
@@ -561,14 +580,15 @@
             pre = conv(xm[i // 2, base : base + TILE + 8, lanes], taps, bias)
             actm[rows, lanes] = (pre * sigmoid(pre)).astype(BF)
             prem[rows, lanes] = pre
-        cols = columns(step_r[8 * i : 8 * i + 8, :], ds_r[8 * i : 8 * i + 8, :])
+        parts = split3(
+            jnp.concatenate([step_r[8 * i : 8 * i + 8, :], ds_r[8 * i : 8 * i + 8, :]], axis=0)
+        )
+        spread = mm(jnp.concatenate(parts, axis=0), expand, TN)
         end, masked = [], []
         for j in range(4):
             lanes = lanes_of(j)
-            step = jnp.where(half_lane, cols[:, 2 * j : 2 * j + 1], cols[:, 2 * j + 1 : 2 * j + 2])
-            ds = jnp.where(
-                half_lane, cols[:, 8 + 2 * j : 9 + 2 * j], cols[:, 9 + 2 * j : 10 + 2 * j]
-            )
+            step = spread[:, lanes]
+            ds = spread[:, lanes_of(4 + j)]
             last = ds[TILE - 1 : TILE, :]
             grow = jnp.exp(ds)
             step_e[rows, lanes] = step
@@ -589,21 +609,8 @@
     mid_ref[...] = jnp.where(high, g_a + ends[0] * ends[1] * g_b, g_b).astype(BF)
 
 
-def edge_kernel(v0, v1, v2, v3, xm, out_ref):
-    quad, r, f = place()
-    high = quad == 1
-    wanted = lax.bitwise_xor(r, jnp.where(high, 0, 3))
-    found = jnp.zeros((16, 4 * TILE), F32)
-    for k, v in enumerate((v0, v1, v2, v3)):
-        rows = jnp.where(high, v[TILE - 16 : TILE, :], v[HALF - 16 : HALF, :]).astype(F32)
-        found = found + jnp.where(wanted == k, rows, 0.0)
-    out_ref[:, 0 : 4 * TILE] = found.astype(BF)
-    last = slice(8 + 2 * TILE - 16, 8 + 2 * TILE)
-    out_ref[:, 4 * TILE : 6 * TILE] = jnp.where(high, xm[1, last, :], xm[0, last, :]).astype(BF)
-
-
 def first_kernel(
-    v0, v1, v2, v3, step_e, toend_e, taps_ref, bias_ref, xs, acts, pres, scaled_s, weighted_s
+    v0, v3, v2, v1, step_e, toend_e, taps_ref, bias_ref, xs, acts, pres, scaled_s, weighted_s
 ):
     quad, r, f = place()
     high = quad == 1
@@ -715,6 +722,14 @@
         lo = (x - hi.astype(F32)).astype(BF)
         found.append(mm(pick, hi, NT) + mm(pick, lo, NT))
     return found
+
+
+def pair_sums(x, two):
+    head = ids((8, 2 * TILE), 1) // HALF + 4 * two
+    pick = (ids((8, 2 * TILE), 0) == head).astype(BF)
+    hi = x.astype(BF)
+    lo = (x - hi.astype(F32)).astype(BF)
+    return mm(pick, hi, NT) + mm(pick, lo, NT)
 
 
 def skip_rows(skip_ref, r):
@@ -988,17 +1003,29 @@
         end_row = endrow_ref[i : i + 1, :]
         gsum = gsum_ref[at8, :]
         end_sum = jnp.zeros((8, TILE), F32)
-        offs, backs = [], []
-        for j in range(4):
-            lanes = lanes_of(j)
-            sigf = patched(acts, lanes, act_p, lanes, i, high).astype(F32)
-            offs.append(dp[rows, lanes].astype(F32) * exp_e[rows, lanes] * off[:, lanes])
-            backs.append(gw[:, lanes] * toend_e[rows, lanes] * sigf)
-            end_sum = end_sum + jnp.where(row8 == 2 * j + lane8 // HALF, end_row[:, lanes], 0.0)
-            here = base_ref[rows, lanes] + gw[:, lanes] * coef_ref[rows, lanes]
-            gp[i // 2, base : base + TILE, lanes] = here
-            tap_sums(here, xs, edge_ref, i, lanes, lanes, high, sums[j])
-        offsum, backsum = head_sums(offs, backs)
+        offsum = jnp.zeros((8, TILE), F32)
+        backsum = jnp.zeros((8, TILE), F32)
+        for two in range(2):
+            lanes2 = slice(2 * two * TILE, (2 * two + 2) * TILE)
+            sigf = jnp.concatenate(
+                [
+                    patched(acts, lanes_of(j), act_p, lanes_of(j), i, high).astype(F32)
+                    for j in (2 * two, 2 * two + 1)
+                ],
+                axis=1,
+            )
+            offsum = offsum + pair_sums(
+                dp[rows, lanes2].astype(F32) * exp_e[rows, lanes2] * off[:, lanes2], two
+            )
+            backsum = backsum + pair_sums(gw[:, lanes2] * toend_e[rows, lanes2] * sigf, two)
+            for j in (2 * two, 2 * two + 1):
+                lanes = lanes_of(j)
+                end_sum = end_sum + jnp.where(
+                    row8 == 2 * j + lane8 // HALF, end_row[:, lanes], 0.0
+                )
+                here = base_ref[rows, lanes] + gw[:, lanes] * coef_ref[rows, lanes]
+                gp[i // 2, base : base + TILE, lanes] = here
+                tap_sums(here, xs, edge_ref, i, lanes, lanes, high, sums[j])
         gsum = gsum + offsum
         stepsum = stepsum_ref[at8, :] + backsum
         back = backsum * step_r[at8, :]
@@ -1112,7 +1139,7 @@
 
 
 def last_kernel(
-    y0, y1, y2, y3, w0, w1, w2, w3, dsig_ref, dmap_ref, ddt_ref, taps_ref, mtaps_ref, bias_ref, mbias_ref, *trio_refs
+    y0, y3, y2, y1, w0, w3, w2, w1, dsig_ref, dmap_ref, ddt_ref, taps_ref, mtaps_ref, bias_ref, mbias_ref, *trio_refs
 ):
     quad, r, f = place()
     ys = (y0, y1, y2, y3)
@@ -1216,12 +1243,16 @@
     *packed, map_params = call(
         pack_kernel,
         (shape(TILE + HALF + 16, narrow, kind=BF),) * 4 + (shape(8, owned),),
-        [hbm, hbm, hbm, vmem, vmem],
+        [hbm, hbm, hbm, hbm, vmem, vmem],
         (vmem,) * 5,
-        [pltpu.VMEM((32, TILE), F32), pltpu.SemaphoreType.DMA((21,))],
+        [
+            pltpu.VMEM((32, TILE), F32),
+            pltpu.VMEM((16, sig_width), BF),
+            pltpu.SemaphoreType.DMA((22,)),
+        ],
         60,
         10**6,
-    )(map_raw, step_size_logits.T, d_out, map_taps, map_bias[None, :])
+    )(sig_raw, map_raw, step_size_logits.T, d_out, map_taps, map_bias[None, :])
     us = [packed[0]] + [lax.ppermute(packed[k], "ctx", inside[k]) for k in (1, 2, 3)]
     map_one = lax.ppermute(map_params, "fsdp", back(ROUTE_ONE))
     map_two = lax.ppermute(map_params, "fsdp", back(ROUTE_TWO))
@@ -1234,8 +1265,18 @@
         60,
         10**6,
     )(sig_raw)
-    vs = [packed[0]] + [lax.ppermute(packed[k], "ctx", inside[k]) for k in (1, 2, 3)]
-    midg, dp, xm, actm, prem, sgrad, step_e, toend_e, exp_e, t_s, step_r, ds_r, sig_r, mine = call(
+    own_u, own_v = call(
+        own_kernel,
+        (shape(TILE + HALF + 16, narrow, kind=BF), shape(TILE, narrow, kind=BF)),
+        [vmem] * 2,
+        (vmem,) * 2,
+        [],
+        16,
+        10**6,
+    )(us[0], packed[0])
+    us[0] = own_u
+    vs = [own_v] + [lax.ppermute(packed[k], "ctx", inside[k]) for k in (1, 2, 3)]
+    midg, dp, xm, actm, prem, sgrad, step_e, toend_e, exp_e, t_s, step_r, ds_r, sig_r, *small = call(
         grads_kernel,
         (
             shape(TILE, narrow, kind=BF),
@@ -1252,16 +1293,17 @@
             shape(32, TILE),
             shape(32, TILE),
             shape(16, TILE),
+            shape(16, wide, kind=BF),
         ),
         [vmem] * 6 + [smem] * 2,
-        (vmem,) * 14,
+        (vmem,) * 15,
         [pltpu.VMEM((4, 8, TILE), F32)],
         24,
         2 * 10**9,
-    )(*us, map_one, map_two, a_log, dt_bias)
+    )(us[0], us[3], us[2], us[1], map_one, map_two, a_log, dt_bias)
+    mine, halo = small
+    halo = lax.ppermute(halo, "ctx", over)
     midg = lax.ppermute(midg, "ctx", over)
-    halo = call(edge_kernel, shape(16, wide, kind=BF), [vmem] * 5, vmem, [], 16, 10**6)(*vs, xm)
-    halo = lax.ppermute(halo, "ctx", over)
     xs, acts, pres, scaled, weighted = call(
         first_kernel,
         (
@@ -1276,7 +1318,7 @@
         [],
         24,
         2 * 10**9,
-    )(*vs, step_e, toend_e, sig_taps, sig_bias_row)
+    )(vs[0], vs[3], vs[2], vs[1], step_e, toend_e, sig_taps, sig_bias_row)
     midf, s_s, delta, edge, act_p, pre_p, scaled_p, weighted_p = call(
         states_kernel,
         (
@@ -1446,7 +1488,7 @@
         [],
         16,
         10**6,
-    )(*ys, *ws)
+    )(ys[0], ys[3], ys[2], ys[1], ws[0], ws[3], ws[2], ws[1])
     return (
         d_sig,
         d_map,

time: 66.6 us -> 62.9 us (0.944)
  waiting for transfers between devices: 16.7 us -> 13.5 us
  Pallas kernels: 20.6 us -> 19.7 us
  local copies, waits for them, and re-layouts: 0.96 us -> 1.86 us
    ppermute x3, starting transfers between devices: 5.24 us -> 0.87 us  [shards_quad(): ys = [ys[0]] + [lax.ppermute(ys[k], 'ctx', inside[k]) for k in (1, 2, 3)]]
    ppermute x1, starting transfers between devices: 0.07 us -> 3.25 us  [shards_quad(): other = lax.ppermute(cross, 'ctx', over)]
    ppermute x6, waiting for transfers between devices: 3.75 us -> 1.65 us  [shards_quad(): lax.ppermute(packed[k], 'ctx', inside[k])]
    ppermute x3, waiting for transfers between devices: 2.03 us -> 0.93 us  [shards_quad(): ys = [ys[0]] + [lax.ppermute(ys[k], 'ctx', inside[k]) for k in (1, 2, 3)]]
    ppermute x1, waiting for transfers between devices: 5.26 us -> 6.24 us  [shards_quad(): midf = lax.ppermute(midf, 'ctx', over)]
    ppermute x1, starting transfers between devices: 2.08 us -> 3 us  [shards_quad(): two = lax.ppermute(two, 'fsdp', ROUTE_TWO)]
    unnamed x14, local copies, waits for them, and re-layouts: 0.96 us -> 1.86 us
    ppermute x1, waiting for transfers between devices: 0.7 us -> 0.01 us  [shards_quad(): halo = lax.ppermute(halo, 'ctx', over)]
  transfers between devices with their start and end apart: 20 -> 20, of which waited for: 10 -> 9; matrix products, arithmetic and copies ran while one was open for 0% -> 0% of each run, Pallas kernels for 23% -> 23%
where the time goes in v5:
time: 62.9 us; the launch traced here: 62.6 us
  starting transfers between devices  26.7 us (42%)
  Pallas kernels  19.7 us (31%)
  waiting for transfers between devices  13.5 us (21%)
  local copies, waits for them, and re-layouts  1.86 us (3%)
  between operations  0.81 us (1%)
    ppermute x6, starting transfers between devices, shards_quad(): lax.ppermute(packed[k], 'ctx', inside[k])  8.25 us
    ppermute x1, waiting for transfers between devices, shards_quad(): midf = lax.ppermute(midf, 'ctx', over)  6.24 us
    pallas_call x1, Pallas kernels, shards_quad(): call(second_kernel, (shape(total, narrow), shape(total, narrow), shape(to...  4.65 us
    ppermute x3, starting transfers between devices, shards_quad(): ws = [ws[0]] + [lax.ppermute(ws[k], 'ctx', inside[k]) for k in (1, 2, 3)]  3.6 us
    ppermute x1, starting transfers between devices, shards_quad(): other = lax.ppermute(cross, 'ctx', over)  3.25 us
    ppermute x3, waiting for transfers between devices, shards_quad(): ws = [ws[0]] + [lax.ppermute(ws[k], 'ctx', inside[k]) for k in (1, 2, 3)]  3.25 us
    pallas_call x1, Pallas kernels, shards_quad(): call(third_kernel, (shape(2, 2 * TILE + 8, narrow), shape(8, 8, TILE), sh...  3.21 us
    pallas_call x1, Pallas kernels, shards_quad(): call(pack_kernel, (shape(TILE + HALF + 16, narrow, kind=BF),) * 4 + (shap...  3.06 us
  transfers between devices with their start and end apart: 20, of which 9 were waited for; matrix products, arithmetic and copies ran while one was open for 0% of the time, Pallas kernels for 23%

profile of v5, /device:TPU:0, one launch (start us, length us, event | category | flops | bytes accessed | tf_op | source)
XLA Modules:
  0.0 62.6 jit_solution(15867065381942831300)
XLA Ops:
  0.6 0.0 copy-start.4
  0.7 0.0 copy-start.6
  0.7 3.1 %shard_map.186 = (bf16[208,512]{1,0:T(8,128)(2,1)}, bf16[208,512]{1,0:T(8,128)(2,1)}, bf16[208,512]{1,0:T(8,128)(2,1)}, bf16[208,512]{1,0:T(8,128)(2,1)}, f32[8,512]{1,0:T(8,128)}) custom-call(bf16[128,2048]{1,0:T(8,128)(2,1)} %sig_ref.3, bf16[128,2048]{1,0:T(8,128)(2,1)} %map_ref.1, f32[32,128]{1,0:T(8,128)} %bitcast.11, bf16[128,2048]{1,0:T(8,128)(2,1)} %dy_ref.1, ...), custom_call_target="tpu_custom_call" | custom-call | flops 1000000 | bytes 10000 | tf_op jit(solution)/shard_map/pallas_call | solution.py:1243
  3.7 4.0 %collective-permute-start = (bf16[208,512]{1,0:T(8,128)(2,1)}, bf16[208,512]{1,0:T(8,128)(2,1)S(1)}, u32[]{:S(2)}, u32[]{:S(2)}) collective-permute-start(bf16[208,512]{1,0:T(8,128)(2,1)} %get-tuple-element.86), channel_id=1, source_target_pairs={{0,12},{4,8},{8,4},{12,0},{16,28},{20,24},{24,20},{28,16},{1,13},{... | collective-permute-start | bytes 638984 | tf_op jit(solution)/shard_map/ppermute | solution.py:1256
  7.8 0.4 collective-permute-start.1
  8.2 0.2 collective-permute-start.2
  8.4 0.0 collective-permute-start.4
  8.4 1.4 %collective-permute-start.3 = (f32[8,512]{1,0:T(8,128)}, f32[8,512]{1,0:T(8,128)S(1)}, u32[]{:S(2)}, u32[]{:S(2)}) collective-permute-start(f32[8,512]{1,0:T(8,128)} %get-tuple-element.89), channel_id=1, source_target_pairs={{0,0},{1,2},{2,1},{3,3},{4,4},{5,6},{6,5},{7,7},{8,8},{9,10},{10,9... | collective-permute-start | bytes 49160 | tf_op jit(solution)/shard_map/ppermute | solution.py:1257
  9.8 1.9 %shard_map.187 = (bf16[128,512]{1,0:T(8,128)(2,1)}, bf16[128,512]{1,0:T(8,128)(2,1)}, bf16[128,512]{1,0:T(8,128)(2,1)}, bf16[128,512]{1,0:T(8,128)(2,1)}) custom-call(bf16[128,2048]{1,0:T(8,128)(2,1)} %sig_ref.3), custom_call_target="tpu_custom_call" | custom-call | flops 1000000 | bytes 10000 | tf_op jit(solution)/shard_map/pallas_call | solution.py:1259
  11.7 0.0 copy-start
  11.8 0.9 %copy-done = bf16[208,512]{1,0:T(8,128)(2,1)S(1)} copy-done((bf16[208,512]{1,0:T(8,128)(2,1)S(1)}, bf16[208,512]{1,0:T(8,128)(2,1)}, u32[]{:S(2)}) %copy-start) | copy-done | bytes 213016
  12.7 0.9 %copy-done.1 = bf16[128,512]{1,0:T(8,128)(2,1)S(1)} copy-done((bf16[128,512]{1,0:T(8,128)(2,1)S(1)}, bf16[128,512]{1,0:T(8,128)(2,1)}, u32[]{:S(2)}) %copy-start.1) | copy-done | bytes 131096
  13.6 0.0 collective-permute-done.4.two_taps
  13.6 2.9 %collective-permute-start.7 = (bf16[128,512]{1,0:T(8,128)(2,1)}, bf16[128,512]{1,0:T(8,128)(2,1)S(1)}, u32[]{:S(2)}, u32[]{:S(2)}) collective-permute-start(bf16[128,512]{1,0:T(8,128)(2,1)} %get-tuple-element.93), channel_id=1, source_target_pairs={{0,12},{4,8},{8,4},{12,0},{16,28},{20,24},{24,20},{28,16},{1,13},{... | collective-permute-start | bytes 393224 | tf_op jit(solution)/shard_map/ppermute | solution.py:1278
  16.5 0.0 collective-permute-done.3.one_taps
  16.5 0.5 collective-permute-start.8
  17.0 0.0 collective-permute-done.u3
  17.0 0.2 collective-permute-start.9
  17.2 0.8 %collective-permute-done.1.u2 = bf16[208,512]{1,0:T(8,128)(2,1)S(1)} collective-permute-done((bf16[208,512]{1,0:T(8,128)(2,1)}, bf16[208,512]{1,0:T(8,128)(2,1)S(1)}, u32[]{:S(2)}, u32[]{:S(2)}) %collective-permute-start.1) | collective-permute-done | bytes 213024 | tf_op jit(solution)/shard_map/ppermute | solution.py:1256
  18.0 0.0 collective-permute-done.2.u1
  18.0 0.0 copy-done.4
  18.0 0.0 copy-done.6
  18.0 0.0 copy-start.2
  18.0 0.0 copy-start.3
  18.0 2.3 %shard_map.189 = (bf16[128,512]{1,0:T(8,128)(2,1)S(1)}, bf16[512,512]{1,0:T(8,128)(2,1)S(1)}, f32[2,264,256]{2,1,0:T(8,128)S(1)}, bf16[512,256]{1,0:T(8,128)(2,1...) custom-call(bf16[208,512]{1,0:T(8,128)(2,1)S(1)} %get-tuple-element., ...), custom_call_target="tpu_custom_call" | custom-call | flops 2000000000 | bytes 20000000 | tf_op jit(solution)/shard_map/pallas_call | solution.py:1279
  20.3 2.7 %collective-permute-start.6 = (bf16[16,768]{1,0:T(8,128)(2,1)S(1)}, bf16[16,768]{1,0:T(8,128)(2,1)S(1)}, u32[]{:S(2)}, u32[]{:S(2)}) collective-permute-start(bf16[16,768]{1,0:T(8,128)(2,1)S(1)} %get-tuple-element.91), channel_id=1, source_target_pairs={{0,16},{4,20},{8,24},{12,28},{16,0},{20,4},{24,8},{28,12},{1,17},{... | collective-permute-start | bytes 73736 | tf_op jit(solution)/shard_map/ppermute | solution.py:1305
  23.0 0.3 collective-permute-start.5
  23.3 0.0 collective-permute-done.7.v3
  23.3 0.0 collective-permute-done.8.v2
  23.3 0.8 %collective-permute-done.9.v1 = bf16[128,512]{1,0:T(8,128)(2,1)S(1)} collective-permute-done((bf16[128,512]{1,0:T(8,128)(2,1)}, bf16[128,512]{1,0:T(8,128)(2,1)S(1)}, u32[]{:S(2)}, u32[]{:S(2)}) %collective-permute-start.9) | collective-permute-done | bytes 131104 | tf_op jit(solution)/shard_map/ppermute | solution.py:1278
  24.1 0.0 copy-done.2
  24.1 0.0 copy-done.3
  24.1 1.1 %shard_map.190 = (f32[2,264,512]{2,1,0:T(8,128)S(1)}, bf16[512,512]{1,0:T(8,128)(2,1)S(1)}, f32[512,512]{1,0:T(8,128)S(1)}, bf16[512,512]{1,0:T(8,128)(2,1)S(1)}, bf16[512,512]{1,0:T(8,128)(2,1)S(1)}) custom-call(bf16[128,512]{1,0:T(8,128)(2,1)S(1)} %get-tuple-element.92.v0, bf16[128,512]{1,0:T(8,128)(2,1)S(1)} %collective-permute-done.7.v3, ...), custom_call_target="tpu_custom_call" | custom-call | flops 2000000000 | bytes 20000000 | tf_op jit(solution)/shard_map/pallas_call | solution.py:1307
  25.2 0.0 collective-permute-done.6.halo_ref
  25.2 0.0 copy-start.5
  25.2 0.4 shard_map.191
  25.7 2.7 %collective-permute-start.10 = (bf16[144,512]{1,0:T(8,128)(2,1)S(1)}, bf16[144,512]{1,0:T(8,128)(2,1)S(1)}, u32[]{:S(2)}, u32[]{:S(2)}) collective-permute-start(bf16[144,512]{1,0:T(8,128)(2,1)S(1)} %get-tuple-element.105), channel_id=1, source_target_pairs={{0,16},{4,20},{8,24},{12,28},{16,0},{20,4},{24,8},{28,12},{1,17},{... | collective-permute-start | bytes 442376 | tf_op jit(solution)/shard_map/ppermute | solution.py:1340
  28.4 0.0 copy-done.5
  28.4 4.7 %shard_map.192 = (f32[512,512]{1,0:T(8,128)S(1)}, f32[512,512]{1,0:T(8,128)S(1)}, f32[512,256]{1,0:T(8,128)S(1)}, f32[512,256]{1,0:T(8,128)S(1)}, f32[32,128]{1,...) custom-call(bf16[512,512]{1,0:T(8,128)(2,1)S(1)} %get-tuple-element.109.dp, ...), custom_call_target="tpu_custom_call" | custom-call | flops 5000000000 | bytes 50000000 | tf_op jit(solution)/shard_map/pallas_call | solution.py:1341
  33.0 0.0 collective-permute-done.5.midg_ref
  33.0 6.2 %collective-permute-done.10.midf_ref = bf16[144,512]{1,0:T(8,128)(2,1)S(1)} collective-permute-done((bf16[144,512]{1,0:T(8,128)(2,1)S(1)}, bf16[144,512]{1,0:T(8,128)(2,1)S(1)}, u32[]{:S(2)}, u32[]{:S(2)}) %collective-permute-start.10) | collective-permute-done | bytes 147488 | tf_op jit(solution)/shard_map/ppermute | solution.py:1340
  39.3 1.2 %shard_map.193 = (bf16[544,128]{1,0:T(8,128)(2,1)S(1)}, bf16[544,128]{1,0:T(8,128)(2,1)S(1)}, bf16[4,128,512]{2,1,0:T(8,128)(2,1)S(1)}, bf16[4,128,512]{2,1,0:T(8,128)(2,1)S(1)}, f32[8,512]{1,0:T(8,128)S(1)}) custom-call(bf16[128,512]{1,0:T(8,128)(2,1)S(1)} %collective-permute-done.5.midg_ref, bf16[144,512]{1,0:T(8,128)(2,1)S(1)} %collective-permute-done.10.midf_ref, ...), custom_call_target="tpu_custom_call" | custom-call | flops 2000000000 | bytes 20000000 | tf_op jit(solution)/shard_map/pallas_call | solution.py:1372
  40.4 0.7 %collective-permute-start.14 = (bf16[544,128]{1,0:T(8,128)(2,1)S(1)}, bf16[544,128]{1,0:T(8,128)(2,1)S(1)}, u32[]{:S(2)}, u32[]{:S(2)}) collective-permute-start(bf16[544,128]{1,0:T(8,128)(2,1)S(1)} %get-tuple-element.139), channel_id=1, source_target_pairs={{0,0},{2,1},{1,2},{3,3},{4,4},{6,5},{5,6},{7,7},{8,8},{10,9},{9,10... | collective-permute-start | bytes 417800 | tf_op jit(solution)/shard_map/ppermute | solution.py:1406
  41.1 3.0 %collective-permute-start.15 = (bf16[544,128]{1,0:T(8,128)(2,1)S(1)}, bf16[544,128]{1,0:T(8,128)(2,1)S(1)}, u32[]{:S(2)}, u32[]{:S(2)}) collective-permute-start(bf16[544,128]{1,0:T(8,128)(2,1)S(1)} %get-tuple-element.140), channel_id=1, source_target_pairs={{0,2},{2,3},{1,0},{3,1},{4,6},{6,7},{5,4},{7,5},{8,10},{10,11},{9,... | collective-permute-start | bytes 417800 | tf_op jit(solution)/shard_map/ppermute | solution.py:1407
  44.1 3.2 %shard_map.194 = (f32[2,264,512]{2,1,0:T(8,128)S(1)}, f32[8,8,128]{2,1,0:T(8,128)S(1)}, f32[8,512]{1,0:T(8,128)S(1)}, f32[24,128]{1,0:T(8,128)S(1)}) custom-call(bf16[4,128,512]{2,1,0:T(8,128)(2,1)S(1)} %get-tuple-element.122.hlow_ref, bf16[4,128,512]{2,1,0:T(8,128)(2,1)S(1)} %get-tuple-element.123.clow_ref, f32[8,512]{1,0:T(8,128)S(1)} %get-tuple-element.124.endrow_ref, ...), custom_call_target="tpu_custom_call" | custom-call | flops 3000000000 | bytes 30000000 | tf_op jit(solution)/shard_map/pallas_call | solution.py:1408
  47.3 0.6 shard_map.195
  47.9 0.2 collective-permute-start.11
  48.1 0.0 collective-permute-done.14.one_ref
  48.1 0.0 collective-permute-done.15.two_ref
  48.2 3.3 %collective-permute-start.16 = (bf16[32,512]{1,0:T(8,128)(2,1)S(1)}, bf16[32,512]{1,0:T(8,128)(2,1)S(1)}, u32[]{:S(2)}, u32[]{:S(2)}) collective-permute-start(bf16[32,512]{1,0:T(8,128)(2,1)S(1)} %shard_map.196.own_ref), channel_id=1, source_target_pairs={{0,16},{4,20},{8,24},{12,28},{16,0},{20,4},{24,8},{28,12},{1,17},{... | collective-permute-start | bytes 98312 | tf_op jit(solution)/shard_map/ppermute | solution.py:1453
  51.4 0.0 collective-permute-start.12
  51.4 0.6 %collective-permute-start.13 = (bf16[128,512]{1,0:T(8,128)(2,1)S(1)}, bf16[128,512]{1,0:T(8,128)(2,1)S(1)}, u32[]{:S(2)}, u32[]{:S(2)}) collective-permute-start(bf16[128,512]{1,0:T(8,128)(2,1)S(1)} %get-tuple-element.136), channel_id=1, source_target_pairs={{0,4},{4,0},{8,12},{12,8},{16,20},{20,16},{24,28},{28,24},{1,5},{5... | collective-permute-start | bytes 393224 | tf_op jit(solution)/shard_map/ppermute | solution.py:1463
  52.1 1.5 %collective-permute-done.16.other_ref = bf16[32,512]{1,0:T(8,128)(2,1)S(1)} collective-permute-done((bf16[32,512]{1,0:T(8,128)(2,1)S(1)}, bf16[32,512]{1,0:T(8,128)(2,1)S(1)}, u32[]{:S(2)}, u32[]{:S(2)}) %collective-permute-start.16) | collective-permute-done | bytes 32800 | tf_op jit(solution)/shard_map/ppermute | solution.py:1453
  53.5 0.1 shard_map.197
  53.7 2.7 %collective-permute-start.17 = (bf16[96,512]{1,0:T(8,128)(2,1)S(1)}, bf16[96,512]{1,0:T(8,128)(2,1)S(1)}, u32[]{:S(2)}, u32[]{:S(2)}) collective-permute-start(bf16[96,512]{1,0:T(8,128)(2,1)S(1)} %get-tuple-element.143), channel_id=1, source_target_pairs={{0,12},{4,8},{8,4},{12,0},{16,28},{20,24},{24,20},{28,16},{1,13},{... | collective-permute-start | bytes 294920 | tf_op jit(solution)/shard_map/ppermute | solution.py:1473
  56.3 0.0 collective-permute-start.18
  56.3 0.0 collective-permute-done.11.y3
  56.3 0.9 %collective-permute-start.19 = (bf16[96,512]{1,0:T(8,128)(2,1)S(1)}, bf16[96,512]{1,0:T(8,128)(2,1)S(1)}, u32[]{:S(2)}, u32[]{:S(2)}) collective-permute-start(bf16[96,512]{1,0:T(8,128)(2,1)S(1)} %get-tuple-element.145), channel_id=1, source_target_pairs={{0,4},{4,0},{8,12},{12,8},{16,20},{20,16},{24,28},{28,24},{1,5},{5... | collective-permute-start | bytes 294920 | tf_op jit(solution)/shard_map/ppermute | solution.py:1473
  57.3 0.1 collective-permute-done.12.y2
  57.4 0.8 %collective-permute-done.13.y1 = bf16[128,512]{1,0:T(8,128)(2,1)S(1)} collective-permute-done((bf16[128,512]{1,0:T(8,128)(2,1)S(1)}, bf16[128,512]{1,0:T(8,128)(2,1)S(1)}, u32[]{:S(2)}, u32[]{:S(2)}) %collective-permute-start.13) | collective-permute-done | bytes 131104 | tf_op jit(solution)/shard_map/ppermute | solution.py:1463
  58.2 2.4 %collective-permute-done.17.w3 = bf16[96,512]{1,0:T(8,128)(2,1)S(1)} collective-permute-done((bf16[96,512]{1,0:T(8,128)(2,1)S(1)}, bf16[96,512]{1,0:T(8,128)(2,1)S(1)}, u32[]{:S(2)}, u32[]{:S(2)}) %collective-permute-start.17) | collective-permute-done | bytes 98336 | tf_op jit(solution)/shard_map/ppermute | solution.py:1473
  60.6 0.5 collective-permute-done.18.w2
  61.1 0.3 collective-permute-done.19.w1
  61.4 1.1 %shard_map.198 = (f32[128,2048]{1,0:T(8,128)}, f32[128,512]{1,0:T(8,128)}, f32[32,128]{1,0:T(8,128)}, f32[4,2048]{1,0:T(4,128)}, f32[4,512]{1,0:T(4,128)}, /*ind...) custom-call(bf16[128,512]{1,0:T(8,128)(2,1)S(1)} %get-tuple-element.133.y0, ...), custom_call_target="tpu_custom_call" | custom-call | flops 1000000 | bytes 10000 | tf_op jit(solution)/shard_map/pallas_call | solution.py:1474
  (3 shorter events, 0.0 us)
Async XLA Ops:
  0.6 17.4 %copy-start.4 = (f32[32]{0:T(128)S(1)}, f32[32]{0:T(128)}, u32[]{:S(2)}) copy-start(f32[32]{0:T(128)} %dtb_ref.1) | copy-start | bytes 388
  0.7 17.4 %copy-start.6 = (f32[32]{0:T(128)S(1)}, f32[32]{0:T(128)}, u32[]{:S(2)}) copy-start(f32[32]{0:T(128)} %alog_ref.3) | copy-start | bytes 388
  3.7 13.3 %collective-permute-start = (bf16[208,512]{1,0:T(8,128)(2,1)}, bf16[208,512]{1,0:T(8,128)(2,1)S(1)}, u32[]{:S(2)}, u32[]{:S(2)}) collective-permute-start(bf16[208,512]{1,0:T(8,128)(2,1)} %get-tuple-element.86), channel_id=1, source_target_pairs={{0,12},{4,8},{8,4},{12,0},{16,28},{20,24},{24,20},{28,16},{1,13},{... | collective-permute-start | bytes 638984 | tf_op jit(solution)/shard_map/ppermute | solution.py:1256
  7.8 10.2 %collective-permute-start.1 = (bf16[208,512]{1,0:T(8,128)(2,1)}, bf16[208,512]{1,0:T(8,128)(2,1)S(1)}, u32[]{:S(2)}, u32[]{:S(2)}) collective-permute-start(bf16[208,512]{1,0:T(8,128)(2,1)} %get-tuple-element.87), channel_id=1, source_target_pairs={{0,8},{4,12},{8,0},{12,4},{16,24},{20,28},{24,16},{28,20},{1,9},{5... | collective-permute-start | bytes 638984 | tf_op jit(solution)/shard_map/ppermute | solution.py:1256
  8.2 9.8 %collective-permute-start.2 = (bf16[208,512]{1,0:T(8,128)(2,1)}, bf16[208,512]{1,0:T(8,128)(2,1)S(1)}, u32[]{:S(2)}, u32[]{:S(2)}) collective-permute-start(bf16[208,512]{1,0:T(8,128)(2,1)} %get-tuple-element.88), channel_id=1, source_target_pairs={{0,4},{4,0},{8,12},{12,8},{16,20},{20,16},{24,28},{28,24},{1,5},{5... | collective-permute-start | bytes 638984 | tf_op jit(solution)/shard_map/ppermute | solution.py:1256
  8.4 5.2 %collective-permute-start.4 = (f32[8,512]{1,0:T(8,128)}, f32[8,512]{1,0:T(8,128)S(1)}, u32[]{:S(2)}, u32[]{:S(2)}) collective-permute-start(f32[8,512]{1,0:T(8,128)} %get-tuple-element.89), channel_id=1, source_target_pairs={{2,0},{3,2},{0,1},{1,3},{6,4},{7,6},{4,5},{5,7},{10,8},{11,10},{8,... | collective-permute-start | bytes 49160 | tf_op jit(solution)/shard_map/ppermute | solution.py:1258
  8.4 8.1 %collective-permute-start.3 = (f32[8,512]{1,0:T(8,128)}, f32[8,512]{1,0:T(8,128)S(1)}, u32[]{:S(2)}, u32[]{:S(2)}) collective-permute-start(f32[8,512]{1,0:T(8,128)} %get-tuple-element.89), channel_id=1, source_target_pairs={{0,0},{1,2},{2,1},{3,3},{4,4},{5,6},{6,5},{7,7},{8,8},{9,10},{10,9... | collective-permute-start | bytes 49160 | tf_op jit(solution)/shard_map/ppermute | solution.py:1257
  11.7 0.9 %copy-start = (bf16[208,512]{1,0:T(8,128)(2,1)S(1)}, bf16[208,512]{1,0:T(8,128)(2,1)}, u32[]{:S(2)}) copy-start(bf16[208,512]{1,0:T(8,128)(2,1)} %get-tuple-element.83.u_ref) | copy-start | bytes 638980
  12.7 0.9 %copy-start.1 = (bf16[128,512]{1,0:T(8,128)(2,1)S(1)}, bf16[128,512]{1,0:T(8,128)(2,1)}, u32[]{:S(2)}) copy-start(bf16[128,512]{1,0:T(8,128)(2,1)} %get-tuple-element.84.v_ref) | copy-start | bytes 393220
  13.6 9.7 %collective-permute-start.7 = (bf16[128,512]{1,0:T(8,128)(2,1)}, bf16[128,512]{1,0:T(8,128)(2,1)S(1)}, u32[]{:S(2)}, u32[]{:S(2)}) collective-permute-start(bf16[128,512]{1,0:T(8,128)(2,1)} %get-tuple-element.93), channel_id=1, source_target_pairs={{0,12},{4,8},{8,4},{12,0},{16,28},{20,24},{24,20},{28,16},{1,13},{... | collective-permute-start | bytes 393224 | tf_op jit(solution)/shard_map/ppermute | solution.py:1278
  16.5 6.8 %collective-permute-start.8 = (bf16[128,512]{1,0:T(8,128)(2,1)}, bf16[128,512]{1,0:T(8,128)(2,1)S(1)}, u32[]{:S(2)}, u32[]{:S(2)}) collective-permute-start(bf16[128,512]{1,0:T(8,128)(2,1)} %get-tuple-element.94), channel_id=1, source_target_pairs={{0,8},{4,12},{8,0},{12,4},{16,24},{20,28},{24,16},{28,20},{1,9},{5... | collective-permute-start | bytes 393224 | tf_op jit(solution)/shard_map/ppermute | solution.py:1278
  17.0 7.1 %collective-permute-start.9 = (bf16[128,512]{1,0:T(8,128)(2,1)}, bf16[128,512]{1,0:T(8,128)(2,1)S(1)}, u32[]{:S(2)}, u32[]{:S(2)}) collective-permute-start(bf16[128,512]{1,0:T(8,128)(2,1)} %get-tuple-element.95), channel_id=1, source_target_pairs={{0,4},{4,0},{8,12},{12,8},{16,20},{20,16},{24,28},{28,24},{1,5},{5... | collective-permute-start | bytes 393224 | tf_op jit(solution)/shard_map/ppermute | solution.py:1278
  18.0 6.1 %copy-start.2 = (f32[4,2048]{1,0:T(4,128)S(1)}, f32[4,2048]{1,0:T(4,128)}, u32[]{:S(2)}) copy-start(f32[4,2048]{1,0:T(4,128)} %taps_ref.7) | copy-start | bytes 98308
  18.0 6.1 %copy-start.3 = (f32[2048]{0:T(1024)S(1)}, f32[2048]{0:T(1024)}, u32[]{:S(2)}) copy-start(f32[2048]{0:T(1024)} %param.17) | copy-start | bytes 24580
  20.3 4.9 %collective-permute-start.6 = (bf16[16,768]{1,0:T(8,128)(2,1)S(1)}, bf16[16,768]{1,0:T(8,128)(2,1)S(1)}, u32[]{:S(2)}, u32[]{:S(2)}) collective-permute-start(bf16[16,768]{1,0:T(8,128)(2,1)S(1)} %get-tuple-element.91), channel_id=1, source_target_pairs={{0,16},{4,20},{8,24},{12,28},{16,0},{20,4},{24,8},{28,12},{1,17},{... | collective-permute-start | bytes 73736 | tf_op jit(solution)/shard_map/ppermute | solution.py:1305
  23.0 10.1 %collective-permute-start.5 = (bf16[128,512]{1,0:T(8,128)(2,1)S(1)}, bf16[128,512]{1,0:T(8,128)(2,1)S(1)}, u32[]{:S(2)}, u32[]{:S(2)}) collective-permute-start(bf16[128,512]{1,0:T(8,128)(2,1)S(1)} %get-tuple-element.90), channel_id=1, source_target_pairs={{0,16},{4,20},{8,24},{12,28},{16,0},{20,4},{24,8},{28,12},{1,17},{... | collective-permute-start | bytes 393224 | tf_op jit(solution)/shard_map/ppermute | solution.py:1306
  25.2 3.1 %copy-start.5 = (f32[32]{0:T(128)S(1)}, f32[32]{0:T(128)}, u32[]{:S(2)}) copy-start(f32[32]{0:T(128)} %skip_ref.1) | copy-start | bytes 388
  25.7 13.6 %collective-permute-start.10 = (bf16[144,512]{1,0:T(8,128)(2,1)S(1)}, bf16[144,512]{1,0:T(8,128)(2,1)S(1)}, u32[]{:S(2)}, u32[]{:S(2)}) collective-permute-start(bf16[144,512]{1,0:T(8,128)(2,1)S(1)} %get-tuple-element.105), channel_id=1, source_target_pairs={{0,16},{4,20},{8,24},{12,28},{16,0},{20,4},{24,8},{28,12},{1,17},{... | collective-permute-start | bytes 442376 | tf_op jit(solution)/shard_map/ppermute | solution.py:1340
  40.4 7.7 %collective-permute-start.14 = (bf16[544,128]{1,0:T(8,128)(2,1)S(1)}, bf16[544,128]{1,0:T(8,128)(2,1)S(1)}, u32[]{:S(2)}, u32[]{:S(2)}) collective-permute-start(bf16[544,128]{1,0:T(8,128)(2,1)S(1)} %get-tuple-element.139), channel_id=1, source_target_pairs={{0,0},{2,1},{1,2},{3,3},{4,4},{6,5},{5,6},{7,7},{8,8},{10,9},{9,10... | collective-permute-start | bytes 417800 | tf_op jit(solution)/shard_map/ppermute | solution.py:1406
  41.1 7.0 %collective-permute-start.15 = (bf16[544,128]{1,0:T(8,128)(2,1)S(1)}, bf16[544,128]{1,0:T(8,128)(2,1)S(1)}, u32[]{:S(2)}, u32[]{:S(2)}) collective-permute-start(bf16[544,128]{1,0:T(8,128)(2,1)S(1)} %get-tuple-element.140), channel_id=1, source_target_pairs={{0,2},{2,3},{1,0},{3,1},{4,6},{6,7},{5,4},{7,5},{8,10},{10,11},{9,... | collective-permute-start | bytes 417800 | tf_op jit(solution)/shard_map/ppermute | solution.py:1407
  47.9 8.4 %collective-permute-start.11 = (bf16[128,512]{1,0:T(8,128)(2,1)S(1)}, bf16[128,512]{1,0:T(8,128)(2,1)S(1)}, u32[]{:S(2)}, u32[]{:S(2)}) collective-permute-start(bf16[128,512]{1,0:T(8,128)(2,1)S(1)} %get-tuple-element.134), channel_id=1, source_target_pairs={{0,12},{4,8},{8,4},{12,0},{16,28},{20,24},{24,20},{28,16},{1,13},{... | collective-permute-start | bytes 393224 | tf_op jit(solution)/shard_map/ppermute | solution.py:1463
  48.2 5.4 %collective-permute-start.16 = (bf16[32,512]{1,0:T(8,128)(2,1)S(1)}, bf16[32,512]{1,0:T(8,128)(2,1)S(1)}, u32[]{:S(2)}, u32[]{:S(2)}) collective-permute-start(bf16[32,512]{1,0:T(8,128)(2,1)S(1)} %shard_map.196.own_ref), channel_id=1, source_target_pairs={{0,16},{4,20},{8,24},{12,28},{16,0},{20,4},{24,8},{28,12},{1,17},{... | collective-permute-start | bytes 98312 | tf_op jit(solution)/shard_map/ppermute | solution.py:1453
  51.4 6.0 %collective-permute-start.12 = (bf16[128,512]{1,0:T(8,128)(2,1)S(1)}, bf16[128,512]{1,0:T(8,128)(2,1)S(1)}, u32[]{:S(2)}, u32[]{:S(2)}) collective-permute-start(bf16[128,512]{1,0:T(8,128)(2,1)S(1)} %get-tuple-element.135), channel_id=1, source_target_pairs={{0,8},{4,12},{8,0},{12,4},{16,24},{20,28},{24,16},{28,20},{1,9},{5... | collective-permute-start | bytes 393224 | tf_op jit(solution)/shard_map/ppermute | solution.py:1463
  51.4 6.8 %collective-permute-start.13 = (bf16[128,512]{1,0:T(8,128)(2,1)S(1)}, bf16[128,512]{1,0:T(8,128)(2,1)S(1)}, u32[]{:S(2)}, u32[]{:S(2)}) collective-permute-start(bf16[128,512]{1,0:T(8,128)(2,1)S(1)} %get-tuple-element.136), channel_id=1, source_target_pairs={{0,4},{4,0},{8,12},{12,8},{16,20},{20,16},{24,28},{28,24},{1,5},{5... | collective-permute-start | bytes 393224 | tf_op jit(solution)/shard_map/ppermute | solution.py:1463
  53.7 7.0 %collective-permute-start.17 = (bf16[96,512]{1,0:T(8,128)(2,1)S(1)}, bf16[96,512]{1,0:T(8,128)(2,1)S(1)}, u32[]{:S(2)}, u32[]{:S(2)}) collective-permute-start(bf16[96,512]{1,0:T(8,128)(2,1)S(1)} %get-tuple-element.143), channel_id=1, source_target_pairs={{0,12},{4,8},{8,4},{12,0},{16,28},{20,24},{24,20},{28,16},{1,13},{... | collective-permute-start | bytes 294920 | tf_op jit(solution)/shard_map/ppermute | solution.py:1473
  56.3 4.8 %collective-permute-start.18 = (bf16[96,512]{1,0:T(8,128)(2,1)S(1)}, bf16[96,512]{1,0:T(8,128)(2,1)S(1)}, u32[]{:S(2)}, u32[]{:S(2)}) collective-permute-start(bf16[96,512]{1,0:T(8,128)(2,1)S(1)} %get-tuple-element.144), channel_id=1, source_target_pairs={{0,8},{4,12},{8,0},{12,4},{16,24},{20,28},{24,16},{28,20},{1,9},{5... | collective-permute-start | bytes 294920 | tf_op jit(solution)/shard_map/ppermute | solution.py:1473
  56.3 5.1 %collective-permute-start.19 = (bf16[96,512]{1,0:T(8,128)(2,1)S(1)}, bf16[96,512]{1,0:T(8,128)(2,1)S(1)}, u32[]{:S(2)}, u32[]{:S(2)}) collective-permute-start(bf16[96,512]{1,0:T(8,128)(2,1)S(1)} %get-tuple-element.145), channel_id=1, source_target_pairs={{0,4},{4,0},{8,12},{12,8},{16,20},{20,16},{24,28},{28,24},{1,5},{5... | collective-permute-start | bytes 294920 | tf_op jit(solution)/shard_map/ppermute | solution.py:1473

commit v6 on v5

--- a/solution.py
+++ b/solution.py
@@ -375,7 +375,7 @@
 
 
 def pack_kernel(sig_ref, map_ref, dt_ref, dy_ref, mtaps_ref, mbias_ref, *rest):
-    u_refs, tap_ref, (dt_in, sig_in, sems) = rest[:4], rest[4], rest[5:]
+    u_refs, tap_ref, (dt_in, sig_in, map_in, sems) = rest[:4], rest[4], rest[5:]
     quad, r, f = place()
     copies = []
     dt_copy = pltpu.make_async_copy(dt_ref, dt_in, sems.at[20])
@@ -383,6 +383,10 @@
     ends = pl.ds(pl.multiple_of(jnp.where(quad == 0, HALF - 16, TILE - 16), 16), 16)
     sig_copy = pltpu.make_async_copy(sig_ref.at[ends, :], sig_in, sems.at[21])
     sig_copy.start()
+    map_copy = pltpu.make_async_copy(
+        map_ref.at[ends, 0 : map_ref.shape[1] // 2], map_in, sems.at[22]
+    )
+    map_copy.start()
 
     def send(source, target):
         copy = pltpu.make_async_copy(source, target, sems.at[len(copies)])
@@ -395,41 +399,51 @@
         cols = at_tile(dest * 4 * TILE, 4 * TILE)
         send(dy_ref.at[:, cols], u_refs[k].at[0:TILE, :])
         group = (2 * f + lax.div(dest, 2)) * TILE
-        for j in range(2):
-            for e in range(2):
-                send(
-                    map_ref.at[e * HALF : (e + 1) * HALF, at_tile(group + j * half)],
-                    u_refs[k].at[TILE : TILE + HALF, lanes_of(2 * j + e)],
-                )
+        for e in range(4):
+            send(
+                map_ref.at[e * HALF // 2 : (e + 1) * HALF // 2, at_tile(group + half)],
+                u_refs[k].at[TILE : TILE + HALF // 2, lanes_of(e)],
+            )
     tap_ref[0:4, :] = mtaps_ref[...]
     tap_ref[4:5, :] = mbias_ref[...]
     tap_ref[5:8, :] = jnp.zeros_like(tap_ref[5:8, :])
     dt_copy.wait()
     sig_copy.wait()
+    map_copy.wait()
     for k in range(4):
         dest = lax.bitwise_xor(r, k)
         hi, mid, lo = split3(dt_in[pl.ds(pl.multiple_of(8 * dest, 8), 8), :])
         edge = sig_in[:, at_tile(dest * 4 * TILE, 4 * TILE)].astype(F32)[8:16]
+        group = (2 * f + lax.div(dest, 2)) * TILE
+        edge_in = map_in[:, at_tile(group)].astype(F32)[8:16]
         top = jnp.concatenate([hi.astype(F32), lo.astype(F32), edge[:, 0 : 2 * TILE]], axis=1)
         low = jnp.concatenate(
-            [mid.astype(F32), edge[:, 2 * TILE : 4 * TILE], jnp.zeros((8, TILE), F32)], axis=1
+            [mid.astype(F32), edge[:, 2 * TILE : 4 * TILE], edge_in], axis=1
         )
-        u_refs[k][TILE + HALF : TILE + HALF + 16, :] = jnp.concatenate([top, low], axis=0).astype(BF)
+        u_refs[k][TILE + HALF // 2 : TILE + HALF // 2 + 16, :] = jnp.concatenate([top, low], axis=0).astype(BF)
     for copy in copies:
         copy.wait()
 
 
-def pack_sig_kernel(sig_ref, *rest):
+def pack_sig_kernel(sig_ref, map_ref, *rest):
     v_refs, sems = rest[:4], rest[4]
-    r = place()[1]
+    quad, r, f = place()
     copies = []
+
+    def send(source, target):
+        copy = pltpu.make_async_copy(source, target, sems.at[len(copies)])
+        copy.start()
+        copies.append(copy)
+
     for k in (1, 2, 3, 0):
         dest = lax.bitwise_xor(r, k)
-        copy = pltpu.make_async_copy(
-            sig_ref.at[:, at_tile(dest * 4 * TILE, 4 * TILE)], v_refs[k], sems.at[k]
-        )
-        copy.start()
-        copies.append(copy)
+        send(sig_ref.at[:, at_tile(dest * 4 * TILE, 4 * TILE)], v_refs[k].at[0:TILE, :])
+        group = (2 * f + lax.div(dest, 2)) * TILE
+        for e in range(4):
+            send(
+                map_ref.at[e * HALF // 2 : (e + 1) * HALF // 2, at_tile(group)],
+                v_refs[k].at[TILE : TILE + HALF // 2, lanes_of(e)],
+            )
     for copy in copies:
         copy.wait()
 
@@ -491,6 +505,20 @@
         boundary_chunk(i, high), patch[:, patch_lanes], ref[i * TILE : i * TILE + 16, lanes]
     )
     return jnp.concatenate([first, ref[i * TILE + 16 : (i + 1) * TILE, lanes]], axis=0)
+
+
+def map_rows(x, segment, start, block):
+    for p in range(2):
+        at = pl.ds(pl.multiple_of(8 + start + p * HALF // 2, 8), HALF // 2)
+        x[segment, at, :] = block[
+            TILE : TILE + HALF // 2, lanes_of(2 * segment + p)
+        ].astype(F32)
+
+
+def own_halo(x, high):
+    first = x[0, 2 * TILE : 2 * TILE + 8, :]
+    x[0, 0:8, :] = jnp.zeros_like(first)
+    x[1, 0:8, :] = jnp.where(high, first, jnp.zeros_like(first))
 
 
 def grads_kernel(
@@ -504,9 +532,9 @@
     dtb_ref,
     mid_ref,
     dp,
-    xm,
-    actm,
-    prem,
+    xo,
+    act_out,
+    pre_out,
     sgrad_s,
     step_e,
     toend_e,
@@ -528,28 +556,23 @@
         mine_ref[8 * j : 8 * j + 8, :] = jnp.where(
             lax.rem(f, 2) == j, one_taps[:, at], two_taps[:, at]
         )
-    edge = jnp.zeros((8, 4 * TILE), F32)
+    edge = jnp.zeros((8, 5 * TILE), F32)
     for k, u in enumerate((u0, u1, u2, u3)):
         s = lax.bitwise_xor(r, k)
         for e, start in ((0, HALF * s), (1, HALF * (3 - s))):
-            for j in range(2):
-                xm[e, pl.ds(pl.multiple_of(8 + start, 8), HALF), lanes_of(j)] = u[
-                    TILE : TILE + HALF, lanes_of(2 * j + e)
-                ].astype(F32)
+            map_rows(xo, e, start, u)
             dp[pl.ds(pl.multiple_of(2 * TILE * e + start, HALF), HALF), :] = u[
                 e * HALF : (e + 1) * HALF, :
             ]
-        packed = u[TILE + HALF : TILE + HALF + 16, :].astype(F32)
+        packed = u[TILE + HALF // 2 : TILE + HALF // 2 + 16, :].astype(F32)
         dt_src[s] = packed[0:8, 0:TILE] + packed[8:16, 0:TILE] + packed[0:8, TILE : 2 * TILE]
         last = jnp.concatenate(
-            [packed[0:8, 2 * TILE : 4 * TILE], packed[8:16, TILE : 3 * TILE]], axis=1
+            [packed[0:8, 2 * TILE : 4 * TILE], packed[8:16, TILE : 4 * TILE]], axis=1
         )
         edge = edge + jnp.where(s == jnp.where(high, 0, 3), last, 0.0)
     last = slice(2 * TILE, 2 * TILE + 8)
-    edge = jnp.concatenate([edge, jnp.where(high, xm[1, last, :], xm[0, last, :])], axis=1)
-    halo_ref[...] = jnp.concatenate([jnp.zeros_like(edge), edge], axis=0).astype(BF)
-    xm[0, 0:8, :] = jnp.zeros((8, 2 * TILE), F32)
-    xm[1, 0:8, :] = jnp.where(high, xm[0, 2 * TILE : 2 * TILE + 8, :], 0.0)
+    edge = jnp.concatenate([edge, jnp.where(high, xo[1, last, :], xo[0, last, :])], axis=1)
+    own_halo(xo, high)
 
     rate8 = -jnp.exp(head_row(alog_ref, r))
     bias8 = head_row(dtb_ref, r)
@@ -574,12 +597,10 @@
     for i in range(4):
         rows = slice(i * TILE, (i + 1) * TILE)
         base = (i % 2) * TILE
-        for j in range(2):
-            lanes = lanes_of(j)
-            taps, bias = map_tap_rows(j, mine_ref)
-            pre = conv(xm[i // 2, base : base + TILE + 8, lanes], taps, bias)
-            actm[rows, lanes] = (pre * sigmoid(pre)).astype(BF)
-            prem[rows, lanes] = pre
+        taps, bias = map_tap_rows(1, mine_ref)
+        pre = conv(xo[i // 2, base : base + TILE + 8, :], taps, bias)
+        act_out[rows, :] = (pre * sigmoid(pre)).astype(BF)
+        pre_out[rows, :] = pre
         parts = split3(
             jnp.concatenate([step_r[8 * i : 8 * i + 8, :], ds_r[8 * i : 8 * i + 8, :]], axis=0)
         )
@@ -603,14 +624,26 @@
                 grown = jnp.concatenate([first, grown[16:]], axis=0)
             masked.append(grown)
         ends.append(jnp.concatenate(end, axis=1))
-        t_s[i] = mm(actm[rows, lanes_of(1)], jnp.concatenate(masked, axis=1), TN)
+        t_s[i] = mm(act_out[rows, :], jnp.concatenate(masked, axis=1), TN)
     g_a = t_s[0] + ends[0] * t_s[1]
     g_b = t_s[2] + ends[2] * t_s[3]
     mid_ref[...] = jnp.where(high, g_a + ends[0] * ends[1] * g_b, g_b).astype(BF)
+    across = [part.astype(F32) for part in split3(ends[0] * ends[1] * ends[2] * ends[3])]
+    raw = jnp.where(high, xo[0, 8:16, :], xo[1, 8:16, :])
+    grown = jnp.where(high, sgrad_s[0:16, :], sgrad_s[2 * TILE : 2 * TILE + 16, :]).astype(F32)
+    pieces = []
+    for k in range(3):
+        pieces.append(
+            jnp.concatenate([across[k], jnp.zeros((1, TILE), F32), raw[k : k + 1]], axis=1)
+        )
+    for k in range(3):
+        pieces.append(jnp.concatenate([grown[k : k + 1], jnp.zeros((1, 2 * TILE), F32)], axis=1))
+    pieces += [jnp.zeros((2, 6 * TILE), F32), edge]
+    halo_ref[...] = jnp.concatenate(pieces, axis=0).astype(BF)
 
 
 def first_kernel(
-    v0, v3, v2, v1, step_e, toend_e, taps_ref, bias_ref, xs, acts, pres, scaled_s, weighted_s
+    v0, v3, v2, v1, step_e, toend_e, taps_ref, bias_ref, mine_ref, xs, acts, pres, scaled_s, weighted_s, xi, act_in, pre_in
 ):
     quad, r, f = place()
     high = quad == 1
@@ -620,11 +653,16 @@
             xs[e, pl.ds(pl.multiple_of(8 + start, 8), HALF), :] = v[
                 e * HALF : (e + 1) * HALF, :
             ].astype(F32)
-    xs[0, 0:8, :] = jnp.zeros((8, 4 * TILE), F32)
-    xs[1, 0:8, :] = jnp.where(high, xs[0, 2 * TILE : 2 * TILE + 8, :], 0.0)
+            map_rows(xi, e, start, v)
+    own_halo(xs, high)
+    own_halo(xi, high)
     for i in range(4):
         rows = slice(i * TILE, (i + 1) * TILE)
         base = (i % 2) * TILE
+        taps, bias = map_tap_rows(0, mine_ref)
+        pre = conv(xi[i // 2, base : base + TILE + 8, :], taps, bias)
+        act_in[rows, :] = (pre * sigmoid(pre)).astype(BF)
+        pre_in[rows, :] = pre
         for j in range(4):
             lanes = lanes_of(j)
             taps, bias = sig_tap_rows(j, taps_ref, bias_ref)
@@ -640,8 +678,9 @@
 def states_kernel(
     halo_ref,
     xs,
-    xm,
-    actm,
+    xi,
+    xo,
+    act_in,
     weighted_s,
     sgrad_s,
     step_e,
@@ -672,7 +711,7 @@
             first = xs[segment, 8:24, lanes]
         else:
             taps, bias = map_tap_rows(j - 4, mine_ref)
-            first = xm[segment, 8:24, lanes_of(j - 4)]
+            first = xi[segment, 8:24, :] if j == 4 else xo[segment, 8:24, :]
         pre = conv(jnp.concatenate([edge[:, lanes], first], axis=0), taps, bias)
         value = (pre * sigmoid(pre)).astype(BF)
         act_p[:, lanes] = value
@@ -684,7 +723,7 @@
     every = slice(0, 4 * TILE)
     for i in range(4):
         s_s[i] = mm(
-            patched(actm, lanes_of(0), act_p, lanes_of(4), i, high),
+            patched(act_in, lanes_of(0), act_p, lanes_of(4), i, high),
             patched(weighted_s, every, weighted_p, every, i, high),
             TN,
         )
@@ -692,19 +731,11 @@
     f_a = ends[1] * s_s[0] + s_s[1]
     f_b = ends[3] * s_s[2] + s_s[3]
     d_b = ends[2] * ends[3]
-    mid_ref[0:TILE, :] = jnp.where(high, d_b * f_a + f_b, f_a).astype(BF)
+    mid_ref[...] = jnp.where(high, d_b * f_a + f_b, f_a).astype(BF)
     grown = sgrad_s[rows16, :].astype(F32)
     out_rows = act_p[:, lanes_of(5)].astype(F32)
     known = jnp.where(ids((16, TILE), 0) < 3, out_rows, 0.0).astype(BF)
     delta_ref[...] = mm(known, grown.astype(BF), TN)
-    hi, mid, lo = [part.astype(F32) for part in split3(ends[0] * ends[1] * d_b)]
-    pieces = [hi, mid, lo, grown[0:1], grown[1:2], grown[2:3]]
-    for k in range(3):
-        pieces.append(
-            jnp.concatenate([out_rows[k : k + 1], jnp.zeros((1, 3 * TILE), F32)], axis=1)
-        )
-    pieces.append(jnp.zeros((7, 4 * TILE), F32))
-    mid_ref[TILE : TILE + 16, :] = jnp.concatenate(pieces, axis=0).astype(BF)
 
 
 def slope_of(pre):
@@ -744,9 +775,11 @@
 def second_kernel(
     dp,
     acts,
-    actm,
+    act_in,
+    act_out,
     pres,
-    prem,
+    pre_in,
+    pre_out,
     scaled_s,
     step_e,
     toend_e,
@@ -754,6 +787,9 @@
     act_p,
     pre_p,
     scaled_p,
+    halo_ref,
+    xo,
+    mine_ref,
     skip_ref,
     base_ref,
     coef_ref,
@@ -762,19 +798,31 @@
     gsum_ref,
     stepsum_ref,
     skip_acc,
+    left_ref,
 ):
     quad, r, f = place()
     high = quad == 1
     skip_row = skip_rows(skip_ref, r)
     skip_acc[...] = jnp.zeros_like(skip_acc)
+    got = halo_ref[...].astype(F32)
+    ends_at = slice(2 * TILE, 2 * TILE + 8)
+    before = jnp.where(high, xo[1, ends_at, :], xo[0, ends_at, :])
+    taps, bias = map_tap_rows(1, mine_ref)
+    pre = conv(jnp.concatenate([before, got[0:8, lanes_of(5)]], axis=0), taps, bias)
+    three = ids((8, TILE), 0) < 3
+    out_rows = jnp.where(three, pre * sigmoid(pre), 0.0)
+    out_rows = jnp.concatenate([out_rows, jnp.zeros((8, TILE), F32)], axis=0).astype(BF)
+    grown = pltpu.roll(got[:, 0 : 4 * TILE], 13, 0)
+    grown = jnp.where(ids((16, 4 * TILE), 0) < 3, grown, 0.0).astype(BF)
+    left_ref[...] = mm(out_rows, grown, TN)
     half_lane = ids((TILE, TILE), 1) < HALF
     row8 = ids((8, TILE), 0)
     col_q = ids((TILE, TILE), 1)
     seen = ids((TILE, TILE), 0) <= col_q
     for i in range(4):
         rows = slice(i * TILE, (i + 1) * TILE)
-        in_map = patched(actm, lanes_of(0), act_p, lanes_of(4), i, high)
-        out_map = patched(actm, lanes_of(1), act_p, lanes_of(5), i, high)
+        in_map = patched(act_in, lanes_of(0), act_p, lanes_of(4), i, high)
+        out_map = patched(act_out, lanes_of(0), act_p, lanes_of(5), i, high)
         score = mm(in_map, out_map, NT)
         ds8 = ds_r[8 * i : 8 * i + 8, :]
         cols = columns(ds8)
@@ -809,9 +857,9 @@
             products.append(diag * sigf)
             skip_acc[:, lanes] += eights(dyf * sigf)
         stepsum_ref[8 * i : 8 * i + 8, :] = head_sums(products)[0]
-        for j in range(2):
+        for j, pre_ref in enumerate((pre_in, pre_out)):
             mslope_ref[rows, lanes_of(j)] = slope_of(
-                patched(prem, lanes_of(j), pre_p, lanes_of(4 + j), i, high)
+                patched(pre_ref, lanes_of(0), pre_p, lanes_of(4 + j), i, high)
             )
         gs = grad_score.astype(BF)
         gmap_ref[rows, lanes_of(0)] = mm(gs, out_map)
@@ -868,6 +916,8 @@
 def maps_kernel(
     midg_ref,
     midf_ref,
+    halo_ref,
+    left_ref,
     s_s,
     t_s,
     delta_ref,
@@ -877,7 +927,8 @@
     weighted_p,
     sgrad_s,
     gmap_ref,
-    xm,
+    xi,
+    xo,
     edge_ref,
     mine_ref,
     one_ref,
@@ -893,14 +944,10 @@
     high = quad == 1
     even = lax.rem(f, 2) == 0
     ends = end_rows_of(exp_e)
-    f_in = midf_ref[0:TILE, :].astype(F32)
-    extra = midf_ref[TILE : TILE + 16, :].astype(F32)
-    row16 = ids((16, 4 * TILE), 0)
-    across = jnp.sum(jnp.where(row16 < 3, extra, 0.0), axis=0, keepdims=True)
-    left_out = jnp.logical_and(row16 >= 3, row16 < 6)
-    grown = jnp.where(left_out, extra, 0.0).astype(BF)
-    out_rows = jnp.where(left_out[:, 0:TILE], pltpu.roll(extra[:, 0:TILE], 13, 0), 0.0).astype(BF)
-    g_in = midg_ref[...].astype(F32) + mm(out_rows, grown, TN)
+    f_in = midf_ref[...].astype(F32)
+    got = halo_ref[:, 0 : 4 * TILE].astype(F32)
+    across = got[0:1] + got[1:2] + got[2:3]
+    g_in = midg_ref[...].astype(F32) + left_ref[...]
     t2 = t_s[2] + jnp.where(high, 0.0, delta_ref[...])
     f_a = ends[1] * s_s[0] + s_s[1]
     h_s[0] = jnp.where(high, f_in, 0.0)
@@ -929,7 +976,9 @@
         for j in range(2):
             here = grads[j] * mslope_ref[rows, lanes_of(j)]
             gm[i // 2, base : base + TILE, lanes_of(j)] = here
-            tap_sums(here, xm, edge_ref, i, lanes_of(j), lanes_of(4 + j), high, sums[j])
+            tap_sums(
+                here, (xi, xo)[j], edge_ref, i, lanes_of(0), lanes_of(4 + j), high, sums[j]
+            )
     fill_pads(gm, high)
     for i in range(4):
         rows = slice(i * TILE, (i + 1) * TILE)
@@ -962,7 +1011,8 @@
     xs,
     dp,
     acts,
-    actm,
+    act_in,
+    act_out,
     edge_ref,
     act_p,
     toend_e,
@@ -998,8 +1048,8 @@
         rows = slice(i * TILE, (i + 1) * TILE)
         at8 = slice(8 * i, 8 * i + 8)
         base = (i % 2) * TILE
-        off = mm(patched(actm, lanes_of(1), act_p, lanes_of(5), i, high), hlow_ref[i])
-        gw = mm(patched(actm, lanes_of(0), act_p, lanes_of(4), i, high), clow_ref[i])
+        off = mm(patched(act_out, lanes_of(0), act_p, lanes_of(5), i, high), hlow_ref[i])
+        gw = mm(patched(act_in, lanes_of(0), act_p, lanes_of(4), i, high), clow_ref[i])
         end_row = endrow_ref[i : i + 1, :]
         gsum = gsum_ref[at8, :]
         end_sum = jnp.zeros((8, TILE), F32)
@@ -1242,13 +1292,14 @@
     sig_bias_row = sig_bias[None, :]
     *packed, map_params = call(
         pack_kernel,
-        (shape(TILE + HALF + 16, narrow, kind=BF),) * 4 + (shape(8, owned),),
+        (shape(TILE + HALF // 2 + 16, narrow, kind=BF),) * 4 + (shape(8, owned),),
         [hbm, hbm, hbm, hbm, vmem, vmem],
         (vmem,) * 5,
         [
             pltpu.VMEM((32, TILE), F32),
             pltpu.VMEM((16, sig_width), BF),
-            pltpu.SemaphoreType.DMA((22,)),
+            pltpu.VMEM((16, map_raw.shape[1] // 2), BF),
+            pltpu.SemaphoreType.DMA((23,)),
         ],
         60,
         10**6,
@@ -1258,16 +1309,19 @@
     map_two = lax.ppermute(map_params, "fsdp", back(ROUTE_TWO))
     packed = call(
         pack_sig_kernel,
-        (shape(TILE, narrow, kind=BF),) * 4,
-        [hbm],
+        (shape(TILE + HALF // 2, narrow, kind=BF),) * 4,
+        [hbm, hbm],
         (vmem,) * 4,
-        [pltpu.SemaphoreType.DMA((4,))],
+        [pltpu.SemaphoreType.DMA((20,))],
         60,
         10**6,
-    )(sig_raw)
+    )(sig_raw, map_raw)
     own_u, own_v = call(
         own_kernel,
-        (shape(TILE + HALF + 16, narrow, kind=BF), shape(TILE, narrow, kind=BF)),
+        (
+            shape(TILE + HALF // 2 + 16, narrow, kind=BF),
+            shape(TILE + HALF // 2, narrow, kind=BF),
+        ),
         [vmem] * 2,
         (vmem,) * 2,
         [],
@@ -1276,14 +1330,14 @@
     )(us[0], packed[0])
     us[0] = own_u
     vs = [own_v] + [lax.ppermute(packed[k], "ctx", inside[k]) for k in (1, 2, 3)]
-    midg, dp, xm, actm, prem, sgrad, step_e, toend_e, exp_e, t_s, step_r, ds_r, sig_r, *small = call(
+    midg, dp, xo, act_out, pre_out, sgrad, step_e, toend_e, exp_e, t_s, step_r, ds_r, sig_r, *small = call(
         grads_kernel,
         (
             shape(TILE, narrow, kind=BF),
             shape(total, narrow, kind=BF),
-            shape(2, 2 * TILE + 8, 2 * TILE),
-            shape(total, 2 * TILE, kind=BF),
-            shape(total, 2 * TILE),
+            shape(2, 2 * TILE + 8, TILE),
+            shape(total, TILE, kind=BF),
+            shape(total, TILE),
             shape(total, narrow, kind=BF),
             shape(total, narrow),
             shape(total, narrow),
@@ -1304,7 +1358,7 @@
     mine, halo = small
     halo = lax.ppermute(halo, "ctx", over)
     midg = lax.ppermute(midg, "ctx", over)
-    xs, acts, pres, scaled, weighted = call(
+    xs, acts, pres, scaled, weighted, xi, act_in, pre_in = call(
         first_kernel,
         (
             shape(2, 2 * TILE + 8, narrow),
@@ -1312,17 +1366,20 @@
             shape(total, narrow),
             shape(total, narrow, kind=BF),
             shape(total, narrow, kind=BF),
+            shape(2, 2 * TILE + 8, TILE),
+            shape(total, TILE, kind=BF),
+            shape(total, TILE),
         ),
-        [vmem] * 8,
-        (vmem,) * 5,
+        [vmem] * 9,
+        (vmem,) * 8,
         [],
         24,
         2 * 10**9,
-    )(vs[0], vs[3], vs[2], vs[1], step_e, toend_e, sig_taps, sig_bias_row)
+    )(vs[0], vs[3], vs[2], vs[1], step_e, toend_e, sig_taps, sig_bias_row, mine)
     midf, s_s, delta, edge, act_p, pre_p, scaled_p, weighted_p = call(
         states_kernel,
         (
-            shape(TILE + 16, narrow, kind=BF),
+            shape(TILE, narrow, kind=BF),
             shape(4, TILE, narrow),
             shape(TILE, narrow),
             shape(8, wide),
@@ -1331,14 +1388,14 @@
             shape(16, narrow, kind=BF),
             shape(16, narrow, kind=BF),
         ),
-        [vmem] * 12,
+        [vmem] * 13,
         (vmem,) * 8,
         [],
         24,
         10**9,
-    )(halo, xs, xm, actm, weighted, sgrad, step_e, toend_e, exp_e, sig_taps, sig_bias_row, mine)
+    )(halo, xs, xi, xo, act_in, weighted, sgrad, step_e, toend_e, exp_e, sig_taps, sig_bias_row, mine)
     midf = lax.ppermute(midf, "ctx", over)
-    base, coef, mslope, gmap, gsum, stepsum, skips = call(
+    base, coef, mslope, gmap, gsum, stepsum, skips, left = call(
         second_kernel,
         (
             shape(total, narrow),
@@ -1348,18 +1405,21 @@
             shape(32, TILE),
             shape(32, TILE),
             shape(8, narrow),
+            shape(TILE, narrow),
         ),
-        [vmem] * 12 + [smem],
-        (vmem,) * 7,
+        [vmem] * 17 + [smem],
+        (vmem,) * 8,
         [],
         24,
         5 * 10**9,
     )(
         dp,
         acts,
-        actm,
+        act_in,
+        act_out,
         pres,
-        prem,
+        pre_in,
+        pre_out,
         scaled,
         step_e,
         toend_e,
@@ -1367,6 +1427,9 @@
         act_p,
         pre_p,
         scaled_p,
+        halo,
+        xo,
+        mine,
         skip_gain,
     )
     one, two, hlow, clow, endrow = call(
@@ -1378,7 +1441,7 @@
             shape(4, TILE, narrow, kind=BF),
             shape(8, narrow),
         ),
-        [vmem] * 14,
+        [vmem] * 17,
         (vmem,) * 5,
         [
             pltpu.VMEM((4, TILE, narrow), F32),
@@ -1390,6 +1453,8 @@
     )(
         midg,
         midf,
+        halo,
+        left,
         s_s,
         t_s,
         delta,
@@ -1399,7 +1464,8 @@
         weighted_p,
         sgrad,
         gmap,
-        xm,
+        xi,
+        xo,
         edge,
         mine,
     )
@@ -1413,7 +1479,7 @@
             shape(8, narrow),
             shape(24, TILE),
         ),
-        [vmem] * 19 + [smem],
+        [vmem] * 20 + [smem],
         (vmem,) * 4,
         [],
         24,
@@ -1425,7 +1491,8 @@
         xs,
         dp,
         acts,
-        actm,
+        act_in,
+        act_out,
         edge,
         act_p,
         toend_e,

time: 62.9 us -> 61 us (0.970)
  waiting for transfers between devices: 13.5 us -> 10.9 us
  starting transfers between devices: 26.7 us -> 28 us
  local copies, waits for them, and re-layouts: 1.86 us -> 0.95 us
    ppermute x1, waiting for transfers between devices: 6.24 us -> 3.39 us  [shards_quad(): midf = lax.ppermute(midf, 'ctx', over)]
    ppermute x6, waiting for transfers between devices: 1.65 us -> 2.84 us  [shards_quad(): lax.ppermute(packed[k], 'ctx', inside[k])]
    unnamed x14, local copies, waits for them, and re-layouts: 1.86 us -> 0.95 us
  transfers between devices with their start and end apart: 20 -> 20, of which waited for: 9 -> 8; matrix products, arithmetic and copies ran while one was open for 0% -> 0% of each run, Pallas kernels for 23% -> 24%
where the time goes in v6:
time: 61 us; the launch traced here: 60.6 us
  starting transfers between devices  28 us (46%)
  Pallas kernels  19.9 us (33%)
  waiting for transfers between devices  10.9 us (18%)
  local copies, waits for them, and re-layouts  0.95 us (2%)
  between operations  0.83 us (1%)
    ppermute x6, starting transfers between devices, shards_quad(): lax.ppermute(packed[k], 'ctx', inside[k])  8.25 us
    pallas_call x1, Pallas kernels, shards_quad(): call(second_kernel, (shape(total, narrow), shape(total, narrow), shape(to...  4.65 us
    ppermute x3, starting transfers between devices, shards_quad(): ws = [ws[0]] + [lax.ppermute(ws[k], 'ctx', inside[k]) for k in (1, 2, 3)]  3.96 us
    ppermute x1, waiting for transfers between devices, shards_quad(): midf = lax.ppermute(midf, 'ctx', over)  3.39 us
    pallas_call x1, Pallas kernels, shards_quad(): call(third_kernel, (shape(2, 2 * TILE + 8, narrow), shape(8, 8, TILE), sh...  3.26 us
    ppermute x1, starting transfers between devices, shards_quad(): two = lax.ppermute(two, 'fsdp', ROUTE_TWO)  3.26 us
    ppermute x1, starting transfers between devices, shards_quad(): other = lax.ppermute(cross, 'ctx', over)  3.23 us
    ppermute x3, waiting for transfers between devices, shards_quad(): ws = [ws[0]] + [lax.ppermute(ws[k], 'ctx', inside[k]) for k in (1, 2, 3)]  3.1 us
  transfers between devices with their start and end apart: 20, of which 8 were waited for; matrix products, arithmetic and copies ran while one was open for 0% of the time, Pallas kernels for 24%

profile of v6, /device:TPU:0, one launch (start us, length us, event | category | flops | bytes accessed | tf_op | source)
XLA Modules:
  0.0 60.6 jit_solution(8498256738777055458)
XLA Ops:
  0.6 3.0 %shard_map.186 = (bf16[176,512]{1,0:T(8,128)(2,1)}, bf16[176,512]{1,0:T(8,128)(2,1)}, bf16[176,512]{1,0:T(8,128)(2,1)}, bf16[176,512]{1,0:T(8,128)(2,1)}, f32[8,512]{1,0:T(8,128)}) custom-call(bf16[128,2048]{1,0:T(8,128)(2,1)} %sig_ref.3, bf16[128,2048]{1,0:T(8,128)(2,1)} %map_ref.3, f32[32,128]{1,0:T(8,128)} %bitcast.11, bf16[128,2048]{1,0:T(8,128)(2,1)} %dy_ref.1, ...), custom_call_target="tpu_custom_call" | custom-call | flops 1000000 | bytes 10000 | tf_op jit(solution)/shard_map/pallas_call | solution.py:1293
  3.7 0.0 copy-start
  3.7 0.0 copy-start.4
  3.7 0.0 copy-start.6
  3.7 4.0 %collective-permute-start = (bf16[176,512]{1,0:T(8,128)(2,1)}, bf16[176,512]{1,0:T(8,128)(2,1)S(1)}, u32[]{:S(2)}, u32[]{:S(2)}) collective-permute-start(bf16[176,512]{1,0:T(8,128)(2,1)} %get-tuple-element.90), channel_id=1, source_target_pairs={{0,12},{4,8},{8,4},{12,0},{16,28},{20,24},{24,20},{28,16},{1,13},{... | collective-permute-start | bytes 540680 | tf_op jit(solution)/shard_map/ppermute | solution.py:1307
  7.8 0.4 collective-permute-start.1
  8.2 0.2 collective-permute-start.2
  8.4 0.0 collective-permute-start.4
  8.4 1.4 %collective-permute-start.3 = (f32[8,512]{1,0:T(8,128)}, f32[8,512]{1,0:T(8,128)S(1)}, u32[]{:S(2)}, u32[]{:S(2)}) collective-permute-start(f32[8,512]{1,0:T(8,128)} %get-tuple-element.93), channel_id=1, source_target_pairs={{0,0},{1,2},{2,1},{3,3},{4,4},{5,6},{6,5},{7,7},{8,8},{9,10},{10,9... | collective-permute-start | bytes 49160 | tf_op jit(solution)/shard_map/ppermute | solution.py:1308
  9.8 2.2 %shard_map.187 = (bf16[160,512]{1,0:T(8,128)(2,1)}, bf16[160,512]{1,0:T(8,128)(2,1)}, bf16[160,512]{1,0:T(8,128)(2,1)}, bf16[160,512]{1,0:T(8,128)(2,1)}) custom-call(bf16[128,2048]{1,0:T(8,128)(2,1)} %sig_ref.3, bf16[128,2048]{1,0:T(8,128)(2,1)} %map_ref.3), custom_call_target="tpu_custom_call" | custom-call | flops 1000000 | bytes 10000 | tf_op jit(solution)/shard_map/pallas_call | solution.py:1310
  12.0 0.0 copy-done
  12.0 0.0 copy-start.1
  12.0 0.9 %copy-done.1 = bf16[160,512]{1,0:T(8,128)(2,1)S(1)} copy-done((bf16[160,512]{1,0:T(8,128)(2,1)S(1)}, bf16[160,512]{1,0:T(8,128)(2,1)}, u32[]{:S(2)}) %copy-start.1) | copy-done | bytes 163864
  13.0 0.0 collective-permute-done.4.two_taps
  13.0 2.9 %collective-permute-start.7 = (bf16[160,512]{1,0:T(8,128)(2,1)}, bf16[160,512]{1,0:T(8,128)(2,1)S(1)}, u32[]{:S(2)}, u32[]{:S(2)}) collective-permute-start(bf16[160,512]{1,0:T(8,128)(2,1)} %get-tuple-element.97), channel_id=1, source_target_pairs={{0,12},{4,8},{8,4},{12,0},{16,28},{20,24},{24,20},{28,16},{1,13},{... | collective-permute-start | bytes 491528 | tf_op jit(solution)/shard_map/ppermute | solution.py:1332
  15.9 0.0 collective-permute-done.3.one_taps
  15.9 0.5 collective-permute-start.8
  16.4 0.0 collective-permute-done.u3
  16.4 0.2 collective-permute-start.9
  16.6 0.0 collective-permute-done.1.u2
  16.6 0.0 collective-permute-done.2.u1
  16.6 0.0 copy-done.4
  16.6 0.0 copy-done.6
  16.6 0.0 copy-start.2
  16.6 0.0 copy-start.3
  16.6 2.1 %shard_map.189 = (bf16[128,512]{1,0:T(8,128)(2,1)S(1)}, bf16[512,512]{1,0:T(8,128)(2,1)S(1)}, f32[2,264,128]{2,1,0:T(8,128)S(1)}, bf16[512,128]{1,0:T(8,128)(2,1...) custom-call(bf16[176,512]{1,0:T(8,128)(2,1)S(1)} %get-tuple-element., ...), custom_call_target="tpu_custom_call" | custom-call | flops 2000000000 | bytes 20000000 | tf_op jit(solution)/shard_map/pallas_call | solution.py:1333
  18.7 2.9 %collective-permute-start.6 = (bf16[16,768]{1,0:T(8,128)(2,1)S(1)}, bf16[16,768]{1,0:T(8,128)(2,1)S(1)}, u32[]{:S(2)}, u32[]{:S(2)}) collective-permute-start(bf16[16,768]{1,0:T(8,128)(2,1)S(1)} %get-tuple-element.95), channel_id=1, source_target_pairs={{0,16},{4,20},{8,24},{12,28},{16,0},{20,4},{24,8},{28,12},{1,17},{... | collective-permute-start | bytes 73736 | tf_op jit(solution)/shard_map/ppermute | solution.py:1359
  21.7 0.1 collective-permute-start.5
  21.7 0.0 collective-permute-done.7.v3
  21.7 1.6 %collective-permute-done.8.v2 = bf16[160,512]{1,0:T(8,128)(2,1)S(1)} collective-permute-done((bf16[160,512]{1,0:T(8,128)(2,1)}, bf16[160,512]{1,0:T(8,128)(2,1)S(1)}, u32[]{:S(2)}, u32[]{:S(2)}) %collective-permute-start.8) | collective-permute-done | bytes 163872 | tf_op jit(solution)/shard_map/ppermute | solution.py:1332
  23.3 1.2 %collective-permute-done.9.v1 = bf16[160,512]{1,0:T(8,128)(2,1)S(1)} collective-permute-done((bf16[160,512]{1,0:T(8,128)(2,1)}, bf16[160,512]{1,0:T(8,128)(2,1)S(1)}, u32[]{:S(2)}, u32[]{:S(2)}) %collective-permute-start.9) | collective-permute-done | bytes 163872 | tf_op jit(solution)/shard_map/ppermute | solution.py:1332
  24.6 0.0 copy-done.2
  24.6 0.0 copy-done.3
  24.6 1.3 %shard_map.190 = (f32[2,264,512]{2,1,0:T(8,128)S(1)}, bf16[512,512]{1,0:T(8,128)(2,1)S(1)}, f32[512,512]{1,0:T(8,128)S(1)}, bf16[512,512]{1,0:T(8,128)(2,1)S(1)}...) custom-call(bf16[160,512]{1,0:T(8,128)(2,1)S(1)} %get-tuple-element., ...), custom_call_target="tpu_custom_call" | custom-call | flops 2000000000 | bytes 20000000 | tf_op jit(solution)/shard_map/pallas_call | solution.py:1361
  25.8 0.0 collective-permute-done.6.halo_ref
  25.8 0.0 copy-start.5
  25.9 0.4 shard_map.191
  26.3 2.7 %collective-permute-start.10 = (bf16[128,512]{1,0:T(8,128)(2,1)S(1)}, bf16[128,512]{1,0:T(8,128)(2,1)S(1)}, u32[]{:S(2)}, u32[]{:S(2)}) collective-permute-start(bf16[128,512]{1,0:T(8,128)(2,1)S(1)} %get-tuple-element.110), channel_id=1, source_target_pairs={{0,16},{4,20},{8,24},{12,28},{16,0},{20,4},{24,8},{28,12},{1,17},{... | collective-permute-start | bytes 393224 | tf_op jit(solution)/shard_map/ppermute | solution.py:1397
  29.0 4.6 %shard_map.192 = (f32[512,512]{1,0:T(8,128)S(1)}, f32[512,512]{1,0:T(8,128)S(1)}, f32[512,256]{1,0:T(8,128)S(1)}, f32[512,256]{1,0:T(8,128)S(1)}, f32[32,128]{1,...) custom-call(bf16[512,512]{1,0:T(8,128)(2,1)S(1)} %get-tuple-element.111.dp, ...), custom_call_target="tpu_custom_call" | custom-call | flops 5000000000 | bytes 50000000 | tf_op jit(solution)/shard_map/pallas_call | solution.py:1398
  33.7 0.0 collective-permute-done.5.midg_ref
  33.7 3.4 %collective-permute-done.10.midf_ref = bf16[128,512]{1,0:T(8,128)(2,1)S(1)} collective-permute-done((bf16[128,512]{1,0:T(8,128)(2,1)S(1)}, bf16[128,512]{1,0:T(8,128)(2,1)S(1)}, u32[]{:S(2)}, u32[]{:S(2)}) %collective-permute-start.10) | collective-permute-done | bytes 131104 | tf_op jit(solution)/shard_map/ppermute | solution.py:1397
  37.1 1.1 %shard_map.193 = (bf16[544,128]{1,0:T(8,128)(2,1)S(1)}, bf16[544,128]{1,0:T(8,128)(2,1)S(1)}, bf16[4,128,512]{2,1,0:T(8,128)(2,1)S(1)}, bf16[4,128,512]{2,1,0:T(8,128)(2,1)S(1)}, f32[8,512]{1,0:T(8,128)S(1)}) custom-call(bf16[128,512]{1,0:T(8,128)(2,1)S(1)} %collective-permute-done.5.midg_ref, bf16[128,512]{1,0:T(8,128)(2,1)S(1)} %collective-permute-done.10.midf_ref, ...), custom_call_target="tpu_custom_call" | custom-call | flops 2000000000 | bytes 20000000 | tf_op jit(solution)/shard_map/pallas_call | solution.py:1435
  38.2 0.7 %collective-permute-start.14 = (bf16[544,128]{1,0:T(8,128)(2,1)S(1)}, bf16[544,128]{1,0:T(8,128)(2,1)S(1)}, u32[]{:S(2)}, u32[]{:S(2)}) collective-permute-start(bf16[544,128]{1,0:T(8,128)(2,1)S(1)} %get-tuple-element.147), channel_id=1, source_target_pairs={{0,0},{2,1},{1,2},{3,3},{4,4},{6,5},{5,6},{7,7},{8,8},{10,9},{9,10... | collective-permute-start | bytes 417800 | tf_op jit(solution)/shard_map/ppermute | solution.py:1472
  38.9 3.3 %collective-permute-start.15 = (bf16[544,128]{1,0:T(8,128)(2,1)S(1)}, bf16[544,128]{1,0:T(8,128)(2,1)S(1)}, u32[]{:S(2)}, u32[]{:S(2)}) collective-permute-start(bf16[544,128]{1,0:T(8,128)(2,1)S(1)} %get-tuple-element.148), channel_id=1, source_target_pairs={{0,2},{2,3},{1,0},{3,1},{4,6},{6,7},{5,4},{7,5},{8,10},{10,11},{9,... | collective-permute-start | bytes 417800 | tf_op jit(solution)/shard_map/ppermute | solution.py:1473
  42.1 3.3 %shard_map.194 = (f32[2,264,512]{2,1,0:T(8,128)S(1)}, f32[8,8,128]{2,1,0:T(8,128)S(1)}, f32[8,512]{1,0:T(8,128)S(1)}, f32[24,128]{1,0:T(8,128)S(1)}) custom-call(bf16[4,128,512]{2,1,0:T(8,128)(2,1)S(1)} %get-tuple-element.130.hlow_ref, bf16[4,128,512]{2,1,0:T(8,128)(2,1)S(1)} %get-tuple-element.131.clow_ref, f32[8,512]{1,0:T(8,128)S(1)} %get-tuple-element.132.endrow_ref, ...), custom_call_target="tpu_custom_call" | custom-call | flops 3000000000 | bytes 30000000 | tf_op jit(solution)/shard_map/pallas_call | solution.py:1474
  45.4 0.6 shard_map.195
  46.0 0.5 collective-permute-start.11
  46.5 0.0 collective-permute-done.14.one_ref
  46.5 0.0 collective-permute-done.15.two_ref
  46.5 3.2 %collective-permute-start.16 = (bf16[32,512]{1,0:T(8,128)(2,1)S(1)}, bf16[32,512]{1,0:T(8,128)(2,1)S(1)}, u32[]{:S(2)}, u32[]{:S(2)}) collective-permute-start(bf16[32,512]{1,0:T(8,128)(2,1)S(1)} %shard_map.196.own_ref), channel_id=1, source_target_pairs={{0,16},{4,20},{8,24},{12,28},{16,0},{20,4},{24,8},{28,12},{1,17},{... | collective-permute-start | bytes 98312 | tf_op jit(solution)/shard_map/ppermute | solution.py:1520
  49.8 0.0 collective-permute-start.12
  49.8 0.9 %collective-permute-start.13 = (bf16[128,512]{1,0:T(8,128)(2,1)S(1)}, bf16[128,512]{1,0:T(8,128)(2,1)S(1)}, u32[]{:S(2)}, u32[]{:S(2)}) collective-permute-start(bf16[128,512]{1,0:T(8,128)(2,1)S(1)} %get-tuple-element.144), channel_id=1, source_target_pairs={{0,4},{4,0},{8,12},{12,8},{16,20},{20,16},{24,28},{28,24},{1,5},{5... | collective-permute-start | bytes 393224 | tf_op jit(solution)/shard_map/ppermute | solution.py:1530
  50.7 1.1 %collective-permute-done.16.other_ref = bf16[32,512]{1,0:T(8,128)(2,1)S(1)} collective-permute-done((bf16[32,512]{1,0:T(8,128)(2,1)S(1)}, bf16[32,512]{1,0:T(8,128)(2,1)S(1)}, u32[]{:S(2)}, u32[]{:S(2)}) %collective-permute-start.16) | collective-permute-done | bytes 32800 | tf_op jit(solution)/shard_map/ppermute | solution.py:1520
  51.8 0.1 shard_map.197
  51.9 2.5 %collective-permute-start.17 = (bf16[96,512]{1,0:T(8,128)(2,1)S(1)}, bf16[96,512]{1,0:T(8,128)(2,1)S(1)}, u32[]{:S(2)}, u32[]{:S(2)}) collective-permute-start(bf16[96,512]{1,0:T(8,128)(2,1)S(1)} %get-tuple-element.151), channel_id=1, source_target_pairs={{0,12},{4,8},{8,4},{12,0},{16,28},{20,24},{24,20},{28,16},{1,13},{... | collective-permute-start | bytes 294920 | tf_op jit(solution)/shard_map/ppermute | solution.py:1540
  54.4 0.1 collective-permute-start.18
  54.5 0.0 collective-permute-done.11.y3
  54.5 1.4 %collective-permute-start.19 = (bf16[96,512]{1,0:T(8,128)(2,1)S(1)}, bf16[96,512]{1,0:T(8,128)(2,1)S(1)}, u32[]{:S(2)}, u32[]{:S(2)}) collective-permute-start(bf16[96,512]{1,0:T(8,128)(2,1)S(1)} %get-tuple-element.153), channel_id=1, source_target_pairs={{0,4},{4,0},{8,12},{12,8},{16,20},{20,16},{24,28},{28,24},{1,5},{5... | collective-permute-start | bytes 294920 | tf_op jit(solution)/shard_map/ppermute | solution.py:1540
  55.9 0.0 collective-permute-done.12.y2
  55.9 0.5 collective-permute-done.13.y1
  56.3 2.4 %collective-permute-done.17.w3 = bf16[96,512]{1,0:T(8,128)(2,1)S(1)} collective-permute-done((bf16[96,512]{1,0:T(8,128)(2,1)S(1)}, bf16[96,512]{1,0:T(8,128)(2,1)S(1)}, u32[]{:S(2)}, u32[]{:S(2)}) %collective-permute-start.17) | collective-permute-done | bytes 98336 | tf_op jit(solution)/shard_map/ppermute | solution.py:1540
  58.7 0.6 %collective-permute-done.18.w2 = bf16[96,512]{1,0:T(8,128)(2,1)S(1)} collective-permute-done((bf16[96,512]{1,0:T(8,128)(2,1)S(1)}, bf16[96,512]{1,0:T(8,128)(2,1)S(1)}, u32[]{:S(2)}, u32[]{:S(2)}) %collective-permute-start.18) | collective-permute-done | bytes 98336 | tf_op jit(solution)/shard_map/ppermute | solution.py:1540
  59.3 0.1 collective-permute-done.19.w1
  59.4 1.1 %shard_map.198 = (f32[128,2048]{1,0:T(8,128)}, f32[128,512]{1,0:T(8,128)}, f32[32,128]{1,0:T(8,128)}, f32[4,2048]{1,0:T(4,128)}, f32[4,512]{1,0:T(4,128)}, /*ind...) custom-call(bf16[128,512]{1,0:T(8,128)(2,1)S(1)} %get-tuple-element.141.y0, ...), custom_call_target="tpu_custom_call" | custom-call | flops 1000000 | bytes 10000 | tf_op jit(solution)/shard_map/pallas_call | solution.py:1541
  (3 shorter events, 0.0 us)
Async XLA Ops:
  3.7 8.3 %copy-start = (bf16[176,512]{1,0:T(8,128)(2,1)S(1)}, bf16[176,512]{1,0:T(8,128)(2,1)}, u32[]{:S(2)}) copy-start(bf16[176,512]{1,0:T(8,128)(2,1)} %get-tuple-element.87.u_ref) | copy-start | bytes 540676
  3.7 12.9 %copy-start.4 = (f32[32]{0:T(128)S(1)}, f32[32]{0:T(128)}, u32[]{:S(2)}) copy-start(f32[32]{0:T(128)} %dtb_ref.1) | copy-start | bytes 388
  3.7 12.9 %copy-start.6 = (f32[32]{0:T(128)S(1)}, f32[32]{0:T(128)}, u32[]{:S(2)}) copy-start(f32[32]{0:T(128)} %alog_ref.3) | copy-start | bytes 388
  3.7 12.6 %collective-permute-start = (bf16[176,512]{1,0:T(8,128)(2,1)}, bf16[176,512]{1,0:T(8,128)(2,1)S(1)}, u32[]{:S(2)}, u32[]{:S(2)}) collective-permute-start(bf16[176,512]{1,0:T(8,128)(2,1)} %get-tuple-element.90), channel_id=1, source_target_pairs={{0,12},{4,8},{8,4},{12,0},{16,28},{20,24},{24,20},{28,16},{1,13},{... | collective-permute-start | bytes 540680 | tf_op jit(solution)/shard_map/ppermute | solution.py:1307
  7.8 8.8 %collective-permute-start.1 = (bf16[176,512]{1,0:T(8,128)(2,1)}, bf16[176,512]{1,0:T(8,128)(2,1)S(1)}, u32[]{:S(2)}, u32[]{:S(2)}) collective-permute-start(bf16[176,512]{1,0:T(8,128)(2,1)} %get-tuple-element.91), channel_id=1, source_target_pairs={{0,8},{4,12},{8,0},{12,4},{16,24},{20,28},{24,16},{28,20},{1,9},{5... | collective-permute-start | bytes 540680 | tf_op jit(solution)/shard_map/ppermute | solution.py:1307
  8.2 8.4 %collective-permute-start.2 = (bf16[176,512]{1,0:T(8,128)(2,1)}, bf16[176,512]{1,0:T(8,128)(2,1)S(1)}, u32[]{:S(2)}, u32[]{:S(2)}) collective-permute-start(bf16[176,512]{1,0:T(8,128)(2,1)} %get-tuple-element.92), channel_id=1, source_target_pairs={{0,4},{4,0},{8,12},{12,8},{16,20},{20,16},{24,28},{28,24},{1,5},{5... | collective-permute-start | bytes 540680 | tf_op jit(solution)/shard_map/ppermute | solution.py:1307
  8.4 4.6 %collective-permute-start.4 = (f32[8,512]{1,0:T(8,128)}, f32[8,512]{1,0:T(8,128)S(1)}, u32[]{:S(2)}, u32[]{:S(2)}) collective-permute-start(f32[8,512]{1,0:T(8,128)} %get-tuple-element.93), channel_id=1, source_target_pairs={{2,0},{3,2},{0,1},{1,3},{6,4},{7,6},{4,5},{5,7},{10,8},{11,10},{8,... | collective-permute-start | bytes 49160 | tf_op jit(solution)/shard_map/ppermute | solution.py:1309
  8.4 7.5 %collective-permute-start.3 = (f32[8,512]{1,0:T(8,128)}, f32[8,512]{1,0:T(8,128)S(1)}, u32[]{:S(2)}, u32[]{:S(2)}) collective-permute-start(f32[8,512]{1,0:T(8,128)} %get-tuple-element.93), channel_id=1, source_target_pairs={{0,0},{1,2},{2,1},{3,3},{4,4},{5,6},{6,5},{7,7},{8,8},{9,10},{10,9... | collective-permute-start | bytes 49160 | tf_op jit(solution)/shard_map/ppermute | solution.py:1308
  12.0 0.9 %copy-start.1 = (bf16[160,512]{1,0:T(8,128)(2,1)S(1)}, bf16[160,512]{1,0:T(8,128)(2,1)}, u32[]{:S(2)}) copy-start(bf16[160,512]{1,0:T(8,128)(2,1)} %get-tuple-element.88.v_ref) | copy-start | bytes 491524
  13.0 8.8 %collective-permute-start.7 = (bf16[160,512]{1,0:T(8,128)(2,1)}, bf16[160,512]{1,0:T(8,128)(2,1)S(1)}, u32[]{:S(2)}, u32[]{:S(2)}) collective-permute-start(bf16[160,512]{1,0:T(8,128)(2,1)} %get-tuple-element.97), channel_id=1, source_target_pairs={{0,12},{4,8},{8,4},{12,0},{16,28},{20,24},{24,20},{28,16},{1,13},{... | collective-permute-start | bytes 491528 | tf_op jit(solution)/shard_map/ppermute | solution.py:1332
  15.9 7.4 %collective-permute-start.8 = (bf16[160,512]{1,0:T(8,128)(2,1)}, bf16[160,512]{1,0:T(8,128)(2,1)S(1)}, u32[]{:S(2)}, u32[]{:S(2)}) collective-permute-start(bf16[160,512]{1,0:T(8,128)(2,1)} %get-tuple-element.98), channel_id=1, source_target_pairs={{0,8},{4,12},{8,0},{12,4},{16,24},{20,28},{24,16},{28,20},{1,9},{5... | collective-permute-start | bytes 491528 | tf_op jit(solution)/shard_map/ppermute | solution.py:1332
  16.4 8.2 %collective-permute-start.9 = (bf16[160,512]{1,0:T(8,128)(2,1)}, bf16[160,512]{1,0:T(8,128)(2,1)S(1)}, u32[]{:S(2)}, u32[]{:S(2)}) collective-permute-start(bf16[160,512]{1,0:T(8,128)(2,1)} %get-tuple-element.99), channel_id=1, source_target_pairs={{0,4},{4,0},{8,12},{12,8},{16,20},{20,16},{24,28},{28,24},{1,5},{5... | collective-permute-start | bytes 491528 | tf_op jit(solution)/shard_map/ppermute | solution.py:1332
  16.6 8.0 %copy-start.2 = (f32[4,2048]{1,0:T(4,128)S(1)}, f32[4,2048]{1,0:T(4,128)}, u32[]{:S(2)}) copy-start(f32[4,2048]{1,0:T(4,128)} %taps_ref.7) | copy-start | bytes 98308
  16.6 7.9 %copy-start.3 = (f32[2048]{0:T(1024)S(1)}, f32[2048]{0:T(1024)}, u32[]{:S(2)}) copy-start(f32[2048]{0:T(1024)} %param.17) | copy-start | bytes 24580
  18.7 7.1 %collective-permute-start.6 = (bf16[16,768]{1,0:T(8,128)(2,1)S(1)}, bf16[16,768]{1,0:T(8,128)(2,1)S(1)}, u32[]{:S(2)}, u32[]{:S(2)}) collective-permute-start(bf16[16,768]{1,0:T(8,128)(2,1)S(1)} %get-tuple-element.95), channel_id=1, source_target_pairs={{0,16},{4,20},{8,24},{12,28},{16,0},{20,4},{24,8},{28,12},{1,17},{... | collective-permute-start | bytes 73736 | tf_op jit(solution)/shard_map/ppermute | solution.py:1359
  21.7 12.0 %collective-permute-start.5 = (bf16[128,512]{1,0:T(8,128)(2,1)S(1)}, bf16[128,512]{1,0:T(8,128)(2,1)S(1)}, u32[]{:S(2)}, u32[]{:S(2)}) collective-permute-start(bf16[128,512]{1,0:T(8,128)(2,1)S(1)} %get-tuple-element.94), channel_id=1, source_target_pairs={{0,16},{4,20},{8,24},{12,28},{16,0},{20,4},{24,8},{28,12},{1,17},{... | collective-permute-start | bytes 393224 | tf_op jit(solution)/shard_map/ppermute | solution.py:1360
  25.8 3.2 %copy-start.5 = (f32[32]{0:T(128)S(1)}, f32[32]{0:T(128)}, u32[]{:S(2)}) copy-start(f32[32]{0:T(128)} %skip_ref.1) | copy-start | bytes 388
  26.3 10.8 %collective-permute-start.10 = (bf16[128,512]{1,0:T(8,128)(2,1)S(1)}, bf16[128,512]{1,0:T(8,128)(2,1)S(1)}, u32[]{:S(2)}, u32[]{:S(2)}) collective-permute-start(bf16[128,512]{1,0:T(8,128)(2,1)S(1)} %get-tuple-element.110), channel_id=1, source_target_pairs={{0,16},{4,20},{8,24},{12,28},{16,0},{20,4},{24,8},{28,12},{1,17},{... | collective-permute-start | bytes 393224 | tf_op jit(solution)/shard_map/ppermute | solution.py:1397
  38.2 8.3 %collective-permute-start.14 = (bf16[544,128]{1,0:T(8,128)(2,1)S(1)}, bf16[544,128]{1,0:T(8,128)(2,1)S(1)}, u32[]{:S(2)}, u32[]{:S(2)}) collective-permute-start(bf16[544,128]{1,0:T(8,128)(2,1)S(1)} %get-tuple-element.147), channel_id=1, source_target_pairs={{0,0},{2,1},{1,2},{3,3},{4,4},{6,5},{5,6},{7,7},{8,8},{10,9},{9,10... | collective-permute-start | bytes 417800 | tf_op jit(solution)/shard_map/ppermute | solution.py:1472
  38.9 7.7 %collective-permute-start.15 = (bf16[544,128]{1,0:T(8,128)(2,1)S(1)}, bf16[544,128]{1,0:T(8,128)(2,1)S(1)}, u32[]{:S(2)}, u32[]{:S(2)}) collective-permute-start(bf16[544,128]{1,0:T(8,128)(2,1)S(1)} %get-tuple-element.148), channel_id=1, source_target_pairs={{0,2},{2,3},{1,0},{3,1},{4,6},{6,7},{5,4},{7,5},{8,10},{10,11},{9,... | collective-permute-start | bytes 417800 | tf_op jit(solution)/shard_map/ppermute | solution.py:1473
  46.0 8.5 %collective-permute-start.11 = (bf16[128,512]{1,0:T(8,128)(2,1)S(1)}, bf16[128,512]{1,0:T(8,128)(2,1)S(1)}, u32[]{:S(2)}, u32[]{:S(2)}) collective-permute-start(bf16[128,512]{1,0:T(8,128)(2,1)S(1)} %get-tuple-element.142), channel_id=1, source_target_pairs={{0,12},{4,8},{8,4},{12,0},{16,28},{20,24},{24,20},{28,16},{1,13},{... | collective-permute-start | bytes 393224 | tf_op jit(solution)/shard_map/ppermute | solution.py:1530
  46.5 5.2 %collective-permute-start.16 = (bf16[32,512]{1,0:T(8,128)(2,1)S(1)}, bf16[32,512]{1,0:T(8,128)(2,1)S(1)}, u32[]{:S(2)}, u32[]{:S(2)}) collective-permute-start(bf16[32,512]{1,0:T(8,128)(2,1)S(1)} %shard_map.196.own_ref), channel_id=1, source_target_pairs={{0,16},{4,20},{8,24},{12,28},{16,0},{20,4},{24,8},{28,12},{1,17},{... | collective-permute-start | bytes 98312 | tf_op jit(solution)/shard_map/ppermute | solution.py:1520
  49.8 6.1 %collective-permute-start.12 = (bf16[128,512]{1,0:T(8,128)(2,1)S(1)}, bf16[128,512]{1,0:T(8,128)(2,1)S(1)}, u32[]{:S(2)}, u32[]{:S(2)}) collective-permute-start(bf16[128,512]{1,0:T(8,128)(2,1)S(1)} %get-tuple-element.143), channel_id=1, source_target_pairs={{0,8},{4,12},{8,0},{12,4},{16,24},{20,28},{24,16},{28,20},{1,9},{5... | collective-permute-start | bytes 393224 | tf_op jit(solution)/shard_map/ppermute | solution.py:1530
  49.8 6.5 %collective-permute-start.13 = (bf16[128,512]{1,0:T(8,128)(2,1)S(1)}, bf16[128,512]{1,0:T(8,128)(2,1)S(1)}, u32[]{:S(2)}, u32[]{:S(2)}) collective-permute-start(bf16[128,512]{1,0:T(8,128)(2,1)S(1)} %get-tuple-element.144), channel_id=1, source_target_pairs={{0,4},{4,0},{8,12},{12,8},{16,20},{20,16},{24,28},{28,24},{1,5},{5... | collective-permute-start | bytes 393224 | tf_op jit(solution)/shard_map/ppermute | solution.py:1530
  51.9 6.8 %collective-permute-start.17 = (bf16[96,512]{1,0:T(8,128)(2,1)S(1)}, bf16[96,512]{1,0:T(8,128)(2,1)S(1)}, u32[]{:S(2)}, u32[]{:S(2)}) collective-permute-start(bf16[96,512]{1,0:T(8,128)(2,1)S(1)} %get-tuple-element.151), channel_id=1, source_target_pairs={{0,12},{4,8},{8,4},{12,0},{16,28},{20,24},{24,20},{28,16},{1,13},{... | collective-permute-start | bytes 294920 | tf_op jit(solution)/shard_map/ppermute | solution.py:1540
  54.4 5.0 %collective-permute-start.18 = (bf16[96,512]{1,0:T(8,128)(2,1)S(1)}, bf16[96,512]{1,0:T(8,128)(2,1)S(1)}, u32[]{:S(2)}, u32[]{:S(2)}) collective-permute-start(bf16[96,512]{1,0:T(8,128)(2,1)S(1)} %get-tuple-element.152), channel_id=1, source_target_pairs={{0,8},{4,12},{8,0},{12,4},{16,24},{20,28},{24,16},{28,20},{1,9},{5... | collective-permute-start | bytes 294920 | tf_op jit(solution)/shard_map/ppermute | solution.py:1540
  54.5 4.9 %collective-permute-start.19 = (bf16[96,512]{1,0:T(8,128)(2,1)S(1)}, bf16[96,512]{1,0:T(8,128)(2,1)S(1)}, u32[]{:S(2)}, u32[]{:S(2)}) collective-permute-start(bf16[96,512]{1,0:T(8,128)(2,1)S(1)} %get-tuple-element.153), channel_id=1, source_target_pairs={{0,4},{4,0},{8,12},{12,8},{16,20},{20,16},{24,28},{28,24},{1,5},{5... | collective-permute-start | bytes 294920 | tf_op jit(solution)/shard_map/ppermute | solution.py:1540

commit v7 on v6

--- a/solution.py
+++ b/solution.py
@@ -448,9 +448,12 @@
         copy.wait()
 
 
-def own_kernel(u_ref, v_ref, u_out, v_out):
-    u_out[...] = u_ref[...]
-    v_out[...] = v_ref[...]
+def own_kernel(ref, out):
+    out[...] = ref[...]
+
+
+def own_later_kernel(ref, after, out):
+    out[...] = ref[...]
 
 
 def sig_tap_rows(j, taps_ref, bias_ref):
@@ -526,6 +529,7 @@
     u3,
     u2,
     u1,
+    own_taps,
     one_taps,
     two_taps,
     alog_ref,
@@ -554,7 +558,9 @@
     at = at_tile(lax.rem(group, 4) * TILE)
     for j in range(2):
         mine_ref[8 * j : 8 * j + 8, :] = jnp.where(
-            lax.rem(f, 2) == j, one_taps[:, at], two_taps[:, at]
+            lax.rem(f, 2) == j,
+            jnp.where(keeps_own(), own_taps[:, at], one_taps[:, at]),
+            two_taps[:, at],
         )
     edge = jnp.zeros((8, 5 * TILE), F32)
     for k, u in enumerate((u0, u1, u2, u3)):
@@ -643,7 +649,7 @@
 
 
 def first_kernel(
-    v0, v3, v2, v1, step_e, toend_e, taps_ref, bias_ref, mine_ref, xs, acts, pres, scaled_s, weighted_s, xi, act_in, pre_in
+    v0, v1, v3, v2, step_e, toend_e, taps_ref, bias_ref, mine_ref, xs, acts, pres, scaled_s, weighted_s, xi, act_in, pre_in
 ):
     quad, r, f = place()
     high = quad == 1
@@ -1125,8 +1131,14 @@
     )
 
 
-def cross_kernel(scale, params_ref, spill_ref, one_ref, two_ref, cross_ref):
-    tails = [ref[4 * TILE : 4 * TILE + 32, :].astype(F32) for ref in (one_ref, two_ref)]
+def keeps_own():
+    f = place()[2]
+    return jnp.logical_or(f == 0, f == 3)
+
+
+def cross_kernel(scale, params_ref, spill_ref, own_ref, one_ref, two_ref, cross_ref):
+    tails = [ref[4 * TILE : 4 * TILE + 32, :].astype(F32) for ref in (own_ref, one_ref, two_ref)]
+    tails = [jnp.where(keeps_own(), tails[0], tails[1]), tails[2]]
     fives = [tail[16:24] + tail[24:32] for tail in tails]
     params = jnp.concatenate(
         [
@@ -1156,7 +1168,7 @@
             y[e * HALF : (e + 1) * HALF, :] = dx[pl.ds(pl.multiple_of(at, HALF), HALF), :]
 
 
-def merge_kernel(own_ref, other_ref, one_ref, two_ref, blk, w0, w1, w2, w3):
+def merge_kernel(own_ref, other_ref, kept_ref, one_ref, two_ref, blk, w0, w1, w2, w3):
     quad, r, f = place()
     lane8 = ids((8, TILE), 1)
     param_rows = split_params(
@@ -1167,7 +1179,7 @@
         s = lax.bitwise_xor(r, k)
         for e, at in ((0, HALF * s), (1, 2 * TILE + HALF * (3 - s))):
             rows = pl.ds(pl.multiple_of(at, HALF), HALF)
-            w[0:HALF, lanes_of(e)] = one_ref[rows, :]
+            w[0:HALF, lanes_of(e)] = jnp.where(keeps_own(), kept_ref[rows, :], one_ref[rows, :])
             w[0:HALF, lanes_of(2 + e)] = two_ref[rows, :]
         here = jnp.where(lane8 < HALF, blk[s], pltpu.roll(blk[7 - s], HALF, 1))
         hi, mid, _ = split3(here)
@@ -1243,7 +1255,7 @@
             mbias_ref[0:1, lanes] = five[4:5]
 
 
-ROUTE_ONE = [(0, 0), (2, 1), (1, 2), (3, 3)]
+ROUTE_ONE = [(2, 1), (1, 2)]
 ROUTE_TWO = [(0, 2), (2, 3), (1, 0), (3, 1)]
 
 
@@ -1316,20 +1328,10 @@
         60,
         10**6,
     )(sig_raw, map_raw)
-    own_u, own_v = call(
-        own_kernel,
-        (
-            shape(TILE + HALF // 2 + 16, narrow, kind=BF),
-            shape(TILE + HALF // 2, narrow, kind=BF),
-        ),
-        [vmem] * 2,
-        (vmem,) * 2,
-        [],
-        16,
-        10**6,
-    )(us[0], packed[0])
-    us[0] = own_u
-    vs = [own_v] + [lax.ppermute(packed[k], "ctx", inside[k]) for k in (1, 2, 3)]
+    us[0] = call(
+        own_kernel, shape(TILE + HALF // 2 + 16, narrow, kind=BF), [vmem], vmem, [], 16, 10**6
+    )(us[0])
+    vs = [None] + [lax.ppermute(packed[k], "ctx", inside[k]) for k in (1, 2, 3)]
     midg, dp, xo, act_out, pre_out, sgrad, step_e, toend_e, exp_e, t_s, step_r, ds_r, sig_r, *small = call(
         grads_kernel,
         (
@@ -1349,15 +1351,24 @@
             shape(16, TILE),
             shape(16, wide, kind=BF),
         ),
-        [vmem] * 6 + [smem] * 2,
+        [vmem] * 7 + [smem] * 2,
         (vmem,) * 15,
         [pltpu.VMEM((4, 8, TILE), F32)],
         24,
         2 * 10**9,
-    )(us[0], us[3], us[2], us[1], map_one, map_two, a_log, dt_bias)
+    )(us[0], us[3], us[2], us[1], map_params, map_one, map_two, a_log, dt_bias)
     mine, halo = small
     halo = lax.ppermute(halo, "ctx", over)
     midg = lax.ppermute(midg, "ctx", over)
+    vs[0] = call(
+        own_later_kernel,
+        shape(TILE + HALF // 2, narrow, kind=BF),
+        [vmem] * 2,
+        vmem,
+        [],
+        16,
+        10**6,
+    )(packed[0], mine)
     xs, acts, pres, scaled, weighted, xi, act_in, pre_in = call(
         first_kernel,
         (
@@ -1375,7 +1386,7 @@
         [],
         24,
         2 * 10**9,
-    )(vs[0], vs[3], vs[2], vs[1], step_e, toend_e, sig_taps, sig_bias_row, mine)
+    )(vs[0], vs[1], vs[3], vs[2], step_e, toend_e, sig_taps, sig_bias_row, mine)
     midf, s_s, delta, edge, act_p, pre_p, scaled_p, weighted_p = call(
         states_kernel,
         (
@@ -1469,6 +1480,7 @@
         edge,
         mine,
     )
+    kept = one
     one = lax.ppermute(one, "fsdp", ROUTE_ONE)
     two = lax.ppermute(two, "fsdp", ROUTE_TWO)
     gp, blk, spill, params = call(
@@ -1511,12 +1523,12 @@
     cross = call(
         functools.partial(cross_kernel, scale),
         shape(32, narrow, kind=BF),
-        [vmem] * 4,
+        [vmem] * 5,
         vmem,
         [],
         16,
         10**6,
-    )(params, spill, one, two)
+    )(params, spill, kept, one, two)
     other = lax.ppermute(cross, "ctx", over)
     ys = call(
         send_kernel,
@@ -1531,12 +1543,12 @@
     ws = call(
         merge_kernel,
         (shape(HALF + 32, narrow, kind=BF),) * 4,
-        [vmem] * 5,
+        [vmem] * 6,
         (vmem,) * 4,
         [],
         16,
         10**6,
-    )(cross, other, one, two, blk)
+    )(cross, other, kept, one, two, blk)
     ws = [ws[0]] + [lax.ppermute(ws[k], "ctx", inside[k]) for k in (1, 2, 3)]
     d_sig, d_map, d_dt, taps, map_taps_grad, bias, map_bias_grad, *trio = call(
         last_kernel,

time: 61 us -> 59.8 us (0.980)
  starting transfers between devices: 28 us -> 23.7 us
  waiting for transfers between devices: 10.9 us -> 14.9 us
  local copies, waits for them, and re-layouts: 0.95 us -> 0.04 us
    ppermute x6 -> x3, starting transfers between devices: 8.25 us -> 4.69 us  [shards_quad(): lax.ppermute(packed[k], 'ctx', inside[k])]
    ppermute x0 -> x3, starting transfers between devices: none -> 3.55 us  [shards_quad(): vs = [None] + [lax.ppermute(packed[k], 'ctx', inside[k]) for k in (1, 2, 3)]]
    ppermute x1, starting transfers between devices: 3.26 us -> 0.02 us  [shards_quad(): two = lax.ppermute(two, 'fsdp', ROUTE_TWO)]
    ppermute x6 -> x3, waiting for transfers between devices: 2.84 us -> 0.67 us  [shards_quad(): lax.ppermute(packed[k], 'ctx', inside[k])]
    ppermute x1, waiting for transfers between devices: 0.01 us -> 1.94 us  [shards_quad(): midg = lax.ppermute(midg, 'ctx', over)]
    ppermute x0 -> x3, waiting for transfers between devices: none -> 1.46 us  [shards_quad(): vs = [None] + [lax.ppermute(packed[k], 'ctx', inside[k]) for k in (1, 2, 3)]]
    ppermute x3, waiting for transfers between devices: 3.1 us -> 4.21 us  [shards_quad(): ws = [ws[0]] + [lax.ppermute(ws[k], 'ctx', inside[k]) for k in (1, 2, 3)]]
    ppermute x1, waiting for transfers between devices: 1.05 us -> 2.09 us  [shards_quad(): other = lax.ppermute(cross, 'ctx', over)]
  transfers between devices with their start and end apart: 20 -> 20, of which waited for: 8 -> 11; matrix products, arithmetic and copies ran while one was open for 0% -> 0% of each run, Pallas kernels for 24% -> 25%
where the time goes in v7:
time: 59.8 us; the launch traced here: 59.4 us
  starting transfers between devices  23.7 us (40%)
  Pallas kernels  20 us (33%)
  waiting for transfers between devices  14.9 us (25%)
  between operations  0.85 us (1%)
    ppermute x3, starting transfers between devices, shards_quad(): lax.ppermute(packed[k], 'ctx', inside[k])  4.69 us
    pallas_call x1, Pallas kernels, shards_quad(): call(second_kernel, (shape(total, narrow), shape(total, narrow), shape(to...  4.65 us
    ppermute x3, waiting for transfers between devices, shards_quad(): ws = [ws[0]] + [lax.ppermute(ws[k], 'ctx', inside[k]) for k in (1, 2, 3)]  4.21 us
    ppermute x3, starting transfers between devices, shards_quad(): ws = [ws[0]] + [lax.ppermute(ws[k], 'ctx', inside[k]) for k in (1, 2, 3)]  3.55 us
    ppermute x3, starting transfers between devices, shards_quad(): vs = [None] + [lax.ppermute(packed[k], 'ctx', inside[k]) for k in (1, 2, 3)]  3.55 us
    pallas_call x1, Pallas kernels, shards_quad(): call(third_kernel, (shape(2, 2 * TILE + 8, narrow), shape(8, 8, TILE), sh...  3.28 us
    ppermute x1, starting transfers between devices, shards_quad(): midf = lax.ppermute(midf, 'ctx', over)  3.21 us
    pallas_call x1, Pallas kernels, shards_quad(): call(pack_kernel, (shape(TILE + HALF // 2 + 16, narrow, kind=BF),) * 4 +...  3.03 us
  transfers between devices with their start and end apart: 20, of which 11 were waited for; matrix products, arithmetic and copies ran while one was open for 0% of the time, Pallas kernels for 25%

profile of v7, /device:TPU:0, one launch (start us, length us, event | category | flops | bytes accessed | tf_op | source)
XLA Modules:
  0.0 59.4 jit_solution(6840604858130031623)
XLA Ops:
  0.6 3.0 %shard_map.186 = (bf16[176,512]{1,0:T(8,128)(2,1)}, bf16[176,512]{1,0:T(8,128)(2,1)}, bf16[176,512]{1,0:T(8,128)(2,1)}, bf16[176,512]{1,0:T(8,128)(2,1)}, f32[8,512]{1,0:T(8,128)}) custom-call(bf16[128,2048]{1,0:T(8,128)(2,1)} %sig_ref.3, bf16[128,2048]{1,0:T(8,128)(2,1)} %map_ref.3, f32[32,128]{1,0:T(8,128)} %bitcast.11, bf16[128,2048]{1,0:T(8,128)(2,1)} %dy_ref.1, ...), custom_call_target="tpu_custom_call" | custom-call | flops 1000000 | bytes 10000 | tf_op jit(solution)/shard_map/pallas_call | solution.py:1305
  3.7 0.0 copy-start
  3.7 0.0 copy-start.4
  3.7 0.0 copy-start.5
  3.7 0.0 copy-start.7
  3.7 4.0 %collective-permute-start = (bf16[176,512]{1,0:T(8,128)(2,1)}, bf16[176,512]{1,0:T(8,128)(2,1)S(1)}, u32[]{:S(2)}, u32[]{:S(2)}) collective-permute-start(bf16[176,512]{1,0:T(8,128)(2,1)} %get-tuple-element.86), channel_id=1, source_target_pairs={{0,12},{4,8},{8,4},{12,0},{16,28},{20,24},{24,20},{28,16},{1,13},{... | collective-permute-start | bytes 540680 | tf_op jit(solution)/shard_map/ppermute | solution.py:1319
  7.8 0.4 collective-permute-start.1
  8.2 0.2 collective-permute-start.2
  8.4 0.0 collective-permute-start.4
  8.4 0.7 %collective-permute-start.3 = (f32[8,512]{1,0:T(8,128)}, f32[8,512]{1,0:T(8,128)S(1)}, u32[]{:S(2)}, u32[]{:S(2)}) collective-permute-start(f32[8,512]{1,0:T(8,128)} %get-tuple-element.89.own_taps), channel_id=1, source_target_pairs={{1,2},{2,1},{5,6},{6,5},{9,10},{10,9},{13,14},{14,13},{17,18},{18,... | collective-permute-start | bytes 49160 | tf_op jit(solution)/shard_map/ppermute | solution.py:1320
  9.1 2.3 %shard_map.189 = (bf16[160,512]{1,0:T(8,128)(2,1)}, bf16[160,512]{1,0:T(8,128)(2,1)}, bf16[160,512]{1,0:T(8,128)(2,1)}, bf16[160,512]{1,0:T(8,128)(2,1)}) custom-call(bf16[128,2048]{1,0:T(8,128)(2,1)} %sig_ref.3, bf16[128,2048]{1,0:T(8,128)(2,1)} %map_ref.3), custom_call_target="tpu_custom_call" | custom-call | flops 1000000 | bytes 10000 | tf_op jit(solution)/shard_map/pallas_call | solution.py:1322
  11.4 0.0 copy-done
  11.4 1.0 %collective-permute-done.4.two_taps = f32[8,512]{1,0:T(8,128)S(1)} collective-permute-done((f32[8,512]{1,0:T(8,128)}, f32[8,512]{1,0:T(8,128)S(1)}, u32[]{:S(2)}, u32[]{:S(2)}) %collective-permute-start.4) | collective-permute-done | bytes 16416 | tf_op jit(solution)/shard_map/ppermute | solution.py:1321
  12.4 1.8 %collective-permute-start.7 = (bf16[160,512]{1,0:T(8,128)(2,1)}, bf16[160,512]{1,0:T(8,128)(2,1)S(1)}, u32[]{:S(2)}, u32[]{:S(2)}) collective-permute-start(bf16[160,512]{1,0:T(8,128)(2,1)} %get-tuple-element.94), channel_id=1, source_target_pairs={{0,4},{4,0},{8,12},{12,8},{16,20},{20,16},{24,28},{28,24},{1,5},{5... | collective-permute-start | bytes 491528 | tf_op jit(solution)/shard_map/ppermute | solution.py:1334
  14.2 0.0 collective-permute-done.3.one_taps
  14.2 1.5 %collective-permute-start.8 = (bf16[160,512]{1,0:T(8,128)(2,1)}, bf16[160,512]{1,0:T(8,128)(2,1)S(1)}, u32[]{:S(2)}, u32[]{:S(2)}) collective-permute-start(bf16[160,512]{1,0:T(8,128)(2,1)} %get-tuple-element.95), channel_id=1, source_target_pairs={{0,12},{4,8},{8,4},{12,0},{16,28},{20,24},{24,20},{28,16},{1,13},{... | collective-permute-start | bytes 491528 | tf_op jit(solution)/shard_map/ppermute | solution.py:1334
  15.7 0.0 collective-permute-done.u3
  15.7 0.2 collective-permute-start.9
  15.9 0.7 %collective-permute-done.1.u2 = bf16[176,512]{1,0:T(8,128)(2,1)S(1)} collective-permute-done((bf16[176,512]{1,0:T(8,128)(2,1)}, bf16[176,512]{1,0:T(8,128)(2,1)S(1)}, u32[]{:S(2)}, u32[]{:S(2)}) %collective-permute-start.1) | collective-permute-done | bytes 180256 | tf_op jit(solution)/shard_map/ppermute | solution.py:1319
  16.6 0.0 collective-permute-done.2.u1
  16.6 0.0 copy-done.4
  16.6 0.0 copy-done.5
  16.6 0.0 copy-done.7
  16.6 2.1 %shard_map.188 = (bf16[128,512]{1,0:T(8,128)(2,1)S(1)}, bf16[512,512]{1,0:T(8,128)(2,1)S(1)}, f32[2,264,128]{2,1,0:T(8,128)S(1)}, bf16[512,128]{1,0:T(8,128)(2,1...) custom-call(bf16[176,512]{1,0:T(8,128)(2,1)S(1)} %shard_map.187.u0, ...), custom_call_target="tpu_custom_call" | custom-call | flops 2000000000 | bytes 20000000 | tf_op jit(solution)/shard_map/pallas_call | solution.py:1335
  18.7 2.7 %collective-permute-start.6 = (bf16[16,768]{1,0:T(8,128)(2,1)S(1)}, bf16[16,768]{1,0:T(8,128)(2,1)S(1)}, u32[]{:S(2)}, u32[]{:S(2)}) collective-permute-start(bf16[16,768]{1,0:T(8,128)(2,1)S(1)} %get-tuple-element.91), channel_id=1, source_target_pairs={{0,16},{4,20},{8,24},{12,28},{16,0},{20,4},{24,8},{28,12},{1,17},{... | collective-permute-start | bytes 73736 | tf_op jit(solution)/shard_map/ppermute | solution.py:1361
  21.4 0.3 collective-permute-start.5
  21.7 0.0 copy-done.1
  21.7 0.0 collective-permute-done.7.v1
  21.7 0.0 collective-permute-done.8.v3
  21.8 1.5 %collective-permute-done.9.v2 = bf16[160,512]{1,0:T(8,128)(2,1)S(1)} collective-permute-done((bf16[160,512]{1,0:T(8,128)(2,1)}, bf16[160,512]{1,0:T(8,128)(2,1)S(1)}, u32[]{:S(2)}, u32[]{:S(2)}) %collective-permute-start.9) | collective-permute-done | bytes 163872 | tf_op jit(solution)/shard_map/ppermute | solution.py:1334
  23.2 0.0 copy-done.2
  23.2 0.0 copy-done.3
  23.2 1.3 %shard_map.191 = (f32[2,264,512]{2,1,0:T(8,128)S(1)}, bf16[512,512]{1,0:T(8,128)(2,1)S(1)}, f32[512,512]{1,0:T(8,128)S(1)}, bf16[512,512]{1,0:T(8,128)(2,1)S(1)}...) custom-call(bf16[160,512]{1,0:T(8,128)(2,1)S(1)} %shard_map.190.v0, ...), custom_call_target="tpu_custom_call" | custom-call | flops 2000000000 | bytes 20000000 | tf_op jit(solution)/shard_map/pallas_call | solution.py:1372
  24.5 0.0 collective-permute-done.6.halo_ref
  24.5 0.0 copy-start.6
  24.5 0.4 shard_map.192
  24.9 3.2 %collective-permute-start.10 = (bf16[128,512]{1,0:T(8,128)(2,1)S(1)}, bf16[128,512]{1,0:T(8,128)(2,1)S(1)}, u32[]{:S(2)}, u32[]{:S(2)}) collective-permute-start(bf16[128,512]{1,0:T(8,128)(2,1)S(1)} %get-tuple-element.106), channel_id=1, source_target_pairs={{0,16},{4,20},{8,24},{12,28},{16,0},{20,4},{24,8},{28,12},{1,17},{... | collective-permute-start | bytes 393224 | tf_op jit(solution)/shard_map/ppermute | solution.py:1408
  28.1 0.0 copy-done.6
  28.1 4.7 %shard_map.193 = (f32[512,512]{1,0:T(8,128)S(1)}, f32[512,512]{1,0:T(8,128)S(1)}, f32[512,256]{1,0:T(8,128)S(1)}, f32[512,256]{1,0:T(8,128)S(1)}, f32[32,128]{1,...) custom-call(bf16[512,512]{1,0:T(8,128)(2,1)S(1)} %get-tuple-element.107.dp, ...), custom_call_target="tpu_custom_call" | custom-call | flops 5000000000 | bytes 50000000 | tf_op jit(solution)/shard_map/pallas_call | solution.py:1409
  32.8 1.9 %collective-permute-done.5.midg_ref = bf16[128,512]{1,0:T(8,128)(2,1)S(1)} collective-permute-done((bf16[128,512]{1,0:T(8,128)(2,1)S(1)}, bf16[128,512]{1,0:T(8,128)(2,1)S(1)}, u32[]{:S(2)}, u32[]{:S(2)}) %collective-permute-start.5) | collective-permute-done | bytes 131104 | tf_op jit(solution)/shard_map/ppermute | solution.py:1362
  34.7 2.8 %collective-permute-done.10.midf_ref = bf16[128,512]{1,0:T(8,128)(2,1)S(1)} collective-permute-done((bf16[128,512]{1,0:T(8,128)(2,1)S(1)}, bf16[128,512]{1,0:T(8,128)(2,1)S(1)}, u32[]{:S(2)}, u32[]{:S(2)}) %collective-permute-start.10) | collective-permute-done | bytes 131104 | tf_op jit(solution)/shard_map/ppermute | solution.py:1408
  37.5 1.1 %shard_map.194 = (bf16[544,128]{1,0:T(8,128)(2,1)S(1)}, bf16[544,128]{1,0:T(8,128)(2,1)S(1)}, bf16[4,128,512]{2,1,0:T(8,128)(2,1)S(1)}, bf16[4,128,512]{2,1,0:T(8,128)(2,1)S(1)}, f32[8,512]{1,0:T(8,128)S(1)}) custom-call(bf16[128,512]{1,0:T(8,128)(2,1)S(1)} %collective-permute-done.5.midg_ref, bf16[128,512]{1,0:T(8,128)(2,1)S(1)} %collective-permute-done.10.midf_ref, ...), custom_call_target="tpu_custom_call" | custom-call | flops 2000000000 | bytes 20000000 | tf_op jit(solution)/shard_map/pallas_call | solution.py:1446
  38.7 0.0 collective-permute-start.15
  38.7 0.7 %collective-permute-start.14 = (bf16[544,128]{1,0:T(8,128)(2,1)S(1)}, bf16[544,128]{1,0:T(8,128)(2,1)S(1)}, u32[]{:S(2)}, u32[]{:S(2)}) collective-permute-start(bf16[544,128]{1,0:T(8,128)(2,1)S(1)} %get-tuple-element.143.own_ref.kept_ref), channel_id=1, source_target_pairs={{2,1},{1,2},{6,5},{5,6},{10,9},{9,10},{14,13},{13,14},{18,17},{17,... | collective-permute-start | bytes 417800 | tf_op jit(solution)/shard_map/ppermute | solution.py:1484
  39.4 3.3 %shard_map.195 = (f32[2,264,512]{2,1,0:T(8,128)S(1)}, f32[8,8,128]{2,1,0:T(8,128)S(1)}, f32[8,512]{1,0:T(8,128)S(1)}, f32[24,128]{1,0:T(8,128)S(1)}) custom-call(bf16[4,128,512]{2,1,0:T(8,128)(2,1)S(1)} %get-tuple-element.126.hlow_ref, bf16[4,128,512]{2,1,0:T(8,128)(2,1)S(1)} %get-tuple-element.127.clow_ref, f32[8,512]{1,0:T(8,128)S(1)} %get-tuple-element.128.endrow_ref, ...), custom_call_target="tpu_custom_call" | custom-call | flops 3000000000 | bytes 30000000 | tf_op jit(solution)/shard_map/pallas_call | solution.py:1486
  42.6 0.6 shard_map.196
  43.2 1.2 %collective-permute-start.11 = (bf16[128,512]{1,0:T(8,128)(2,1)S(1)}, bf16[128,512]{1,0:T(8,128)(2,1)S(1)}, u32[]{:S(2)}, u32[]{:S(2)}) collective-permute-start(bf16[128,512]{1,0:T(8,128)(2,1)S(1)} %get-tuple-element.138), channel_id=1, source_target_pairs={{0,12},{4,8},{8,4},{12,0},{16,28},{20,24},{24,20},{28,16},{1,13},{... | collective-permute-start | bytes 393224 | tf_op jit(solution)/shard_map/ppermute | solution.py:1542
  44.5 0.0 collective-permute-done.15.two_ref
  44.5 0.0 collective-permute-done.14.one_ref
  44.5 2.5 %collective-permute-start.16 = (bf16[32,512]{1,0:T(8,128)(2,1)S(1)}, bf16[32,512]{1,0:T(8,128)(2,1)S(1)}, u32[]{:S(2)}, u32[]{:S(2)}) collective-permute-start(bf16[32,512]{1,0:T(8,128)(2,1)S(1)} %shard_map.197.own_ref), channel_id=1, source_target_pairs={{0,16},{4,20},{8,24},{12,28},{16,0},{20,4},{24,8},{28,12},{1,17},{... | collective-permute-start | bytes 98312 | tf_op jit(solution)/shard_map/ppermute | solution.py:1532
  47.0 0.0 collective-permute-start.12
  47.0 0.6 collective-permute-start.13
  47.6 2.1 %collective-permute-done.16.other_ref = bf16[32,512]{1,0:T(8,128)(2,1)S(1)} collective-permute-done((bf16[32,512]{1,0:T(8,128)(2,1)S(1)}, bf16[32,512]{1,0:T(8,128)(2,1)S(1)}, u32[]{:S(2)}, u32[]{:S(2)}) %collective-permute-start.16) | collective-permute-done | bytes 32800 | tf_op jit(solution)/shard_map/ppermute | solution.py:1532
  49.7 0.1 shard_map.198
  49.8 1.9 %collective-permute-start.17 = (bf16[96,512]{1,0:T(8,128)(2,1)S(1)}, bf16[96,512]{1,0:T(8,128)(2,1)S(1)}, u32[]{:S(2)}, u32[]{:S(2)}) collective-permute-start(bf16[96,512]{1,0:T(8,128)(2,1)S(1)} %get-tuple-element.147), channel_id=1, source_target_pairs={{0,12},{4,8},{8,4},{12,0},{16,28},{20,24},{24,20},{28,16},{1,13},{... | collective-permute-start | bytes 294920 | tf_op jit(solution)/shard_map/ppermute | solution.py:1552
  51.7 0.0 collective-permute-start.18
  51.7 0.0 collective-permute-done.11.y3
  51.7 1.6 %collective-permute-start.19 = (bf16[96,512]{1,0:T(8,128)(2,1)S(1)}, bf16[96,512]{1,0:T(8,128)(2,1)S(1)}, u32[]{:S(2)}, u32[]{:S(2)}) collective-permute-start(bf16[96,512]{1,0:T(8,128)(2,1)S(1)} %get-tuple-element.149), channel_id=1, source_target_pairs={{0,4},{4,0},{8,12},{12,8},{16,20},{20,16},{24,28},{28,24},{1,5},{5... | collective-permute-start | bytes 294920 | tf_op jit(solution)/shard_map/ppermute | solution.py:1552
  53.3 0.3 collective-permute-done.12.y2
  53.7 0.4 collective-permute-done.13.y1
  54.1 2.4 %collective-permute-done.17.w3 = bf16[96,512]{1,0:T(8,128)(2,1)S(1)} collective-permute-done((bf16[96,512]{1,0:T(8,128)(2,1)S(1)}, bf16[96,512]{1,0:T(8,128)(2,1)S(1)}, u32[]{:S(2)}, u32[]{:S(2)}) %collective-permute-start.17) | collective-permute-done | bytes 98336 | tf_op jit(solution)/shard_map/ppermute | solution.py:1552
  56.5 1.5 %collective-permute-done.18.w2 = bf16[96,512]{1,0:T(8,128)(2,1)S(1)} collective-permute-done((bf16[96,512]{1,0:T(8,128)(2,1)S(1)}, bf16[96,512]{1,0:T(8,128)(2,1)S(1)}, u32[]{:S(2)}, u32[]{:S(2)}) %collective-permute-start.18) | collective-permute-done | bytes 98336 | tf_op jit(solution)/shard_map/ppermute | solution.py:1552
  57.9 0.4 collective-permute-done.19.w1
  58.3 1.1 %shard_map.199 = (f32[128,2048]{1,0:T(8,128)}, f32[128,512]{1,0:T(8,128)}, f32[32,128]{1,0:T(8,128)}, f32[4,2048]{1,0:T(4,128)}, f32[4,512]{1,0:T(4,128)}, /*ind...) custom-call(bf16[128,512]{1,0:T(8,128)(2,1)S(1)} %get-tuple-element.137.y0, ...), custom_call_target="tpu_custom_call" | custom-call | flops 1000000 | bytes 10000 | tf_op jit(solution)/shard_map/pallas_call | solution.py:1553
  (6 shorter events, 0.1 us)
Async XLA Ops:
  3.7 7.7 %copy-start = (bf16[176,512]{1,0:T(8,128)(2,1)S(1)}, bf16[176,512]{1,0:T(8,128)(2,1)}, u32[]{:S(2)}) copy-start(bf16[176,512]{1,0:T(8,128)(2,1)} %get-tuple-element.85.ref) | copy-start | bytes 540676
  3.7 12.9 %copy-start.4 = (f32[8,512]{1,0:T(8,128)S(1)}, f32[8,512]{1,0:T(8,128)}, u32[]{:S(2)}) copy-start(f32[8,512]{1,0:T(8,128)} %get-tuple-element.89.own_taps) | copy-start | bytes 49156
  3.7 12.9 %copy-start.5 = (f32[32]{0:T(128)S(1)}, f32[32]{0:T(128)}, u32[]{:S(2)}) copy-start(f32[32]{0:T(128)} %dtb_ref.1) | copy-start | bytes 388
  3.7 12.9 %copy-start.7 = (f32[32]{0:T(128)S(1)}, f32[32]{0:T(128)}, u32[]{:S(2)}) copy-start(f32[32]{0:T(128)} %alog_ref.3) | copy-start | bytes 388
  3.7 12.0 %collective-permute-start = (bf16[176,512]{1,0:T(8,128)(2,1)}, bf16[176,512]{1,0:T(8,128)(2,1)S(1)}, u32[]{:S(2)}, u32[]{:S(2)}) collective-permute-start(bf16[176,512]{1,0:T(8,128)(2,1)} %get-tuple-element.86), channel_id=1, source_target_pairs={{0,12},{4,8},{8,4},{12,0},{16,28},{20,24},{24,20},{28,16},{1,13},{... | collective-permute-start | bytes 540680 | tf_op jit(solution)/shard_map/ppermute | solution.py:1319
  7.8 8.8 %collective-permute-start.1 = (bf16[176,512]{1,0:T(8,128)(2,1)}, bf16[176,512]{1,0:T(8,128)(2,1)S(1)}, u32[]{:S(2)}, u32[]{:S(2)}) collective-permute-start(bf16[176,512]{1,0:T(8,128)(2,1)} %get-tuple-element.87), channel_id=1, source_target_pairs={{0,8},{4,12},{8,0},{12,4},{16,24},{20,28},{24,16},{28,20},{1,9},{5... | collective-permute-start | bytes 540680 | tf_op jit(solution)/shard_map/ppermute | solution.py:1319
  8.2 8.4 %collective-permute-start.2 = (bf16[176,512]{1,0:T(8,128)(2,1)}, bf16[176,512]{1,0:T(8,128)(2,1)S(1)}, u32[]{:S(2)}, u32[]{:S(2)}) collective-permute-start(bf16[176,512]{1,0:T(8,128)(2,1)} %get-tuple-element.88), channel_id=1, source_target_pairs={{0,4},{4,0},{8,12},{12,8},{16,20},{20,16},{24,28},{28,24},{1,5},{5... | collective-permute-start | bytes 540680 | tf_op jit(solution)/shard_map/ppermute | solution.py:1319
  8.4 3.9 %collective-permute-start.4 = (f32[8,512]{1,0:T(8,128)}, f32[8,512]{1,0:T(8,128)S(1)}, u32[]{:S(2)}, u32[]{:S(2)}) collective-permute-start(f32[8,512]{1,0:T(8,128)} %get-tuple-element.89.own_taps), channel_id=1, source_target_pairs={{2,0},{3,2},{0,1},{1,3},{6,4},{7,6},{4,5},{5,7},{10,8},{11,10},{8,... | collective-permute-start | bytes 49160 | tf_op jit(solution)/shard_map/ppermute | solution.py:1321
  8.4 5.8 %collective-permute-start.3 = (f32[8,512]{1,0:T(8,128)}, f32[8,512]{1,0:T(8,128)S(1)}, u32[]{:S(2)}, u32[]{:S(2)}) collective-permute-start(f32[8,512]{1,0:T(8,128)} %get-tuple-element.89.own_taps), channel_id=1, source_target_pairs={{1,2},{2,1},{5,6},{6,5},{9,10},{10,9},{13,14},{14,13},{17,18},{18,... | collective-permute-start | bytes 49160 | tf_op jit(solution)/shard_map/ppermute | solution.py:1320
  12.4 9.4 %collective-permute-start.7 = (bf16[160,512]{1,0:T(8,128)(2,1)}, bf16[160,512]{1,0:T(8,128)(2,1)S(1)}, u32[]{:S(2)}, u32[]{:S(2)}) collective-permute-start(bf16[160,512]{1,0:T(8,128)(2,1)} %get-tuple-element.94), channel_id=1, source_target_pairs={{0,4},{4,0},{8,12},{12,8},{16,20},{20,16},{24,28},{28,24},{1,5},{5... | collective-permute-start | bytes 491528 | tf_op jit(solution)/shard_map/ppermute | solution.py:1334
  14.2 7.5 %collective-permute-start.8 = (bf16[160,512]{1,0:T(8,128)(2,1)}, bf16[160,512]{1,0:T(8,128)(2,1)S(1)}, u32[]{:S(2)}, u32[]{:S(2)}) collective-permute-start(bf16[160,512]{1,0:T(8,128)(2,1)} %get-tuple-element.95), channel_id=1, source_target_pairs={{0,12},{4,8},{8,4},{12,0},{16,28},{20,24},{24,20},{28,16},{1,13},{... | collective-permute-start | bytes 491528 | tf_op jit(solution)/shard_map/ppermute | solution.py:1334
  15.7 6.0 %copy-start.1 = (bf16[160,512]{1,0:T(8,128)(2,1)S(1)}, bf16[160,512]{1,0:T(8,128)(2,1)}, u32[]{:S(2)}) copy-start(bf16[160,512]{1,0:T(8,128)(2,1)} %get-tuple-element.92.ref) | copy-start | bytes 491524
  15.7 7.5 %copy-start.2 = (f32[4,2048]{1,0:T(4,128)S(1)}, f32[4,2048]{1,0:T(4,128)}, u32[]{:S(2)}) copy-start(f32[4,2048]{1,0:T(4,128)} %taps_ref.7) | copy-start | bytes 98308
  15.7 7.5 %copy-start.3 = (f32[2048]{0:T(1024)S(1)}, f32[2048]{0:T(1024)}, u32[]{:S(2)}) copy-start(f32[2048]{0:T(1024)} %param.17) | copy-start | bytes 24580
  15.7 7.5 %collective-permute-start.9 = (bf16[160,512]{1,0:T(8,128)(2,1)}, bf16[160,512]{1,0:T(8,128)(2,1)S(1)}, u32[]{:S(2)}, u32[]{:S(2)}) collective-permute-start(bf16[160,512]{1,0:T(8,128)(2,1)} %get-tuple-element.96), channel_id=1, source_target_pairs={{0,8},{4,12},{8,0},{12,4},{16,24},{20,28},{24,16},{28,20},{1,9},{5... | collective-permute-start | bytes 491528 | tf_op jit(solution)/shard_map/ppermute | solution.py:1334
  18.7 5.8 %collective-permute-start.6 = (bf16[16,768]{1,0:T(8,128)(2,1)S(1)}, bf16[16,768]{1,0:T(8,128)(2,1)S(1)}, u32[]{:S(2)}, u32[]{:S(2)}) collective-permute-start(bf16[16,768]{1,0:T(8,128)(2,1)S(1)} %get-tuple-element.91), channel_id=1, source_target_pairs={{0,16},{4,20},{8,24},{12,28},{16,0},{20,4},{24,8},{28,12},{1,17},{... | collective-permute-start | bytes 73736 | tf_op jit(solution)/shard_map/ppermute | solution.py:1361
  21.4 13.4 %collective-permute-start.5 = (bf16[128,512]{1,0:T(8,128)(2,1)S(1)}, bf16[128,512]{1,0:T(8,128)(2,1)S(1)}, u32[]{:S(2)}, u32[]{:S(2)}) collective-permute-start(bf16[128,512]{1,0:T(8,128)(2,1)S(1)} %get-tuple-element.90), channel_id=1, source_target_pairs={{0,16},{4,20},{8,24},{12,28},{16,0},{20,4},{24,8},{28,12},{1,17},{... | collective-permute-start | bytes 393224 | tf_op jit(solution)/shard_map/ppermute | solution.py:1362
  24.5 3.6 %copy-start.6 = (f32[32]{0:T(128)S(1)}, f32[32]{0:T(128)}, u32[]{:S(2)}) copy-start(f32[32]{0:T(128)} %skip_ref.1) | copy-start | bytes 388
  24.9 12.6 %collective-permute-start.10 = (bf16[128,512]{1,0:T(8,128)(2,1)S(1)}, bf16[128,512]{1,0:T(8,128)(2,1)S(1)}, u32[]{:S(2)}, u32[]{:S(2)}) collective-permute-start(bf16[128,512]{1,0:T(8,128)(2,1)S(1)} %get-tuple-element.106), channel_id=1, source_target_pairs={{0,16},{4,20},{8,24},{12,28},{16,0},{20,4},{24,8},{28,12},{1,17},{... | collective-permute-start | bytes 393224 | tf_op jit(solution)/shard_map/ppermute | solution.py:1408
  38.7 5.8 %collective-permute-start.15 = (bf16[544,128]{1,0:T(8,128)(2,1)S(1)}, bf16[544,128]{1,0:T(8,128)(2,1)S(1)}, u32[]{:S(2)}, u32[]{:S(2)}) collective-permute-start(bf16[544,128]{1,0:T(8,128)(2,1)S(1)} %get-tuple-element.144), channel_id=1, source_target_pairs={{0,2},{2,3},{1,0},{3,1},{4,6},{6,7},{5,4},{7,5},{8,10},{10,11},{9,... | collective-permute-start | bytes 417800 | tf_op jit(solution)/shard_map/ppermute | solution.py:1485
  38.7 5.8 %collective-permute-start.14 = (bf16[544,128]{1,0:T(8,128)(2,1)S(1)}, bf16[544,128]{1,0:T(8,128)(2,1)S(1)}, u32[]{:S(2)}, u32[]{:S(2)}) collective-permute-start(bf16[544,128]{1,0:T(8,128)(2,1)S(1)} %get-tuple-element.143.own_ref.kept_ref), channel_id=1, source_target_pairs={{2,1},{1,2},{6,5},{5,6},{10,9},{9,10},{14,13},{13,14},{18,17},{17,... | collective-permute-start | bytes 417800 | tf_op jit(solution)/shard_map/ppermute | solution.py:1484
  43.2 8.5 %collective-permute-start.11 = (bf16[128,512]{1,0:T(8,128)(2,1)S(1)}, bf16[128,512]{1,0:T(8,128)(2,1)S(1)}, u32[]{:S(2)}, u32[]{:S(2)}) collective-permute-start(bf16[128,512]{1,0:T(8,128)(2,1)S(1)} %get-tuple-element.138), channel_id=1, source_target_pairs={{0,12},{4,8},{8,4},{12,0},{16,28},{20,24},{24,20},{28,16},{1,13},{... | collective-permute-start | bytes 393224 | tf_op jit(solution)/shard_map/ppermute | solution.py:1542
  44.5 5.2 %collective-permute-start.16 = (bf16[32,512]{1,0:T(8,128)(2,1)S(1)}, bf16[32,512]{1,0:T(8,128)(2,1)S(1)}, u32[]{:S(2)}, u32[]{:S(2)}) collective-permute-start(bf16[32,512]{1,0:T(8,128)(2,1)S(1)} %shard_map.197.own_ref), channel_id=1, source_target_pairs={{0,16},{4,20},{8,24},{12,28},{16,0},{20,4},{24,8},{28,12},{1,17},{... | collective-permute-start | bytes 98312 | tf_op jit(solution)/shard_map/ppermute | solution.py:1532
  47.0 6.7 %collective-permute-start.12 = (bf16[128,512]{1,0:T(8,128)(2,1)S(1)}, bf16[128,512]{1,0:T(8,128)(2,1)S(1)}, u32[]{:S(2)}, u32[]{:S(2)}) collective-permute-start(bf16[128,512]{1,0:T(8,128)(2,1)S(1)} %get-tuple-element.139), channel_id=1, source_target_pairs={{0,8},{4,12},{8,0},{12,4},{16,24},{20,28},{24,16},{28,20},{1,9},{5... | collective-permute-start | bytes 393224 | tf_op jit(solution)/shard_map/ppermute | solution.py:1542
  47.0 7.1 %collective-permute-start.13 = (bf16[128,512]{1,0:T(8,128)(2,1)S(1)}, bf16[128,512]{1,0:T(8,128)(2,1)S(1)}, u32[]{:S(2)}, u32[]{:S(2)}) collective-permute-start(bf16[128,512]{1,0:T(8,128)(2,1)S(1)} %get-tuple-element.140), channel_id=1, source_target_pairs={{0,4},{4,0},{8,12},{12,8},{16,20},{20,16},{24,28},{28,24},{1,5},{5... | collective-permute-start | bytes 393224 | tf_op jit(solution)/shard_map/ppermute | solution.py:1542
  49.8 6.7 %collective-permute-start.17 = (bf16[96,512]{1,0:T(8,128)(2,1)S(1)}, bf16[96,512]{1,0:T(8,128)(2,1)S(1)}, u32[]{:S(2)}, u32[]{:S(2)}) collective-permute-start(bf16[96,512]{1,0:T(8,128)(2,1)S(1)} %get-tuple-element.147), channel_id=1, source_target_pairs={{0,12},{4,8},{8,4},{12,0},{16,28},{20,24},{24,20},{28,16},{1,13},{... | collective-permute-start | bytes 294920 | tf_op jit(solution)/shard_map/ppermute | solution.py:1552
  51.7 6.2 %collective-permute-start.18 = (bf16[96,512]{1,0:T(8,128)(2,1)S(1)}, bf16[96,512]{1,0:T(8,128)(2,1)S(1)}, u32[]{:S(2)}, u32[]{:S(2)}) collective-permute-start(bf16[96,512]{1,0:T(8,128)(2,1)S(1)} %get-tuple-element.148), channel_id=1, source_target_pairs={{0,8},{4,12},{8,0},{12,4},{16,24},{20,28},{24,16},{28,20},{1,9},{5... | collective-permute-start | bytes 294920 | tf_op jit(solution)/shard_map/ppermute | solution.py:1552
  51.7 6.6 %collective-permute-start.19 = (bf16[96,512]{1,0:T(8,128)(2,1)S(1)}, bf16[96,512]{1,0:T(8,128)(2,1)S(1)}, u32[]{:S(2)}, u32[]{:S(2)}) collective-permute-start(bf16[96,512]{1,0:T(8,128)(2,1)S(1)} %get-tuple-element.149), channel_id=1, source_target_pairs={{0,4},{4,0},{8,12},{12,8},{16,20},{20,16},{24,28},{28,24},{1,5},{5... | collective-permute-start | bytes 294920 | tf_op jit(solution)/shard_map/ppermute | solution.py:1552

commit v8 on v7

--- a/solution.py
+++ b/solution.py
@@ -374,8 +374,8 @@
     return pl.ds(pl.multiple_of(start, TILE), width)
 
 
-def pack_kernel(sig_ref, map_ref, dt_ref, dy_ref, mtaps_ref, mbias_ref, *rest):
-    u_refs, tap_ref, (dt_in, sig_in, map_in, sems) = rest[:4], rest[4], rest[5:]
+def pack_kernel(sig_ref, map_ref, dt_ref, dy_ref, *rest):
+    u_refs, (dt_in, sig_in, map_in, sems) = rest[:4], rest[4:]
     quad, r, f = place()
     copies = []
     dt_copy = pltpu.make_async_copy(dt_ref, dt_in, sems.at[20])
@@ -404,9 +404,6 @@
                 map_ref.at[e * HALF // 2 : (e + 1) * HALF // 2, at_tile(group + half)],
                 u_refs[k].at[TILE : TILE + HALF // 2, lanes_of(e)],
             )
-    tap_ref[0:4, :] = mtaps_ref[...]
-    tap_ref[4:5, :] = mbias_ref[...]
-    tap_ref[5:8, :] = jnp.zeros_like(tap_ref[5:8, :])
     dt_copy.wait()
     sig_copy.wait()
     map_copy.wait()
@@ -1289,7 +1286,7 @@
             in_specs=in_specs,
             out_specs=out_specs,
             scratch_shapes=scratch,
-            compiler_params=pltpu.CompilerParams(vmem_limit_bytes=mib * 1024 * 1024),
+            compiler_params=pltpu.CompilerParams(vmem_limit_bytes=int(mib * 1024 * 1024)),
             cost_estimate=pl.CostEstimate(flops=cost, bytes_accessed=cost // 100, transcendentals=0),
         )
 
@@ -1302,20 +1299,23 @@
     wide, narrow = 6 * TILE, 4 * TILE
     owned = map_taps.shape[1]
     sig_bias_row = sig_bias[None, :]
-    *packed, map_params = call(
+    packed = call(
         pack_kernel,
-        (shape(TILE + HALF // 2 + 16, narrow, kind=BF),) * 4 + (shape(8, owned),),
-        [hbm, hbm, hbm, hbm, vmem, vmem],
-        (vmem,) * 5,
+        (shape(TILE + HALF // 2 + 16, narrow, kind=BF),) * 4,
+        [hbm] * 4,
+        (vmem,) * 4,
         [
             pltpu.VMEM((32, TILE), F32),
             pltpu.VMEM((16, sig_width), BF),
             pltpu.VMEM((16, map_raw.shape[1] // 2), BF),
             pltpu.SemaphoreType.DMA((23,)),
         ],
-        60,
+        53.2,
         10**6,
-    )(sig_raw, map_raw, step_size_logits.T, d_out, map_taps, map_bias[None, :])
+    )(sig_raw, map_raw, step_size_logits.T, d_out)
+    map_params = jnp.concatenate(
+        [map_taps, map_bias[None, :], jnp.zeros((3, owned), F32)], axis=0
+    )
     us = [packed[0]] + [lax.ppermute(packed[k], "ctx", inside[k]) for k in (1, 2, 3)]
     map_one = lax.ppermute(map_params, "fsdp", back(ROUTE_ONE))
     map_two = lax.ppermute(map_params, "fsdp", back(ROUTE_TWO))

time: 59.8 us -> 58.6 us (0.980)
  Pallas kernels: 20 us -> 18.4 us
  local copies, waits for them, and re-layouts: 0.04 us -> 0.83 us
    ppermute x1, waiting for transfers between devices: 1.94 us -> 0.39 us  [shards_quad(): midg = lax.ppermute(midg, 'ctx', over)]
    pallas_call x1, Pallas kernels: 3.03 us -> 1.49 us  [shards_quad(): call(pack_kernel, (shape(TILE + HALF // 2 + 16, narrow, kind=BF),) * 4, [...]
    ppermute x1, waiting for transfers between devices: 2.81 us -> 4.21 us  [shards_quad(): midf = lax.ppermute(midf, 'ctx', over)]
    unnamed x16 -> x18, local copies, waits for them, and re-layouts: 0.04 us -> 0.75 us
where the time goes in v8:
time: 58.6 us; the launch traced here: 58.4 us
  starting transfers between devices  23.6 us (40%)
  Pallas kernels  18.4 us (31%)
  waiting for transfers between devices  14.6 us (25%)
  local copies, waits for them, and re-layouts  0.83 us (1%)
  between operations  0.83 us (1%)
    ppermute x3, starting transfers between devices, shards_quad(): lax.ppermute(packed[k], 'ctx', inside[k])  4.69 us
    pallas_call x1, Pallas kernels, shards_quad(): call(second_kernel, (shape(total, narrow), shape(total, narrow), shape(to...  4.65 us
    ppermute x1, waiting for transfers between devices, shards_quad(): midf = lax.ppermute(midf, 'ctx', over)  4.21 us
    ppermute x3, waiting for transfers between devices, shards_quad(): ws = [ws[0]] + [lax.ppermute(ws[k], 'ctx', inside[k]) for k in (1, 2, 3)]  4.21 us
    ppermute x3, starting transfers between devices, shards_quad(): ws = [ws[0]] + [lax.ppermute(ws[k], 'ctx', inside[k]) for k in (1, 2, 3)]  3.55 us
    ppermute x3, starting transfers between devices, shards_quad(): vs = [None] + [lax.ppermute(packed[k], 'ctx', inside[k]) for k in (1, 2, 3)]  3.55 us
    pallas_call x1, Pallas kernels, shards_quad(): call(third_kernel, (shape(2, 2 * TILE + 8, narrow), shape(8, 8, TILE), sh...  3.28 us
    ppermute x1, starting transfers between devices, shards_quad(): midf = lax.ppermute(midf, 'ctx', over)  3.14 us
  transfers between devices with their start and end apart: 20, of which 11 were waited for; matrix products, arithmetic and copies ran while one was open for 0% of the time, Pallas kernels for 25%

profile of v8, /device:TPU:0, one launch (start us, length us, event | category | flops | bytes accessed | tf_op | source)
XLA Modules:
  0.0 58.4 jit_solution(2961050603232971691)
XLA Ops:
  0.6 0.0 copy-start.2
  0.7 0.7 %copy-done.2 = f32[128,32]{0,1:T(8,128)S(1)} copy-done((f32[128,32]{0,1:T(8,128)S(1)}, f32[128,32]{0,1:T(8,128)}, u32[]{:S(2)}) %copy-start.2) | copy-done | bytes 16408
  1.4 1.5 %shard_map.186 = (bf16[176,512]{1,0:T(8,128)(2,1)S(1)}, bf16[176,512]{1,0:T(8,128)(2,1)S(1)}, bf16[176,512]{1,0:T(8,128)(2,1)S(1)}, bf16[176,512]{1,0:T(8,128)(2,1)S(1)}) custom-call(bf16[128,2048]{1,0:T(8,128)(2,1)} %sig_ref.3, bf16[128,2048]{1,0:T(8,128)(2,1)} %map_ref.3, f32[32,128]{1,0:T(8,128)S(1)} %bitcast.9, bf16[128,2048]{1,0:T(8,128)(2,1)} %dy_ref.1), custom_call_target="tpu_custom_call" | custom-call | flops 1000000 | bytes 10000 | tf_op jit(solution)/shard_map/pallas_call | solution.py:1302
  2.9 0.0 copy-start.4
  2.9 0.0 copy-start.6
  2.9 4.0 %collective-permute-start = (bf16[176,512]{1,0:T(8,128)(2,1)S(1)}, bf16[176,512]{1,0:T(8,128)(2,1)S(1)}, u32[]{:S(2)}, u32[]{:S(2)}) collective-permute-start(bf16[176,512]{1,0:T(8,128)(2,1)S(1)} %get-tuple-element.85), channel_id=1, source_target_pairs={{0,12},{4,8},{8,4},{12,0},{16,28},{20,24},{24,20},{28,16},{1,13},{... | collective-permute-start | bytes 540680 | tf_op jit(solution)/shard_map/ppermute | solution.py:1319
  6.9 0.4 collective-permute-start.1
  7.4 0.2 collective-permute-start.2
  7.6 0.1 pad.2.clone
  7.7 0.0 copy-done.7
  7.7 0.0 copy-done.8
  7.7 0.1 maximum_maximum_fusion.own_taps
  7.7 0.0 collective-permute-start.4
  7.7 0.7 %collective-permute-start.3 = (f32[8,512]{1,0:T(8,128)S(1)}, f32[8,512]{1,0:T(8,128)S(1)}, u32[]{:S(2)}, u32[]{:S(2)}) collective-permute-start(f32[8,512]{1,0:T(8,128)S(1)} %maximum_maximum_fusion.own_taps), channel_id=1, source_target_pairs={{1,2},{2,1},{5,6},{6,5},{9,10},{10,9},{13,14},{14,13},{17,18},{18,... | collective-permute-start | bytes 49160 | tf_op jit(solution)/shard_map/ppermute | solution.py:1320
  8.4 2.2 %shard_map.189 = (bf16[160,512]{1,0:T(8,128)(2,1)}, bf16[160,512]{1,0:T(8,128)(2,1)}, bf16[160,512]{1,0:T(8,128)(2,1)}, bf16[160,512]{1,0:T(8,128)(2,1)}) custom-call(bf16[128,2048]{1,0:T(8,128)(2,1)} %sig_ref.3, bf16[128,2048]{1,0:T(8,128)(2,1)} %map_ref.3), custom_call_target="tpu_custom_call" | custom-call | flops 1000000 | bytes 10000 | tf_op jit(solution)/shard_map/pallas_call | solution.py:1322
  10.7 0.8 %collective-permute-done.4.two_taps = f32[8,512]{1,0:T(8,128)S(1)} collective-permute-done((f32[8,512]{1,0:T(8,128)S(1)}, f32[8,512]{1,0:T(8,128)S(1)}, u32[]{:S(2)}, u32[]{:S(2)}) %collective-permute-start.4) | collective-permute-done | bytes 16416 | tf_op jit(solution)/shard_map/ppermute | solution.py:1321
  11.5 1.8 %collective-permute-start.7 = (bf16[160,512]{1,0:T(8,128)(2,1)}, bf16[160,512]{1,0:T(8,128)(2,1)S(1)}, u32[]{:S(2)}, u32[]{:S(2)}) collective-permute-start(bf16[160,512]{1,0:T(8,128)(2,1)} %get-tuple-element.92), channel_id=1, source_target_pairs={{0,4},{4,0},{8,12},{12,8},{16,20},{20,16},{24,28},{28,24},{1,5},{5... | collective-permute-start | bytes 491528 | tf_op jit(solution)/shard_map/ppermute | solution.py:1334
  13.3 0.0 collective-permute-done.3.one_taps
  13.3 1.5 %collective-permute-start.8 = (bf16[160,512]{1,0:T(8,128)(2,1)}, bf16[160,512]{1,0:T(8,128)(2,1)S(1)}, u32[]{:S(2)}, u32[]{:S(2)}) collective-permute-start(bf16[160,512]{1,0:T(8,128)(2,1)} %get-tuple-element.93), channel_id=1, source_target_pairs={{0,12},{4,8},{8,4},{12,0},{16,28},{20,24},{24,20},{28,16},{1,13},{... | collective-permute-start | bytes 491528 | tf_op jit(solution)/shard_map/ppermute | solution.py:1334
  14.8 0.0 collective-permute-done.u3
  14.8 0.2 collective-permute-start.9
  15.0 0.5 collective-permute-done.1.u2
  15.6 0.0 collective-permute-done.2.u1
  15.6 0.0 copy-done.4
  15.6 0.0 copy-done.6
  15.6 2.1 %shard_map.188 = (bf16[128,512]{1,0:T(8,128)(2,1)S(1)}, bf16[512,512]{1,0:T(8,128)(2,1)S(1)}, f32[2,264,128]{2,1,0:T(8,128)S(1)}, bf16[512,128]{1,0:T(8,128)(2,1...) custom-call(bf16[176,512]{1,0:T(8,128)(2,1)S(1)} %shard_map.187.u0, ...), custom_call_target="tpu_custom_call" | custom-call | flops 2000000000 | bytes 20000000 | tf_op jit(solution)/shard_map/pallas_call | solution.py:1335
  17.7 2.7 %collective-permute-start.6 = (bf16[16,768]{1,0:T(8,128)(2,1)S(1)}, bf16[16,768]{1,0:T(8,128)(2,1)S(1)}, u32[]{:S(2)}, u32[]{:S(2)}) collective-permute-start(bf16[16,768]{1,0:T(8,128)(2,1)S(1)} %get-tuple-element.89), channel_id=1, source_target_pairs={{0,16},{4,20},{8,24},{12,28},{16,0},{20,4},{24,8},{28,12},{1,17},{... | collective-permute-start | bytes 73736 | tf_op jit(solution)/shard_map/ppermute | solution.py:1361
  20.3 0.3 collective-permute-start.5
  20.7 0.0 copy-done
  20.7 0.0 collective-permute-done.7.v1
  20.7 0.0 collective-permute-done.8.v3
  20.7 1.5 %collective-permute-done.9.v2 = bf16[160,512]{1,0:T(8,128)(2,1)S(1)} collective-permute-done((bf16[160,512]{1,0:T(8,128)(2,1)}, bf16[160,512]{1,0:T(8,128)(2,1)S(1)}, u32[]{:S(2)}, u32[]{:S(2)}) %collective-permute-start.9) | collective-permute-done | bytes 163872 | tf_op jit(solution)/shard_map/ppermute | solution.py:1334
  22.2 0.0 copy-done.1
  22.2 1.3 %shard_map.191 = (f32[2,264,512]{2,1,0:T(8,128)S(1)}, bf16[512,512]{1,0:T(8,128)(2,1)S(1)}, f32[512,512]{1,0:T(8,128)S(1)}, bf16[512,512]{1,0:T(8,128)(2,1)S(1)}...) custom-call(bf16[160,512]{1,0:T(8,128)(2,1)S(1)} %shard_map.190.v0, ...), custom_call_target="tpu_custom_call" | custom-call | flops 2000000000 | bytes 20000000 | tf_op jit(solution)/shard_map/pallas_call | solution.py:1372
  23.5 0.0 collective-permute-done.6.halo_ref
  23.5 0.0 copy-start.5
  23.5 0.4 shard_map.192
  23.9 3.1 %collective-permute-start.10 = (bf16[128,512]{1,0:T(8,128)(2,1)S(1)}, bf16[128,512]{1,0:T(8,128)(2,1)S(1)}, u32[]{:S(2)}, u32[]{:S(2)}) collective-permute-start(bf16[128,512]{1,0:T(8,128)(2,1)S(1)} %get-tuple-element.104), channel_id=1, source_target_pairs={{0,16},{4,20},{8,24},{12,28},{16,0},{20,4},{24,8},{28,12},{1,17},{... | collective-permute-start | bytes 393224 | tf_op jit(solution)/shard_map/ppermute | solution.py:1408
  27.0 4.7 %shard_map.193 = (f32[512,512]{1,0:T(8,128)S(1)}, f32[512,512]{1,0:T(8,128)S(1)}, f32[512,256]{1,0:T(8,128)S(1)}, f32[512,256]{1,0:T(8,128)S(1)}, f32[32,128]{1,...) custom-call(bf16[512,512]{1,0:T(8,128)(2,1)S(1)} %get-tuple-element.105.dp, ...), custom_call_target="tpu_custom_call" | custom-call | flops 5000000000 | bytes 50000000 | tf_op jit(solution)/shard_map/pallas_call | solution.py:1409
  31.7 0.4 collective-permute-done.5.midg_ref
  32.1 4.2 %collective-permute-done.10.midf_ref = bf16[128,512]{1,0:T(8,128)(2,1)S(1)} collective-permute-done((bf16[128,512]{1,0:T(8,128)(2,1)S(1)}, bf16[128,512]{1,0:T(8,128)(2,1)S(1)}, u32[]{:S(2)}, u32[]{:S(2)}) %collective-permute-start.10) | collective-permute-done | bytes 131104 | tf_op jit(solution)/shard_map/ppermute | solution.py:1408
  36.3 1.1 %shard_map.194 = (bf16[544,128]{1,0:T(8,128)(2,1)S(1)}, bf16[544,128]{1,0:T(8,128)(2,1)S(1)}, bf16[4,128,512]{2,1,0:T(8,128)(2,1)S(1)}, bf16[4,128,512]{2,1,0:T(8,128)(2,1)S(1)}, f32[8,512]{1,0:T(8,128)S(1)}) custom-call(bf16[128,512]{1,0:T(8,128)(2,1)S(1)} %collective-permute-done.5.midg_ref, bf16[128,512]{1,0:T(8,128)(2,1)S(1)} %collective-permute-done.10.midf_ref, ...), custom_call_target="tpu_custom_call" | custom-call | flops 2000000000 | bytes 20000000 | tf_op jit(solution)/shard_map/pallas_call | solution.py:1446
  37.4 0.2 collective-permute-start.15
  37.7 0.7 %collective-permute-start.14 = (bf16[544,128]{1,0:T(8,128)(2,1)S(1)}, bf16[544,128]{1,0:T(8,128)(2,1)S(1)}, u32[]{:S(2)}, u32[]{:S(2)}) collective-permute-start(bf16[544,128]{1,0:T(8,128)(2,1)S(1)} %get-tuple-element.141.own_ref.kept_ref), channel_id=1, source_target_pairs={{2,1},{1,2},{6,5},{5,6},{10,9},{9,10},{14,13},{13,14},{18,17},{17,... | collective-permute-start | bytes 417800 | tf_op jit(solution)/shard_map/ppermute | solution.py:1484
  38.3 3.3 %shard_map.195 = (f32[2,264,512]{2,1,0:T(8,128)S(1)}, f32[8,8,128]{2,1,0:T(8,128)S(1)}, f32[8,512]{1,0:T(8,128)S(1)}, f32[24,128]{1,0:T(8,128)S(1)}) custom-call(bf16[4,128,512]{2,1,0:T(8,128)(2,1)S(1)} %get-tuple-element.124.hlow_ref, bf16[4,128,512]{2,1,0:T(8,128)(2,1)S(1)} %get-tuple-element.125.clow_ref, f32[8,512]{1,0:T(8,128)S(1)} %get-tuple-element.126.endrow_ref, ...), custom_call_target="tpu_custom_call" | custom-call | flops 3000000000 | bytes 30000000 | tf_op jit(solution)/shard_map/pallas_call | solution.py:1486
  41.6 0.6 shard_map.196
  42.2 1.3 %collective-permute-start.11 = (bf16[128,512]{1,0:T(8,128)(2,1)S(1)}, bf16[128,512]{1,0:T(8,128)(2,1)S(1)}, u32[]{:S(2)}, u32[]{:S(2)}) collective-permute-start(bf16[128,512]{1,0:T(8,128)(2,1)S(1)} %get-tuple-element.136), channel_id=1, source_target_pairs={{0,12},{4,8},{8,4},{12,0},{16,28},{20,24},{24,20},{28,16},{1,13},{... | collective-permute-start | bytes 393224 | tf_op jit(solution)/shard_map/ppermute | solution.py:1542
  43.5 0.0 collective-permute-done.15.two_ref
  43.5 0.0 collective-permute-done.14.one_ref
  43.5 2.3 %collective-permute-start.16 = (bf16[32,512]{1,0:T(8,128)(2,1)S(1)}, bf16[32,512]{1,0:T(8,128)(2,1)S(1)}, u32[]{:S(2)}, u32[]{:S(2)}) collective-permute-start(bf16[32,512]{1,0:T(8,128)(2,1)S(1)} %shard_map.197.own_ref), channel_id=1, source_target_pairs={{0,16},{4,20},{8,24},{12,28},{16,0},{20,4},{24,8},{28,12},{1,17},{... | collective-permute-start | bytes 98312 | tf_op jit(solution)/shard_map/ppermute | solution.py:1532
  45.8 0.0 collective-permute-start.12
  45.8 0.6 %collective-permute-start.13 = (bf16[128,512]{1,0:T(8,128)(2,1)S(1)}, bf16[128,512]{1,0:T(8,128)(2,1)S(1)}, u32[]{:S(2)}, u32[]{:S(2)}) collective-permute-start(bf16[128,512]{1,0:T(8,128)(2,1)S(1)} %get-tuple-element.138), channel_id=1, source_target_pairs={{0,4},{4,0},{8,12},{12,8},{16,20},{20,16},{24,28},{28,24},{1,5},{5... | collective-permute-start | bytes 393224 | tf_op jit(solution)/shard_map/ppermute | solution.py:1542
  46.4 2.3 %collective-permute-done.16.other_ref = bf16[32,512]{1,0:T(8,128)(2,1)S(1)} collective-permute-done((bf16[32,512]{1,0:T(8,128)(2,1)S(1)}, bf16[32,512]{1,0:T(8,128)(2,1)S(1)}, u32[]{:S(2)}, u32[]{:S(2)}) %collective-permute-start.16) | collective-permute-done | bytes 32800 | tf_op jit(solution)/shard_map/ppermute | solution.py:1532
  48.7 0.1 shard_map.198
  48.8 1.9 %collective-permute-start.17 = (bf16[96,512]{1,0:T(8,128)(2,1)S(1)}, bf16[96,512]{1,0:T(8,128)(2,1)S(1)}, u32[]{:S(2)}, u32[]{:S(2)}) collective-permute-start(bf16[96,512]{1,0:T(8,128)(2,1)S(1)} %get-tuple-element.145), channel_id=1, source_target_pairs={{0,12},{4,8},{8,4},{12,0},{16,28},{20,24},{24,20},{28,16},{1,13},{... | collective-permute-start | bytes 294920 | tf_op jit(solution)/shard_map/ppermute | solution.py:1552
  50.7 0.0 collective-permute-start.18
  50.7 0.0 collective-permute-done.11.y3
  50.7 1.7 %collective-permute-start.19 = (bf16[96,512]{1,0:T(8,128)(2,1)S(1)}, bf16[96,512]{1,0:T(8,128)(2,1)S(1)}, u32[]{:S(2)}, u32[]{:S(2)}) collective-permute-start(bf16[96,512]{1,0:T(8,128)(2,1)S(1)} %get-tuple-element.147), channel_id=1, source_target_pairs={{0,4},{4,0},{8,12},{12,8},{16,20},{20,16},{24,28},{28,24},{1,5},{5... | collective-permute-start | bytes 294920 | tf_op jit(solution)/shard_map/ppermute | solution.py:1552
  52.4 0.4 collective-permute-done.12.y2
  52.8 0.3 collective-permute-done.13.y1
  53.0 2.5 %collective-permute-done.17.w3 = bf16[96,512]{1,0:T(8,128)(2,1)S(1)} collective-permute-done((bf16[96,512]{1,0:T(8,128)(2,1)S(1)}, bf16[96,512]{1,0:T(8,128)(2,1)S(1)}, u32[]{:S(2)}, u32[]{:S(2)}) %collective-permute-start.17) | collective-permute-done | bytes 98336 | tf_op jit(solution)/shard_map/ppermute | solution.py:1552
  55.5 1.5 %collective-permute-done.18.w2 = bf16[96,512]{1,0:T(8,128)(2,1)S(1)} collective-permute-done((bf16[96,512]{1,0:T(8,128)(2,1)S(1)}, bf16[96,512]{1,0:T(8,128)(2,1)S(1)}, u32[]{:S(2)}, u32[]{:S(2)}) %collective-permute-start.18) | collective-permute-done | bytes 98336 | tf_op jit(solution)/shard_map/ppermute | solution.py:1552
  57.0 0.2 collective-permute-done.19.w1
  57.2 1.1 %shard_map.199 = (f32[128,2048]{1,0:T(8,128)}, f32[128,512]{1,0:T(8,128)}, f32[32,128]{1,0:T(8,128)}, f32[4,2048]{1,0:T(4,128)}, f32[4,512]{1,0:T(4,128)}, /*ind...) custom-call(bf16[128,512]{1,0:T(8,128)(2,1)S(1)} %get-tuple-element.135.y0, ...), custom_call_target="tpu_custom_call" | custom-call | flops 1000000 | bytes 10000 | tf_op jit(solution)/shard_map/pallas_call | solution.py:1553
  (11 shorter events, 0.1 us)
Async XLA Ops:
  0.6 0.7 %copy-start.2 = (f32[128,32]{0,1:T(8,128)S(1)}, f32[128,32]{0,1:T(8,128)}, u32[]{:S(2)}) copy-start(f32[128,32]{0,1:T(8,128)} %param.13) | copy-start | bytes 49156
  1.4 6.3 %copy-start.7 = (f32[4,512]{1,0:T(4,128)S(1)}, f32[4,512]{1,0:T(4,128)}, u32[]{:S(2)}) copy-start(f32[4,512]{1,0:T(4,128)} %param.16) | copy-start | bytes 24580
  1.4 6.3 %copy-start.8 = (f32[512]{0:T(512)S(1)}, f32[512]{0:T(512)}, u32[]{:S(2)}) copy-start(f32[512]{0:T(512)} %param.18) | copy-start | bytes 6148
  2.9 12.7 %copy-start.4 = (f32[32]{0:T(128)S(1)}, f32[32]{0:T(128)}, u32[]{:S(2)}) copy-start(f32[32]{0:T(128)} %dtb_ref.1) | copy-start | bytes 388
  2.9 12.7 %copy-start.6 = (f32[32]{0:T(128)S(1)}, f32[32]{0:T(128)}, u32[]{:S(2)}) copy-start(f32[32]{0:T(128)} %alog_ref.3) | copy-start | bytes 388
  2.9 11.9 %collective-permute-start = (bf16[176,512]{1,0:T(8,128)(2,1)S(1)}, bf16[176,512]{1,0:T(8,128)(2,1)S(1)}, u32[]{:S(2)}, u32[]{:S(2)}) collective-permute-start(bf16[176,512]{1,0:T(8,128)(2,1)S(1)} %get-tuple-element.85), channel_id=1, source_target_pairs={{0,12},{4,8},{8,4},{12,0},{16,28},{20,24},{24,20},{28,16},{1,13},{... | collective-permute-start | bytes 540680 | tf_op jit(solution)/shard_map/ppermute | solution.py:1319
  6.9 8.6 %collective-permute-start.1 = (bf16[176,512]{1,0:T(8,128)(2,1)S(1)}, bf16[176,512]{1,0:T(8,128)(2,1)S(1)}, u32[]{:S(2)}, u32[]{:S(2)}) collective-permute-start(bf16[176,512]{1,0:T(8,128)(2,1)S(1)} %get-tuple-element.86), channel_id=1, source_target_pairs={{0,8},{4,12},{8,0},{12,4},{16,24},{20,28},{24,16},{28,20},{1,9},{5... | collective-permute-start | bytes 540680 | tf_op jit(solution)/shard_map/ppermute | solution.py:1319
  7.4 8.2 %collective-permute-start.2 = (bf16[176,512]{1,0:T(8,128)(2,1)S(1)}, bf16[176,512]{1,0:T(8,128)(2,1)S(1)}, u32[]{:S(2)}, u32[]{:S(2)}) collective-permute-start(bf16[176,512]{1,0:T(8,128)(2,1)S(1)} %get-tuple-element.87), channel_id=1, source_target_pairs={{0,4},{4,0},{8,12},{12,8},{16,20},{20,16},{24,28},{28,24},{1,5},{5... | collective-permute-start | bytes 540680 | tf_op jit(solution)/shard_map/ppermute | solution.py:1319
  7.7 3.7 %collective-permute-start.4 = (f32[8,512]{1,0:T(8,128)S(1)}, f32[8,512]{1,0:T(8,128)S(1)}, u32[]{:S(2)}, u32[]{:S(2)}) collective-permute-start(f32[8,512]{1,0:T(8,128)S(1)} %maximum_maximum_fusion.own_taps), channel_id=1, source_target_pairs={{2,0},{3,2},{0,1},{1,3},{6,4},{7,6},{4,5},{5,7},{10,8},{11,10},{8,... | collective-permute-start | bytes 49160 | tf_op jit(solution)/shard_map/ppermute | solution.py:1321
  7.7 5.6 %collective-permute-start.3 = (f32[8,512]{1,0:T(8,128)S(1)}, f32[8,512]{1,0:T(8,128)S(1)}, u32[]{:S(2)}, u32[]{:S(2)}) collective-permute-start(f32[8,512]{1,0:T(8,128)S(1)} %maximum_maximum_fusion.own_taps), channel_id=1, source_target_pairs={{1,2},{2,1},{5,6},{6,5},{9,10},{10,9},{13,14},{14,13},{17,18},{18,... | collective-permute-start | bytes 49160 | tf_op jit(solution)/shard_map/ppermute | solution.py:1320
  11.5 9.2 %collective-permute-start.7 = (bf16[160,512]{1,0:T(8,128)(2,1)}, bf16[160,512]{1,0:T(8,128)(2,1)S(1)}, u32[]{:S(2)}, u32[]{:S(2)}) collective-permute-start(bf16[160,512]{1,0:T(8,128)(2,1)} %get-tuple-element.92), channel_id=1, source_target_pairs={{0,4},{4,0},{8,12},{12,8},{16,20},{20,16},{24,28},{28,24},{1,5},{5... | collective-permute-start | bytes 491528 | tf_op jit(solution)/shard_map/ppermute | solution.py:1334
  13.3 7.4 %collective-permute-start.8 = (bf16[160,512]{1,0:T(8,128)(2,1)}, bf16[160,512]{1,0:T(8,128)(2,1)S(1)}, u32[]{:S(2)}, u32[]{:S(2)}) collective-permute-start(bf16[160,512]{1,0:T(8,128)(2,1)} %get-tuple-element.93), channel_id=1, source_target_pairs={{0,12},{4,8},{8,4},{12,0},{16,28},{20,24},{24,20},{28,16},{1,13},{... | collective-permute-start | bytes 491528 | tf_op jit(solution)/shard_map/ppermute | solution.py:1334
  14.8 5.8 %copy-start = (bf16[160,512]{1,0:T(8,128)(2,1)S(1)}, bf16[160,512]{1,0:T(8,128)(2,1)}, u32[]{:S(2)}) copy-start(bf16[160,512]{1,0:T(8,128)(2,1)} %get-tuple-element.90.ref) | copy-start | bytes 491524
  14.8 7.4 %copy-start.1 = (f32[4,2048]{1,0:T(4,128)S(1)}, f32[4,2048]{1,0:T(4,128)}, u32[]{:S(2)}) copy-start(f32[4,2048]{1,0:T(4,128)} %taps_ref.7) | copy-start | bytes 98308
  14.8 7.4 %copy-start.3 = (f32[2048]{0:T(1024)S(1)}, f32[2048]{0:T(1024)}, u32[]{:S(2)}) copy-start(f32[2048]{0:T(1024)} %param.17) | copy-start | bytes 24580
  14.8 7.3 %collective-permute-start.9 = (bf16[160,512]{1,0:T(8,128)(2,1)}, bf16[160,512]{1,0:T(8,128)(2,1)S(1)}, u32[]{:S(2)}, u32[]{:S(2)}) collective-permute-start(bf16[160,512]{1,0:T(8,128)(2,1)} %get-tuple-element.94), channel_id=1, source_target_pairs={{0,8},{4,12},{8,0},{12,4},{16,24},{20,28},{24,16},{28,20},{1,9},{5... | collective-permute-start | bytes 491528 | tf_op jit(solution)/shard_map/ppermute | solution.py:1334
  17.7 5.8 %collective-permute-start.6 = (bf16[16,768]{1,0:T(8,128)(2,1)S(1)}, bf16[16,768]{1,0:T(8,128)(2,1)S(1)}, u32[]{:S(2)}, u32[]{:S(2)}) collective-permute-start(bf16[16,768]{1,0:T(8,128)(2,1)S(1)} %get-tuple-element.89), channel_id=1, source_target_pairs={{0,16},{4,20},{8,24},{12,28},{16,0},{20,4},{24,8},{28,12},{1,17},{... | collective-permute-start | bytes 73736 | tf_op jit(solution)/shard_map/ppermute | solution.py:1361
  20.3 11.8 %collective-permute-start.5 = (bf16[128,512]{1,0:T(8,128)(2,1)S(1)}, bf16[128,512]{1,0:T(8,128)(2,1)S(1)}, u32[]{:S(2)}, u32[]{:S(2)}) collective-permute-start(bf16[128,512]{1,0:T(8,128)(2,1)S(1)} %get-tuple-element.88), channel_id=1, source_target_pairs={{0,16},{4,20},{8,24},{12,28},{16,0},{20,4},{24,8},{28,12},{1,17},{... | collective-permute-start | bytes 393224 | tf_op jit(solution)/shard_map/ppermute | solution.py:1362
  23.5 3.6 %copy-start.5 = (f32[32]{0:T(128)S(1)}, f32[32]{0:T(128)}, u32[]{:S(2)}) copy-start(f32[32]{0:T(128)} %skip_ref.1) | copy-start | bytes 388
  23.9 12.4 %collective-permute-start.10 = (bf16[128,512]{1,0:T(8,128)(2,1)S(1)}, bf16[128,512]{1,0:T(8,128)(2,1)S(1)}, u32[]{:S(2)}, u32[]{:S(2)}) collective-permute-start(bf16[128,512]{1,0:T(8,128)(2,1)S(1)} %get-tuple-element.104), channel_id=1, source_target_pairs={{0,16},{4,20},{8,24},{12,28},{16,0},{20,4},{24,8},{28,12},{1,17},{... | collective-permute-start | bytes 393224 | tf_op jit(solution)/shard_map/ppermute | solution.py:1408
  37.4 6.1 %collective-permute-start.15 = (bf16[544,128]{1,0:T(8,128)(2,1)S(1)}, bf16[544,128]{1,0:T(8,128)(2,1)S(1)}, u32[]{:S(2)}, u32[]{:S(2)}) collective-permute-start(bf16[544,128]{1,0:T(8,128)(2,1)S(1)} %get-tuple-element.142), channel_id=1, source_target_pairs={{0,2},{2,3},{1,0},{3,1},{4,6},{6,7},{5,4},{7,5},{8,10},{10,11},{9,... | collective-permute-start | bytes 417800 | tf_op jit(solution)/shard_map/ppermute | solution.py:1485
  37.7 5.8 %collective-permute-start.14 = (bf16[544,128]{1,0:T(8,128)(2,1)S(1)}, bf16[544,128]{1,0:T(8,128)(2,1)S(1)}, u32[]{:S(2)}, u32[]{:S(2)}) collective-permute-start(bf16[544,128]{1,0:T(8,128)(2,1)S(1)} %get-tuple-element.141.own_ref.kept_ref), channel_id=1, source_target_pairs={{2,1},{1,2},{6,5},{5,6},{10,9},{9,10},{14,13},{13,14},{18,17},{17,... | collective-permute-start | bytes 417800 | tf_op jit(solution)/shard_map/ppermute | solution.py:1484
  42.2 8.5 %collective-permute-start.11 = (bf16[128,512]{1,0:T(8,128)(2,1)S(1)}, bf16[128,512]{1,0:T(8,128)(2,1)S(1)}, u32[]{:S(2)}, u32[]{:S(2)}) collective-permute-start(bf16[128,512]{1,0:T(8,128)(2,1)S(1)} %get-tuple-element.136), channel_id=1, source_target_pairs={{0,12},{4,8},{8,4},{12,0},{16,28},{20,24},{24,20},{28,16},{1,13},{... | collective-permute-start | bytes 393224 | tf_op jit(solution)/shard_map/ppermute | solution.py:1542
  43.5 5.2 %collective-permute-start.16 = (bf16[32,512]{1,0:T(8,128)(2,1)S(1)}, bf16[32,512]{1,0:T(8,128)(2,1)S(1)}, u32[]{:S(2)}, u32[]{:S(2)}) collective-permute-start(bf16[32,512]{1,0:T(8,128)(2,1)S(1)} %shard_map.197.own_ref), channel_id=1, source_target_pairs={{0,16},{4,20},{8,24},{12,28},{16,0},{20,4},{24,8},{28,12},{1,17},{... | collective-permute-start | bytes 98312 | tf_op jit(solution)/shard_map/ppermute | solution.py:1532
  45.8 6.9 %collective-permute-start.12 = (bf16[128,512]{1,0:T(8,128)(2,1)S(1)}, bf16[128,512]{1,0:T(8,128)(2,1)S(1)}, u32[]{:S(2)}, u32[]{:S(2)}) collective-permute-start(bf16[128,512]{1,0:T(8,128)(2,1)S(1)} %get-tuple-element.137), channel_id=1, source_target_pairs={{0,8},{4,12},{8,0},{12,4},{16,24},{20,28},{24,16},{28,20},{1,9},{5... | collective-permute-start | bytes 393224 | tf_op jit(solution)/shard_map/ppermute | solution.py:1542
  45.8 7.2 %collective-permute-start.13 = (bf16[128,512]{1,0:T(8,128)(2,1)S(1)}, bf16[128,512]{1,0:T(8,128)(2,1)S(1)}, u32[]{:S(2)}, u32[]{:S(2)}) collective-permute-start(bf16[128,512]{1,0:T(8,128)(2,1)S(1)} %get-tuple-element.138), channel_id=1, source_target_pairs={{0,4},{4,0},{8,12},{12,8},{16,20},{20,16},{24,28},{28,24},{1,5},{5... | collective-permute-start | bytes 393224 | tf_op jit(solution)/shard_map/ppermute | solution.py:1542
  48.8 6.7 %collective-permute-start.17 = (bf16[96,512]{1,0:T(8,128)(2,1)S(1)}, bf16[96,512]{1,0:T(8,128)(2,1)S(1)}, u32[]{:S(2)}, u32[]{:S(2)}) collective-permute-start(bf16[96,512]{1,0:T(8,128)(2,1)S(1)} %get-tuple-element.145), channel_id=1, source_target_pairs={{0,12},{4,8},{8,4},{12,0},{16,28},{20,24},{24,20},{28,16},{1,13},{... | collective-permute-start | bytes 294920 | tf_op jit(solution)/shard_map/ppermute | solution.py:1552
  50.7 6.3 %collective-permute-start.18 = (bf16[96,512]{1,0:T(8,128)(2,1)S(1)}, bf16[96,512]{1,0:T(8,128)(2,1)S(1)}, u32[]{:S(2)}, u32[]{:S(2)}) collective-permute-start(bf16[96,512]{1,0:T(8,128)(2,1)S(1)} %get-tuple-element.146), channel_id=1, source_target_pairs={{0,8},{4,12},{8,0},{12,4},{16,24},{20,28},{24,16},{28,20},{1,9},{5... | collective-permute-start | bytes 294920 | tf_op jit(solution)/shard_map/ppermute | solution.py:1552
  50.7 6.5 %collective-permute-start.19 = (bf16[96,512]{1,0:T(8,128)(2,1)S(1)}, bf16[96,512]{1,0:T(8,128)(2,1)S(1)}, u32[]{:S(2)}, u32[]{:S(2)}) collective-permute-start(bf16[96,512]{1,0:T(8,128)(2,1)S(1)} %get-tuple-element.147), channel_id=1, source_target_pairs={{0,4},{4,0},{8,12},{12,8},{16,20},{20,16},{24,28},{28,24},{1,5},{5... | collective-permute-start | bytes 294920 | tf_op jit(solution)/shard_map/ppermute | solution.py:1552
